TPU v7x, 32 devices: a whole 2x2x4 slice. The times are simulated.
32 devices in a mesh: row: 8 (over z, y), col: 4 (over x, core).
Axes of the slice: x: 2, y: 2, z: 4, core: 2. Of those that a mesh axis runs over, the one named last changes fastest.
Arguments:
- object_field: float32 [2, 4096, 2048], P(None, 'row', 'col'), may hold values from -6 to 6
- probe: float32 [2, 256, 256], replicated, may hold values from -6 to 6
- amplitudes: bfloat16 [8, 4, 2, 2, 256, 256], P('row', 'col'), may hold values from 0.29882812 to 6
- offsets: int32 [8, 4, 2, 2, 2], P('row', 'col'), may hold values from 0 to 511, as said below
Outputs:
- object_out: float32 [2, 4096, 2048], P(None, 'row', 'col')
- probe_out: float32 [2, 256, 256], replicated
Inputs may be any that keep to these rules, and one draw needn't show every extreme that they name: `offsets`: every window lies inside the object of 4096 x 2048 cells.
All inputs are finite; a program needn't handle non-finite values.
Results may differ from a plain program's by a relative error of at most 0.0003.
Values sent between devices are 32-bit elements; how exact they have to be, the bound alone decides.
No kernel may reach another device: no remote copies, remote signals or barrier semaphores. Data moves between devices by JAX's collectives and lax.ppermute only.
A program may use at most 192 MiB of HBM per device.

v0:
```python
import math

import jax
import jax.numpy as jnp
from jax import lax
from jax.sharding import PartitionSpec as P

softening = 0.1
object_damping = 0.5
probe_damping = 1.0


def shifted(array, axis, by):
    peers = lax.axis_size(axis)
    pairs = [(i, i + by) for i in range(peers) if 0 <= i + by < peers]
    return lax.ppermute(array, axis, pairs)


def dft_tables(length):
    index_rows = lax.broadcasted_iota(jnp.int32, (length, length), 0)
    index_cols = lax.broadcasted_iota(jnp.int32, (length, length), 1)
    phase = (index_rows * index_cols % length).astype(jnp.float32) * (2.0 * math.pi / length)
    factor = 1.0 / math.sqrt(length)
    return (jnp.cos(phase) * factor, jnp.sin(phase) * factor)


def left_apply(table, stacked):
    return jnp.einsum("mn,bnk->bmk", table, stacked, precision=lax.Precision.HIGHEST)


def right_apply(stacked, table):
    return jnp.einsum("bmn,nk->bmk", stacked, table, precision=lax.Precision.HIGHEST)


def transform(real_part, imag_part, cosine, sine, direction):
    mid_real = left_apply(cosine, real_part) + direction * left_apply(sine, imag_part)
    mid_imag = left_apply(cosine, imag_part) - direction * left_apply(sine, real_part)
    out_real = right_apply(mid_real, cosine) + direction * right_apply(mid_imag, sine)
    out_imag = right_apply(mid_imag, cosine) - direction * right_apply(mid_real, sine)
    return (out_real, out_imag)


def place_sum(accumulator, pieces, corners):
    piece_shape = pieces.shape[1:]

    def add_piece(number, running):
        anchor = (jnp.int32(0), corners[number, 0], corners[number, 1])
        present = lax.dynamic_slice(running, anchor, piece_shape)
        return lax.dynamic_update_slice(running, present + pieces[number], anchor)

    return lax.fori_loop(0, pieces.shape[0], add_piece, accumulator)


def local(object_field, probe, amplitudes, offsets):
    window = probe.shape[1]
    tile_rows = object_field.shape[1]
    tile_cols = object_field.shape[2]
    cosine, sine = dft_tables(window)
    own_offsets = offsets[0, 0]
    measured_all = amplitudes[0, 0]
    current_object = object_field
    current_probe = probe
    for sweep in range(own_offsets.shape[0]):
        right_cells = shifted(current_object[:, :, :window], "col", -1)
        widened = jnp.concatenate([current_object, right_cells], axis=2)
        lower_cells = shifted(widened[:, :window, :], "row", -1)
        extended = jnp.concatenate([widened, lower_cells], axis=1)
        corners = own_offsets[sweep]
        patches = jax.vmap(
            lambda corner: lax.dynamic_slice(
                extended, (jnp.int32(0), corner[0], corner[1]), (2, window, window)
            )
        )(corners)
        patch_real = patches[:, 0]
        patch_imag = patches[:, 1]
        probe_real = current_probe[0]
        probe_imag = current_probe[1]
        wave_real = probe_real * patch_real - probe_imag * patch_imag
        wave_imag = probe_real * patch_imag + probe_imag * patch_real
        far_real, far_imag = transform(wave_real, wave_imag, cosine, sine, 1.0)
        scaled = measured_all[sweep].astype(jnp.float32) * lax.rsqrt(
            far_real * far_real + far_imag * far_imag + softening
        )
        back_real, back_imag = transform(far_real * scaled, far_imag * scaled, cosine, sine, -1.0)
        diff_real = back_real - wave_real
        diff_imag = back_imag - wave_imag
        object_real = probe_real * diff_real + probe_imag * diff_imag
        object_imag = probe_real * diff_imag - probe_imag * diff_real
        intensity = probe_real * probe_real + probe_imag * probe_imag
        probe_num = jnp.stack(
            [
                jnp.sum(patch_real * diff_real + patch_imag * diff_imag, axis=0),
                jnp.sum(patch_real * diff_imag - patch_imag * diff_real, axis=0),
            ]
        )
        probe_den = jnp.sum(patch_real * patch_real + patch_imag * patch_imag, axis=0)
        height = tile_rows + window
        breadth = tile_cols + window
        spread = jnp.broadcast_to(intensity[None], object_real.shape)
        object_terms = jnp.stack([object_real, object_imag, spread], axis=1)
        accumulator = place_sum(jnp.zeros((3, height, breadth), jnp.float32), object_terms, corners)
        from_upper = shifted(accumulator[:, tile_rows:, :], "row", 1)
        merged = accumulator[:, :tile_rows, :].at[:, :window, :].add(from_upper)
        from_left = shifted(merged[:, :, tile_cols:], "col", 1)
        combined = merged[:, :, :tile_cols].at[:, :, :window].add(from_left)
        numerator = combined[:2]
        denominator = combined[2]
        new_object = current_object + numerator / (denominator + object_damping)[None]
        total_num, total_den = lax.psum((probe_num, probe_den), ("row", "col"))
        current_probe = current_probe + total_num / (total_den + probe_damping)[None]
        current_object = new_object
    return (current_object, current_probe)


def solution(mesh):
    placed = (
        P(None, "row", "col"),
        P(),
        P("row", "col", None, None, None, None),
        P("row", "col", None, None, None),
    )
    return jax.shard_map(
        local, mesh=mesh, in_specs=placed, out_specs=(P(None, "row", "col"), P()), check_vma=False
    )
```

profile of v0, /device:TPU:0, one launch (start us, length us, event | category | flops | bytes accessed | tf_op | source)
XLA Modules:
  0.0 653.3 jit_solution(11050811889432547860)
XLA Ops:
  10.2 3.0 collective-permute-done
  17.7 27.4 %collective-permute-done.1 = f32[2,256,768]{2,1,0:T(8,128)S(1)} collective-permute-done((f32[2,256,768]{2,1,0:T(8,128)}, f32[2,256,768]{2,1,0:T(8,128)S(1)}, u32[]{:S(2)}, u32[]{:S(2)}) %collective-permute-start.1) | collective-permute-done | bytes 1572896 | tf_op jit(solution)/shard_map/ppermute | solution.py:16
  45.2 4.3 pad_maximum_fusion
  49.6 6.5 while.34
  50.2 2.6 bitcast_dynamic-update-slice_fusion.4
  53.5 2.6 bitcast_dynamic-update-slice_fusion.4
  84.9 3.0 fusion.37
  89.2 3.4 broadcast.124.clone
  92.6 29.6 %while.32 = (s32[]{:T(128)}, f32[3,768,768]{2,1,0:T(8,128)}, s32[2,2]{1,0:T(2,128)S(1)}, f32[2,3,256,256]{3,2,0,1:T(8,128)}, s32[]{:T(128)}, /*index=5*/s32[]{:T(128)}, s32[]{:T(128)}) while((s32[]{:T(128)}, f32[3,768,768]{2,1,0:T(8,128)}, s32[2,2]{1,0:T(2,128)S(1)}, f32[2,3,256,256]{3,2,0,1:T(8,128)}, s32[]{:T(128)}, /*index=5*/s32[]{:T(128)}, ...), condition=%wide.region_1.2_spmd, body=%wide.region_0.1_spmd.sunk | while | flops 196616 | bytes 3932341 | solution.py:51
  99.0 8.5 %dynamic_update_slice.16 = f32[3,768,768]{2,1,0:T(8,128)} dynamic-update-slice(f32[3,768,768]{2,1,0:T(8,128)} %get-tuple-element.449, f32[3,256,256]{2,1,0:T(8,128)S(1)} %bitcast_add_fusion.4, s32[]{:T(128)} %constant.171.clone.1..sunk, s32[]{:T(128)S(6)} %select_n.253, s32[]{:T(128)S(6)} %select_n.254) | dynamic-update-slice | bytes 1572868 | tf_op jit(solution)/shard_map/while/body/eval_jaxpr/dynamic_update_slice | solution.py:49
  113.9 8.4 %dynamic_update_slice.16 = f32[3,768,768]{2,1,0:T(8,128)} dynamic-update-slice(f32[3,768,768]{2,1,0:T(8,128)} %get-tuple-element.449, f32[3,256,256]{2,1,0:T(8,128)S(1)} %bitcast_add_fusion.4, s32[]{:T(128)} %constant.171.clone.1..sunk, s32[]{:T(128)S(6)} %select_n.253, s32[]{:T(128)S(6)} %select_n.254) | dynamic-update-slice | bytes 1572868 | tf_op jit(solution)/shard_map/while/body/eval_jaxpr/dynamic_update_slice | solution.py:49
  124.1 6.9 %collective-permute-start.2 = (f32[3,256,768]{2,1,0:T(8,128)S(1)}, f32[3,256,768]{2,1,0:T(8,128)S(1)}, u32[]{:S(2)}, u32[]{:S(2)}) collective-permute-start(f32[3,256,768]{2,1,0:T(8,128)S(1)} %slice.212), channel_id=1, source_target_pairs={{0,4},{4,8},{8,12},{12,16},{16,20},{20,24},{24,28},{1,5},{5,9},{9,... | collective-permute-start | bytes 7077896 | tf_op jit(solution)/shard_map/ppermute | solution.py:16
  131.1 2.6 slice.210
  133.7 39.0 %collective-permute-done.2 = f32[3,256,768]{2,1,0:T(8,128)S(1)} collective-permute-done((f32[3,256,768]{2,1,0:T(8,128)S(1)}, f32[3,256,768]{2,1,0:T(8,128)S(1)}, u32[]{:S(2)}, u32[]{:S(2)}) %collective-permute-start.2) | collective-permute-done | bytes 2359328 | tf_op jit(solution)/shard_map/ppermute | solution.py:16
  174.8 12.0 %collective-permute-start.3 = (f32[3,512,256]{2,1,0:T(8,128)S(1)}, f32[3,512,256]{2,1,0:T(8,128)S(1)}, u32[]{:S(2)}, u32[]{:S(2)}) collective-permute-start(f32[3,512,256]{2,1,0:T(8,128)S(1)} %slice.269), channel_id=1, source_target_pairs={{0,1},{1,2},{2,3},{4,5},{5,6},{6,7},{8,9},{9,10},{10,11},{12,13},{... | collective-permute-start | bytes 4718600 | tf_op jit(solution)/shard_map/ppermute | solution.py:16
  187.2 2.4 collective-permute-done.3
  192.3 17.1 %collective-permute-done.4 = f32[2,512,256]{2,1,0:T(8,128)S(1)} collective-permute-done((f32[2,512,256]{2,1,0:T(8,128)S(1)}, f32[2,512,256]{2,1,0:T(8,128)S(1)}, u32[]{:S(2)}, u32[]{:S(2)}) %collective-permute-start.4) | collective-permute-done | bytes 1048608 | tf_op jit(solution)/shard_map/ppermute | solution.py:16
  213.1 145.2 %all-reduce.7.cloned.1.call-done = (f32[2,256,256]{2,1,0:T(8,128)}, f32[256,256]{1,0:T(8,128)}) async-done(((f32[2,256,256]{2,1,0:T(8,128)}, f32[256,256]{1,0:T(8,128)}), (f32[2,256,256]{2,1,0:T(8,128)}, f32[256,256]{1,0:T(8,128)})) %all-reduce.7.cloned.1.call-update) | async-done | bytes 786448 | tf_op jit(solution)/shard_map/psum | solution.py:109
  360.6 4.0 pad_maximum_fusion.1
  365.7 8.7 %while.35 = (s32[]{:T(128)}, f32[2,768,768]{2,1,0:T(8,128)}, s32[2,3]{1,0:T(2,128)S(1)}, f32[2,2,256,256]{3,2,0,1:T(8,128)}, s32[]{:T(128)}) while((s32[]{:T(128)}, f32[2,768,768]{2,1,0:T(8,128)}, s32[2,3]{1,0:T(2,128)S(1)}, f32[2,2,256,256]{3,2,0,1:T(8,128)}, s32[]{:T(128)}) %tuple.133), condition=%wide.while_cond.5, body=%wide.while_body.5.sunk | while | flops 2 | bytes 1050217 | solution.py:70
  366.3 3.5 bitcast_dynamic-update-slice_fusion.5
  370.5 3.5 bitcast_dynamic-update-slice_fusion.5
  404.2 3.0 fusion.29
  408.5 3.4 broadcast.124
  411.9 32.2 %while.33 = (s32[]{:T(128)}, f32[3,768,768]{2,1,0:T(8,128)}, s32[2,2]{1,0:T(2,128)S(1)}, f32[2,3,256,256]{3,2,0,1:T(8,128)}, s32[]{:T(128)}, /*index=5*/s32[]{:T(128)}, s32[]{:T(128)}) while((s32[]{:T(128)}, f32[3,768,768]{2,1,0:T(8,128)}, s32[2,2]{1,0:T(2,128)S(1)}, f32[2,3,256,256]{3,2,0,1:T(8,128)}, s32[]{:T(128)}, /*index=5*/s32[]{:T(128)}, ...), condition=%wide.region_8.9_spmd, body=%wide.region_7.8_spmd.sunk | while | flops 196616 | bytes 3932341 | solution.py:51
  418.5 9.5 %dynamic_update_slice.17 = f32[3,768,768]{2,1,0:T(8,128)} dynamic-update-slice(f32[3,768,768]{2,1,0:T(8,128)} %get-tuple-element.485, f32[3,256,256]{2,1,0:T(8,128)S(1)} %bitcast_add_fusion.5, s32[]{:T(128)} %constant.171.clone.1..sunk.1, s32[]{:T(128)S(6)} %select_n.255, s32[]{:T(128)S(6)} %select_n.256) | dynamic-update-slice | bytes 1572868 | tf_op jit(solution)/shard_map/while/body/eval_jaxpr/dynamic_update_slice | solution.py:49
  434.6 9.6 %dynamic_update_slice.17 = f32[3,768,768]{2,1,0:T(8,128)} dynamic-update-slice(f32[3,768,768]{2,1,0:T(8,128)} %get-tuple-element.485, f32[3,256,256]{2,1,0:T(8,128)S(1)} %bitcast_add_fusion.5, s32[]{:T(128)} %constant.171.clone.1..sunk.1, s32[]{:T(128)S(6)} %select_n.255, s32[]{:T(128)S(6)} %select_n.256) | dynamic-update-slice | bytes 1572868 | tf_op jit(solution)/shard_map/while/body/eval_jaxpr/dynamic_update_slice | solution.py:49
  446.0 2.5 collective-permute-start.6
  448.5 2.6 slice.228
  451.2 47.7 %collective-permute-done.6 = f32[3,256,768]{2,1,0:T(8,128)S(1)} collective-permute-done((f32[3,256,768]{2,1,0:T(8,128)S(1)}, f32[3,256,768]{2,1,0:T(8,128)S(1)}, u32[]{:S(2)}, u32[]{:S(2)}) %collective-permute-start.6) | collective-permute-done | bytes 2359328 | tf_op jit(solution)/shard_map/ppermute | solution.py:16
  504.2 2.5 collective-permute-start.7
  507.5 129.3 %all-reduce.5.cloned.1.call-done = (f32[2,256,256]{2,1,0:T(8,128)}, f32[256,256]{1,0:T(8,128)}) async-done(((f32[2,256,256]{2,1,0:T(8,128)}, f32[256,256]{1,0:T(8,128)}), (f32[2,256,256]{2,1,0:T(8,128)}, f32[256,256]{1,0:T(8,128)})) %all-reduce.5.cloned.1.call-update) | async-done | bytes 786448 | tf_op jit(solution)/shard_map/psum | solution.py:109
  (128 shorter events, 112.1 us)
Async XLA Ops:
  7.2 2.8 copy-start.2
  7.2 351.2 %all-reduce.7.cloned.1.call-start = ((), (), s32[]{:S(2)}) async-start(), calls=%async_computation.1 | async-start | bytes 1572864 | tf_op jit(solution)/shard_map/psum | solution.py:109
  8.7 4.6 collective-permute-start
  10.1 7.3 %copy-start.12 = (s32[1,1,2,2,2]{4,3,2,1,0:T(2,128)S(1)}, s32[1,1,2,2,2]{4,3,2,1,0:T(2,128)}, u32[]{:S(2)}) copy-start(s32[1,1,2,2,2]{4,3,2,1,0:T(2,128)} %param.19) | copy-start | bytes 100
  10.2 7.5 %copy-start.5 = (f32[2,256,256]{2,1,0:T(8,128)S(1)}, f32[2,256,256]{2,1,0:T(8,128)}, u32[]{:S(2)}) copy-start(f32[2,256,256]{2,1,0:T(8,128)} %param.17) | copy-start | bytes 1572868
  13.3 1.6 copy-start.1
  16.2 29.0 %collective-permute-start.1 = (f32[2,256,768]{2,1,0:T(8,128)}, f32[2,256,768]{2,1,0:T(8,128)S(1)}, u32[]{:S(2)}, u32[]{:S(2)}) collective-permute-start(f32[2,256,768]{2,1,0:T(8,128)} %slice.266), channel_id=1, source_target_pairs={{4,0},{8,4},{12,8},{16,12},{20,16},{24,20},{28,24},{5,1},{9,5},{13... | collective-permute-start | bytes 4718600 | tf_op jit(solution)/shard_map/ppermute | solution.py:16
  65.4 5.9 copy-start.13
  124.1 48.6 %collective-permute-start.2 = (f32[3,256,768]{2,1,0:T(8,128)S(1)}, f32[3,256,768]{2,1,0:T(8,128)S(1)}, u32[]{:S(2)}, u32[]{:S(2)}) collective-permute-start(f32[3,256,768]{2,1,0:T(8,128)S(1)} %slice.212), channel_id=1, source_target_pairs={{0,4},{4,8},{8,12},{12,16},{16,20},{20,24},{24,28},{1,5},{5,9},{9,... | collective-permute-start | bytes 7077896 | tf_op jit(solution)/shard_map/ppermute | solution.py:16
  174.8 14.9 %collective-permute-start.3 = (f32[3,512,256]{2,1,0:T(8,128)S(1)}, f32[3,512,256]{2,1,0:T(8,128)S(1)}, u32[]{:S(2)}, u32[]{:S(2)}) collective-permute-start(f32[3,512,256]{2,1,0:T(8,128)S(1)} %slice.269), channel_id=1, source_target_pairs={{0,1},{1,2},{2,3},{4,5},{5,6},{6,7},{8,9},{9,10},{10,11},{12,13},{... | collective-permute-start | bytes 4718600 | tf_op jit(solution)/shard_map/ppermute | solution.py:16
  187.2 2.9 copy-start.3
  190.8 21.4 %copy-start.8 = (f32[256,256]{1,0:T(8,128)S(1)}, f32[256,256]{1,0:T(8,128)}, u32[]{:S(2)}) copy-start(f32[256,256]{1,0:T(8,128)} %get-tuple-element.236) | copy-start | bytes 786436
  190.8 21.4 %copy-start.9 = (f32[256,256]{1,0:T(8,128)S(1)}, f32[256,256]{1,0:T(8,128)}, u32[]{:S(2)}) copy-start(f32[256,256]{1,0:T(8,128)} %get-tuple-element.237) | copy-start | bytes 786436
  190.8 18.5 %collective-permute-start.4 = (f32[2,512,256]{2,1,0:T(8,128)S(1)}, f32[2,512,256]{2,1,0:T(8,128)S(1)}, u32[]{:S(2)}, u32[]{:S(2)}) collective-permute-start(f32[2,512,256]{2,1,0:T(8,128)S(1)} %slice.273), channel_id=1, source_target_pairs={{1,0},{2,1},{3,2},{5,4},{6,5},{7,6},{9,8},{10,9},{11,10},{13,12},{... | collective-permute-start | bytes 3145736 | tf_op jit(solution)/shard_map/ppermute | solution.py:16
  209.4 1.5 copy-start.6
  210.9 149.7 %collective-permute-start.5 = (f32[2,256,768]{2,1,0:T(8,128)}, f32[2,256,768]{2,1,0:T(8,128)}, u32[]{:S(2)}, u32[]{:S(2)}) collective-permute-start(f32[2,256,768]{2,1,0:T(8,128)} %pad_maximum_fusion.2), channel_id=1, source_target_pairs={{4,0},{8,4},{12,8},{16,12},{20,16},{24,20},{28,24},{5,1},{9,5},{13... | collective-permute-start | bytes 4718600 | tf_op jit(solution)/shard_map/ppermute | solution.py:16
  213.0 423.8 %all-reduce.5.cloned.1.call-start = ((), (), s32[]{:S(2)}) async-start(), calls=%async_computation | async-start | bytes 1572864 | tf_op jit(solution)/shard_map/psum | solution.py:109
  358.3 2.3 copy-start.7
  384.8 5.7 copy-start.14
  398.4 5.8 copy-start.4
  446.0 52.9 %collective-permute-start.6 = (f32[3,256,768]{2,1,0:T(8,128)S(1)}, f32[3,256,768]{2,1,0:T(8,128)S(1)}, u32[]{:S(2)}, u32[]{:S(2)}) collective-permute-start(f32[3,256,768]{2,1,0:T(8,128)S(1)} %slice.230), channel_id=1, source_target_pairs={{0,4},{4,8},{8,12},{12,16},{16,20},{20,24},{24,28},{1,5},{5,9},{9,... | collective-permute-start | bytes 7077896 | tf_op jit(solution)/shard_map/ppermute | solution.py:16
  500.8 2.1 copy-start
  502.9 3.7 copy-start.10
  502.9 3.7 copy-start.11
  504.2 137.7 %collective-permute-start.7 = (f32[3,512,256]{2,1,0:T(8,128)}, f32[3,512,256]{2,1,0:T(8,128)}, u32[]{:S(2)}, u32[]{:S(2)}) collective-permute-start(f32[3,512,256]{2,1,0:T(8,128)} %slice.277), channel_id=1, source_target_pairs={{0,1},{1,2},{2,3},{4,5},{5,6},{6,7},{8,9},{9,10},{10,11},{12,13},{... | collective-permute-start | bytes 4718600 | tf_op jit(solution)/shard_map/ppermute | solution.py:16
Sparse Core Ops, SparseCore 0:
  213.2 145.1 all-reduce.6
  507.6 129.1 all-reduce.4
where the time goes:
time: 665 us; the launch traced here: 653 us
  waiting for transfers between devices  411 us (62%)
  local copies, waits for them, and re-layouts  81.5 us (12%)
  matrix products  62.9 us (9%)
  other arithmetic  37 us (6%)
  starting transfers between devices  29.3 us (4%)
  loops' own time  16.4 us (2%)
  between operations  15.1 us (2%)
    psum x2, waiting for transfers between devices, local(): total_num, total_den = lax.psum((probe_num, probe_den), ('row', 'col'))  275 us
    ppermute x8, waiting for transfers between devices, shifted(): return lax.ppermute(array, axis, pairs)  137 us
    dynamic_update_slice x4, local copies, waits for them, and re-layouts, add_piece(): return lax.dynamic_update_slice(running, present + pieces[number], anchor)  36 us
    dot_general x16, matrix products, right_apply(): jnp.einsum('bmn,nk->bmk', stacked, table, precision=lax.Precision.HIGHEST)  32.6 us
    dot_general x16, matrix products, left_apply(): jnp.einsum('mn,bnk->bmk', table, stacked, precision=lax.Precision.HIGHEST)  30.2 us
    ppermute x8, starting transfers between devices, shifted(): return lax.ppermute(array, axis, pairs)  29.2 us
    another operation x2, loops' own time, place_sum(): return lax.fori_loop(0, pieces.shape[0], add_piece, accumulator)  15.9 us
    gather x12, local copies, waits for them, and re-layouts  14.8 us
  transfers between devices with their start and end apart: 10, of which 8 were waited for; matrix products, arithmetic and copies ran while one was open for 2% of the time, Pallas kernels for 0%

commit v1 on v0

v1 whole, which is shorter than its diff:
```python
import functools
import math

import jax
import jax.numpy as jnp
import ml_dtypes
import numpy as np
from jax import lax
from jax.experimental import pallas as pl
from jax.experimental.pallas import tpu as pltpu
from jax.sharding import PartitionSpec as P

softening = 0.1
object_damping = 0.5
probe_damping = 1.0
MIB = 1 << 20
lane = 128
VMEM = pltpu.VMEM
SMEM = pltpu.SMEM


def shifted(array, axis, by):
    peers = lax.axis_size(axis)
    pairs = [(i, i + by) for i in range(peers) if 0 <= i + by < peers]
    return lax.ppermute(array, axis, pairs)


def swapped(array, axis, mask):
    peers = lax.axis_size(axis)
    return lax.ppermute(array, axis, [(i, i ^ mask) for i in range(peers)])


def handed_on(array, axis):
    peers = lax.axis_size(axis)
    pairs = [(i, i + 2 - 4 * (i % 2)) for i in range(peers)]
    return lax.ppermute(array, axis, [(i, k) for i, k in pairs if 0 <= k < peers])


def dft_tables(length):
    index = np.arange(length)
    phase = (index[:, None] * index[None, :] % length) * (2.0 * math.pi / length)
    cosine = np.cos(phase) / math.sqrt(length)
    sine = np.sin(phase) / math.sqrt(length)
    full = np.block([[cosine, -sine], [sine, cosine]])
    high = full.astype(ml_dtypes.bfloat16)
    low = (full - high.astype(np.float64)).astype(ml_dtypes.bfloat16)
    return high, low, np.ascontiguousarray(high.T), np.ascontiguousarray(low.T)


def halves(value):
    high = value.astype(jnp.bfloat16)
    return high, (value - high.astype(jnp.float32)).astype(jnp.bfloat16)


def product(a, b):
    return jnp.dot(a, b, preferred_element_type=jnp.float32)


def left_product(high, low, real, imag):
    side = real.shape[0]
    real_high, real_low = halves(real)
    imag_high, imag_low = halves(imag)
    top = jnp.concatenate([real_high, imag_high], axis=0)
    rest = jnp.concatenate([real_low, imag_low], axis=0)
    out = product(high, top) + product(high, rest) + product(low, top)
    return out[:side], out[side:]


def right_product(real, imag, high, low):
    side = real.shape[1]
    real_high, real_low = halves(real)
    imag_high, imag_low = halves(imag)
    top = jnp.concatenate([real_high, imag_high], axis=1)
    rest = jnp.concatenate([real_low, imag_low], axis=1)
    out = product(top, high) + product(rest, high) + product(top, low)
    return out[:, :side], out[:, side:]


def split_column(column):
    return lax.div(column, lane), lax.rem(column, lane)


def taken(ref, plane, row, column, side):
    first, shift = split_column(column)
    count = side // lane + 1
    slabs = [ref[plane, first + k, pl.ds(row, side), :] for k in range(count)]
    return pltpu.roll(jnp.concatenate(slabs, axis=1), count * lane - shift, 1)[:, :side]


def turned(value, shift):
    side = value.shape[0]
    wide = jnp.concatenate([value, jnp.zeros((side, lane), jnp.float32)], axis=1)
    return pltpu.roll(wide, shift, 1)


def add_slabs(ref, lead, row, first, wide):
    side = wide.shape[0]
    for k in range(wide.shape[1] // lane):
        spot = lead + (first + k, pl.ds(row, side), slice(None))
        ref[spot] += wide[:, k * lane : (k + 1) * lane]


def columns(number):
    return slice(number * lane, (number + 1) * lane)


def scan_kernel(
    sweep, pieces, offsets_ref, probe_ref, amplitude_ref, ah_ref, al_ref, bh_ref, bl_ref, *refs
):
    if pieces:
        own_ref, right_ref, lower_ref, corner_ref = refs[:4]
        terms_refs, sums_ref, field_ref = refs[4:6], refs[6], refs[7]
        rows, cols = own_ref.shape[1:]
        slabs = cols // lane
        for plane in range(2):
            for k in range(slabs):
                field_ref[plane, k, :rows] = own_ref[plane, :, columns(k)]
                field_ref[plane, k, rows:] = lower_ref[plane, :, columns(k)]
            for k in range(right_ref.shape[2] // lane):
                field_ref[plane, slabs + k, :rows] = right_ref[plane, :, columns(k)]
                field_ref[plane, slabs + k, rows:] = corner_ref[plane, :, columns(k)]
    else:
        field_ref = refs[0]
        terms_refs, sums_ref = refs[1:3], refs[3]
    side = probe_ref.shape[1]
    probe_real, probe_imag = probe_ref[0], probe_ref[1]
    for scan in range(2):
        place = ((4 * 2 + sweep) * 2 + scan) * 2
        row, column = offsets_ref[place], offsets_ref[place + 1]
        patch_real = taken(field_ref, 0, row, column, side)
        patch_imag = taken(field_ref, 1, row, column, side)
        wave_real = probe_real * patch_real - probe_imag * patch_imag
        wave_imag = probe_real * patch_imag + probe_imag * patch_real
        mid = left_product(bh_ref[...], bl_ref[...], wave_real, wave_imag)
        far_real, far_imag = right_product(*mid, ah_ref[...], al_ref[...])
        scale = amplitude_ref[scan].astype(jnp.float32) * lax.rsqrt(
            far_real * far_real + far_imag * far_imag + softening
        )
        mid = left_product(ah_ref[...], al_ref[...], far_real * scale, far_imag * scale)
        back_real, back_imag = right_product(*mid, bh_ref[...], bl_ref[...])
        diff_real = back_real - wave_real
        diff_imag = back_imag - wave_imag
        terms_refs[scan][0] = probe_real * diff_real + probe_imag * diff_imag
        terms_refs[scan][1] = probe_real * diff_imag - probe_imag * diff_real
        sums = (
            patch_real * diff_real + patch_imag * diff_imag,
            patch_real * diff_imag - patch_imag * diff_real,
            patch_real * patch_real + patch_imag * patch_imag,
        )
        for number, value in enumerate(sums):
            if scan == 0:
                sums_ref[number] = value
            else:
                sums_ref[number] += value


def scan_step(sweep, offsets, probe, amplitudes, tables, *field):
    side = probe.shape[1]
    pieces = len(field) == 4
    shapes = [jax.ShapeDtypeStruct((2, side, side), jnp.float32)] * 2
    shapes.append(jax.ShapeDtypeStruct((3, side, side), jnp.float32))
    if pieces:
        rows, cols = field[0].shape[1:]
        shapes.append(jax.ShapeDtypeStruct((2, (cols + side) // lane, rows + side, lane), jnp.float32))
    return pl.pallas_call(
        functools.partial(scan_kernel, sweep, pieces),
        out_shape=shapes,
        in_specs=[pl.BlockSpec(memory_space=SMEM)] + [pl.BlockSpec(memory_space=VMEM)] * (6 + len(field)),
        out_specs=[pl.BlockSpec(memory_space=VMEM)] * len(shapes),
        compiler_params=pltpu.CompilerParams(vmem_limit_bytes=40 * MIB),
        name="scan",
    )(offsets, probe, amplitudes, *tables, *field)


def density_kernel(sweep, reach, offsets_ref, probe_ref, out_ref, total_ref):
    side = probe_ref.shape[1]
    slabs, height = out_ref.shape[:2]
    breadth = slabs * lane
    tile = height - side if reach else height
    span = breadth - side if reach else breadth
    total_ref[...] = jnp.zeros_like(total_ref)
    power = probe_ref[0] * probe_ref[0] + probe_ref[1] * probe_ref[1]
    steps = (-1, 0, 1) if reach else (-1, 0)
    for down in steps:
        for along in steps:
            for scan in range(2):
                place = ((((down + 1) * 3 + along + 1) * 2 + sweep) * 2 + scan) * 2
                row = offsets_ref[place] + side + down * tile
                column = offsets_ref[place + 1] + side + along * span

                @pl.when((row > 0) & (row < side + height) & (column > 0) & (column < side + breadth))
                def _():
                    first, shift = split_column(column)
                    add_slabs(total_ref, (), row, first, turned(power, shift))

    out_ref[...] = total_ref[side // lane : side // lane + slabs, side : side + height]


def density(sweep, reach, offsets, probe, tile):
    side = probe.shape[1]
    extra = side if reach else 0
    height, slabs = tile[0] + extra, (tile[1] + extra) // lane
    return pl.pallas_call(
        functools.partial(density_kernel, sweep, reach),
        out_shape=jax.ShapeDtypeStruct((slabs, height, lane), jnp.float32),
        in_specs=[pl.BlockSpec(memory_space=SMEM), pl.BlockSpec(memory_space=VMEM)],
        out_specs=pl.BlockSpec(memory_space=VMEM),
        scratch_shapes=[VMEM((slabs + 2 * side // lane + 1, height + 2 * side, lane), jnp.float32)],
        compiler_params=pltpu.CompilerParams(vmem_limit_bytes=24 * MIB),
        name="density",
    )(offsets, probe)


def add_windows(total_ref, offsets_ref, sweep, down, tile, side, limit, terms):
    for scan in range(2):
        place = ((((down + 1) * 3 + 1) * 2 + sweep) * 2 + scan) * 2
        row = offsets_ref[place] + side + down * tile
        first, shift = split_column(offsets_ref[place + 1])

        @pl.when((row > 0) & (row < side + limit))
        def _():
            for plane in range(2):
                add_slabs(total_ref, (plane,), row, first, turned(terms[scan][plane], shift))


def gather_kernel(sweep, tile, parity_ref, offsets_ref, *refs):
    own, partner, passed = refs[0:2], refs[2:4], refs[4:6]
    out_ref, left_ref, right_ref, total_ref = refs[6:]
    slabs, height = out_ref.shape[1:3]
    edge = left_ref.shape[1]
    side = edge * lane
    total_ref[...] = jnp.zeros_like(total_ref)
    odd = parity_ref[0] == 1
    add_windows(total_ref, offsets_ref, sweep, 0, tile, side, height, own)

    @pl.when(odd)
    def _():
        add_windows(total_ref, offsets_ref, sweep, -1, tile, side, height, partner)
        add_windows(total_ref, offsets_ref, sweep, 1, tile, side, height, passed)

    @pl.when(jnp.logical_not(odd))
    def _():
        add_windows(total_ref, offsets_ref, sweep, 1, tile, side, height, partner)
        add_windows(total_ref, offsets_ref, sweep, -1, tile, side, height, passed)

    out_ref[...] = total_ref[:, :, side : side + height]
    left_ref[...] = total_ref[:, :edge, side : side + height]
    right_ref[...] = total_ref[:, slabs - edge :, side : side + height]


def gather_all(sweep, parity, offsets, own, partner, passed, tile):
    side = own[0].shape[2]
    height, slabs = tile[0] + side, (tile[1] + side) // lane
    edge = jax.ShapeDtypeStruct((2, side // lane, height, lane), jnp.float32)
    return pl.pallas_call(
        functools.partial(gather_kernel, sweep, tile[0]),
        out_shape=[jax.ShapeDtypeStruct((2, slabs, height, lane), jnp.float32), edge, edge],
        in_specs=[pl.BlockSpec(memory_space=SMEM)] * 2 + [pl.BlockSpec(memory_space=VMEM)] * 6,
        out_specs=[pl.BlockSpec(memory_space=VMEM)] * 3,
        scratch_shapes=[VMEM((2, slabs, height + 2 * side, lane), jnp.float32)],
        compiler_params=pltpu.CompilerParams(vmem_limit_bytes=40 * MIB),
        name="gather",
    )(parity, offsets, *own, *partner, *passed)


def renew_kernel(field_ref, density_ref, terms_ref, left_ref, right_ref, out_ref):
    slabs = field_ref.shape[1]
    edge = left_ref.shape[1]
    for k in range(slabs):
        part = 1.0 / (density_ref[k] + object_damping)
        for plane in range(2):
            terms = terms_ref[plane, k]
            if k < edge:
                terms += left_ref[plane, k]
            if k >= slabs - edge:
                terms += right_ref[plane, k - (slabs - edge)]
            out_ref[plane, k] = field_ref[plane, k] + terms * part


def renew(field, dense, terms, left, right):
    return pl.pallas_call(
        renew_kernel,
        out_shape=jax.ShapeDtypeStruct(field.shape, jnp.float32),
        in_specs=[pl.BlockSpec(memory_space=VMEM)] * 5,
        out_specs=pl.BlockSpec(memory_space=VMEM),
        compiler_params=pltpu.CompilerParams(vmem_limit_bytes=40 * MIB),
        name="renew",
    )(field, dense, terms, left, right)


def settle_kernel(sweep, offsets_ref, *refs):
    own, upper = refs[0:2], refs[2:4]
    out_ref, right_ref, total_ref = refs[4:]
    slabs, tile = out_ref.shape[1:3]
    side = right_ref.shape[1] * lane
    total_ref[...] = jnp.zeros_like(total_ref)
    add_windows(total_ref, offsets_ref, sweep, 0, tile, side, tile, own)
    add_windows(total_ref, offsets_ref, sweep, -1, tile, side, tile, upper)
    out_ref[...] = total_ref[:, :slabs, side : side + tile]
    right_ref[...] = total_ref[:, slabs:, side : side + tile]


def settle(sweep, offsets, own, upper, tile):
    side = own[0].shape[2]
    slabs, edge = tile[1] // lane, side // lane
    return pl.pallas_call(
        functools.partial(settle_kernel, sweep),
        out_shape=[
            jax.ShapeDtypeStruct((2, slabs, tile[0], lane), jnp.float32),
            jax.ShapeDtypeStruct((2, edge, tile[0], lane), jnp.float32),
        ],
        in_specs=[pl.BlockSpec(memory_space=SMEM)] + [pl.BlockSpec(memory_space=VMEM)] * 4,
        out_specs=[pl.BlockSpec(memory_space=VMEM)] * 2,
        scratch_shapes=[VMEM((2, slabs + edge, tile[0] + 2 * side, lane), jnp.float32)],
        compiler_params=pltpu.CompilerParams(vmem_limit_bytes=40 * MIB),
        name="settle",
    )(offsets, *own, *upper)


def final_kernel(field_ref, density_ref, terms_ref, left_ref, out_ref):
    slabs, tile = terms_ref.shape[1:3]
    for k in range(slabs):
        part = 1.0 / (density_ref[k] + object_damping)
        for plane in range(2):
            terms = terms_ref[plane, k]
            if k < left_ref.shape[1]:
                terms += left_ref[plane, k]
            out_ref[plane, :, columns(k)] = field_ref[plane, k, :tile] + terms * part


def final(field, dense, terms, left):
    slabs, tile = terms.shape[1:3]
    return pl.pallas_call(
        final_kernel,
        out_shape=jax.ShapeDtypeStruct((2, tile, slabs * lane), jnp.float32),
        in_specs=[pl.BlockSpec(memory_space=VMEM)] * 4,
        out_specs=pl.BlockSpec(memory_space=VMEM),
        compiler_params=pltpu.CompilerParams(vmem_limit_bytes=40 * MIB),
        name="final",
    )(field, dense, terms, left)


def all_summed(value):
    steps = []
    for bit in range(int(math.log2(lax.axis_size("col")))):
        mine = lax.rem(lax.axis_index("col") >> bit, 2)
        half = value.shape[0] // 2
        kept = lax.dynamic_slice_in_dim(value, mine * half, half, 0)
        sent = lax.dynamic_slice_in_dim(value, (1 - mine) * half, half, 0)
        value = kept + swapped(sent, "col", 1 << bit)
        steps.append((bit, mine))
    for bit in range(int(math.log2(lax.axis_size("row")))):
        value = value + swapped(value, "row", 1 << bit)
    for bit, mine in reversed(steps):
        other = swapped(value, "col", 1 << bit)
        first = jnp.where(mine == 0, value, other)
        second = jnp.where(mine == 0, other, value)
        value = jnp.concatenate([first, second], axis=0)
    return value


def local(tables, object_field, probe, amplitudes, offsets):
    side = probe.shape[1]
    tile = object_field.shape[1:]
    own_offsets = offsets[0, 0].reshape(-1)
    measured = amplitudes[0, 0]
    parity = lax.rem(lax.axis_index("row"), 2).reshape(1)

    lower = shifted(object_field[:, :side, :], "row", -1)
    right = shifted(object_field[:, :, :side], "col", -1)
    column = jnp.concatenate([shifted(own_offsets, "row", 1), own_offsets, shifted(own_offsets, "row", -1)])
    near = jnp.stack([shifted(column, "col", 1), column, shifted(column, "col", -1)])
    near = near.reshape(3, 3, -1).transpose(1, 0, 2).reshape(-1)
    corner = shifted(lower[:, :, :side], "col", -1)

    dense = density(0, True, near, probe, tile)
    terms_0, terms_1, sums, field = scan_step(
        0, near, probe, measured[0], tables, object_field, right, lower, corner
    )
    own = (terms_0, terms_1)
    partner = [swapped(t, "row", 1) for t in own]
    passed = [handed_on(t, "row") for t in partner]
    total = all_summed(sums.reshape(-1, side)).reshape(3, side, side)
    probe = probe + total[:2] / (total[2] + probe_damping)[None]
    terms, to_left, to_right = gather_all(0, parity, near, own, partner, passed, tile)
    left = shifted(to_right, "col", 1)
    right = shifted(to_left, "col", -1)
    field = renew(field, dense, terms, left, right)

    dense = density(1, False, near, probe, tile)
    terms_0, terms_1, sums = scan_step(1, near, probe, measured[1], tables, field)
    own = (terms_0, terms_1)
    upper = [shifted(t, "row", 1) for t in own]
    total = all_summed(sums.reshape(-1, side)).reshape(3, side, side)
    probe = probe + total[:2] / (total[2] + probe_damping)[None]
    terms, to_right = settle(1, near, own, upper, tile)
    left = shifted(to_right, "col", 1)
    return final(field, dense, terms, left), probe


def solution(mesh):
    placed = (
        P(None, "row", "col"),
        P(),
        P("row", "col", None, None, None, None),
        P("row", "col", None, None, None),
    )

    def whole(object_field, probe, amplitudes, offsets):
        tables = tuple(jnp.asarray(t) for t in dft_tables(probe.shape[1]))
        body = jax.shard_map(
            lambda *args: local(args[:4], *args[4:]),
            mesh=mesh,
            in_specs=(P(),) * 4 + placed,
            out_specs=(P(None, "row", "col"), P()),
            check_vma=False,
        )
        return body(*tables, object_field, probe, amplitudes, offsets)

    return whole
```

time: 665 us -> 255 us (0.38); the launches traced: 653 us -> 254 us
  waiting for transfers between devices: 411 us -> 119 us
  matrix products: 62.9 us -> 0 us
  local copies, waits for them, and re-layouts: 81.5 us -> 18.9 us
  starting transfers between devices: 29.3 us -> 74.3 us
  Pallas kernels: 0 us -> 33.5 us
  other arithmetic: 37 us -> 7.17 us
  loops' own time: 16.4 us -> 0 us
  between operations: 15.1 us -> 1.12 us
    psum x2 -> x0, waiting for transfers between devices: 275 us -> none  [local(): total_num, total_den = lax.psum((probe_num, probe_den), ('row', 'col'))]
    ppermute x8 -> x12, waiting for transfers between devices: 137 us -> 30.3 us  [shifted(): return lax.ppermute(array, axis, pairs)]
    ppermute x0 -> x18, waiting for transfers between devices: none -> 88.4 us  [the longest x16 88.4 us: swapped(): return lax.ppermute(array, axis, [(i, i ^ mask) for i in range(peers)])]
    dot_general x32 -> x0, matrix products: 62.9 us -> none  [the longest x16 32.6 us: right_apply(): jnp.einsum('bmn,nk->bmk', stacked, table, precision=lax.Precision.HIGHEST)]
    ppermute x0 -> x18, starting transfers between devices: none -> 47.6 us  [the longest x16 41 us: swapped(): return lax.ppermute(array, axis, [(i, i ^ mask) for i in range(peers)])]
    dynamic_update_slice x4 -> x0, local copies, waits for them, and re-layouts: 36 us -> none  [add_piece(): return lax.dynamic_update_slice(running, present + pieces[number], anchor)]
    pallas_call x0 -> x8, Pallas kernels: none -> 33.5 us  [the longest x2 15.7 us: scan_step(): pl.pallas_call(functools.partial(scan_kernel, sweep, pieces), out_shape=s...]
    another operation x4 -> x0, loops' own time: 16.4 us -> none  [the longest x2 15.9 us: place_sum(): return lax.fori_loop(0, pieces.shape[0], add_piece, accumulator)]
  transfers between devices with their start and end apart: 10 -> 30, of which waited for: 8 -> 12; matrix products, arithmetic and copies ran while one was open for 2% -> 4% of each run, Pallas kernels for 0% -> 5%
where the time goes in v1:
time: 255 us; the launch traced here: 254 us
  waiting for transfers between devices  119 us (47%)
  starting transfers between devices  74.3 us (29%)
  Pallas kernels  33.5 us (13%)
  local copies, waits for them, and re-layouts  18.9 us (7%)
  other arithmetic  7.17 us (3%)
    ppermute x16, waiting for transfers between devices, swapped(): return lax.ppermute(array, axis, [(i, i ^ mask) for i in range(peers)])  88.4 us
    ppermute x16, starting transfers between devices, swapped(): return lax.ppermute(array, axis, [(i, i ^ mask) for i in range(peers)])  41 us
    ppermute x12, waiting for transfers between devices, shifted(): return lax.ppermute(array, axis, pairs)  30.3 us
    ppermute x12, starting transfers between devices, shifted(): return lax.ppermute(array, axis, pairs)  26.7 us
    pallas_call x2, Pallas kernels, scan_step(): pl.pallas_call(functools.partial(scan_kernel, sweep, pieces), out_shape=s...  15.7 us
    unnamed x42, local copies, waits for them, and re-layouts  12.5 us
    ppermute x2, starting transfers between devices, handed_on(): lax.ppermute(array, axis, [(i, k) for i, k in pairs if 0 <= k < peers])  6.56 us
    pallas_call x1, Pallas kernels, renew(): pl.pallas_call(renew_kernel, out_shape=jax.ShapeDtypeStruct(field.shape,...  5.21 us
  transfers between devices with their start and end apart: 30, of which 12 were waited for; matrix products, arithmetic and copies ran while one was open for 4% of the time, Pallas kernels for 5%

profile of v1, /device:TPU:0, one launch (start us, length us, event | category | flops | bytes accessed | tf_op | source)
XLA Modules:
  0.0 253.7 jit_solution(7505180833327010190)
XLA Ops:
  5.9 24.4 %collective-permute-done.5.refs_2_ = f32[2,256,512]{2,1,0:T(8,128)S(1)} collective-permute-done((f32[2,256,512]{2,1,0:T(8,128)S(1)}, f32[2,256,512]{2,1,0:T(8,128)S(1)}, u32[]{:S(2)}, u32[]{:S(2)}) %collective-permute-start.5) | collective-permute-done | bytes 1048608 | tf_op jit(solution)/shard_map/ppermute | solution.py:25
  33.5 4.5 %collective-permute-start = (s32[8]{0:T(128)S(1)}, s32[8]{0:T(128)S(1)}, u32[]{:S(2)}, u32[]{:S(2)}) collective-permute-start(s32[8]{0:T(128)S(1)} %reshape_squeeze.3), channel_id=1, source_target_pairs={{0,4},{4,8},{8,12},{12,16},{16,20},{20,24},{24,28},{1,5},{5,9},{9,... | collective-permute-start | bytes 104 | tf_op jit(solution)/shard_map/ppermute | solution.py:25
  39.3 1.8 slice_bitcast_fusion
  41.1 2.3 collective-permute-done.1
  46.6 3.6 %collective-permute-done.3 = s32[24]{0:T(128)S(1)} collective-permute-done((s32[24]{0:T(128)S(1)}, s32[24]{0:T(128)S(1)}, u32[]{:S(2)}, u32[]{:S(2)}) %collective-permute-start.3) | collective-permute-done | bytes 128 | tf_op jit(solution)/shard_map/ppermute | solution.py:25
  55.7 8.4 %scan.2 = (f32[2,256,256]{2,1,0:T(8,128)S(1)}, f32[2,256,256]{2,1,0:T(8,128)S(1)}, f32[3,256,256]{2,1,0:T(8,128)S(1)}, f32[2,6,768,128]{3,2,1,0:T(8,128)S(1)}) custom-call(s32[72]{0:T(128)S(1)} %reshape.41.offsets_ref, f32[2,256,256]{2,1,0:T(8,128)S(1)} %copy-done.3, bf16[2,256,256]{2,1,0:T(8,128)(2,1)S(1)} %copy-done.13, bf16[512,512]{1,0:T(8,128)(2,1)S(1)} %copy-done.6, ...), custom_call_target="tpu_custom_call" | custom-call | tf_op jit(solution)/shard_map/scan/pallas_call | solution.py:165
  64.1 2.2 copy-done.1
  68.2 2.4 collective-permute-start.13
  76.1 5.1 %collective-permute-done.14 = f32[192,256]{1,0:T(8,128)} collective-permute-done((f32[192,256]{1,0:T(8,128)}, f32[192,256]{1,0:T(8,128)}, u32[]{:S(2)}, u32[]{:S(2)}) %collective-permute-start.14) | collective-permute-done | bytes 196640 | tf_op jit(solution)/shard_map/ppermute | solution.py:30
  83.9 19.5 %collective-permute-done.15 = f32[192,256]{1,0:T(8,128)S(1)} collective-permute-done((f32[192,256]{1,0:T(8,128)S(1)}, f32[192,256]{1,0:T(8,128)S(1)}, u32[]{:S(2)}, u32[]{:S(2)}) %collective-permute-start.15) | collective-permute-done | bytes 196640 | tf_op jit(solution)/shard_map/ppermute | solution.py:30
  105.1 3.1 %collective-permute-start.10 = (f32[2,256,256]{2,1,0:T(8,128)S(1)}, f32[2,256,256]{2,1,0:T(8,128)}, u32[]{:S(2)}, u32[]{:S(2)}) collective-permute-start(f32[2,256,256]{2,1,0:T(8,128)S(1)} %collective-permute-done.8.refs_3_), channel_id=1, source_target_pairs={{0,8},{8,16},{12,4},{16,24},{20,12},{28,20},{1,9},{9,17},{13,5},{1... | collective-permute-start | bytes 1572872 | tf_op jit(solution)/shard_map/ppermute | solution.py:36
  108.2 3.4 %collective-permute-start.9 = (f32[2,256,256]{2,1,0:T(8,128)S(1)}, f32[2,256,256]{2,1,0:T(8,128)}, u32[]{:S(2)}, u32[]{:S(2)}) collective-permute-start(f32[2,256,256]{2,1,0:T(8,128)S(1)} %collective-permute-done.7.refs_2_), channel_id=1, source_target_pairs={{0,8},{8,16},{12,4},{16,24},{20,12},{28,20},{1,9},{9,17},{13,5},{1... | collective-permute-start | bytes 1572872 | tf_op jit(solution)/shard_map/ppermute | solution.py:36
  112.2 23.1 %collective-permute-done.17 = f32[192,256]{1,0:T(8,128)S(1)} collective-permute-done((f32[192,256]{1,0:T(8,128)S(1)}, f32[192,256]{1,0:T(8,128)S(1)}, u32[]{:S(2)}, u32[]{:S(2)}) %collective-permute-start.17) | collective-permute-done | bytes 196640 | tf_op jit(solution)/shard_map/ppermute | solution.py:30
  136.0 1.8 collective-permute-start.18
  137.8 4.7 %gather.1 = (f32[2,6,768,128]{3,2,1,0:T(8,128)S(1)}, f32[2,2,768,128]{3,2,1,0:T(8,128)}, f32[2,2,768,128]{3,2,1,0:T(8,128)}) custom-call(s32[1]{0:T(128)} %bitcast.2.parity_ref, s32[72]{0:T(128)S(1)} %reshape.41.offsets_ref, f32[2,256,256]{2,1,0:T(8,128)S(1)} %copy-done.16, f32[2,256,256]{2,1,0:T(8,128)S(1)} %copy-done.18, ...), custom_call_target="tpu_custom_call" | custom-call | tf_op jit(solution)/shard_map/gather/pallas_call | solution.py:255
  142.5 2.2 copy-done.2
  150.3 2.9 %density.2.density_ref = f32[6,768,128]{2,1,0:T(8,128)S(1)} custom-call(s32[72]{0:T(128)S(1)} %reshape.41.offsets_ref, f32[2,256,256]{2,1,0:T(8,128)S(1)} %copy-done.3), custom_call_target="tpu_custom_call" | custom-call | tf_op jit(solution)/shard_map/density/pallas_call | solution.py:203
  154.5 5.2 %renew.1.refs_0_.field_ref = f32[2,6,768,128]{3,2,1,0:T(8,128)S(1)} custom-call(f32[2,6,768,128]{3,2,1,0:T(8,128)} %copy-done.1, f32[6,768,128]{2,1,0:T(8,128)S(1)} %density.2.density_ref, f32[2,6,768,128]{3,2,1,0:T(8,128)} %copy-done.2, f32[2,2,768,128]{3,2,1,0:T(8,128)S(1)} %collective-permute-done.11.left_ref, ...), custom_call_target="tpu_custom_call" | custom-call | tf_op jit(solution)/shard_map/renew/pallas_call | solution.py:281
  159.7 7.3 %scan.3 = (f32[2,256,256]{2,1,0:T(8,128)S(1)}, f32[2,256,256]{2,1,0:T(8,128)S(1)}, f32[3,256,256]{2,1,0:T(8,128)S(1)}) custom-call(s32[72]{0:T(128)S(1)} %reshape.41.offsets_ref, f32[2,256,256]{2,1,0:T(8,128)S(1)} %divide_add_fusion.1.probe_ref, bf16[2,256,256]{2,1,0:T(8,128)(2,1)S(1)} %get-tuple-element.30.amplitude_ref, bf16[512,512]{1,0:T(8,128)(2,1)S(1)} %copy-done.6, ...), custom_call_target="tpu_custom_call" | custom-call | tf_op jit(solution)/shard_map/scan/pallas_call | solution.py:165
  167.1 14.0 %collective-permute-start.23 = (f32[384,256]{1,0:T(8,128)S(1)}, f32[384,256]{1,0:T(8,128)S(1)}, u32[]{:S(2)}, u32[]{:S(2)}) collective-permute-start(f32[384,256]{1,0:T(8,128)S(1)} %constant_dynamic-slice_fusion.1), channel_id=1, source_target_pairs={{0,1},{1,0},{2,3},{3,2},{4,5},{5,4},{6,7},{7,6},{8,9},{9,8},{10,11... | collective-permute-start | bytes 1179656 | tf_op jit(solution)/shard_map/ppermute | solution.py:30
  182.7 7.7 %collective-permute-start.20 = (f32[2,256,256]{2,1,0:T(8,128)S(1)}, f32[2,256,256]{2,1,0:T(8,128)S(1)}, u32[]{:S(2)}, u32[]{:S(2)}) collective-permute-start(f32[2,256,256]{2,1,0:T(8,128)S(1)} %get-tuple-element.21.refs_0_), channel_id=1, source_target_pairs={{0,4},{4,8},{8,12},{12,16},{16,20},{20,24},{24,28},{1,5},{5,9},{9,... | collective-permute-start | bytes 1572872 | tf_op jit(solution)/shard_map/ppermute | solution.py:25
  190.4 2.3 collective-permute-start.21
  192.7 2.9 %collective-permute-start.25 = (f32[192,256]{1,0:T(8,128)S(1)}, f32[192,256]{1,0:T(8,128)S(1)}, u32[]{:S(2)}, u32[]{:S(2)}) collective-permute-start(f32[192,256]{1,0:T(8,128)S(1)} %dynamic-slice_add_fusion.2), channel_id=1, source_target_pairs={{0,4},{4,0},{8,12},{12,8},{16,20},{20,16},{24,28},{28,24},{1,5},{5... | collective-permute-start | bytes 589832 | tf_op jit(solution)/shard_map/ppermute | solution.py:30
  195.7 21.8 %collective-permute-done.25 = f32[192,256]{1,0:T(8,128)S(1)} collective-permute-done((f32[192,256]{1,0:T(8,128)S(1)}, f32[192,256]{1,0:T(8,128)S(1)}, u32[]{:S(2)}, u32[]{:S(2)}) %collective-permute-start.25) | collective-permute-done | bytes 196640 | tf_op jit(solution)/shard_map/ppermute | solution.py:30
  217.5 2.4 collective-permute-start.26
  219.8 5.1 %collective-permute-done.26 = f32[192,256]{1,0:T(8,128)S(1)} collective-permute-done((f32[192,256]{1,0:T(8,128)S(1)}, f32[192,256]{1,0:T(8,128)S(1)}, u32[]{:S(2)}, u32[]{:S(2)}) %collective-permute-start.26) | collective-permute-done | bytes 196640 | tf_op jit(solution)/shard_map/ppermute | solution.py:30
  225.0 2.8 %collective-permute-start.27 = (f32[192,256]{1,0:T(8,128)S(1)}, f32[192,256]{1,0:T(8,128)S(1)}, u32[]{:S(2)}, u32[]{:S(2)}) collective-permute-start(f32[192,256]{1,0:T(8,128)S(1)} %add.76), channel_id=1, source_target_pairs={{0,16},{4,20},{8,24},{12,28},{16,0},{20,4},{24,8},{28,12},{1,17},{... | collective-permute-start | bytes 589832 | tf_op jit(solution)/shard_map/ppermute | solution.py:30
  227.8 1.8 settle.1
  231.0 5.6 %collective-permute-done.27 = f32[192,256]{1,0:T(8,128)S(1)} collective-permute-done((f32[192,256]{1,0:T(8,128)S(1)}, f32[192,256]{1,0:T(8,128)S(1)}, u32[]{:S(2)}, u32[]{:S(2)}) %collective-permute-start.27) | collective-permute-done | bytes 196640 | tf_op jit(solution)/shard_map/ppermute | solution.py:30
  236.6 1.8 collective-permute-start.28
  238.4 5.4 %collective-permute-done.28 = f32[192,256]{1,0:T(8,128)S(1)} collective-permute-done((f32[192,256]{1,0:T(8,128)S(1)}, f32[192,256]{1,0:T(8,128)S(1)}, u32[]{:S(2)}, u32[]{:S(2)}) %collective-permute-start.28) | collective-permute-done | bytes 196640 | tf_op jit(solution)/shard_map/ppermute | solution.py:30
  243.8 5.6 %collective-permute-start.29 = (f32[384,256]{1,0:T(8,128)S(1)}, f32[384,256]{1,0:T(8,128)S(1)}, u32[]{:S(2)}, u32[]{:S(2)}) collective-permute-start(f32[384,256]{1,0:T(8,128)S(1)} %pad_maximum_fusion.3), channel_id=1, source_target_pairs={{0,1},{1,0},{2,3},{3,2},{4,5},{5,4},{6,7},{7,6},{8,9},{9,8},{10,11... | collective-permute-start | bytes 1179656 | tf_op jit(solution)/shard_map/ppermute | solution.py:30
  (116 shorter events, 45.5 us)
Async XLA Ops:
  2.1 48.3 %copy-start.3 = (f32[2,256,256]{2,1,0:T(8,128)S(1)}, f32[2,256,256]{2,1,0:T(8,128)}, u32[]{:S(2)}) copy-start(f32[2,256,256]{2,1,0:T(8,128)} %probe_ref.3) | copy-start | bytes 1572868
  2.1 28.2 %collective-permute-start.5 = (f32[2,256,512]{2,1,0:T(8,128)S(1)}, f32[2,256,512]{2,1,0:T(8,128)S(1)}, u32[]{:S(2)}, u32[]{:S(2)}) collective-permute-start(f32[2,256,512]{2,1,0:T(8,128)S(1)} %slice.41), channel_id=1, source_target_pairs={{4,0},{8,4},{12,8},{16,12},{20,16},{24,20},{28,24},{5,1},{9,5},{13... | collective-permute-start | bytes 3145736 | tf_op jit(solution)/shard_map/ppermute | solution.py:25
  4.6 45.7 %collective-permute-start.4 = (f32[2,512,256]{2,1,0:T(8,128)}, f32[2,512,256]{2,1,0:T(8,128)}, u32[]{:S(2)}, u32[]{:S(2)}) collective-permute-start(f32[2,512,256]{2,1,0:T(8,128)} %slice.40), channel_id=1, source_target_pairs={{1,0},{2,1},{3,2},{5,4},{6,5},{7,6},{9,8},{10,9},{11,10},{13,12},{... | collective-permute-start | bytes 3145736 | tf_op jit(solution)/shard_map/ppermute | solution.py:25
  32.1 18.3 %collective-permute-start.6 = (f32[2,256,256]{2,1,0:T(8,128)}, f32[2,256,256]{2,1,0:T(8,128)}, u32[]{:S(2)}, u32[]{:S(2)}) collective-permute-start(f32[2,256,256]{2,1,0:T(8,128)} %slice.50), channel_id=1, source_target_pairs={{1,0},{2,1},{3,2},{5,4},{6,5},{7,6},{9,8},{10,9},{11,10},{13,12},{... | collective-permute-start | bytes 1572872 | tf_op jit(solution)/shard_map/ppermute | solution.py:25
  33.5 7.6 %collective-permute-start = (s32[8]{0:T(128)S(1)}, s32[8]{0:T(128)S(1)}, u32[]{:S(2)}, u32[]{:S(2)}) collective-permute-start(s32[8]{0:T(128)S(1)} %reshape_squeeze.3), channel_id=1, source_target_pairs={{0,4},{4,8},{8,12},{12,16},{16,20},{20,24},{24,28},{1,5},{5,9},{9,... | collective-permute-start | bytes 104 | tf_op jit(solution)/shard_map/ppermute | solution.py:25
  38.0 5.4 %collective-permute-start.1 = (s32[8]{0:T(128)S(1)}, s32[8]{0:T(128)S(1)}, u32[]{:S(2)}, u32[]{:S(2)}) collective-permute-start(s32[8]{0:T(128)S(1)} %reshape_squeeze.3), channel_id=1, source_target_pairs={{4,0},{8,4},{12,8},{16,12},{20,16},{24,20},{28,24},{5,1},{9,5},{13... | collective-permute-start | bytes 104 | tf_op jit(solution)/shard_map/ppermute | solution.py:25
  43.5 3.0 %collective-permute-start.2 = (s32[24]{0:T(128)S(1)}, s32[24]{0:T(128)S(1)}, u32[]{:S(2)}, u32[]{:S(2)}) collective-permute-start(s32[24]{0:T(128)S(1)} %pad_add_fusion), channel_id=1, source_target_pairs={{0,1},{1,2},{2,3},{4,5},{5,6},{6,7},{8,9},{9,10},{10,11},{12,13},{... | collective-permute-start | bytes 296 | tf_op jit(solution)/shard_map/ppermute | solution.py:25
  45.1 5.1 %collective-permute-start.3 = (s32[24]{0:T(128)S(1)}, s32[24]{0:T(128)S(1)}, u32[]{:S(2)}, u32[]{:S(2)}) collective-permute-start(s32[24]{0:T(128)S(1)} %pad_add_fusion), channel_id=1, source_target_pairs={{1,0},{2,1},{3,2},{5,4},{6,5},{7,6},{9,8},{10,9},{11,10},{13,12},{... | collective-permute-start | bytes 296 | tf_op jit(solution)/shard_map/ppermute | solution.py:25
  68.2 3.7 %collective-permute-start.13 = (f32[384,256]{1,0:T(8,128)S(1)}, f32[384,256]{1,0:T(8,128)S(1)}, u32[]{:S(2)}, u32[]{:S(2)}) collective-permute-start(f32[384,256]{1,0:T(8,128)S(1)} %constant_dynamic-slice_fusion.3), channel_id=1, source_target_pairs={{0,1},{1,0},{2,3},{3,2},{4,5},{5,4},{6,7},{7,6},{8,9},{9,8},{10,11... | collective-permute-start | bytes 1179656 | tf_op jit(solution)/shard_map/ppermute | solution.py:30
  70.5 67.3 %copy-start.16 = (f32[2,256,256]{2,1,0:T(8,128)S(1)}, f32[2,256,256]{2,1,0:T(8,128)}, u32[]{:S(2)}) copy-start(f32[2,256,256]{2,1,0:T(8,128)} %copy-done.15) | copy-start | bytes 1572868
  73.7 7.5 %collective-permute-start.14 = (f32[192,256]{1,0:T(8,128)}, f32[192,256]{1,0:T(8,128)}, u32[]{:S(2)}, u32[]{:S(2)}) collective-permute-start(f32[192,256]{1,0:T(8,128)} %constant_dynamic-slice_fusion.2), channel_id=1, source_target_pairs={{0,2},{1,3},{2,0},{3,1},{4,6},{5,7},{6,4},{7,5},{8,10},{9,11},{10,... | collective-permute-start | bytes 589832 | tf_op jit(solution)/shard_map/ppermute | solution.py:30
  74.1 31.0 %collective-permute-start.8 = (f32[2,256,256]{2,1,0:T(8,128)S(1)}, f32[2,256,256]{2,1,0:T(8,128)S(1)}, u32[]{:S(2)}, u32[]{:S(2)}) collective-permute-start(f32[2,256,256]{2,1,0:T(8,128)S(1)} %copy-done.18), channel_id=1, source_target_pairs={{0,4},{4,0},{8,12},{12,8},{16,20},{20,16},{24,28},{28,24},{1,5},{5... | collective-permute-start | bytes 1572872 | tf_op jit(solution)/shard_map/ppermute | solution.py:30
  75.6 32.6 %collective-permute-start.7 = (f32[2,256,256]{2,1,0:T(8,128)}, f32[2,256,256]{2,1,0:T(8,128)S(1)}, u32[]{:S(2)}, u32[]{:S(2)}) collective-permute-start(f32[2,256,256]{2,1,0:T(8,128)} %copy-done.15), channel_id=1, source_target_pairs={{0,4},{4,0},{8,12},{12,8},{16,20},{20,16},{24,28},{28,24},{1,5},{5... | collective-permute-start | bytes 1572872 | tf_op jit(solution)/shard_map/ppermute | solution.py:30
  82.3 21.1 %collective-permute-start.15 = (f32[192,256]{1,0:T(8,128)S(1)}, f32[192,256]{1,0:T(8,128)S(1)}, u32[]{:S(2)}, u32[]{:S(2)}) collective-permute-start(f32[192,256]{1,0:T(8,128)S(1)} %dynamic-slice_add_fusion.3), channel_id=1, source_target_pairs={{0,4},{4,0},{8,12},{12,8},{16,20},{20,16},{24,28},{28,24},{1,5},{5... | collective-permute-start | bytes 589832 | tf_op jit(solution)/shard_map/ppermute | solution.py:30
  103.4 8.2 %collective-permute-start.16 = (f32[192,256]{1,0:T(8,128)S(1)}, f32[192,256]{1,0:T(8,128)S(1)}, u32[]{:S(2)}, u32[]{:S(2)}) collective-permute-start(f32[192,256]{1,0:T(8,128)S(1)} %add.68), channel_id=1, source_target_pairs={{0,8},{4,12},{8,0},{12,4},{16,24},{20,28},{24,16},{28,20},{1,9},{5... | collective-permute-start | bytes 589832 | tf_op jit(solution)/shard_map/ppermute | solution.py:30
  105.1 32.7 %collective-permute-start.10 = (f32[2,256,256]{2,1,0:T(8,128)S(1)}, f32[2,256,256]{2,1,0:T(8,128)}, u32[]{:S(2)}, u32[]{:S(2)}) collective-permute-start(f32[2,256,256]{2,1,0:T(8,128)S(1)} %collective-permute-done.8.refs_3_), channel_id=1, source_target_pairs={{0,8},{8,16},{12,4},{16,24},{20,12},{28,20},{1,9},{9,17},{13,5},{1... | collective-permute-start | bytes 1572872 | tf_op jit(solution)/shard_map/ppermute | solution.py:36
  108.2 29.6 %collective-permute-start.9 = (f32[2,256,256]{2,1,0:T(8,128)S(1)}, f32[2,256,256]{2,1,0:T(8,128)}, u32[]{:S(2)}, u32[]{:S(2)}) collective-permute-start(f32[2,256,256]{2,1,0:T(8,128)S(1)} %collective-permute-done.7.refs_2_), channel_id=1, source_target_pairs={{0,8},{8,16},{12,4},{16,24},{20,12},{28,20},{1,9},{9,17},{13,5},{1... | collective-permute-start | bytes 1572872 | tf_op jit(solution)/shard_map/ppermute | solution.py:36
  111.7 23.6 %collective-permute-start.17 = (f32[192,256]{1,0:T(8,128)S(1)}, f32[192,256]{1,0:T(8,128)S(1)}, u32[]{:S(2)}, u32[]{:S(2)}) collective-permute-start(f32[192,256]{1,0:T(8,128)S(1)} %add.69), channel_id=1, source_target_pairs={{0,16},{4,20},{8,24},{12,28},{16,0},{20,4},{24,8},{28,12},{1,17},{... | collective-permute-start | bytes 589832 | tf_op jit(solution)/shard_map/ppermute | solution.py:30
  136.0 11.4 %collective-permute-start.18 = (f32[192,256]{1,0:T(8,128)}, f32[192,256]{1,0:T(8,128)}, u32[]{:S(2)}, u32[]{:S(2)}) collective-permute-start(f32[192,256]{1,0:T(8,128)} %add.70), channel_id=1, source_target_pairs={{0,2},{1,3},{2,0},{3,1},{4,6},{5,7},{6,4},{7,5},{8,10},{9,11},{10,... | collective-permute-start | bytes 589832 | tf_op jit(solution)/shard_map/ppermute | solution.py:30
  144.7 9.8 %collective-permute-start.11 = (f32[2,2,768,128]{3,2,1,0:T(8,128)}, f32[2,2,768,128]{3,2,1,0:T(8,128)S(1)}, u32[]{:S(2)}, u32[]{:S(2)}) collective-permute-start(f32[2,2,768,128]{3,2,1,0:T(8,128)} %get-tuple-element.18), channel_id=1, source_target_pairs={{0,1},{1,2},{2,3},{4,5},{5,6},{6,7},{8,9},{9,10},{10,11},{12,13},{... | collective-permute-start | bytes 4718600 | tf_op jit(solution)/shard_map/ppermute | solution.py:25
  146.1 8.4 %collective-permute-start.12 = (f32[2,2,768,128]{3,2,1,0:T(8,128)}, f32[2,2,768,128]{3,2,1,0:T(8,128)}, u32[]{:S(2)}, u32[]{:S(2)}) collective-permute-start(f32[2,2,768,128]{3,2,1,0:T(8,128)} %get-tuple-element.19), channel_id=1, source_target_pairs={{1,0},{2,1},{3,2},{5,4},{6,5},{7,6},{9,8},{10,9},{11,10},{13,12},{... | collective-permute-start | bytes 4718600 | tf_op jit(solution)/shard_map/ppermute | solution.py:25
  149.2 4.0 %collective-permute-start.19 = (f32[384,256]{1,0:T(8,128)}, f32[384,256]{1,0:T(8,128)}, u32[]{:S(2)}, u32[]{:S(2)}) collective-permute-start(f32[384,256]{1,0:T(8,128)} %pad_maximum_fusion.2), channel_id=1, source_target_pairs={{0,1},{1,0},{2,3},{3,2},{4,5},{5,4},{6,7},{7,6},{8,9},{9,8},{10,11... | collective-permute-start | bytes 1179656 | tf_op jit(solution)/shard_map/ppermute | solution.py:30
  167.1 15.3 %collective-permute-start.23 = (f32[384,256]{1,0:T(8,128)S(1)}, f32[384,256]{1,0:T(8,128)S(1)}, u32[]{:S(2)}, u32[]{:S(2)}) collective-permute-start(f32[384,256]{1,0:T(8,128)S(1)} %constant_dynamic-slice_fusion.1), channel_id=1, source_target_pairs={{0,1},{1,0},{2,3},{3,2},{4,5},{5,4},{6,7},{7,6},{8,9},{9,8},{10,11... | collective-permute-start | bytes 1179656 | tf_op jit(solution)/shard_map/ppermute | solution.py:30
  182.6 10.1 %collective-permute-start.24 = (f32[192,256]{1,0:T(8,128)S(1)}, f32[192,256]{1,0:T(8,128)S(1)}, u32[]{:S(2)}, u32[]{:S(2)}) collective-permute-start(f32[192,256]{1,0:T(8,128)S(1)} %constant_dynamic-slice_fusion), channel_id=1, source_target_pairs={{0,2},{1,3},{2,0},{3,1},{4,6},{5,7},{6,4},{7,5},{8,10},{9,11},{10,... | collective-permute-start | bytes 589832 | tf_op jit(solution)/shard_map/ppermute | solution.py:30
  182.7 45.1 %collective-permute-start.20 = (f32[2,256,256]{2,1,0:T(8,128)S(1)}, f32[2,256,256]{2,1,0:T(8,128)S(1)}, u32[]{:S(2)}, u32[]{:S(2)}) collective-permute-start(f32[2,256,256]{2,1,0:T(8,128)S(1)} %get-tuple-element.21.refs_0_), channel_id=1, source_target_pairs={{0,4},{4,8},{8,12},{12,16},{16,20},{20,24},{24,28},{1,5},{5,9},{9,... | collective-permute-start | bytes 1572872 | tf_op jit(solution)/shard_map/ppermute | solution.py:25
  190.4 37.4 %collective-permute-start.21 = (f32[2,256,256]{2,1,0:T(8,128)S(1)}, f32[2,256,256]{2,1,0:T(8,128)S(1)}, u32[]{:S(2)}, u32[]{:S(2)}) collective-permute-start(f32[2,256,256]{2,1,0:T(8,128)S(1)} %get-tuple-element.22.refs_1_), channel_id=1, source_target_pairs={{0,4},{4,8},{8,12},{12,16},{16,20},{20,24},{24,28},{1,5},{5,9},{9,... | collective-permute-start | bytes 1572872 | tf_op jit(solution)/shard_map/ppermute | solution.py:25
  192.7 24.7 %collective-permute-start.25 = (f32[192,256]{1,0:T(8,128)S(1)}, f32[192,256]{1,0:T(8,128)S(1)}, u32[]{:S(2)}, u32[]{:S(2)}) collective-permute-start(f32[192,256]{1,0:T(8,128)S(1)} %dynamic-slice_add_fusion.2), channel_id=1, source_target_pairs={{0,4},{4,0},{8,12},{12,8},{16,20},{20,16},{24,28},{28,24},{1,5},{5... | collective-permute-start | bytes 589832 | tf_op jit(solution)/shard_map/ppermute | solution.py:30
  217.5 7.4 %collective-permute-start.26 = (f32[192,256]{1,0:T(8,128)S(1)}, f32[192,256]{1,0:T(8,128)S(1)}, u32[]{:S(2)}, u32[]{:S(2)}) collective-permute-start(f32[192,256]{1,0:T(8,128)S(1)} %add.75), channel_id=1, source_target_pairs={{0,8},{4,12},{8,0},{12,4},{16,24},{20,28},{24,16},{28,20},{1,9},{5... | collective-permute-start | bytes 589832 | tf_op jit(solution)/shard_map/ppermute | solution.py:30
  225.0 11.6 %collective-permute-start.27 = (f32[192,256]{1,0:T(8,128)S(1)}, f32[192,256]{1,0:T(8,128)S(1)}, u32[]{:S(2)}, u32[]{:S(2)}) collective-permute-start(f32[192,256]{1,0:T(8,128)S(1)} %add.76), channel_id=1, source_target_pairs={{0,16},{4,20},{8,24},{12,28},{16,0},{20,4},{24,8},{28,12},{1,17},{... | collective-permute-start | bytes 589832 | tf_op jit(solution)/shard_map/ppermute | solution.py:30
  229.6 21.3 %collective-permute-start.22 = (f32[2,2,512,128]{3,2,1,0:T(8,128)S(1)}, f32[2,2,512,128]{3,2,1,0:T(8,128)S(1)}, u32[]{:S(2)}, u32[]{:S(2)}) collective-permute-start(f32[2,2,512,128]{3,2,1,0:T(8,128)S(1)} %get-tuple-element.24), channel_id=1, source_target_pairs={{0,1},{1,2},{2,3},{4,5},{5,6},{6,7},{8,9},{9,10},{10,11},{12,13},{... | collective-permute-start | bytes 3145736 | tf_op jit(solution)/shard_map/ppermute | solution.py:25
  236.6 7.1 %collective-permute-start.28 = (f32[192,256]{1,0:T(8,128)S(1)}, f32[192,256]{1,0:T(8,128)S(1)}, u32[]{:S(2)}, u32[]{:S(2)}) collective-permute-start(f32[192,256]{1,0:T(8,128)S(1)} %add.77), channel_id=1, source_target_pairs={{0,2},{1,3},{2,0},{3,1},{4,6},{5,7},{6,4},{7,5},{8,10},{9,11},{10,... | collective-permute-start | bytes 589832 | tf_op jit(solution)/shard_map/ppermute | solution.py:30
  243.8 8.8 %collective-permute-start.29 = (f32[384,256]{1,0:T(8,128)S(1)}, f32[384,256]{1,0:T(8,128)S(1)}, u32[]{:S(2)}, u32[]{:S(2)}) collective-permute-start(f32[384,256]{1,0:T(8,128)S(1)} %pad_maximum_fusion.3), channel_id=1, source_target_pairs={{0,1},{1,0},{2,3},{3,2},{4,5},{5,4},{6,7},{7,6},{8,9},{9,8},{10,11... | collective-permute-start | bytes 1179656 | tf_op jit(solution)/shard_map/ppermute | solution.py:30
  (19 other events, 121.2 us)

commit v2 on v1

v2 whole, which is shorter than its diff:
```python
import functools
import math

import jax
import jax.numpy as jnp
import ml_dtypes
import numpy as np
from jax import lax
from jax.experimental import pallas as pl
from jax.experimental.pallas import tpu as pltpu
from jax.sharding import PartitionSpec as P

softening = 0.1
object_damping = 0.5
probe_damping = 1.0
MIB = 1 << 20
lane = 128
VMEM = pltpu.VMEM
SMEM = pltpu.SMEM


def shifted(array, axis, by):
    peers = lax.axis_size(axis)
    pairs = [(i, i + by) for i in range(peers) if 0 <= i + by < peers]
    return lax.ppermute(array, axis, pairs)


def swapped(array, axis, mask):
    peers = lax.axis_size(axis)
    return lax.ppermute(array, axis, [(i, i ^ mask) for i in range(peers)])


def dft_tables(length):
    index = np.arange(length)
    phase = (index[:, None] * index[None, :] % length) * (2.0 * math.pi / length)
    cosine = np.cos(phase) / math.sqrt(length)
    sine = np.sin(phase) / math.sqrt(length)
    full = np.block([[cosine, -sine], [sine, cosine]])
    high = full.astype(ml_dtypes.bfloat16)
    low = (full - high.astype(np.float64)).astype(ml_dtypes.bfloat16)
    return high, low, np.ascontiguousarray(high.T), np.ascontiguousarray(low.T)


def halves(value):
    high = value.astype(jnp.bfloat16)
    return high, (value - high.astype(jnp.float32)).astype(jnp.bfloat16)


def product(a, b):
    return jnp.dot(a, b, preferred_element_type=jnp.float32)


def left_product(high, low, real, imag):
    side = real.shape[0]
    real_high, real_low = halves(real)
    imag_high, imag_low = halves(imag)
    top = jnp.concatenate([real_high, imag_high], axis=0)
    rest = jnp.concatenate([real_low, imag_low], axis=0)
    out = product(high, top) + product(high, rest) + product(low, top)
    return out[:side], out[side:]


def right_product(real, imag, high, low):
    side = real.shape[1]
    real_high, real_low = halves(real)
    imag_high, imag_low = halves(imag)
    top = jnp.concatenate([real_high, imag_high], axis=1)
    rest = jnp.concatenate([real_low, imag_low], axis=1)
    out = product(top, high) + product(rest, high) + product(top, low)
    return out[:, :side], out[:, side:]


def split_column(column):
    return lax.div(column, lane), lax.rem(column, lane)


def taken(ref, plane, row, column, side):
    first, shift = split_column(column)
    count = side // lane + 1
    slabs = [ref[plane, first + k, pl.ds(row, side), :] for k in range(count)]
    return pltpu.roll(jnp.concatenate(slabs, axis=1), count * lane - shift, 1)[:, :side]


def turned(value, shift):
    side = value.shape[0]
    wide = jnp.concatenate([value, jnp.zeros((side, lane), jnp.float32)], axis=1)
    return pltpu.roll(wide, shift, 1)


def add_slabs(ref, lead, row, first, wide):
    side = wide.shape[0]
    for k in range(wide.shape[1] // lane):
        spot = lead + (first + k, pl.ds(row, side), slice(None))
        ref[spot] += wide[:, k * lane : (k + 1) * lane]


def columns(number):
    return slice(number * lane, (number + 1) * lane)


def whole_spec(count):
    return [pl.BlockSpec(memory_space=VMEM)] * count


def offsets_spec():
    return pl.BlockSpec(memory_space=SMEM)


def shape_of(*dims):
    return jax.ShapeDtypeStruct(dims, jnp.float32)


def cost(flops, moved):
    return pl.CostEstimate(flops=flops, bytes_accessed=moved, transcendentals=0)


def place_of(down, along, sweep, scan):
    return ((((down + 1) * 2 + along + 1) * 2 + sweep) * 2 + scan) * 2


def scan_kernel(
    sweep, flat, offsets_ref, probe_ref, amplitude_ref, ah_ref, al_ref, bh_ref, bl_ref, *refs
):
    own_ref, right_ref, first_ref, second_ref, corner_ref = refs[:5]
    terms_ref, down_first_ref, down_second_ref, beside_ref, cross_ref, sums_ref = refs[5:11]
    field_ref, total_ref = refs[11:]
    side = probe_ref.shape[1]
    edge = side // lane
    slabs, rows = terms_ref.shape[1:3]

    def slab(ref, plane, k):
        return ref[plane, :, columns(k)] if flat else ref[plane, k]

    for plane in range(2):
        for k in range(slabs):
            field_ref[plane, k, :rows] = slab(own_ref, plane, k)
        for k in range(edge):
            field_ref[plane, slabs + k, :rows] = slab(right_ref, plane, k)
            field_ref[plane, k, rows:] = slab(first_ref, plane, k)
            field_ref[plane, slabs + k, rows:] = slab(corner_ref, plane, k)
        for k in range(edge, slabs):
            field_ref[plane, k, rows:] = slab(second_ref, plane, k - edge)
    total_ref[...] = jnp.zeros_like(total_ref)
    probe_real, probe_imag = probe_ref[0], probe_ref[1]
    for scan in range(2):
        place = place_of(0, 0, sweep, scan)
        row, column = offsets_ref[place], offsets_ref[place + 1]
        first, shift = split_column(column)
        patch_real = taken(field_ref, 0, row, column, side)
        patch_imag = taken(field_ref, 1, row, column, side)
        wave_real = probe_real * patch_real - probe_imag * patch_imag
        wave_imag = probe_real * patch_imag + probe_imag * patch_real
        mid = left_product(bh_ref[...], bl_ref[...], wave_real, wave_imag)
        far_real, far_imag = right_product(*mid, ah_ref[...], al_ref[...])
        scale = amplitude_ref[scan].astype(jnp.float32) * lax.rsqrt(
            far_real * far_real + far_imag * far_imag + softening
        )
        mid = left_product(ah_ref[...], al_ref[...], far_real * scale, far_imag * scale)
        back_real, back_imag = right_product(*mid, bh_ref[...], bl_ref[...])
        diff_real = back_real - wave_real
        diff_imag = back_imag - wave_imag
        term_real = probe_real * diff_real + probe_imag * diff_imag
        term_imag = probe_real * diff_imag - probe_imag * diff_real
        add_slabs(total_ref, (0,), row, first, turned(term_real, shift))
        add_slabs(total_ref, (1,), row, first, turned(term_imag, shift))
        sums = (
            patch_real * diff_real + patch_imag * diff_imag,
            patch_real * diff_imag - patch_imag * diff_real,
            patch_real * patch_real + patch_imag * patch_imag,
        )
        for number, value in enumerate(sums):
            if scan == 0:
                sums_ref[number] = value
            else:
                sums_ref[number] += value
    terms_ref[...] = total_ref[:, :slabs, :rows]
    beside_ref[...] = total_ref[:, slabs:, :rows]
    cross_ref[...] = total_ref[:, slabs:, rows:]
    down_first_ref[...] = total_ref[:, :edge, rows:]
    down_second_ref[...] = total_ref[:, edge:slabs, rows:]


def scan_step(sweep, flat, offsets, probe, amplitudes, tables, *field):
    side = probe.shape[1]
    edge = side // lane
    rows = field[1].shape[1 if flat else 2]
    slabs = field[0].shape[2] // lane if flat else field[0].shape[1]
    shapes = [
        shape_of(2, slabs, rows, lane),
        shape_of(2, edge, side, lane),
        shape_of(2, slabs - edge, side, lane),
        shape_of(2, edge, rows, lane),
        shape_of(2, edge, side, lane),
        shape_of(3, side, side),
    ]
    return pl.pallas_call(
        functools.partial(scan_kernel, sweep, flat),
        out_shape=shapes,
        in_specs=[offsets_spec()] + whole_spec(6 + len(field)),
        out_specs=whole_spec(len(shapes)),
        scratch_shapes=[VMEM((2, slabs + edge, rows + side, lane), jnp.float32)] * 2,
        compiler_params=pltpu.CompilerParams(vmem_limit_bytes=22 * MIB),
        cost_estimate=cost(7_000_000_000, 12 * MIB),
        name="scan",
    )(offsets, probe, amplitudes, *tables, *field)


def density_kernel(sweep, offsets_ref, probe_ref, out_ref, total_ref):
    side = probe_ref.shape[1]
    slabs, tile = out_ref.shape[:2]
    span = slabs * lane
    total_ref[...] = jnp.zeros_like(total_ref)
    power = probe_ref[0] * probe_ref[0] + probe_ref[1] * probe_ref[1]
    for down in (-1, 0):
        for along in (-1, 0):
            for scan in range(2):
                place = place_of(down, along, sweep, scan)
                row = offsets_ref[place] + side + down * tile
                column = offsets_ref[place + 1] + side + along * span

                @pl.when((row > 0) & (column > 0))
                def _():
                    first, shift = split_column(column)
                    add_slabs(total_ref, (), row, first, turned(power, shift))

    out_ref[...] = total_ref[side // lane : side // lane + slabs, side : side + tile]


def density(sweep, offsets, probe, tile):
    side = probe.shape[1]
    slabs = tile[1] // lane
    return pl.pallas_call(
        functools.partial(density_kernel, sweep),
        out_shape=shape_of(slabs, tile[0], lane),
        in_specs=[offsets_spec()] + whole_spec(1),
        out_specs=whole_spec(1)[0],
        scratch_shapes=[VMEM((slabs + 2 * side // lane, tile[0] + 2 * side, lane), jnp.float32)],
        compiler_params=pltpu.CompilerParams(vmem_limit_bytes=8 * MIB),
        cost_estimate=cost(1_000_000, 6 * MIB),
        name="density",
    )(offsets, probe)


def renew_kernel(flat, last, *refs):
    field_ref, density_ref, terms_ref, left_ref, first_ref, second_ref = refs[:6]
    out_ref = refs[6]
    slabs, rows = terms_ref.shape[1:3]
    edge, side = first_ref.shape[1:3]
    for k in range(slabs):
        part = 1.0 / (density_ref[k] + object_damping)
        for plane in range(2):
            upper = first_ref[plane, k] if k < edge else second_ref[plane, k - edge]
            top = terms_ref[plane, k, :side] + upper
            rest = terms_ref[plane, k, side:]
            if k < edge:
                top += left_ref[plane, k, :side]
                rest += left_ref[plane, k, side:]
            before = field_ref[plane, :, columns(k)] if flat else field_ref[plane, k]
            top = before[:side] + top * part[:side]
            rest = before[side:] + rest * part[side:]
            if last:
                out_ref[plane, :side, columns(k)] = top
                out_ref[plane, side:, columns(k)] = rest
                continue
            out_ref[plane, k, :side] = top
            out_ref[plane, k, side:] = rest
            up_first_ref, up_second_ref, beside_ref = refs[7:]
            if k < edge:
                up_first_ref[plane, k] = top
                beside_ref[plane, k, :side] = top
                beside_ref[plane, k, side:] = rest
            else:
                up_second_ref[plane, k - edge] = top


def renew(flat, last, field, dense, terms, left, first, second):
    slabs, rows = terms.shape[1:3]
    edge, side = first.shape[1:3]
    if last:
        shapes = [shape_of(2, rows, slabs * lane)]
    else:
        shapes = [
            shape_of(2, slabs, rows, lane),
            shape_of(2, edge, side, lane),
            shape_of(2, slabs - edge, side, lane),
            shape_of(2, edge, rows, lane),
        ]
    return pl.pallas_call(
        functools.partial(renew_kernel, flat, last),
        out_shape=shapes,
        in_specs=whole_spec(6),
        out_specs=whole_spec(len(shapes)),
        compiler_params=pltpu.CompilerParams(vmem_limit_bytes=4 * MIB),
        cost_estimate=cost(4_000_000, 10 * MIB),
        name="renew",
    )(field, dense, terms, left, first, second)


def all_summed(value):
    steps = []
    for bit in range(int(math.log2(lax.axis_size("col")))):
        mine = lax.rem(lax.axis_index("col") >> bit, 2)
        half = value.shape[0] // 2
        kept = lax.dynamic_slice_in_dim(value, mine * half, half, 0)
        sent = lax.dynamic_slice_in_dim(value, (1 - mine) * half, half, 0)
        value = kept + swapped(sent, "col", 1 << bit)
        steps.append((bit, mine))
    for bit in range(int(math.log2(lax.axis_size("row")))):
        value = value + swapped(value, "row", 1 << bit)
    for bit, mine in reversed(steps):
        other = swapped(value, "col", 1 << bit)
        first = jnp.where(mine == 0, value, other)
        second = jnp.where(mine == 0, other, value)
        value = jnp.concatenate([first, second], axis=0)
    return value


def local(tables, object_field, probe, amplitudes, offsets):
    side = probe.shape[1]
    tile = object_field.shape[1:]
    measured = amplitudes[0, 0]
    own_offsets = offsets[0, 0].reshape(-1)

    first = shifted(object_field[:, :side, :side], "row", -1)
    second = shifted(object_field[:, :side, side:], "row", -1)
    right = shifted(object_field[:, :, :side], "col", -1)
    near = jnp.stack([shifted(own_offsets, "row", 1), own_offsets])
    near = jnp.stack([shifted(near, "col", 1), near], axis=1).reshape(-1)
    dense = density(0, near, probe, tile)
    first, dense = lax.optimization_barrier((first, dense))
    corner = shifted(first, "col", -1)
    field = object_field
    for sweep in range(offsets.shape[2]):
        flat = sweep == 0
        last = sweep == offsets.shape[2] - 1
        terms, down_first, down_second, beside, cross, sums = scan_step(
            sweep, flat, near, probe, measured[sweep], tables, field, right, first, second, corner
        )
        cross = shifted(cross, "col", 1)
        second = shifted(down_second, "row", 1)
        left = shifted(beside, "col", 1)
        total = all_summed(sums.reshape(-1, side)).reshape(3, side, side)
        first = shifted(down_first + cross, "row", 1)
        if sweep > 0:
            dense = density(sweep, near, probe, tile)
        probe = probe + total[:2] / (total[2] + probe_damping)[None]
        renewed = renew(flat, last, field, dense, terms, left, first, second)
        field = renewed[0]
        if not last:
            first = shifted(renewed[1], "row", -1)
            second = shifted(renewed[2], "row", -1)
            right = shifted(renewed[3], "col", -1)
            corner = shifted(first, "col", -1)
    return field, probe


def solution(mesh):
    placed = (
        P(None, "row", "col"),
        P(),
        P("row", "col", None, None, None, None),
        P("row", "col", None, None, None),
    )

    def whole(object_field, probe, amplitudes, offsets):
        tables = tuple(jnp.asarray(t) for t in dft_tables(probe.shape[1]))
        body = jax.shard_map(
            lambda *args: local(args[:4], *args[4:]),
            mesh=mesh,
            in_specs=(P(),) * 4 + placed,
            out_specs=(P(None, "row", "col"), P()),
            check_vma=False,
        )
        return body(*tables, object_field, probe, amplitudes, offsets)

    return whole
```

time: 255 us -> 217 us (0.85)
  waiting for transfers between devices: 119 us -> 89.2 us
  Pallas kernels: 33.5 us -> 25.6 us
  starting transfers between devices: 74.3 us -> 70.1 us
    ppermute x16 -> x14, waiting for transfers between devices: 88.4 us -> 37 us  [swapped(): return lax.ppermute(array, axis, [(i, i ^ mask) for i in range(peers)])]
    ppermute x12 -> x18, waiting for transfers between devices: 30.3 us -> 52.2 us  [shifted(): return lax.ppermute(array, axis, pairs)]
    ppermute x12 -> x18, starting transfers between devices: 26.7 us -> 37.3 us  [shifted(): return lax.ppermute(array, axis, pairs)]
    ppermute x16 -> x14, starting transfers between devices: 41 us -> 32.8 us  [swapped(): return lax.ppermute(array, axis, [(i, i ^ mask) for i in range(peers)])]
    pallas_call x8 -> x6, Pallas kernels: 33.5 us -> 25.6 us  [the longest x2 17.9 us: scan_step(): pl.pallas_call(functools.partial(scan_kernel, sweep, flat), out_shape=sha...]
    ppermute x2 -> x0, starting transfers between devices: 6.56 us -> none  [handed_on(): lax.ppermute(array, axis, [(i, k) for i, k in pairs if 0 <= k < peers])]
    unnamed x42 -> x48, local copies, waits for them, and re-layouts: 12.5 us -> 14.8 us
  transfers between devices with their start and end apart: 30 -> 32, of which waited for: 12 -> 18; matrix products, arithmetic and copies ran while one was open for 4% -> 4% of each run, Pallas kernels for 5% -> 4%
where the time goes in v2:
time: 217 us; the launch traced here: 216 us
  waiting for transfers between devices  89.2 us (41%)
  starting transfers between devices  70.1 us (32%)
  Pallas kernels  25.6 us (12%)
  local copies, waits for them, and re-layouts  21.1 us (10%)
  other arithmetic  8.59 us (4%)
    ppermute x18, waiting for transfers between devices, shifted(): return lax.ppermute(array, axis, pairs)  52.2 us
    ppermute x18, starting transfers between devices, shifted(): return lax.ppermute(array, axis, pairs)  37.3 us
    ppermute x14, waiting for transfers between devices, swapped(): return lax.ppermute(array, axis, [(i, i ^ mask) for i in range(peers)])  37 us
    ppermute x14, starting transfers between devices, swapped(): return lax.ppermute(array, axis, [(i, i ^ mask) for i in range(peers)])  32.8 us
    pallas_call x2, Pallas kernels, scan_step(): pl.pallas_call(functools.partial(scan_kernel, sweep, flat), out_shape=sha...  17.9 us
    unnamed x48, local copies, waits for them, and re-layouts  14.8 us
    pallas_call x2, Pallas kernels, renew(): pl.pallas_call(functools.partial(renew_kernel, flat, last), out_shape=sha...  4.89 us
  transfers between devices with their start and end apart: 32, of which 18 were waited for; matrix products, arithmetic and copies ran while one was open for 4% of the time, Pallas kernels for 4%

profile of v2, /device:TPU:0, one launch (start us, length us, event | category | flops | bytes accessed | tf_op | source)
XLA Modules:
  0.0 215.8 jit_solution(16104685185314466708)
XLA Ops:
  0.6 2.4 %fusion.1 = (f32[2,256,256]{2,1,0:T(8,128)}, f32[2,256,256]{2,1,0:T(8,128)}) fusion(f32[2,512,512]{2,1,0:T(8,128)} %refs_0_.3), kind=kLoop, calls=%fused_computation.29 | loop fusion | bytes 2097152 | tf_op jit(solution)/shard_map/slice | solution.py:325
  6.8 5.5 %collective-permute-start.1 = (s32[8]{0:T(128)S(1)}, s32[8]{0:T(128)S(1)}, u32[]{:S(2)}, u32[]{:S(2)}) collective-permute-start(s32[8]{0:T(128)S(1)} %reshape_squeeze.3), channel_id=1, source_target_pairs={{0,4},{4,8},{8,12},{12,16},{16,20},{20,24},{24,28},{1,5},{5,9},{9,... | collective-permute-start | bytes 104 | tf_op jit(solution)/shard_map/ppermute | solution.py:25
  13.6 2.2 %collective-permute-start.2 = (s32[2,8]{1,0:T(2,128)S(1)}, s32[2,8]{1,0:T(2,128)S(1)}, u32[]{:S(2)}, u32[]{:S(2)}) collective-permute-start(s32[2,8]{1,0:T(2,128)S(1)} %get-tuple-element.50), channel_id=1, source_target_pairs={{0,1},{1,2},{2,3},{4,5},{5,6},{6,7},{8,9},{9,10},{10,11},{12,13},{... | collective-permute-start | bytes 200 | tf_op jit(solution)/shard_map/ppermute | solution.py:25
  22.5 9.8 %collective-permute-done.4.refs_3_ = f32[2,256,256]{2,1,0:T(8,128)} collective-permute-done((f32[2,256,256]{2,1,0:T(8,128)}, f32[2,256,256]{2,1,0:T(8,128)}, u32[]{:S(2)}, u32[]{:S(2)}) %collective-permute-start.4) | collective-permute-done | bytes 524320 | tf_op jit(solution)/shard_map/ppermute | solution.py:25
  37.6 9.5 %scan.2 = (f32[2,4,512,128]{3,2,1,0:T(8,128)S(1)}, f32[2,2,256,128]{3,2,1,0:T(8,128)S(1)}, f32[2,2,256,128]{3,2,1,0:T(8,128)S(1)}, f32[2,2,512,128]{3,2,1,0:T(8,...) custom-call(s32[32]{0:T(128)S(1)} %reshape.31.offsets_ref, f32[2,256,256]{2,1,0:T(8,128)S(1)} %copy-done.4, ...), custom_call_target="tpu_custom_call" | custom-call | flops 7000000000 | bytes 12582912 | tf_op jit(solution)/shard_map/scan/pallas_call | solution.py:196
  59.9 2.6 %collective-permute-start.7 = (f32[2,2,256,128]{3,2,1,0:T(8,128)}, f32[2,2,256,128]{3,2,1,0:T(8,128)}, u32[]{:S(2)}, u32[]{:S(2)}) collective-permute-start(f32[2,2,256,128]{3,2,1,0:T(8,128)} %copy-done.12), channel_id=1, source_target_pairs={{0,1},{1,2},{2,3},{4,5},{5,6},{6,7},{8,9},{9,10},{10,11},{12,13},{... | collective-permute-start | bytes 1572872 | tf_op jit(solution)/shard_map/ppermute | solution.py:25
  62.5 2.6 %collective-permute-start.6 = (f32[2,2,512,128]{3,2,1,0:T(8,128)}, f32[2,2,512,128]{3,2,1,0:T(8,128)}, u32[]{:S(2)}, u32[]{:S(2)}) collective-permute-start(f32[2,2,512,128]{3,2,1,0:T(8,128)} %copy-done.10), channel_id=1, source_target_pairs={{0,1},{1,2},{2,3},{4,5},{5,6},{6,7},{8,9},{9,10},{10,11},{12,13},{... | collective-permute-start | bytes 3145736 | tf_op jit(solution)/shard_map/ppermute | solution.py:25
  66.7 3.4 %collective-permute-start.12 = (f32[192,256]{1,0:T(8,128)S(1)}, f32[192,256]{1,0:T(8,128)S(1)}, u32[]{:S(2)}, u32[]{:S(2)}) collective-permute-start(f32[192,256]{1,0:T(8,128)S(1)} %dynamic-slice_add_fusion.3), channel_id=1, source_target_pairs={{0,4},{4,0},{8,12},{12,8},{16,20},{20,16},{24,28},{28,24},{1,5},{5... | collective-permute-start | bytes 589832 | tf_op jit(solution)/shard_map/ppermute | solution.py:30
  70.2 4.6 %collective-permute-done.12 = f32[192,256]{1,0:T(8,128)S(1)} collective-permute-done((f32[192,256]{1,0:T(8,128)S(1)}, f32[192,256]{1,0:T(8,128)S(1)}, u32[]{:S(2)}, u32[]{:S(2)}) %collective-permute-start.12) | collective-permute-done | bytes 196640 | tf_op jit(solution)/shard_map/ppermute | solution.py:30
  74.8 3.3 %collective-permute-start.13 = (f32[192,256]{1,0:T(8,128)S(1)}, f32[192,256]{1,0:T(8,128)S(1)}, u32[]{:S(2)}, u32[]{:S(2)}) collective-permute-start(f32[192,256]{1,0:T(8,128)S(1)} %add.75), channel_id=1, source_target_pairs={{0,8},{4,12},{8,0},{12,4},{16,24},{20,28},{24,16},{28,20},{1,9},{5... | collective-permute-start | bytes 589832 | tf_op jit(solution)/shard_map/ppermute | solution.py:30
  78.1 4.2 %collective-permute-start.9 = (f32[2,2,256,128]{3,2,1,0:T(8,128)}, f32[2,2,256,128]{3,2,1,0:T(8,128)}, u32[]{:S(2)}, u32[]{:S(2)}) collective-permute-start(f32[2,2,256,128]{3,2,1,0:T(8,128)} %copy-done.11), channel_id=1, source_target_pairs={{0,4},{4,8},{8,12},{12,16},{16,20},{20,24},{24,28},{1,5},{5,9},{9,... | collective-permute-start | bytes 1572872 | tf_op jit(solution)/shard_map/ppermute | solution.py:25
  82.3 2.0 add.68
  84.4 2.1 collective-permute-start.8
  86.5 3.1 %collective-permute-start.14 = (f32[192,256]{1,0:T(8,128)S(1)}, f32[192,256]{1,0:T(8,128)S(1)}, u32[]{:S(2)}, u32[]{:S(2)}) collective-permute-start(f32[192,256]{1,0:T(8,128)S(1)} %add.76), channel_id=1, source_target_pairs={{0,16},{4,20},{8,24},{12,28},{16,0},{20,4},{24,8},{28,12},{1,17},{... | collective-permute-start | bytes 589832 | tf_op jit(solution)/shard_map/ppermute | solution.py:30
  89.6 7.6 %collective-permute-done.14 = f32[192,256]{1,0:T(8,128)S(1)} collective-permute-done((f32[192,256]{1,0:T(8,128)S(1)}, f32[192,256]{1,0:T(8,128)S(1)}, u32[]{:S(2)}, u32[]{:S(2)}) %collective-permute-start.14) | collective-permute-done | bytes 196640 | tf_op jit(solution)/shard_map/ppermute | solution.py:30
  98.6 4.2 %collective-permute-done.8.refs_4_ = f32[2,2,256,128]{3,2,1,0:T(8,128)} collective-permute-done((f32[2,2,256,128]{3,2,1,0:T(8,128)}, f32[2,2,256,128]{3,2,1,0:T(8,128)}, u32[]{:S(2)}, u32[]{:S(2)}) %collective-permute-start.8) | collective-permute-done | bytes 524320 | tf_op jit(solution)/shard_map/ppermute | solution.py:25
  104.4 3.0 %renew.2 = (f32[2,4,512,128]{3,2,1,0:T(8,128)S(1)}, f32[2,2,256,128]{3,2,1,0:T(8,128)}, f32[2,2,256,128]{3,2,1,0:T(8,128)S(1)}, f32[2,2,512,128]{3,2,1,0:T(8,128)}) custom-call(f32[2,512,512]{2,1,0:T(8,128)S(1)} %copy-done, f32[4,512,128]{2,1,0:T(8,128)S(1)} %density.2.refs_1_, f32[2,4,512,128]{3,2,1,0:T(8,128)S(1)} %copy-done.2, ...), custom_call_target="tpu_custom_call" | custom-call | flops 4000000 | bytes 10485760 | tf_op jit(solution)/shard_map/renew/pallas_call | solution.py:288
  114.0 17.2 %collective-permute-done.18.refs_2_ = f32[2,2,256,128]{3,2,1,0:T(8,128)S(1)} collective-permute-done((f32[2,2,256,128]{3,2,1,0:T(8,128)}, f32[2,2,256,128]{3,2,1,0:T(8,128)S(1)}, u32[]{:S(2)}, u32[]{:S(2)}) %collective-permute-start.18) | collective-permute-done | bytes 524320 | tf_op jit(solution)/shard_map/ppermute | solution.py:25
  134.0 5.5 %collective-permute-done.19.refs_3_ = f32[2,2,256,128]{3,2,1,0:T(8,128)S(1)} collective-permute-done((f32[2,2,256,128]{3,2,1,0:T(8,128)}, f32[2,2,256,128]{3,2,1,0:T(8,128)S(1)}, u32[]{:S(2)}, u32[]{:S(2)}) %collective-permute-start.19) | collective-permute-done | bytes 524320 | tf_op jit(solution)/shard_map/ppermute | solution.py:25
  139.5 8.4 %scan.3 = (f32[2,4,512,128]{3,2,1,0:T(8,128)S(1)}, f32[2,2,256,128]{3,2,1,0:T(8,128)S(1)}, f32[2,2,256,128]{3,2,1,0:T(8,128)S(1)}, f32[2,2,512,128]{3,2,1,0:T(8,...) custom-call(s32[32]{0:T(128)S(1)} %reshape.31.offsets_ref, ...), custom_call_target="tpu_custom_call" | custom-call | flops 7000000000 | bytes 12582912 | tf_op jit(solution)/shard_map/scan/pallas_call | solution.py:196
  151.4 7.1 %collective-permute-done.26 = f32[192,256]{1,0:T(8,128)S(1)} collective-permute-done((f32[192,256]{1,0:T(8,128)S(1)}, f32[192,256]{1,0:T(8,128)S(1)}, u32[]{:S(2)}, u32[]{:S(2)}) %collective-permute-start.26) | collective-permute-done | bytes 196640 | tf_op jit(solution)/shard_map/ppermute | solution.py:30
  158.5 2.4 %collective-permute-start.27 = (f32[192,256]{1,0:T(8,128)S(1)}, f32[192,256]{1,0:T(8,128)S(1)}, u32[]{:S(2)}, u32[]{:S(2)}) collective-permute-start(f32[192,256]{1,0:T(8,128)S(1)} %dynamic-slice_add_fusion.2), channel_id=1, source_target_pairs={{0,4},{4,0},{8,12},{12,8},{16,20},{20,16},{24,28},{28,24},{1,5},{5... | collective-permute-start | bytes 589832 | tf_op jit(solution)/shard_map/ppermute | solution.py:30
  161.0 4.6 %collective-permute-done.27 = f32[192,256]{1,0:T(8,128)S(1)} collective-permute-done((f32[192,256]{1,0:T(8,128)S(1)}, f32[192,256]{1,0:T(8,128)S(1)}, u32[]{:S(2)}, u32[]{:S(2)}) %collective-permute-start.27) | collective-permute-done | bytes 196640 | tf_op jit(solution)/shard_map/ppermute | solution.py:30
  165.6 6.6 %collective-permute-start.28 = (f32[192,256]{1,0:T(8,128)S(1)}, f32[192,256]{1,0:T(8,128)S(1)}, u32[]{:S(2)}, u32[]{:S(2)}) collective-permute-start(f32[192,256]{1,0:T(8,128)S(1)} %add.83), channel_id=1, source_target_pairs={{0,8},{4,12},{8,0},{12,4},{16,24},{20,28},{24,16},{28,20},{1,9},{5... | collective-permute-start | bytes 589832 | tf_op jit(solution)/shard_map/ppermute | solution.py:30
  173.5 2.7 %collective-permute-done.28 = f32[192,256]{1,0:T(8,128)S(1)} collective-permute-done((f32[192,256]{1,0:T(8,128)S(1)}, f32[192,256]{1,0:T(8,128)S(1)}, u32[]{:S(2)}, u32[]{:S(2)}) %collective-permute-start.28) | collective-permute-done | bytes 196640 | tf_op jit(solution)/shard_map/ppermute | solution.py:30
  176.3 2.7 %collective-permute-start.29 = (f32[192,256]{1,0:T(8,128)S(1)}, f32[192,256]{1,0:T(8,128)S(1)}, u32[]{:S(2)}, u32[]{:S(2)}) collective-permute-start(f32[192,256]{1,0:T(8,128)S(1)} %add.84), channel_id=1, source_target_pairs={{0,16},{4,20},{8,24},{12,28},{16,0},{20,4},{24,8},{28,12},{1,17},{... | collective-permute-start | bytes 589832 | tf_op jit(solution)/shard_map/ppermute | solution.py:30
  180.3 6.4 %collective-permute-done.29 = f32[192,256]{1,0:T(8,128)S(1)} collective-permute-done((f32[192,256]{1,0:T(8,128)S(1)}, f32[192,256]{1,0:T(8,128)S(1)}, u32[]{:S(2)}, u32[]{:S(2)}) %collective-permute-start.29) | collective-permute-done | bytes 196640 | tf_op jit(solution)/shard_map/ppermute | solution.py:30
  187.5 3.0 %collective-permute-start.24 = (f32[2,2,256,128]{3,2,1,0:T(8,128)S(1)}, f32[2,2,256,128]{3,2,1,0:T(8,128)S(1)}, u32[]{:S(2)}, u32[]{:S(2)}) collective-permute-start(f32[2,2,256,128]{3,2,1,0:T(8,128)S(1)} %get-tuple-element.36), channel_id=1, source_target_pairs={{0,4},{4,8},{8,12},{12,16},{16,20},{20,24},{24,28},{1,5},{5,9},{9,... | collective-permute-start | bytes 1572872 | tf_op jit(solution)/shard_map/ppermute | solution.py:25
  190.6 1.9 collective-permute-start.23
  192.9 4.8 %collective-permute-start.31 = (f32[384,256]{1,0:T(8,128)S(1)}, f32[384,256]{1,0:T(8,128)S(1)}, u32[]{:S(2)}, u32[]{:S(2)}) collective-permute-start(f32[384,256]{1,0:T(8,128)S(1)} %pad_maximum_fusion.3), channel_id=1, source_target_pairs={{0,1},{1,0},{2,3},{3,2},{4,5},{5,4},{6,7},{7,6},{8,9},{9,8},{10,11... | collective-permute-start | bytes 1179656 | tf_op jit(solution)/shard_map/ppermute | solution.py:30
  199.1 3.7 %collective-permute-done.24.refs_5_ = f32[2,2,256,128]{3,2,1,0:T(8,128)S(1)} collective-permute-done((f32[2,2,256,128]{3,2,1,0:T(8,128)S(1)}, f32[2,2,256,128]{3,2,1,0:T(8,128)S(1)}, u32[]{:S(2)}, u32[]{:S(2)}) %collective-permute-start.24) | collective-permute-done | bytes 524320 | tf_op jit(solution)/shard_map/ppermute | solution.py:25
  202.8 10.1 %collective-permute-done.23.refs_4_ = f32[2,2,256,128]{3,2,1,0:T(8,128)S(1)} collective-permute-done((f32[2,2,256,128]{3,2,1,0:T(8,128)S(1)}, f32[2,2,256,128]{3,2,1,0:T(8,128)S(1)}, u32[]{:S(2)}, u32[]{:S(2)}) %collective-permute-start.23) | collective-permute-done | bytes 524320 | tf_op jit(solution)/shard_map/ppermute | solution.py:25
  (123 shorter events, 55.2 us)
Async XLA Ops:
  3.1 17.1 %collective-permute-start = (f32[2,256,256]{2,1,0:T(8,128)}, f32[2,256,256]{2,1,0:T(8,128)}, u32[]{:S(2)}, u32[]{:S(2)}) collective-permute-start(f32[2,256,256]{2,1,0:T(8,128)} %get-tuple-element.39), channel_id=1, source_target_pairs={{4,0},{8,4},{12,8},{16,12},{20,16},{24,20},{28,24},{5,1},{9,5},{13... | collective-permute-start | bytes 1572872 | tf_op jit(solution)/shard_map/ppermute | solution.py:25
  5.4 26.9 %collective-permute-start.3 = (f32[2,512,256]{2,1,0:T(8,128)}, f32[2,512,256]{2,1,0:T(8,128)}, u32[]{:S(2)}, u32[]{:S(2)}) collective-permute-start(f32[2,512,256]{2,1,0:T(8,128)} %slice.41), channel_id=1, source_target_pairs={{1,0},{2,1},{3,2},{5,4},{6,5},{7,6},{9,8},{10,9},{11,10},{13,12},{... | collective-permute-start | bytes 3145736 | tf_op jit(solution)/shard_map/ppermute | solution.py:25
  6.8 6.8 %collective-permute-start.1 = (s32[8]{0:T(128)S(1)}, s32[8]{0:T(128)S(1)}, u32[]{:S(2)}, u32[]{:S(2)}) collective-permute-start(s32[8]{0:T(128)S(1)} %reshape_squeeze.3), channel_id=1, source_target_pairs={{0,4},{4,8},{8,12},{12,16},{16,20},{20,24},{24,28},{1,5},{5,9},{9,... | collective-permute-start | bytes 104 | tf_op jit(solution)/shard_map/ppermute | solution.py:25
  13.6 3.5 %collective-permute-start.2 = (s32[2,8]{1,0:T(2,128)S(1)}, s32[2,8]{1,0:T(2,128)S(1)}, u32[]{:S(2)}, u32[]{:S(2)}) collective-permute-start(s32[2,8]{1,0:T(2,128)S(1)} %get-tuple-element.50), channel_id=1, source_target_pairs={{0,1},{1,2},{2,3},{4,5},{5,6},{6,7},{8,9},{9,10},{10,11},{12,13},{... | collective-permute-start | bytes 200 | tf_op jit(solution)/shard_map/ppermute | solution.py:25
  15.8 16.6 %collective-permute-start.4 = (f32[2,256,256]{2,1,0:T(8,128)}, f32[2,256,256]{2,1,0:T(8,128)}, u32[]{:S(2)}, u32[]{:S(2)}) collective-permute-start(f32[2,256,256]{2,1,0:T(8,128)} %get-tuple-element.38), channel_id=1, source_target_pairs={{4,0},{8,4},{12,8},{16,12},{20,16},{24,20},{28,24},{5,1},{9,5},{13... | collective-permute-start | bytes 1572872 | tf_op jit(solution)/shard_map/ppermute | solution.py:25
  20.2 12.2 %collective-permute-start.5 = (f32[2,256,256]{2,1,0:T(8,128)}, f32[2,256,256]{2,1,0:T(8,128)}, u32[]{:S(2)}, u32[]{:S(2)}) collective-permute-start(f32[2,256,256]{2,1,0:T(8,128)} %collective-permute-done.refs_2_), channel_id=1, source_target_pairs={{1,0},{2,1},{3,2},{5,4},{6,5},{7,6},{9,8},{10,9},{11,10},{13,12},{... | collective-permute-start | bytes 1572872 | tf_op jit(solution)/shard_map/ppermute | solution.py:25
  52.7 2.9 %collective-permute-start.10 = (f32[384,256]{1,0:T(8,128)}, f32[384,256]{1,0:T(8,128)}, u32[]{:S(2)}, u32[]{:S(2)}) collective-permute-start(f32[384,256]{1,0:T(8,128)} %constant_dynamic-slice_fusion.3), channel_id=1, source_target_pairs={{0,1},{1,0},{2,3},{3,2},{4,5},{5,4},{6,7},{7,6},{8,9},{9,8},{10,11... | collective-permute-start | bytes 1179656 | tf_op jit(solution)/shard_map/ppermute | solution.py:30
  58.2 7.5 %collective-permute-start.11 = (f32[192,256]{1,0:T(8,128)}, f32[192,256]{1,0:T(8,128)}, u32[]{:S(2)}, u32[]{:S(2)}) collective-permute-start(f32[192,256]{1,0:T(8,128)} %constant_dynamic-slice_fusion.2), channel_id=1, source_target_pairs={{0,2},{1,3},{2,0},{3,1},{4,6},{5,7},{6,4},{7,5},{8,10},{9,11},{10,... | collective-permute-start | bytes 589832 | tf_op jit(solution)/shard_map/ppermute | solution.py:30
  59.9 22.4 %collective-permute-start.7 = (f32[2,2,256,128]{3,2,1,0:T(8,128)}, f32[2,2,256,128]{3,2,1,0:T(8,128)}, u32[]{:S(2)}, u32[]{:S(2)}) collective-permute-start(f32[2,2,256,128]{3,2,1,0:T(8,128)} %copy-done.12), channel_id=1, source_target_pairs={{0,1},{1,2},{2,3},{4,5},{5,6},{6,7},{8,9},{9,10},{10,11},{12,13},{... | collective-permute-start | bytes 1572872 | tf_op jit(solution)/shard_map/ppermute | solution.py:25
  62.5 40.3 %collective-permute-start.6 = (f32[2,2,512,128]{3,2,1,0:T(8,128)}, f32[2,2,512,128]{3,2,1,0:T(8,128)}, u32[]{:S(2)}, u32[]{:S(2)}) collective-permute-start(f32[2,2,512,128]{3,2,1,0:T(8,128)} %copy-done.10), channel_id=1, source_target_pairs={{0,1},{1,2},{2,3},{4,5},{5,6},{6,7},{8,9},{9,10},{10,11},{12,13},{... | collective-permute-start | bytes 3145736 | tf_op jit(solution)/shard_map/ppermute | solution.py:25
  66.7 8.1 %collective-permute-start.12 = (f32[192,256]{1,0:T(8,128)S(1)}, f32[192,256]{1,0:T(8,128)S(1)}, u32[]{:S(2)}, u32[]{:S(2)}) collective-permute-start(f32[192,256]{1,0:T(8,128)S(1)} %dynamic-slice_add_fusion.3), channel_id=1, source_target_pairs={{0,4},{4,0},{8,12},{12,8},{16,20},{20,16},{24,28},{28,24},{1,5},{5... | collective-permute-start | bytes 589832 | tf_op jit(solution)/shard_map/ppermute | solution.py:30
  74.8 11.6 %collective-permute-start.13 = (f32[192,256]{1,0:T(8,128)S(1)}, f32[192,256]{1,0:T(8,128)S(1)}, u32[]{:S(2)}, u32[]{:S(2)}) collective-permute-start(f32[192,256]{1,0:T(8,128)S(1)} %add.75), channel_id=1, source_target_pairs={{0,8},{4,12},{8,0},{12,4},{16,24},{20,28},{24,16},{28,20},{1,9},{5... | collective-permute-start | bytes 589832 | tf_op jit(solution)/shard_map/ppermute | solution.py:30
  78.1 20.5 %collective-permute-start.9 = (f32[2,2,256,128]{3,2,1,0:T(8,128)}, f32[2,2,256,128]{3,2,1,0:T(8,128)}, u32[]{:S(2)}, u32[]{:S(2)}) collective-permute-start(f32[2,2,256,128]{3,2,1,0:T(8,128)} %copy-done.11), channel_id=1, source_target_pairs={{0,4},{4,8},{8,12},{12,16},{16,20},{20,24},{24,28},{1,5},{5,9},{9,... | collective-permute-start | bytes 1572872 | tf_op jit(solution)/shard_map/ppermute | solution.py:25
  84.4 18.4 %collective-permute-start.8 = (f32[2,2,256,128]{3,2,1,0:T(8,128)}, f32[2,2,256,128]{3,2,1,0:T(8,128)}, u32[]{:S(2)}, u32[]{:S(2)}) collective-permute-start(f32[2,2,256,128]{3,2,1,0:T(8,128)} %add.68), channel_id=1, source_target_pairs={{0,4},{4,8},{8,12},{12,16},{16,20},{20,24},{24,28},{1,5},{5,9},{9,... | collective-permute-start | bytes 1572872 | tf_op jit(solution)/shard_map/ppermute | solution.py:25
  86.5 10.8 %collective-permute-start.14 = (f32[192,256]{1,0:T(8,128)S(1)}, f32[192,256]{1,0:T(8,128)S(1)}, u32[]{:S(2)}, u32[]{:S(2)}) collective-permute-start(f32[192,256]{1,0:T(8,128)S(1)} %add.76), channel_id=1, source_target_pairs={{0,16},{4,20},{8,24},{12,28},{16,0},{20,4},{24,8},{28,12},{1,17},{... | collective-permute-start | bytes 589832 | tf_op jit(solution)/shard_map/ppermute | solution.py:30
  98.0 12.1 %collective-permute-start.15 = (f32[192,256]{1,0:T(8,128)}, f32[192,256]{1,0:T(8,128)}, u32[]{:S(2)}, u32[]{:S(2)}) collective-permute-start(f32[192,256]{1,0:T(8,128)} %add.77), channel_id=1, source_target_pairs={{0,2},{1,3},{2,0},{3,1},{4,6},{5,7},{6,4},{7,5},{8,10},{9,11},{10,... | collective-permute-start | bytes 589832 | tf_op jit(solution)/shard_map/ppermute | solution.py:30
  108.7 22.4 %collective-permute-start.18 = (f32[2,2,256,128]{3,2,1,0:T(8,128)}, f32[2,2,256,128]{3,2,1,0:T(8,128)S(1)}, u32[]{:S(2)}, u32[]{:S(2)}) collective-permute-start(f32[2,2,256,128]{3,2,1,0:T(8,128)} %get-tuple-element.30), channel_id=1, source_target_pairs={{4,0},{8,4},{12,8},{16,12},{20,16},{24,20},{28,24},{5,1},{9,5},{13... | collective-permute-start | bytes 1572872 | tf_op jit(solution)/shard_map/ppermute | solution.py:25
  111.1 21.5 %collective-permute-start.16 = (f32[384,256]{1,0:T(8,128)S(1)}, f32[384,256]{1,0:T(8,128)}, u32[]{:S(2)}, u32[]{:S(2)}) collective-permute-start(f32[384,256]{1,0:T(8,128)S(1)} %pad_maximum_fusion.2), channel_id=1, source_target_pairs={{0,1},{1,0},{2,3},{3,2},{4,5},{5,4},{6,7},{7,6},{8,9},{9,8},{10,11... | collective-permute-start | bytes 1179656 | tf_op jit(solution)/shard_map/ppermute | solution.py:30
  111.2 28.3 %collective-permute-start.17 = (f32[2,2,512,128]{3,2,1,0:T(8,128)}, f32[2,2,512,128]{3,2,1,0:T(8,128)S(1)}, u32[]{:S(2)}, u32[]{:S(2)}) collective-permute-start(f32[2,2,512,128]{3,2,1,0:T(8,128)} %get-tuple-element.29), channel_id=1, source_target_pairs={{1,0},{2,1},{3,2},{5,4},{6,5},{7,6},{9,8},{10,9},{11,10},{13,12},{... | collective-permute-start | bytes 3145736 | tf_op jit(solution)/shard_map/ppermute | solution.py:25
  112.7 26.8 %collective-permute-start.19 = (f32[2,2,256,128]{3,2,1,0:T(8,128)}, f32[2,2,256,128]{3,2,1,0:T(8,128)S(1)}, u32[]{:S(2)}, u32[]{:S(2)}) collective-permute-start(f32[2,2,256,128]{3,2,1,0:T(8,128)} %copy-done.13), channel_id=1, source_target_pairs={{4,0},{8,4},{12,8},{16,12},{20,16},{24,20},{28,24},{5,1},{9,5},{13... | collective-permute-start | bytes 1572872 | tf_op jit(solution)/shard_map/ppermute | solution.py:25
  131.2 8.3 %collective-permute-start.20 = (f32[2,2,256,128]{3,2,1,0:T(8,128)S(1)}, f32[2,2,256,128]{3,2,1,0:T(8,128)S(1)}, u32[]{:S(2)}, u32[]{:S(2)}) collective-permute-start(f32[2,2,256,128]{3,2,1,0:T(8,128)S(1)} %collective-permute-done.18.refs_2_), channel_id=1, source_target_pairs={{1,0},{2,1},{3,2},{5,4},{6,5},{7,6},{9,8},{10,9},{11,10},{13,12},{... | collective-permute-start | bytes 1572872 | tf_op jit(solution)/shard_map/ppermute | solution.py:25
  148.0 3.2 %collective-permute-start.25 = (f32[384,256]{1,0:T(8,128)S(1)}, f32[384,256]{1,0:T(8,128)S(1)}, u32[]{:S(2)}, u32[]{:S(2)}) collective-permute-start(f32[384,256]{1,0:T(8,128)S(1)} %constant_dynamic-slice_fusion.1), channel_id=1, source_target_pairs={{0,1},{1,0},{2,3},{3,2},{4,5},{5,4},{6,7},{7,6},{8,9},{9,8},{10,11... | collective-permute-start | bytes 1179656 | tf_op jit(solution)/shard_map/ppermute | solution.py:30
  151.3 7.2 %collective-permute-start.26 = (f32[192,256]{1,0:T(8,128)S(1)}, f32[192,256]{1,0:T(8,128)S(1)}, u32[]{:S(2)}, u32[]{:S(2)}) collective-permute-start(f32[192,256]{1,0:T(8,128)S(1)} %constant_dynamic-slice_fusion), channel_id=1, source_target_pairs={{0,2},{1,3},{2,0},{3,1},{4,6},{5,7},{6,4},{7,5},{8,10},{9,11},{10,... | collective-permute-start | bytes 589832 | tf_op jit(solution)/shard_map/ppermute | solution.py:30
  158.5 7.0 %collective-permute-start.27 = (f32[192,256]{1,0:T(8,128)S(1)}, f32[192,256]{1,0:T(8,128)S(1)}, u32[]{:S(2)}, u32[]{:S(2)}) collective-permute-start(f32[192,256]{1,0:T(8,128)S(1)} %dynamic-slice_add_fusion.2), channel_id=1, source_target_pairs={{0,4},{4,0},{8,12},{12,8},{16,20},{20,16},{24,28},{28,24},{1,5},{5... | collective-permute-start | bytes 589832 | tf_op jit(solution)/shard_map/ppermute | solution.py:30
  165.6 10.6 %collective-permute-start.28 = (f32[192,256]{1,0:T(8,128)S(1)}, f32[192,256]{1,0:T(8,128)S(1)}, u32[]{:S(2)}, u32[]{:S(2)}) collective-permute-start(f32[192,256]{1,0:T(8,128)S(1)} %add.83), channel_id=1, source_target_pairs={{0,8},{4,12},{8,0},{12,4},{16,24},{20,28},{24,16},{28,20},{1,9},{5... | collective-permute-start | bytes 589832 | tf_op jit(solution)/shard_map/ppermute | solution.py:30
  172.2 18.3 %collective-permute-start.22 = (f32[2,2,256,128]{3,2,1,0:T(8,128)S(1)}, f32[2,2,256,128]{3,2,1,0:T(8,128)S(1)}, u32[]{:S(2)}, u32[]{:S(2)}) collective-permute-start(f32[2,2,256,128]{3,2,1,0:T(8,128)S(1)} %get-tuple-element.35), channel_id=1, source_target_pairs={{0,1},{1,2},{2,3},{4,5},{5,6},{6,7},{8,9},{9,10},{10,11},{12,13},{... | collective-permute-start | bytes 1572872 | tf_op jit(solution)/shard_map/ppermute | solution.py:25
  176.3 10.4 %collective-permute-start.29 = (f32[192,256]{1,0:T(8,128)S(1)}, f32[192,256]{1,0:T(8,128)S(1)}, u32[]{:S(2)}, u32[]{:S(2)}) collective-permute-start(f32[192,256]{1,0:T(8,128)S(1)} %add.84), channel_id=1, source_target_pairs={{0,16},{4,20},{8,24},{12,28},{16,0},{20,4},{24,8},{28,12},{1,17},{... | collective-permute-start | bytes 589832 | tf_op jit(solution)/shard_map/ppermute | solution.py:30
  179.0 33.9 %collective-permute-start.21 = (f32[2,2,512,128]{3,2,1,0:T(8,128)S(1)}, f32[2,2,512,128]{3,2,1,0:T(8,128)S(1)}, u32[]{:S(2)}, u32[]{:S(2)}) collective-permute-start(f32[2,2,512,128]{3,2,1,0:T(8,128)S(1)} %get-tuple-element.33), channel_id=1, source_target_pairs={{0,1},{1,2},{2,3},{4,5},{5,6},{6,7},{8,9},{9,10},{10,11},{12,13},{... | collective-permute-start | bytes 3145736 | tf_op jit(solution)/shard_map/ppermute | solution.py:25
  186.7 6.1 %collective-permute-start.30 = (f32[192,256]{1,0:T(8,128)S(1)}, f32[192,256]{1,0:T(8,128)S(1)}, u32[]{:S(2)}, u32[]{:S(2)}) collective-permute-start(f32[192,256]{1,0:T(8,128)S(1)} %add.85), channel_id=1, source_target_pairs={{0,2},{1,3},{2,0},{3,1},{4,6},{5,7},{6,4},{7,5},{8,10},{9,11},{10,... | collective-permute-start | bytes 589832 | tf_op jit(solution)/shard_map/ppermute | solution.py:30
  187.5 15.3 %collective-permute-start.24 = (f32[2,2,256,128]{3,2,1,0:T(8,128)S(1)}, f32[2,2,256,128]{3,2,1,0:T(8,128)S(1)}, u32[]{:S(2)}, u32[]{:S(2)}) collective-permute-start(f32[2,2,256,128]{3,2,1,0:T(8,128)S(1)} %get-tuple-element.36), channel_id=1, source_target_pairs={{0,4},{4,8},{8,12},{12,16},{16,20},{20,24},{24,28},{1,5},{5,9},{9,... | collective-permute-start | bytes 1572872 | tf_op jit(solution)/shard_map/ppermute | solution.py:25
  190.6 22.3 %collective-permute-start.23 = (f32[2,2,256,128]{3,2,1,0:T(8,128)S(1)}, f32[2,2,256,128]{3,2,1,0:T(8,128)S(1)}, u32[]{:S(2)}, u32[]{:S(2)}) collective-permute-start(f32[2,2,256,128]{3,2,1,0:T(8,128)S(1)} %add.80), channel_id=1, source_target_pairs={{0,4},{4,8},{8,12},{12,16},{16,20},{20,24},{24,28},{1,5},{5,9},{9,... | collective-permute-start | bytes 1572872 | tf_op jit(solution)/shard_map/ppermute | solution.py:25
  192.9 21.9 %collective-permute-start.31 = (f32[384,256]{1,0:T(8,128)S(1)}, f32[384,256]{1,0:T(8,128)S(1)}, u32[]{:S(2)}, u32[]{:S(2)}) collective-permute-start(f32[384,256]{1,0:T(8,128)S(1)} %pad_maximum_fusion.3), channel_id=1, source_target_pairs={{0,1},{1,0},{2,3},{3,2},{4,5},{5,4},{6,7},{7,6},{8,9},{9,8},{10,11... | collective-permute-start | bytes 1179656 | tf_op jit(solution)/shard_map/ppermute | solution.py:30
  (24 other events, 81.1 us)

commit v3 on v2

--- a/solution.py
+++ b/solution.py
@@ -15,14 +15,14 @@
 probe_damping = 1.0
 MIB = 1 << 20
 lane = 128
+SCAN_LIMIT = 24 * MIB
 VMEM = pltpu.VMEM
 SMEM = pltpu.SMEM
 
 
 def shifted(array, axis, by):
     peers = lax.axis_size(axis)
-    pairs = [(i, i + by) for i in range(peers) if 0 <= i + by < peers]
-    return lax.ppermute(array, axis, pairs)
+    return lax.ppermute(array, axis, [(i, (i + by) % peers) for i in range(peers)])
 
 
 def swapped(array, axis, mask):
@@ -30,15 +30,14 @@
     return lax.ppermute(array, axis, [(i, i ^ mask) for i in range(peers)])
 
 
-def dft_tables(length):
+def dft_table(length):
     index = np.arange(length)
     phase = (index[:, None] * index[None, :] % length) * (2.0 * math.pi / length)
-    cosine = np.cos(phase) / math.sqrt(length)
-    sine = np.sin(phase) / math.sqrt(length)
-    full = np.block([[cosine, -sine], [sine, cosine]])
-    high = full.astype(ml_dtypes.bfloat16)
-    low = (full - high.astype(np.float64)).astype(ml_dtypes.bfloat16)
-    return high, low, np.ascontiguousarray(high.T), np.ascontiguousarray(low.T)
+    parts = []
+    for value in (np.cos(phase) / math.sqrt(length), np.sin(phase) / math.sqrt(length)):
+        high = value.astype(ml_dtypes.bfloat16)
+        parts += [high, (value - high.astype(np.float64)).astype(ml_dtypes.bfloat16)]
+    return np.stack(parts)
 
 
 def halves(value):
@@ -118,29 +117,67 @@
     return ((((down + 1) * 2 + along + 1) * 2 + sweep) * 2 + scan) * 2
 
 
-def scan_kernel(
-    sweep, flat, offsets_ref, probe_ref, amplitude_ref, ah_ref, al_ref, bh_ref, bl_ref, *refs
-):
-    own_ref, right_ref, first_ref, second_ref, corner_ref = refs[:5]
-    terms_ref, down_first_ref, down_second_ref, beside_ref, cross_ref, sums_ref = refs[5:11]
-    field_ref, total_ref = refs[11:]
+def halves_of(bit, half):
+    mine = lax.rem(lax.axis_index("col") >> bit, 2)
+    kept = pl.ds(pl.multiple_of(mine * half, 8), half)
+    return kept, pl.ds(pl.multiple_of((1 - mine) * half, 8), half)
+
+
+def scan_kernel(sweep, flat, offsets_ref, *refs):
+    probe_hbm, amplitude_hbm, table_hbm, own_hbm, right_hbm, first_hbm, second_hbm, corner_hbm = refs[:8]
+    terms_hbm, down_first_hbm, down_second_hbm, beside_hbm, cross_hbm, kept_hbm, sent_hbm = refs[8:15]
+    field_ref, total_ref, probe_ref, amplitude_ref, table_ref, forth_ref, back_ref, sums_ref = refs[15:23]
+    field_sem, small_sem, out_sem = refs[23:]
     side = probe_ref.shape[1]
     edge = side // lane
-    slabs, rows = terms_ref.shape[1:3]
-
-    def slab(ref, plane, k):
-        return ref[plane, :, columns(k)] if flat else ref[plane, k]
-
-    for plane in range(2):
+    slabs, rows = terms_hbm.shape[1:3]
+
+    copies = []
+
+    def fetch(source, target):
+        copies.append(pltpu.make_async_copy(source, target, field_sem))
+
+    small = [
+        pltpu.make_async_copy(table_hbm, table_ref, small_sem.at[0]),
+        pltpu.make_async_copy(probe_hbm, probe_ref, small_sem.at[1]),
+        pltpu.make_async_copy(amplitude_hbm.at[sweep], amplitude_ref, small_sem.at[2]),
+    ]
+    if flat:
         for k in range(slabs):
-            field_ref[plane, k, :rows] = slab(own_ref, plane, k)
+            fetch(own_hbm.at[:, :, columns(k)], field_ref.at[:, k, :rows])
         for k in range(edge):
-            field_ref[plane, slabs + k, :rows] = slab(right_ref, plane, k)
-            field_ref[plane, k, rows:] = slab(first_ref, plane, k)
-            field_ref[plane, slabs + k, rows:] = slab(corner_ref, plane, k)
+            fetch(right_hbm.at[:, :, columns(k)], field_ref.at[:, slabs + k, :rows])
+            fetch(first_hbm.at[:, :, columns(k)], field_ref.at[:, k, rows:])
+            fetch(corner_hbm.at[:, :, columns(k)], field_ref.at[:, slabs + k, rows:])
         for k in range(edge, slabs):
-            field_ref[plane, k, rows:] = slab(second_ref, plane, k - edge)
+            fetch(second_hbm.at[:, :, columns(k - edge)], field_ref.at[:, k, rows:])
+    else:
+        fetch(own_hbm, field_ref.at[:, :slabs, :rows])
+        fetch(right_hbm, field_ref.at[:, slabs:, :rows])
+        fetch(first_hbm, field_ref.at[:, :edge, rows:])
+        fetch(second_hbm, field_ref.at[:, edge:slabs, rows:])
+        fetch(corner_hbm, field_ref.at[:, slabs:, rows:])
+    small[0].start()
+    for copy in copies:
+        copy.start()
+    for copy in small[1:]:
+        copy.start()
     total_ref[...] = jnp.zeros_like(total_ref)
+    small[0].wait()
+    for part in range(2):
+        cosine, sine = table_ref[part], table_ref[2 + part]
+        forth_ref[part, :side, :side] = cosine
+        forth_ref[part, side:, side:] = cosine
+        forth_ref[part, :side, side:] = -sine
+        forth_ref[part, side:, :side] = sine
+        back_ref[part, :side, :side] = cosine
+        back_ref[part, side:, side:] = cosine
+        back_ref[part, :side, side:] = sine
+        back_ref[part, side:, :side] = -sine
+    for copy in small[1:]:
+        copy.wait()
+    for copy in copies:
+        copy.wait()
     probe_real, probe_imag = probe_ref[0], probe_ref[1]
     for scan in range(2):
         place = place_of(0, 0, sweep, scan)
@@ -150,13 +187,13 @@
         patch_imag = taken(field_ref, 1, row, column, side)
         wave_real = probe_real * patch_real - probe_imag * patch_imag
         wave_imag = probe_real * patch_imag + probe_imag * patch_real
-        mid = left_product(bh_ref[...], bl_ref[...], wave_real, wave_imag)
-        far_real, far_imag = right_product(*mid, ah_ref[...], al_ref[...])
+        mid = left_product(back_ref[0], back_ref[1], wave_real, wave_imag)
+        far_real, far_imag = right_product(*mid, forth_ref[0], forth_ref[1])
         scale = amplitude_ref[scan].astype(jnp.float32) * lax.rsqrt(
             far_real * far_real + far_imag * far_imag + softening
         )
-        mid = left_product(ah_ref[...], al_ref[...], far_real * scale, far_imag * scale)
-        back_real, back_imag = right_product(*mid, bh_ref[...], bl_ref[...])
+        mid = left_product(forth_ref[0], forth_ref[1], far_real * scale, far_imag * scale)
+        back_real, back_imag = right_product(*mid, back_ref[0], back_ref[1])
         diff_real = back_real - wave_real
         diff_imag = back_imag - wave_imag
         term_real = probe_real * diff_real + probe_imag * diff_imag
@@ -169,18 +206,29 @@
             patch_real * patch_real + patch_imag * patch_imag,
         )
         for number, value in enumerate(sums):
+            spot = slice(number * side, (number + 1) * side)
             if scan == 0:
-                sums_ref[number] = value
+                sums_ref[spot] = value
             else:
-                sums_ref[number] += value
-    terms_ref[...] = total_ref[:, :slabs, :rows]
-    beside_ref[...] = total_ref[:, slabs:, :rows]
-    cross_ref[...] = total_ref[:, slabs:, rows:]
-    down_first_ref[...] = total_ref[:, :edge, rows:]
-    down_second_ref[...] = total_ref[:, edge:slabs, rows:]
-
-
-def scan_step(sweep, flat, offsets, probe, amplitudes, tables, *field):
+                sums_ref[spot] += value
+    kept, sent = halves_of(0, kept_hbm.shape[0])
+    outs = [
+        (sums_ref.at[sent], sent_hbm),
+        (sums_ref.at[kept], kept_hbm),
+        (total_ref.at[:, slabs:, rows:], cross_hbm),
+        (total_ref.at[:, edge:slabs, rows:], down_second_hbm),
+        (total_ref.at[:, :edge, rows:], down_first_hbm),
+        (total_ref.at[:, slabs:, :rows], beside_hbm),
+        (total_ref.at[:, :slabs, :rows], terms_hbm),
+    ]
+    outs = [pltpu.make_async_copy(source, target, out_sem) for source, target in outs]
+    for copy in outs:
+        copy.start()
+    for copy in outs:
+        copy.wait()
+
+
+def scan_step(sweep, flat, offsets, probe, amplitudes, table, *field):
     side = probe.shape[1]
     edge = side // lane
     rows = field[1].shape[1 if flat else 2]
@@ -191,18 +239,31 @@
         shape_of(2, slabs - edge, side, lane),
         shape_of(2, edge, rows, lane),
         shape_of(2, edge, side, lane),
-        shape_of(3, side, side),
+        shape_of(3 * side // 2, side),
+        shape_of(3 * side // 2, side),
     ]
     return pl.pallas_call(
         functools.partial(scan_kernel, sweep, flat),
         out_shape=shapes,
-        in_specs=[offsets_spec()] + whole_spec(6 + len(field)),
-        out_specs=whole_spec(len(shapes)),
-        scratch_shapes=[VMEM((2, slabs + edge, rows + side, lane), jnp.float32)] * 2,
-        compiler_params=pltpu.CompilerParams(vmem_limit_bytes=22 * MIB),
+        in_specs=[offsets_spec()] + [pl.BlockSpec(memory_space=pl.ANY)] * (3 + len(field)),
+        out_specs=[pl.BlockSpec(memory_space=pl.ANY)] * len(shapes),
+        scratch_shapes=[
+            VMEM((2, slabs + edge, rows + side, lane), jnp.float32),
+            VMEM((2, slabs + edge, rows + side, lane), jnp.float32),
+            VMEM(probe.shape, jnp.float32),
+            VMEM(amplitudes.shape[1:], amplitudes.dtype),
+            VMEM(table.shape, table.dtype),
+            VMEM((2, 2 * side, 2 * side), table.dtype),
+            VMEM((2, 2 * side, 2 * side), table.dtype),
+            VMEM((3 * side, side), jnp.float32),
+            pltpu.SemaphoreType.DMA,
+            pltpu.SemaphoreType.DMA((3,)),
+            pltpu.SemaphoreType.DMA,
+        ],
+        compiler_params=pltpu.CompilerParams(vmem_limit_bytes=SCAN_LIMIT),
         cost_estimate=cost(7_000_000_000, 12 * MIB),
         name="scan",
-    )(offsets, probe, amplitudes, *tables, *field)
+    )(offsets, probe, amplitudes, table, *field)
 
 
 def density_kernel(sweep, offsets_ref, probe_ref, out_ref, total_ref):
@@ -296,54 +357,126 @@
     )(field, dense, terms, left, first, second)
 
 
-def all_summed(value):
-    steps = []
-    for bit in range(int(math.log2(lax.axis_size("col")))):
-        mine = lax.rem(lax.axis_index("col") >> bit, 2)
-        half = value.shape[0] // 2
-        kept = lax.dynamic_slice_in_dim(value, mine * half, half, 0)
-        sent = lax.dynamic_slice_in_dim(value, (1 - mine) * half, half, 0)
-        value = kept + swapped(sent, "col", 1 << bit)
-        steps.append((bit, mine))
-    for bit in range(int(math.log2(lax.axis_size("row")))):
-        value = value + swapped(value, "row", 1 << bit)
-    for bit, mine in reversed(steps):
-        other = swapped(value, "col", 1 << bit)
-        first = jnp.where(mine == 0, value, other)
-        second = jnp.where(mine == 0, other, value)
-        value = jnp.concatenate([first, second], axis=0)
-    return value
-
-
-def local(tables, object_field, probe, amplitudes, offsets):
+def fold_kernel(bit, value_ref, came_ref, kept_ref, sent_ref, total_ref):
+    total_ref[...] = value_ref[...] + came_ref[...]
+    kept, sent = halves_of(bit, kept_ref.shape[0])
+    kept_ref[...] = total_ref[kept]
+    sent_ref[...] = total_ref[sent]
+
+
+def fold(bit, value, came):
+    rows, side = value.shape
+    return pl.pallas_call(
+        functools.partial(fold_kernel, bit),
+        out_shape=[shape_of(rows // 2, side)] * 2,
+        in_specs=whole_spec(2),
+        out_specs=whole_spec(2),
+        scratch_shapes=[VMEM(value.shape, jnp.float32)],
+        compiler_params=pltpu.CompilerParams(vmem_limit_bytes=4 * MIB),
+        cost_estimate=cost(100_000, MIB),
+        name="fold",
+    )(value, came)
+
+
+def join_kernel(bit, value_ref, other_ref, out_ref):
+    kept, sent = halves_of(bit, value_ref.shape[0])
+    out_ref[kept] = value_ref[...]
+    out_ref[sent] = other_ref[...]
+
+
+def join(bit, value, other):
+    rows, side = value.shape
+    return pl.pallas_call(
+        functools.partial(join_kernel, bit),
+        out_shape=shape_of(2 * rows, side),
+        in_specs=whole_spec(2),
+        out_specs=whole_spec(1)[0],
+        compiler_params=pltpu.CompilerParams(vmem_limit_bytes=4 * MIB),
+        cost_estimate=cost(100_000, MIB),
+        name="join",
+    )(value, other)
+
+
+def illuminate_kernel(value_ref, other_ref, probe_ref, out_ref, total_ref):
+    kept, sent = halves_of(0, value_ref.shape[0])
+    total_ref[kept] = value_ref[...]
+    total_ref[sent] = other_ref[...]
+    side = probe_ref.shape[1]
+    part = 1.0 / (total_ref[2 * side :] + probe_damping)
+    out_ref[0] = probe_ref[0] + total_ref[:side] * part
+    out_ref[1] = probe_ref[1] + total_ref[side : 2 * side] * part
+
+
+def illuminate(value, other, probe):
+    rows, side = value.shape
+    return pl.pallas_call(
+        illuminate_kernel,
+        out_shape=shape_of(*probe.shape),
+        in_specs=whole_spec(3),
+        out_specs=whole_spec(1)[0],
+        scratch_shapes=[VMEM((2 * rows, side), jnp.float32)],
+        compiler_params=pltpu.CompilerParams(vmem_limit_bytes=6 * MIB),
+        cost_estimate=cost(1_000_000, 2 * MIB),
+        name="illuminate",
+    )(value, other, probe)
+
+
+def tied(*values):
+    return lax.optimization_barrier(values)
+
+
+def local(table, object_field, probe, amplitudes, offsets):
     side = probe.shape[1]
     tile = object_field.shape[1:]
     measured = amplitudes[0, 0]
     own_offsets = offsets[0, 0].reshape(-1)
-
-    first = shifted(object_field[:, :side, :side], "row", -1)
-    second = shifted(object_field[:, :side, side:], "row", -1)
+    col_bits = int(math.log2(lax.axis_size("col")))
+    row_bits = int(math.log2(lax.axis_size("row")))
+
+    strip, whole = tied(object_field[:, :side, :side], object_field)
+    first = shifted(strip, "row", -1)
+    second = shifted(whole[:, :side, side:], "row", -1)
     right = shifted(object_field[:, :, :side], "col", -1)
     near = jnp.stack([shifted(own_offsets, "row", 1), own_offsets])
     near = jnp.stack([shifted(near, "col", 1), near], axis=1).reshape(-1)
     dense = density(0, near, probe, tile)
-    first, dense = lax.optimization_barrier((first, dense))
+    first, dense = tied(first, dense)
     corner = shifted(first, "col", -1)
     field = object_field
     for sweep in range(offsets.shape[2]):
         flat = sweep == 0
         last = sweep == offsets.shape[2] - 1
-        terms, down_first, down_second, beside, cross, sums = scan_step(
-            sweep, flat, near, probe, measured[sweep], tables, field, right, first, second, corner
+        terms, down_first, down_second, beside, cross, kept, sent = scan_step(
+            sweep, flat, near, probe, measured, table, field, right, first, second, corner
         )
         cross = shifted(cross, "col", 1)
         second = shifted(down_second, "row", 1)
         left = shifted(beside, "col", 1)
-        total = all_summed(sums.reshape(-1, side)).reshape(3, side, side)
+        came = swapped(sent, "col", 1)
+        for bit in range(1, col_bits):
+            kept, sent = fold(bit, kept, came)
+            came = swapped(sent, "col", 1 << bit)
+        came, cross = tied(came, cross)
+        total = kept + came
         first = shifted(down_first + cross, "row", 1)
+        for bit in range(row_bits):
+            came = swapped(total, "row", 1 << bit)
+            if bit == 0:
+                came, second = tied(came, second)
+            if bit == 1 and not last:
+                came, first, left = tied(came, first, left)
+            if bit == 2 and last:
+                came, left = tied(came, left)
+            total = total + came
+        for bit in reversed(range(1, col_bits)):
+            other = swapped(total, "col", 1 << bit)
+            if last and bit == col_bits - 1:
+                other, first = tied(other, first)
+            total = join(bit, total, other)
+        other = swapped(total, "col", 1)
         if sweep > 0:
             dense = density(sweep, near, probe, tile)
-        probe = probe + total[:2] / (total[2] + probe_damping)[None]
+        probe = illuminate(total, other, probe)
         renewed = renew(flat, last, field, dense, terms, left, first, second)
         field = renewed[0]
         if not last:
@@ -363,14 +496,14 @@
     )
 
     def whole(object_field, probe, amplitudes, offsets):
-        tables = tuple(jnp.asarray(t) for t in dft_tables(probe.shape[1]))
+        table = jnp.asarray(dft_table(probe.shape[1]))
         body = jax.shard_map(
-            lambda *args: local(args[:4], *args[4:]),
+            local,
             mesh=mesh,
-            in_specs=(P(),) * 4 + placed,
+            in_specs=(P(),) + placed,
             out_specs=(P(None, "row", "col"), P()),
             check_vma=False,
         )
-        return body(*tables, object_field, probe, amplitudes, offsets)
+        return body(table, object_field, probe, amplitudes, offsets)
 
     return whole

time: 217 us -> 182 us (0.84)
  starting transfers between devices: 70.1 us -> 52.3 us
  local copies, waits for them, and re-layouts: 21.1 us -> 6.45 us
  other arithmetic: 8.59 us -> 0.33 us
  waiting for transfers between devices: 89.2 us -> 95.5 us
    unnamed x48 -> x12, local copies, waits for them, and re-layouts: 14.8 us -> 1.06 us
    ppermute x14, waiting for transfers between devices: 37 us -> 47.4 us  [swapped(): return lax.ppermute(array, axis, [(i, i ^ mask) for i in range(peers)])]
    ppermute x18, starting transfers between devices: 37.3 us -> 27.2 us  [shifted(): lax.ppermute(array, axis, [(i, (i + by) % peers) for i in range(peers)])]
    ppermute x14, starting transfers between devices: 32.8 us -> 25.1 us  [swapped(): return lax.ppermute(array, axis, [(i, i ^ mask) for i in range(peers)])]
    ppermute x18, waiting for transfers between devices: 52.2 us -> 48.2 us  [shifted(): lax.ppermute(array, axis, [(i, (i + by) % peers) for i in range(peers)])]
    add x14 -> x8, other arithmetic: 4.1 us -> 0.21 us  [the longest x6 0.15 us: local(): total = total + came]
    pallas_call x2, Pallas kernels: 4.89 us -> 2.38 us  [renew(): pl.pallas_call(functools.partial(renew_kernel, flat, last), out_shape=sha...]
    select_n x4 -> x0, other arithmetic: 2.24 us -> none  [all_summed(): first = jnp.where(mine == 0, value, other)]
  transfers between devices with their start and end apart: 32 -> 32, of which waited for: 18 -> 19; matrix products, arithmetic and copies ran while one was open for 4% -> 2% of each run, Pallas kernels for 4% -> 3%
where the time goes in v3:
time: 182 us; the launch traced here: 181 us
  waiting for transfers between devices  95.5 us (52%)
  starting transfers between devices  52.3 us (29%)
  Pallas kernels  25.2 us (14%)
  local copies, waits for them, and re-layouts  6.45 us (4%)
    ppermute x18, waiting for transfers between devices, shifted(): lax.ppermute(array, axis, [(i, (i + by) % peers) for i in range(peers)])  48.2 us
    ppermute x14, waiting for transfers between devices, swapped(): return lax.ppermute(array, axis, [(i, i ^ mask) for i in range(peers)])  47.4 us
    ppermute x18, starting transfers between devices, shifted(): lax.ppermute(array, axis, [(i, (i + by) % peers) for i in range(peers)])  27.2 us
    ppermute x14, starting transfers between devices, swapped(): return lax.ppermute(array, axis, [(i, i ^ mask) for i in range(peers)])  25.1 us
    pallas_call x2, Pallas kernels, scan_step(): pl.pallas_call(functools.partial(scan_kernel, sweep, flat), out_shape=sha...  18.7 us
  transfers between devices with their start and end apart: 32, of which 19 were waited for; matrix products, arithmetic and copies ran while one was open for 2% of the time, Pallas kernels for 3%

profile of v3, /device:TPU:0, one launch (start us, length us, event | category | flops | bytes accessed | tf_op | source)
XLA Modules:
  0.0 180.7 jit_solution(657538341119334873)
XLA Ops:
  0.7 2.0 %slice.9 = f32[2,256,256]{2,1,0:T(8,128)} slice(f32[2,512,512]{2,1,0:T(8,128)} %refs_0_.3), slice={[0:2], [0:256], [0:256]} | slice | bytes 1048576 | tf_op jit(solution)/shard_map/slice | solution.py:436
  2.7 6.0 %collective-permute-start = (f32[2,256,256]{2,1,0:T(8,128)}, f32[2,256,256]{2,1,0:T(8,128)}, u32[]{:S(2)}, u32[]{:S(2)}) collective-permute-start(f32[2,256,256]{2,1,0:T(8,128)} %slice.9), channel_id=1, source_target_pairs={{0,28},{4,0},{8,4},{12,8},{16,12},{20,16},{24,20},{28,24},{1,29},{... | collective-permute-start | bytes 1572872 | tf_op jit(solution)/shard_map/ppermute | solution.py:25
  8.7 2.3 %slice.10 = f32[2,512,256]{2,1,0:T(8,128)} slice(f32[2,512,512]{2,1,0:T(8,128)} %refs_0_.3), slice={[0:2], [0:512], [0:256]} | slice | bytes 2097152 | tf_op jit(solution)/shard_map/slice | solution.py:439
  12.6 5.3 %collective-permute-done.1 = s32[8]{0:T(128)S(1)} collective-permute-done((s32[8]{0:T(128)S(1)}, s32[8]{0:T(128)S(1)}, u32[]{:S(2)}, u32[]{:S(2)}) %collective-permute-start.1) | collective-permute-done | bytes 64 | tf_op jit(solution)/shard_map/ppermute | solution.py:25
  18.1 3.0 %collective-permute-done.2 = s32[2,8]{1,0:T(2,128)S(1)} collective-permute-done((s32[2,8]{1,0:T(2,128)S(1)}, s32[2,8]{1,0:T(2,128)S(1)}, u32[]{:S(2)}, u32[]{:S(2)}) %collective-permute-start.2) | collective-permute-done | bytes 96 | tf_op jit(solution)/shard_map/ppermute | solution.py:25
  22.6 10.5 %collective-permute-done.4.refs_6_ = f32[2,256,256]{2,1,0:T(8,128)} collective-permute-done((f32[2,256,256]{2,1,0:T(8,128)}, f32[2,256,256]{2,1,0:T(8,128)}, u32[]{:S(2)}, u32[]{:S(2)}) %collective-permute-start.4) | collective-permute-done | bytes 524320 | tf_op jit(solution)/shard_map/ppermute | solution.py:25
  34.2 9.9 %scan.2 = (f32[2,4,512,128]{3,2,1,0:T(8,128)S(1)}, f32[2,2,256,128]{3,2,1,0:T(8,128)S(1)}, f32[2,2,256,128]{3,2,1,0:T(8,128)S(1)}, f32[2,2,512,128]{3,2,1,0:T(8,...) custom-call(s32[32]{0:T(128)S(1)} %reshape.7.offsets_ref, ...), custom_call_target="tpu_custom_call" | custom-call | flops 7000000000 | bytes 12582912 | tf_op jit(solution)/shard_map/scan/pallas_call | solution.py:245
  46.6 8.2 %collective-permute-done.8 = f32[2,2,256,128]{3,2,1,0:T(8,128)S(1)} collective-permute-done((f32[2,2,256,128]{3,2,1,0:T(8,128)S(1)}, f32[2,2,256,128]{3,2,1,0:T(8,128)S(1)}, u32[]{:S(2)}, u32[]{:S(2)}) %collective-permute-start.8) | collective-permute-done | bytes 524320 | tf_op jit(solution)/shard_map/ppermute | solution.py:25
  55.7 6.3 %collective-permute-done.10.refs_5_ = f32[2,2,256,128]{3,2,1,0:T(8,128)S(1)} collective-permute-done((f32[2,2,256,128]{3,2,1,0:T(8,128)S(1)}, f32[2,2,256,128]{3,2,1,0:T(8,128)S(1)}, u32[]{:S(2)}, u32[]{:S(2)}) %collective-permute-start.10) | collective-permute-done | bytes 524320 | tf_op jit(solution)/shard_map/ppermute | solution.py:25
  62.0 7.6 %collective-permute-done.9 = f32[192,256]{1,0:T(8,128)S(1)} collective-permute-done((f32[192,256]{1,0:T(8,128)S(1)}, f32[192,256]{1,0:T(8,128)S(1)}, u32[]{:S(2)}, u32[]{:S(2)}) %collective-permute-start.9) | collective-permute-done | bytes 196640 | tf_op jit(solution)/shard_map/ppermute | solution.py:30
  69.8 5.7 %collective-permute-done.11 = f32[192,256]{1,0:T(8,128)S(1)} collective-permute-done((f32[192,256]{1,0:T(8,128)S(1)}, f32[192,256]{1,0:T(8,128)S(1)}, u32[]{:S(2)}, u32[]{:S(2)}) %collective-permute-start.11) | collective-permute-done | bytes 196640 | tf_op jit(solution)/shard_map/ppermute | solution.py:30
  76.0 3.9 %collective-permute-start.18 = (f32[2,2,256,128]{3,2,1,0:T(8,128)S(1)}, f32[2,2,256,128]{3,2,1,0:T(8,128)S(1)}, u32[]{:S(2)}, u32[]{:S(2)}) collective-permute-start(f32[2,2,256,128]{3,2,1,0:T(8,128)S(1)} %get-tuple-element.65), channel_id=1, source_target_pairs={{0,28},{4,0},{8,4},{12,8},{16,12},{20,16},{24,20},{28,24},{1,29},{... | collective-permute-start | bytes 1572872 | tf_op jit(solution)/shard_map/ppermute | solution.py:25
  79.9 8.3 %collective-permute-start.17 = (f32[2,2,512,128]{3,2,1,0:T(8,128)S(1)}, f32[2,2,512,128]{3,2,1,0:T(8,128)S(1)}, u32[]{:S(2)}, u32[]{:S(2)}) collective-permute-start(f32[2,2,512,128]{3,2,1,0:T(8,128)S(1)} %get-tuple-element.64), channel_id=1, source_target_pairs={{0,3},{1,0},{2,1},{3,2},{4,7},{5,4},{6,5},{7,6},{8,11},{9,8},{10,9... | collective-permute-start | bytes 3145736 | tf_op jit(solution)/shard_map/ppermute | solution.py:25
  88.2 2.5 %collective-permute-start.14 = (f32[192,256]{1,0:T(8,128)S(1)}, f32[192,256]{1,0:T(8,128)S(1)}, u32[]{:S(2)}, u32[]{:S(2)}) collective-permute-start(f32[192,256]{1,0:T(8,128)S(1)} %add.33), channel_id=1, source_target_pairs={{0,16},{4,20},{8,24},{12,28},{16,0},{20,4},{24,8},{28,12},{1,17},{... | collective-permute-start | bytes 589832 | tf_op jit(solution)/shard_map/ppermute | solution.py:30
  90.7 10.5 %collective-permute-done.14 = f32[192,256]{1,0:T(8,128)S(1)} collective-permute-done((f32[192,256]{1,0:T(8,128)S(1)}, f32[192,256]{1,0:T(8,128)S(1)}, u32[]{:S(2)}, u32[]{:S(2)}) %collective-permute-start.14) | collective-permute-done | bytes 196640 | tf_op jit(solution)/shard_map/ppermute | solution.py:30
  101.5 4.3 %collective-permute-start.20 = (f32[2,2,256,128]{3,2,1,0:T(8,128)S(1)}, f32[2,2,256,128]{3,2,1,0:T(8,128)S(1)}, u32[]{:S(2)}, u32[]{:S(2)}) collective-permute-start(f32[2,2,256,128]{3,2,1,0:T(8,128)S(1)} %collective-permute-done.18.refs_5_), channel_id=1, source_target_pairs={{0,3},{1,0},{2,1},{3,2},{4,7},{5,4},{6,5},{7,6},{8,11},{9,8},{10,9... | collective-permute-start | bytes 1572872 | tf_op jit(solution)/shard_map/ppermute | solution.py:25
  107.1 2.5 %collective-permute-start.16 = (f32[384,256]{1,0:T(8,128)S(1)}, f32[384,256]{1,0:T(8,128)S(1)}, u32[]{:S(2)}, u32[]{:S(2)}) collective-permute-start(f32[384,256]{1,0:T(8,128)S(1)} %join.2.value_ref), channel_id=1, source_target_pairs={{0,1},{1,0},{2,3},{3,2},{4,5},{5,4},{6,7},{7,6},{8,9},{9,8},{10,11... | collective-permute-start | bytes 1179656 | tf_op jit(solution)/shard_map/ppermute | solution.py:30
  111.1 1.7 collective-permute-done.19.refs_6_
  113.8 8.8 %scan.3 = (f32[2,4,512,128]{3,2,1,0:T(8,128)S(1)}, f32[2,2,256,128]{3,2,1,0:T(8,128)S(1)}, f32[2,2,256,128]{3,2,1,0:T(8,128)S(1)}, f32[2,2,512,128]{3,2,1,0:T(8,...) custom-call(s32[32]{0:T(128)S(1)} %reshape.7.offsets_ref, ...), custom_call_target="tpu_custom_call" | custom-call | flops 7000000000 | bytes 12582912 | tf_op jit(solution)/shard_map/scan/pallas_call | solution.py:245
  122.6 2.3 %collective-permute-start.21 = (f32[384,256]{1,0:T(8,128)S(1)}, f32[384,256]{1,0:T(8,128)S(1)}, u32[]{:S(2)}, u32[]{:S(2)}) collective-permute-start(f32[384,256]{1,0:T(8,128)S(1)} %get-tuple-element.69), channel_id=1, source_target_pairs={{0,1},{1,0},{2,3},{3,2},{4,5},{5,4},{6,7},{7,6},{8,9},{9,8},{10,11... | collective-permute-start | bytes 1179656 | tf_op jit(solution)/shard_map/ppermute | solution.py:30
  125.0 2.0 %collective-permute-start.28 = (f32[2,2,512,128]{3,2,1,0:T(8,128)S(1)}, f32[2,2,512,128]{3,2,1,0:T(8,128)S(1)}, u32[]{:S(2)}, u32[]{:S(2)}) collective-permute-start(f32[2,2,512,128]{3,2,1,0:T(8,128)S(1)} %get-tuple-element.76), channel_id=1, source_target_pairs={{0,1},{1,2},{2,3},{3,0},{4,5},{5,6},{6,7},{7,4},{8,9},{9,10},{10,1... | collective-permute-start | bytes 3145736 | tf_op jit(solution)/shard_map/ppermute | solution.py:25
  127.7 1.6 collective-permute-start.22
  129.3 6.3 %collective-permute-done.23 = f32[2,2,256,128]{3,2,1,0:T(8,128)S(1)} collective-permute-done((f32[2,2,256,128]{3,2,1,0:T(8,128)S(1)}, f32[2,2,256,128]{3,2,1,0:T(8,128)S(1)}, u32[]{:S(2)}, u32[]{:S(2)}) %collective-permute-start.23) | collective-permute-done | bytes 524320 | tf_op jit(solution)/shard_map/ppermute | solution.py:25
  135.7 2.1 %collective-permute-start.24 = (f32[192,256]{1,0:T(8,128)S(1)}, f32[192,256]{1,0:T(8,128)S(1)}, u32[]{:S(2)}, u32[]{:S(2)}) collective-permute-start(f32[192,256]{1,0:T(8,128)S(1)} %add.35), channel_id=1, source_target_pairs={{0,4},{4,0},{8,12},{12,8},{16,20},{20,16},{24,28},{28,24},{1,5},{5... | collective-permute-start | bytes 589832 | tf_op jit(solution)/shard_map/ppermute | solution.py:30
  137.8 5.9 %collective-permute-done.25.refs_5_ = f32[2,2,256,128]{3,2,1,0:T(8,128)S(1)} collective-permute-done((f32[2,2,256,128]{3,2,1,0:T(8,128)S(1)}, f32[2,2,256,128]{3,2,1,0:T(8,128)S(1)}, u32[]{:S(2)}, u32[]{:S(2)}) %collective-permute-start.25) | collective-permute-done | bytes 524320 | tf_op jit(solution)/shard_map/ppermute | solution.py:25
  143.7 2.0 %collective-permute-done.24 = f32[192,256]{1,0:T(8,128)S(1)} collective-permute-done((f32[192,256]{1,0:T(8,128)S(1)}, f32[192,256]{1,0:T(8,128)S(1)}, u32[]{:S(2)}, u32[]{:S(2)}) %collective-permute-start.24) | collective-permute-done | bytes 196640 | tf_op jit(solution)/shard_map/ppermute | solution.py:30
  145.9 5.5 %collective-permute-done.26 = f32[192,256]{1,0:T(8,128)S(1)} collective-permute-done((f32[192,256]{1,0:T(8,128)S(1)}, f32[192,256]{1,0:T(8,128)S(1)}, u32[]{:S(2)}, u32[]{:S(2)}) %collective-permute-start.26) | collective-permute-done | bytes 196640 | tf_op jit(solution)/shard_map/ppermute | solution.py:30
  152.0 7.6 %collective-permute-done.27 = f32[192,256]{1,0:T(8,128)S(1)} collective-permute-done((f32[192,256]{1,0:T(8,128)S(1)}, f32[192,256]{1,0:T(8,128)S(1)}, u32[]{:S(2)}, u32[]{:S(2)}) %collective-permute-start.27) | collective-permute-done | bytes 196640 | tf_op jit(solution)/shard_map/ppermute | solution.py:30
  160.4 5.0 %collective-permute-done.29.other_ref = f32[192,256]{1,0:T(8,128)S(1)} collective-permute-done((f32[192,256]{1,0:T(8,128)S(1)}, f32[192,256]{1,0:T(8,128)S(1)}, u32[]{:S(2)}, u32[]{:S(2)}) %collective-permute-start.29) | collective-permute-done | bytes 196640 | tf_op jit(solution)/shard_map/ppermute | solution.py:30
  165.5 11.0 %collective-permute-start.31 = (f32[384,256]{1,0:T(8,128)S(1)}, f32[384,256]{1,0:T(8,128)S(1)}, u32[]{:S(2)}, u32[]{:S(2)}) collective-permute-start(f32[384,256]{1,0:T(8,128)S(1)} %join.3.value_ref), channel_id=1, source_target_pairs={{0,1},{1,0},{2,3},{3,2},{4,5},{5,4},{6,7},{7,6},{8,9},{9,8},{10,11... | collective-permute-start | bytes 1179656 | tf_op jit(solution)/shard_map/ppermute | solution.py:30
  176.5 1.4 density.3.refs_1_
  177.9 1.8 %renew.3 = f32[2,512,512]{2,1,0:T(8,128)} custom-call(f32[2,4,512,128]{3,2,1,0:T(8,128)S(1)} %get-tuple-element.62.refs_3_.refs_0_, f32[4,512,128]{2,1,0:T(8,128)S(1)} %density.3.refs_1_, f32[2,4,512,128]{3,2,1,0:T(8,128)S(1)} %get-tuple-element.67.refs_2_, f32[2,2,512,128]{3,2,1,0:T(8,128)S(1)} %collective-permute-done.28.refs_3_, ...), custom_call_target="tpu_custom_call" | custom-call | flops 4000000 | bytes 10485760 | tf_op jit(solution)/shard_map/renew/pallas_call | solution.py:349
  (75 shorter events, 15.9 us)
Async XLA Ops:
  2.7 19.9 %collective-permute-start = (f32[2,256,256]{2,1,0:T(8,128)}, f32[2,256,256]{2,1,0:T(8,128)}, u32[]{:S(2)}, u32[]{:S(2)}) collective-permute-start(f32[2,256,256]{2,1,0:T(8,128)} %slice.9), channel_id=1, source_target_pairs={{0,28},{4,0},{8,4},{12,8},{16,12},{20,16},{24,20},{28,24},{1,29},{... | collective-permute-start | bytes 1572872 | tf_op jit(solution)/shard_map/ppermute | solution.py:25
  11.0 22.1 %collective-permute-start.3 = (f32[2,512,256]{2,1,0:T(8,128)}, f32[2,512,256]{2,1,0:T(8,128)}, u32[]{:S(2)}, u32[]{:S(2)}) collective-permute-start(f32[2,512,256]{2,1,0:T(8,128)} %slice.10), channel_id=1, source_target_pairs={{0,3},{1,0},{2,1},{3,2},{4,7},{5,4},{6,5},{7,6},{8,11},{9,8},{10,9... | collective-permute-start | bytes 3145736 | tf_op jit(solution)/shard_map/ppermute | solution.py:25
  11.7 6.2 %collective-permute-start.1 = (s32[8]{0:T(128)S(1)}, s32[8]{0:T(128)S(1)}, u32[]{:S(2)}, u32[]{:S(2)}) collective-permute-start(s32[8]{0:T(128)S(1)} %reshape_squeeze.3), channel_id=1, source_target_pairs={{0,4},{4,8},{8,12},{12,16},{16,20},{20,24},{24,28},{28,0},{1,5},{5... | collective-permute-start | bytes 104 | tf_op jit(solution)/shard_map/ppermute | solution.py:25
  17.9 3.1 %collective-permute-start.2 = (s32[2,8]{1,0:T(2,128)S(1)}, s32[2,8]{1,0:T(2,128)S(1)}, u32[]{:S(2)}, u32[]{:S(2)}) collective-permute-start(s32[2,8]{1,0:T(2,128)S(1)} %get-tuple-element.84), channel_id=1, source_target_pairs={{0,1},{1,2},{2,3},{3,0},{4,5},{5,6},{6,7},{7,4},{8,9},{9,10},{10,1... | collective-permute-start | bytes 200 | tf_op jit(solution)/shard_map/ppermute | solution.py:25
  18.0 15.1 %collective-permute-start.4 = (f32[2,256,256]{2,1,0:T(8,128)}, f32[2,256,256]{2,1,0:T(8,128)}, u32[]{:S(2)}, u32[]{:S(2)}) collective-permute-start(f32[2,256,256]{2,1,0:T(8,128)} %slice.11), channel_id=1, source_target_pairs={{0,28},{4,0},{8,4},{12,8},{16,12},{20,16},{24,20},{28,24},{1,29},{... | collective-permute-start | bytes 1572872 | tf_op jit(solution)/shard_map/ppermute | solution.py:25
  22.6 10.5 %collective-permute-start.5 = (f32[2,256,256]{2,1,0:T(8,128)}, f32[2,256,256]{2,1,0:T(8,128)S(1)}, u32[]{:S(2)}, u32[]{:S(2)}) collective-permute-start(f32[2,256,256]{2,1,0:T(8,128)} %collective-permute-done.refs_5_), channel_id=1, source_target_pairs={{0,3},{1,0},{2,1},{3,2},{4,7},{5,4},{6,5},{7,6},{8,11},{9,8},{10,9... | collective-permute-start | bytes 1572872 | tf_op jit(solution)/shard_map/ppermute | solution.py:25
  44.0 1.8 collective-permute-start.6
  44.2 10.7 %collective-permute-start.8 = (f32[2,2,256,128]{3,2,1,0:T(8,128)S(1)}, f32[2,2,256,128]{3,2,1,0:T(8,128)S(1)}, u32[]{:S(2)}, u32[]{:S(2)}) collective-permute-start(f32[2,2,256,128]{3,2,1,0:T(8,128)S(1)} %get-tuple-element.52), channel_id=1, source_target_pairs={{0,1},{1,2},{2,3},{3,0},{4,5},{5,6},{6,7},{7,4},{8,9},{9,10},{10,1... | collective-permute-start | bytes 1572872 | tf_op jit(solution)/shard_map/ppermute | solution.py:25
  44.6 30.8 %collective-permute-start.13 = (f32[2,2,512,128]{3,2,1,0:T(8,128)S(1)}, f32[2,2,512,128]{3,2,1,0:T(8,128)S(1)}, u32[]{:S(2)}, u32[]{:S(2)}) collective-permute-start(f32[2,2,512,128]{3,2,1,0:T(8,128)S(1)} %get-tuple-element.58), channel_id=1, source_target_pairs={{0,1},{1,2},{2,3},{3,0},{4,5},{5,6},{6,7},{7,4},{8,9},{9,10},{10,1... | collective-permute-start | bytes 3145736 | tf_op jit(solution)/shard_map/ppermute | solution.py:25
  45.0 17.0 %collective-permute-start.10 = (f32[2,2,256,128]{3,2,1,0:T(8,128)S(1)}, f32[2,2,256,128]{3,2,1,0:T(8,128)S(1)}, u32[]{:S(2)}, u32[]{:S(2)}) collective-permute-start(f32[2,2,256,128]{3,2,1,0:T(8,128)S(1)} %get-tuple-element.54), channel_id=1, source_target_pairs={{0,4},{4,8},{8,12},{12,16},{16,20},{20,24},{24,28},{28,0},{1,5},{5... | collective-permute-start | bytes 1572872 | tf_op jit(solution)/shard_map/ppermute | solution.py:25
  45.9 9.0 %collective-permute-start.7 = (f32[192,256]{1,0:T(8,128)S(1)}, f32[192,256]{1,0:T(8,128)S(1)}, u32[]{:S(2)}, u32[]{:S(2)}) collective-permute-start(f32[192,256]{1,0:T(8,128)S(1)} %get-tuple-element.51), channel_id=1, source_target_pairs={{0,2},{1,3},{2,0},{3,1},{4,6},{5,7},{6,4},{7,5},{8,10},{9,11},{10,... | collective-permute-start | bytes 589832 | tf_op jit(solution)/shard_map/ppermute | solution.py:30
  54.9 20.5 %collective-permute-start.12 = (f32[2,2,256,128]{3,2,1,0:T(8,128)S(1)}, f32[2,2,256,128]{3,2,1,0:T(8,128)S(1)}, u32[]{:S(2)}, u32[]{:S(2)}) collective-permute-start(f32[2,2,256,128]{3,2,1,0:T(8,128)S(1)} %add.32), channel_id=1, source_target_pairs={{0,4},{4,8},{8,12},{12,16},{16,20},{20,24},{24,28},{28,0},{1,5},{5... | collective-permute-start | bytes 1572872 | tf_op jit(solution)/shard_map/ppermute | solution.py:25
  55.0 14.6 %collective-permute-start.9 = (f32[192,256]{1,0:T(8,128)S(1)}, f32[192,256]{1,0:T(8,128)S(1)}, u32[]{:S(2)}, u32[]{:S(2)}) collective-permute-start(f32[192,256]{1,0:T(8,128)S(1)} %add.30), channel_id=1, source_target_pairs={{0,4},{4,0},{8,12},{12,8},{16,20},{20,16},{24,28},{28,24},{1,5},{5... | collective-permute-start | bytes 589832 | tf_op jit(solution)/shard_map/ppermute | solution.py:30
  69.7 5.7 %collective-permute-start.11 = (f32[192,256]{1,0:T(8,128)S(1)}, f32[192,256]{1,0:T(8,128)S(1)}, u32[]{:S(2)}, u32[]{:S(2)}) collective-permute-start(f32[192,256]{1,0:T(8,128)S(1)} %add.31), channel_id=1, source_target_pairs={{0,8},{4,12},{8,0},{12,4},{16,24},{20,28},{24,16},{28,20},{1,9},{5... | collective-permute-start | bytes 589832 | tf_op jit(solution)/shard_map/ppermute | solution.py:30
  76.0 25.5 %collective-permute-start.18 = (f32[2,2,256,128]{3,2,1,0:T(8,128)S(1)}, f32[2,2,256,128]{3,2,1,0:T(8,128)S(1)}, u32[]{:S(2)}, u32[]{:S(2)}) collective-permute-start(f32[2,2,256,128]{3,2,1,0:T(8,128)S(1)} %get-tuple-element.65), channel_id=1, source_target_pairs={{0,28},{4,0},{8,4},{12,8},{16,12},{20,16},{24,20},{28,24},{1,29},{... | collective-permute-start | bytes 1572872 | tf_op jit(solution)/shard_map/ppermute | solution.py:25
  79.9 32.9 %collective-permute-start.17 = (f32[2,2,512,128]{3,2,1,0:T(8,128)S(1)}, f32[2,2,512,128]{3,2,1,0:T(8,128)S(1)}, u32[]{:S(2)}, u32[]{:S(2)}) collective-permute-start(f32[2,2,512,128]{3,2,1,0:T(8,128)S(1)} %get-tuple-element.64), channel_id=1, source_target_pairs={{0,3},{1,0},{2,1},{3,2},{4,7},{5,4},{6,5},{7,6},{8,11},{9,8},{10,9... | collective-permute-start | bytes 3145736 | tf_op jit(solution)/shard_map/ppermute | solution.py:25
  88.2 13.0 %collective-permute-start.14 = (f32[192,256]{1,0:T(8,128)S(1)}, f32[192,256]{1,0:T(8,128)S(1)}, u32[]{:S(2)}, u32[]{:S(2)}) collective-permute-start(f32[192,256]{1,0:T(8,128)S(1)} %add.33), channel_id=1, source_target_pairs={{0,16},{4,20},{8,24},{12,28},{16,0},{20,4},{24,8},{28,12},{1,17},{... | collective-permute-start | bytes 589832 | tf_op jit(solution)/shard_map/ppermute | solution.py:30
  101.2 5.9 %collective-permute-start.15 = (f32[192,256]{1,0:T(8,128)S(1)}, f32[192,256]{1,0:T(8,128)S(1)}, u32[]{:S(2)}, u32[]{:S(2)}) collective-permute-start(f32[192,256]{1,0:T(8,128)S(1)} %add.34.value_ref), channel_id=1, source_target_pairs={{0,2},{1,3},{2,0},{3,1},{4,6},{5,7},{6,4},{7,5},{8,10},{9,11},{10,... | collective-permute-start | bytes 589832 | tf_op jit(solution)/shard_map/ppermute | solution.py:30
  101.3 11.5 %collective-permute-start.19 = (f32[2,2,256,128]{3,2,1,0:T(8,128)S(1)}, f32[2,2,256,128]{3,2,1,0:T(8,128)S(1)}, u32[]{:S(2)}, u32[]{:S(2)}) collective-permute-start(f32[2,2,256,128]{3,2,1,0:T(8,128)S(1)} %get-tuple-element.66), channel_id=1, source_target_pairs={{0,28},{4,0},{8,4},{12,8},{16,12},{20,16},{24,20},{28,24},{1,29},{... | collective-permute-start | bytes 1572872 | tf_op jit(solution)/shard_map/ppermute | solution.py:25
  101.5 12.2 %collective-permute-start.20 = (f32[2,2,256,128]{3,2,1,0:T(8,128)S(1)}, f32[2,2,256,128]{3,2,1,0:T(8,128)S(1)}, u32[]{:S(2)}, u32[]{:S(2)}) collective-permute-start(f32[2,2,256,128]{3,2,1,0:T(8,128)S(1)} %collective-permute-done.18.refs_5_), channel_id=1, source_target_pairs={{0,3},{1,0},{2,1},{3,2},{4,7},{5,4},{6,5},{7,6},{8,11},{9,8},{10,9... | collective-permute-start | bytes 1572872 | tf_op jit(solution)/shard_map/ppermute | solution.py:25
  107.1 3.8 %collective-permute-start.16 = (f32[384,256]{1,0:T(8,128)S(1)}, f32[384,256]{1,0:T(8,128)S(1)}, u32[]{:S(2)}, u32[]{:S(2)}) collective-permute-start(f32[384,256]{1,0:T(8,128)S(1)} %join.2.value_ref), channel_id=1, source_target_pairs={{0,1},{1,0},{2,3},{3,2},{4,5},{5,4},{6,7},{7,6},{8,9},{9,8},{10,11... | collective-permute-start | bytes 1179656 | tf_op jit(solution)/shard_map/ppermute | solution.py:30
  122.6 5.0 %collective-permute-start.21 = (f32[384,256]{1,0:T(8,128)S(1)}, f32[384,256]{1,0:T(8,128)S(1)}, u32[]{:S(2)}, u32[]{:S(2)}) collective-permute-start(f32[384,256]{1,0:T(8,128)S(1)} %get-tuple-element.69), channel_id=1, source_target_pairs={{0,1},{1,0},{2,3},{3,2},{4,5},{5,4},{6,7},{7,6},{8,9},{9,8},{10,11... | collective-permute-start | bytes 1179656 | tf_op jit(solution)/shard_map/ppermute | solution.py:30
  124.9 10.7 %collective-permute-start.23 = (f32[2,2,256,128]{3,2,1,0:T(8,128)S(1)}, f32[2,2,256,128]{3,2,1,0:T(8,128)S(1)}, u32[]{:S(2)}, u32[]{:S(2)}) collective-permute-start(f32[2,2,256,128]{3,2,1,0:T(8,128)S(1)} %get-tuple-element.72), channel_id=1, source_target_pairs={{0,1},{1,2},{2,3},{3,0},{4,5},{5,6},{6,7},{7,4},{8,9},{9,10},{10,1... | collective-permute-start | bytes 1572872 | tf_op jit(solution)/shard_map/ppermute | solution.py:25
  125.0 27.1 %collective-permute-start.28 = (f32[2,2,512,128]{3,2,1,0:T(8,128)S(1)}, f32[2,2,512,128]{3,2,1,0:T(8,128)S(1)}, u32[]{:S(2)}, u32[]{:S(2)}) collective-permute-start(f32[2,2,512,128]{3,2,1,0:T(8,128)S(1)} %get-tuple-element.76), channel_id=1, source_target_pairs={{0,1},{1,2},{2,3},{3,0},{4,5},{5,6},{6,7},{7,4},{8,9},{9,10},{10,1... | collective-permute-start | bytes 3145736 | tf_op jit(solution)/shard_map/ppermute | solution.py:25
  127.0 16.7 %collective-permute-start.25 = (f32[2,2,256,128]{3,2,1,0:T(8,128)S(1)}, f32[2,2,256,128]{3,2,1,0:T(8,128)S(1)}, u32[]{:S(2)}, u32[]{:S(2)}) collective-permute-start(f32[2,2,256,128]{3,2,1,0:T(8,128)S(1)} %get-tuple-element.74), channel_id=1, source_target_pairs={{0,4},{4,8},{8,12},{12,16},{16,20},{20,24},{24,28},{28,0},{1,5},{5... | collective-permute-start | bytes 1572872 | tf_op jit(solution)/shard_map/ppermute | solution.py:25
  127.7 7.9 %collective-permute-start.22 = (f32[192,256]{1,0:T(8,128)S(1)}, f32[192,256]{1,0:T(8,128)S(1)}, u32[]{:S(2)}, u32[]{:S(2)}) collective-permute-start(f32[192,256]{1,0:T(8,128)S(1)} %get-tuple-element.71), channel_id=1, source_target_pairs={{0,2},{1,3},{2,0},{3,1},{4,6},{5,7},{6,4},{7,5},{8,10},{9,11},{10,... | collective-permute-start | bytes 589832 | tf_op jit(solution)/shard_map/ppermute | solution.py:30
  135.7 10.0 %collective-permute-start.24 = (f32[192,256]{1,0:T(8,128)S(1)}, f32[192,256]{1,0:T(8,128)S(1)}, u32[]{:S(2)}, u32[]{:S(2)}) collective-permute-start(f32[192,256]{1,0:T(8,128)S(1)} %add.35), channel_id=1, source_target_pairs={{0,4},{4,0},{8,12},{12,8},{16,20},{20,16},{24,28},{28,24},{1,5},{5... | collective-permute-start | bytes 589832 | tf_op jit(solution)/shard_map/ppermute | solution.py:30
  145.7 5.7 %collective-permute-start.26 = (f32[192,256]{1,0:T(8,128)S(1)}, f32[192,256]{1,0:T(8,128)S(1)}, u32[]{:S(2)}, u32[]{:S(2)}) collective-permute-start(f32[192,256]{1,0:T(8,128)S(1)} %add.36), channel_id=1, source_target_pairs={{0,8},{4,12},{8,0},{12,4},{16,24},{20,28},{24,16},{28,20},{1,9},{5... | collective-permute-start | bytes 589832 | tf_op jit(solution)/shard_map/ppermute | solution.py:30
  145.8 14.5 %collective-permute-start.30 = (f32[2,2,256,128]{3,2,1,0:T(8,128)S(1)}, f32[2,2,256,128]{3,2,1,0:T(8,128)S(1)}, u32[]{:S(2)}, u32[]{:S(2)}) collective-permute-start(f32[2,2,256,128]{3,2,1,0:T(8,128)S(1)} %add.39), channel_id=1, source_target_pairs={{0,4},{4,8},{8,12},{12,16},{16,20},{20,24},{24,28},{28,0},{1,5},{5... | collective-permute-start | bytes 1572872 | tf_op jit(solution)/shard_map/ppermute | solution.py:25
  151.5 8.2 %collective-permute-start.27 = (f32[192,256]{1,0:T(8,128)S(1)}, f32[192,256]{1,0:T(8,128)S(1)}, u32[]{:S(2)}, u32[]{:S(2)}) collective-permute-start(f32[192,256]{1,0:T(8,128)S(1)} %add.37), channel_id=1, source_target_pairs={{0,16},{4,20},{8,24},{12,28},{16,0},{20,4},{24,8},{28,12},{1,17},{... | collective-permute-start | bytes 589832 | tf_op jit(solution)/shard_map/ppermute | solution.py:30
  159.7 5.7 %collective-permute-start.29 = (f32[192,256]{1,0:T(8,128)S(1)}, f32[192,256]{1,0:T(8,128)S(1)}, u32[]{:S(2)}, u32[]{:S(2)}) collective-permute-start(f32[192,256]{1,0:T(8,128)S(1)} %add.38.value_ref), channel_id=1, source_target_pairs={{0,2},{1,3},{2,0},{3,1},{4,6},{5,7},{6,4},{7,5},{8,10},{9,11},{10,... | collective-permute-start | bytes 589832 | tf_op jit(solution)/shard_map/ppermute | solution.py:30
  165.5 14.2 %collective-permute-start.31 = (f32[384,256]{1,0:T(8,128)S(1)}, f32[384,256]{1,0:T(8,128)S(1)}, u32[]{:S(2)}, u32[]{:S(2)}) collective-permute-start(f32[384,256]{1,0:T(8,128)S(1)} %join.3.value_ref), channel_id=1, source_target_pairs={{0,1},{1,0},{2,3},{3,2},{4,5},{5,4},{6,7},{7,6},{8,9},{9,8},{10,11... | collective-permute-start | bytes 1179656 | tf_op jit(solution)/shard_map/ppermute | solution.py:30
  (6 other events, 111.9 us)

commit v4 on v3

v4 whole, which is shorter than its diff:
```python
import functools
import math

import jax
import jax.numpy as jnp
import ml_dtypes
import numpy as np
from jax import lax
from jax.experimental import pallas as pl
from jax.experimental.pallas import tpu as pltpu
from jax.sharding import PartitionSpec as P

softening = 0.1
object_damping = 0.5
probe_damping = 1.0
MIB = 1 << 20
lane = 128
SCAN_LIMIT = 24 * MIB
VMEM = pltpu.VMEM
SMEM = pltpu.SMEM


def shifted(array, axis, by):
    peers = lax.axis_size(axis)
    return lax.ppermute(array, axis, [(i, (i + by) % peers) for i in range(peers)])


def swapped(array, axis, mask):
    peers = lax.axis_size(axis)
    return lax.ppermute(array, axis, [(i, i ^ mask) for i in range(peers)])


def handed_on(array, axis):
    peers = lax.axis_size(axis)
    return lax.ppermute(array, axis, [(i, (i + 2 - 4 * (i % 2)) % peers) for i in range(peers)])


def dft_tables(length):
    half = length // 2
    index = np.arange(half)
    parts = []
    for odd in range(2):
        phase = ((2 * index[:, None] + odd) * index[None, :] % length) * (2.0 * math.pi / length)
        real, imag = np.cos(phase) / math.sqrt(length), -np.sin(phase) / math.sqrt(length)
        full = np.block([[real, -imag], [imag, real]])
        for value in (full, full.T):
            high = value.astype(ml_dtypes.bfloat16)
            parts += [high, (value - high.astype(np.float64)).astype(ml_dtypes.bfloat16)]
    return np.stack(parts)


def halves(value):
    high = value.astype(jnp.bfloat16)
    return high, (value - high.astype(jnp.float32)).astype(jnp.bfloat16)


def product(a, b):
    return jnp.dot(a, b, preferred_element_type=jnp.float32)


def left_product(table_ref, number, data):
    top, rest = halves(data)
    high, low = table_ref[2 * number], table_ref[2 * number + 1]
    return product(high, top) + product(high, rest) + product(low, top)


def right_product(data, table_ref, number):
    top, rest = halves(data)
    high, low = table_ref[2 * number], table_ref[2 * number + 1]
    return product(top, high) + product(rest, high) + product(top, low)


def stacked(values, axis):
    return jnp.concatenate(values, axis=axis)


def forward(table_ref, real, imag):
    half = real.shape[0] // 2
    even = stacked([real[:half] + real[half:], imag[:half] + imag[half:]], 0)
    odd = stacked([real[:half] - real[half:], imag[:half] - imag[half:]], 0)
    even, odd = left_product(table_ref, 0, even), left_product(table_ref, 2, odd)
    real, imag = stacked([even[:half], odd[:half]], 0), stacked([even[half:], odd[half:]], 0)
    even = stacked([real[:, :half] + real[:, half:], imag[:, :half] + imag[:, half:]], 1)
    odd = stacked([real[:, :half] - real[:, half:], imag[:, :half] - imag[:, half:]], 1)
    even, odd = right_product(even, table_ref, 1), right_product(odd, table_ref, 3)
    return stacked([even[:, :half], odd[:, :half]], 1), stacked([even[:, half:], odd[:, half:]], 1)


def backward(table_ref, real, imag):
    half = real.shape[0] // 2
    even = left_product(table_ref, 1, stacked([real[:half], imag[:half]], 0))
    odd = left_product(table_ref, 3, stacked([real[half:], imag[half:]], 0))
    one, two = even + odd, even - odd
    real, imag = stacked([one[:half], two[:half]], 0), stacked([one[half:], two[half:]], 0)
    even = right_product(stacked([real[:, :half], imag[:, :half]], 1), table_ref, 0)
    odd = right_product(stacked([real[:, half:], imag[:, half:]], 1), table_ref, 2)
    one, two = even + odd, even - odd
    return stacked([one[:, :half], two[:, :half]], 1), stacked([one[:, half:], two[:, half:]], 1)


def reorder_kernel(amplitude_ref, out_ref):
    side = amplitude_ref.shape[3]
    half = side // 2

    def choice(axis):
        target = lax.broadcasted_iota(jnp.int32, (side, side), axis)
        source = lax.broadcasted_iota(jnp.int32, (side, side), 1 - axis)
        wanted = jnp.where(target < half, 2 * target, 2 * (target - half) + 1)
        return jnp.where(source == wanted, 1.0, 0.0).astype(jnp.bfloat16)

    rows, cols = choice(0), choice(1)
    for sweep in range(amplitude_ref.shape[0]):
        for scan in range(amplitude_ref.shape[1]):
            moved = product(rows, amplitude_ref[sweep, scan]).astype(jnp.bfloat16)
            out_ref[sweep, scan] = product(moved, cols).astype(jnp.bfloat16)


def reorder(amplitudes):
    return pl.pallas_call(
        reorder_kernel,
        out_shape=jax.ShapeDtypeStruct(amplitudes.shape, amplitudes.dtype),
        in_specs=[pl.BlockSpec(memory_space=VMEM)],
        out_specs=pl.BlockSpec(memory_space=VMEM),
        compiler_params=pltpu.CompilerParams(vmem_limit_bytes=8 * MIB),
        cost_estimate=pl.CostEstimate(flops=300_000_000, bytes_accessed=MIB, transcendentals=0),
        name="reorder",
    )(amplitudes)


def split_column(column):
    return lax.div(column, lane), lax.rem(column, lane)


def taken(ref, plane, row, column, side):
    first, shift = split_column(column)
    count = side // lane + 1
    slabs = [ref[plane, first + k, pl.ds(row, side), :] for k in range(count)]
    return pltpu.roll(jnp.concatenate(slabs, axis=1), count * lane - shift, 1)[:, :side]


def turned(value, shift):
    side = value.shape[0]
    wide = jnp.concatenate([value, jnp.zeros((side, lane), jnp.float32)], axis=1)
    return pltpu.roll(wide, shift, 1)


def add_slabs(ref, lead, row, first, wide):
    side = wide.shape[0]
    for k in range(wide.shape[1] // lane):
        spot = lead + (first + k, pl.ds(row, side), slice(None))
        ref[spot] += wide[:, k * lane : (k + 1) * lane]


def columns(number):
    return slice(number * lane, (number + 1) * lane)


def whole_spec(count):
    return [pl.BlockSpec(memory_space=VMEM)] * count


def offsets_spec():
    return pl.BlockSpec(memory_space=SMEM)


def shape_of(*dims):
    return jax.ShapeDtypeStruct(dims, jnp.float32)


def cost(flops, moved):
    return pl.CostEstimate(flops=flops, bytes_accessed=moved, transcendentals=0)


def corner_of(offsets_ref, down, along, sweep, scan):
    spot = (down + 1, along + 1, sweep, scan)
    return offsets_ref[spot + (0,)], offsets_ref[spot + (1,)]


def halves_of(bit, half):
    mine = lax.rem(lax.axis_index("col") >> bit, 2)
    kept = pl.ds(pl.multiple_of(mine * half, 8), half)
    return kept, pl.ds(pl.multiple_of((1 - mine) * half, 8), half)


def scan_kernel(sweep, last, counts, offsets_ref, *refs):
    inputs, outputs, scratch = counts
    probe_hbm, amplitude_hbm, table_hbm = refs[:3]
    field_in = refs[3:inputs]
    outs_hbm = refs[inputs : inputs + outputs]
    rest = refs[inputs + outputs :]
    probe_ref, amplitude_ref, table_ref, sums_ref, windows_ref = rest[:5]
    small_sem, field_sem, out_sem = rest[5:8]
    side = probe_ref.shape[1]
    copies = []

    def fetch(source, target):
        copies.append(pltpu.make_async_copy(source, target, field_sem))

    small = [
        pltpu.make_async_copy(table_hbm, table_ref, small_sem.at[0]),
        pltpu.make_async_copy(probe_hbm, probe_ref, small_sem.at[1]),
        pltpu.make_async_copy(amplitude_hbm.at[sweep], amplitude_ref, small_sem.at[2]),
    ]
    if last:
        field_ref = field_in[0]
    else:
        own_hbm, right_hbm, first_hbm, second_hbm, corner_hbm = field_in
        field_ref = rest[8]
        rows, edge = own_hbm.shape[1], side // lane
        slabs = own_hbm.shape[2] // lane
        for k in range(slabs):
            fetch(own_hbm.at[:, :, columns(k)], field_ref.at[:, k, :rows])
        for k in range(edge):
            fetch(right_hbm.at[:, :, columns(k)], field_ref.at[:, slabs + k, :rows])
            fetch(first_hbm.at[:, :, columns(k)], field_ref.at[:, k, rows:])
            fetch(corner_hbm.at[:, :, columns(k)], field_ref.at[:, slabs + k, rows:])
        for k in range(edge, slabs):
            fetch(second_hbm.at[:, :, columns(k - edge)], field_ref.at[:, k, rows:])
    small[0].start()
    for copy in copies:
        copy.start()
    for copy in small[1:]:
        copy.start()
    small[0].wait()
    for copy in small[1:]:
        copy.wait()
    for copy in copies:
        copy.wait()
    probe_real, probe_imag = probe_ref[0], probe_ref[1]
    pending = []
    for scan in range(2):
        row, column = offsets_ref[0, 0, sweep, scan, 0], offsets_ref[0, 0, sweep, scan, 1]
        patch_real = taken(field_ref, 0, row, column, side)
        patch_imag = taken(field_ref, 1, row, column, side)
        wave_real = probe_real * patch_real - probe_imag * patch_imag
        wave_imag = probe_real * patch_imag + probe_imag * patch_real
        far_real, far_imag = forward(table_ref, wave_real, wave_imag)
        scale = amplitude_ref[scan].astype(jnp.float32) * lax.rsqrt(
            far_real * far_real + far_imag * far_imag + softening
        )
        back_real, back_imag = backward(table_ref, far_real * scale, far_imag * scale)
        diff_real = back_real - wave_real
        diff_imag = back_imag - wave_imag
        term_real = probe_real * diff_real + probe_imag * diff_imag
        term_imag = probe_real * diff_imag - probe_imag * diff_real
        windows_ref[scan, 0] = term_real
        windows_ref[scan, 1] = term_imag
        copy = pltpu.make_async_copy(windows_ref.at[scan], outs_hbm[2].at[scan], out_sem)
        copy.start()
        pending.append(copy)
        sums = (
            patch_real * diff_real + patch_imag * diff_imag,
            patch_real * diff_imag - patch_imag * diff_real,
            patch_real * patch_real + patch_imag * patch_imag,
        )
        for number, value in enumerate(sums):
            spot = slice(number * side, (number + 1) * side)
            if scan == 0:
                sums_ref[spot] = value
            else:
                sums_ref[spot] += value
    kept, sent = halves_of(0, outs_hbm[0].shape[0])
    outs = [(sums_ref.at[sent], outs_hbm[1]), (sums_ref.at[kept], outs_hbm[0])]
    outs = [pltpu.make_async_copy(source, target, out_sem) for source, target in outs]
    for copy in outs:
        copy.start()
    for copy in pending + outs:
        copy.wait()


def scan_step(sweep, last, offsets, probe, amplitudes, table, *field):
    side = probe.shape[1]
    shapes = [shape_of(3 * side // 2, side)] * 2 + [shape_of(2, 2, side, side)]
    scratch = [
        VMEM(probe.shape, jnp.float32),
        VMEM(amplitudes.shape[1:], amplitudes.dtype),
        VMEM(table.shape, table.dtype),
        VMEM((3 * side, side), jnp.float32),
        VMEM((2, 2, side, side), jnp.float32),
        pltpu.SemaphoreType.DMA((3,)),
        pltpu.SemaphoreType.DMA,
        pltpu.SemaphoreType.DMA,
    ]
    if not last:
        rows, cols = field[0].shape[1:]
        scratch.append(VMEM((2, (cols + side) // lane, rows + side, lane), jnp.float32))
    anywhere = pl.BlockSpec(memory_space=pl.ANY)
    counts = (3 + len(field), len(shapes), len(scratch))
    return pl.pallas_call(
        functools.partial(scan_kernel, sweep, last, counts),
        out_shape=shapes,
        in_specs=[offsets_spec()] + [anywhere] * 3 + (whole_spec(1) if last else [anywhere] * len(field)),
        out_specs=[anywhere] * len(shapes),
        scratch_shapes=scratch,
        compiler_params=pltpu.CompilerParams(vmem_limit_bytes=SCAN_LIMIT),
        cost_estimate=cost(7_000_000_000, 12 * MIB),
        name="scan",
    )(offsets, probe, amplitudes, table, *field)


def place_kernel(sweep, offsets_ref, windows_ref, total_ref, *edge_refs):
    side = windows_ref.shape[2]
    edge = side // lane
    slabs, height = total_ref.shape[1:3]
    total_ref[...] = jnp.zeros_like(total_ref)
    for scan in range(2):
        row, column = offsets_ref[0, 0, sweep, scan, 0], offsets_ref[0, 0, sweep, scan, 1]
        first, shift = split_column(column)
        for plane in range(2):
            add_slabs(total_ref, (plane,), row, first, turned(windows_ref[scan, plane], shift))
    for ref, start in zip(edge_refs, (slabs - edge, 0)):
        ref[...] = total_ref[:, start : start + edge, side : height - side]


def place(sweep, offsets, windows, tile, sides):
    side = windows.shape[2]
    edge = side // lane
    height, slabs = tile[0] + side, tile[1] // lane + edge
    shapes = [shape_of(2, slabs, height, lane)] + [shape_of(2, edge, height - 2 * side, lane)] * sides
    return pl.pallas_call(
        functools.partial(place_kernel, sweep),
        out_shape=shapes,
        in_specs=[offsets_spec()] + whole_spec(1),
        out_specs=whole_spec(len(shapes)),
        compiler_params=pltpu.CompilerParams(vmem_limit_bytes=4 * MIB),
        cost_estimate=cost(1_000_000, 6 * MIB),
        name="place",
    )(offsets, windows)


def density_kernel(sweep, reach, offsets_ref, probe_ref, out_ref, total_ref):
    side = probe_ref.shape[1]
    slabs, height = out_ref.shape[:2]
    breadth = slabs * lane
    tile = height - side if reach else height
    span = breadth - side if reach else breadth
    total_ref[...] = jnp.zeros_like(total_ref)
    power = probe_ref[0] * probe_ref[0] + probe_ref[1] * probe_ref[1]
    steps = (-1, 0, 1) if reach else (-1, 0)
    for down in steps:
        for along in steps:
            for scan in range(2):
                row, column = corner_of(offsets_ref, down, along, sweep, scan)
                row += side + down * tile
                column += side + along * span

                @pl.when((row > 0) & (row < side + height) & (column > 0) & (column < side + breadth))
                def _():
                    first, shift = split_column(column)
                    add_slabs(total_ref, (), row, first, turned(power, shift))

    out_ref[...] = total_ref[side // lane : side // lane + slabs, side : side + height]


def density(sweep, reach, offsets, probe, tile):
    side = probe.shape[1]
    extra = side if reach else 0
    height, slabs = tile[0] + extra, (tile[1] + extra) // lane
    return pl.pallas_call(
        functools.partial(density_kernel, sweep, reach),
        out_shape=shape_of(slabs, height, lane),
        in_specs=[offsets_spec()] + whole_spec(1),
        out_specs=whole_spec(1)[0],
        scratch_shapes=[VMEM((slabs + 2 * side // lane, height + 2 * side, lane), jnp.float32)],
        compiler_params=pltpu.CompilerParams(vmem_limit_bytes=10 * MIB),
        cost_estimate=cost(1_000_000, 6 * MIB),
        name="density",
    )(offsets, probe)


def gather_kernel(sweep, below_of, offsets_ref, total_ref, windows_ref, all_ref, *refs):
    edge_refs, strip_ref = refs[:-1], refs[-1]
    slabs, side = all_ref.shape[1:3]
    height = total_ref.shape[2]
    edge = side // lane
    below = below_of()
    strip_ref[...] = jnp.zeros_like(strip_ref)
    for scan in range(2):
        row, column = corner_of(offsets_ref, 2 * below - 1, -1, sweep, scan)
        row += (2 * below - 1) * side
        first, shift = split_column(column)

        @pl.when((row > 0) & (row < 2 * side))
        def _():
            for plane in range(2):
                add_slabs(strip_ref, (plane,), row, first, turned(windows_ref[scan, plane], shift))

    base = pl.multiple_of(below * (height - side), 8)
    for plane in range(2):
        for k in range(slabs):
            value = strip_ref[plane, k, side : 2 * side] + total_ref[plane, k, pl.ds(base, side)]
            all_ref[plane, k] = value
            if k >= slabs - edge:
                edge_refs[0][plane, k - (slabs - edge)] = value
            elif k < edge and len(edge_refs) > 1:
                edge_refs[1][plane, k] = value


def partner_below():
    return 1 - lax.rem(lax.axis_index("row"), 2)


def other_below():
    return lax.rem(lax.axis_index("row"), 2)


def never_below():
    return jnp.int32(0)


def gather(sweep, below_of, offsets, total, windows, sides):
    side = windows.shape[2]
    slabs = total.shape[1]
    return pl.pallas_call(
        functools.partial(gather_kernel, sweep, below_of),
        out_shape=[shape_of(2, slabs, side, lane)] + [shape_of(2, side // lane, side, lane)] * sides,
        in_specs=[offsets_spec()] + whole_spec(2),
        out_specs=whole_spec(1 + sides),
        scratch_shapes=[VMEM((2, slabs, 3 * side, lane), jnp.float32)],
        compiler_params=pltpu.CompilerParams(vmem_limit_bytes=8 * MIB),
        cost_estimate=cost(1_000_000, 6 * MIB),
        name="gather",
    )(offsets, total, windows)


def widen_kernel(*refs):
    own_ref, right_ref, first_ref, second_ref, corner_ref, density_ref, total_ref = refs[:7]
    near_ref, far_ref, left_refs, right_refs, out_ref = refs[7], refs[8], refs[9:12], refs[12:15], refs[15]
    side = near_ref.shape[2]
    edge = side // lane
    slabs = out_ref.shape[1] - edge
    rows = out_ref.shape[2] - side
    odd = lax.rem(lax.axis_index("row"), 2) == 1
    for k in range(slabs + edge):
        for top, bottom in ((0, side), (side, rows), (rows, rows + side)):
            part = 1.0 / (density_ref[k, top:bottom] + object_damping)
            for plane in range(2):
                if top == rows:
                    if k < edge:
                        before = first_ref[plane, :, columns(k)]
                    elif k < slabs:
                        before = second_ref[plane, :, columns(k - edge)]
                    else:
                        before = corner_ref[plane, :, columns(k - slabs)]
                elif k < slabs:
                    before = own_ref[plane, top:bottom, columns(k)]
                else:
                    before = right_ref[plane, top:bottom, columns(k - slabs)]

                def picked(number, refs_of, at):
                    if top == side:
                        return refs_of[0][plane, at]
                    near, far = refs_of[1][plane, at], refs_of[2][plane, at]
                    return jnp.where(odd, near, far) if top == 0 else jnp.where(odd, far, near)

                if top == side:
                    terms = total_ref[plane, k, top:bottom]
                else:
                    terms = picked(0, (None, near_ref, far_ref), k)
                if k < edge:
                    terms += picked(0, left_refs, k)
                if k >= slabs:
                    terms += picked(0, right_refs, k - slabs)
                out_ref[plane, k, top:bottom] = before + terms * part


def widen(pieces, dense, total, near, far, left, right):
    return pl.pallas_call(
        widen_kernel,
        out_shape=shape_of(*total.shape),
        in_specs=whole_spec(15),
        out_specs=whole_spec(1)[0],
        compiler_params=pltpu.CompilerParams(vmem_limit_bytes=6 * MIB),
        cost_estimate=cost(4_000_000, 20 * MIB),
        name="widen",
    )(*pieces, dense, total, near, far, *left, *right)


def renew_kernel(field_ref, density_ref, total_ref, top_ref, left_top_ref, left_rest_ref, out_ref):
    slabs, rows = density_ref.shape[:2]
    edge, side = left_top_ref.shape[1:3]
    for k in range(slabs):
        part = 1.0 / (density_ref[k] + object_damping)
        for plane in range(2):
            top = top_ref[plane, k]
            rest = total_ref[plane, k, side:rows]
            if k < edge:
                top += left_top_ref[plane, k]
                rest += left_rest_ref[plane, k]
            out_ref[plane, :side, columns(k)] = field_ref[plane, k, :side] + top * part[:side]
            out_ref[plane, side:, columns(k)] = field_ref[plane, k, side:rows] + rest * part[side:]


def renew(field, dense, total, top, left_top, left_rest):
    slabs, rows = dense.shape[:2]
    return pl.pallas_call(
        renew_kernel,
        out_shape=shape_of(2, rows, slabs * lane),
        in_specs=whole_spec(6),
        out_specs=whole_spec(1)[0],
        compiler_params=pltpu.CompilerParams(vmem_limit_bytes=4 * MIB),
        cost_estimate=cost(4_000_000, 10 * MIB),
        name="renew",
    )(field, dense, total, top, left_top, left_rest)


def fold_kernel(bit, value_ref, came_ref, kept_ref, sent_ref, total_ref):
    total_ref[...] = value_ref[...] + came_ref[...]
    kept, sent = halves_of(bit, kept_ref.shape[0])
    kept_ref[...] = total_ref[kept]
    sent_ref[...] = total_ref[sent]


def fold(bit, value, came):
    rows, side = value.shape
    return pl.pallas_call(
        functools.partial(fold_kernel, bit),
        out_shape=[shape_of(rows // 2, side)] * 2,
        in_specs=whole_spec(2),
        out_specs=whole_spec(2),
        scratch_shapes=[VMEM(value.shape, jnp.float32)],
        compiler_params=pltpu.CompilerParams(vmem_limit_bytes=4 * MIB),
        cost_estimate=cost(100_000, MIB),
        name="fold",
    )(value, came)


def join_kernel(bit, value_ref, other_ref, out_ref):
    kept, sent = halves_of(bit, value_ref.shape[0])
    out_ref[kept] = value_ref[...]
    out_ref[sent] = other_ref[...]


def join(bit, value, other):
    rows, side = value.shape
    return pl.pallas_call(
        functools.partial(join_kernel, bit),
        out_shape=shape_of(2 * rows, side),
        in_specs=whole_spec(2),
        out_specs=whole_spec(1)[0],
        compiler_params=pltpu.CompilerParams(vmem_limit_bytes=4 * MIB),
        cost_estimate=cost(100_000, MIB),
        name="join",
    )(value, other)


def illuminate_kernel(value_ref, other_ref, probe_ref, out_ref, total_ref):
    kept, sent = halves_of(0, value_ref.shape[0])
    total_ref[kept] = value_ref[...]
    total_ref[sent] = other_ref[...]
    side = probe_ref.shape[1]
    part = 1.0 / (total_ref[2 * side :] + probe_damping)
    out_ref[0] = probe_ref[0] + total_ref[:side] * part
    out_ref[1] = probe_ref[1] + total_ref[side : 2 * side] * part


def illuminate(value, other, probe):
    rows, side = value.shape
    return pl.pallas_call(
        illuminate_kernel,
        out_shape=shape_of(*probe.shape),
        in_specs=whole_spec(3),
        out_specs=whole_spec(1)[0],
        scratch_shapes=[VMEM((2 * rows, side), jnp.float32)],
        compiler_params=pltpu.CompilerParams(vmem_limit_bytes=6 * MIB),
        cost_estimate=cost(1_000_000, 2 * MIB),
        name="illuminate",
    )(value, other, probe)


def tied(*values):
    return lax.optimization_barrier(values)


def local(table, object_field, probe, amplitudes, offsets):
    side = probe.shape[1]
    tile = object_field.shape[1:]
    measured = reorder(amplitudes[0, 0])
    col_bits = int(math.log2(lax.axis_size("col")))
    row_bits = int(math.log2(lax.axis_size("row")))

    strip, rest = tied(object_field[:, :side, :side], object_field)
    first = shifted(strip, "row", -1)
    second = shifted(rest[:, :side, side:], "row", -1)
    right = shifted(object_field[:, :, :side], "col", -1)
    near = jnp.concatenate([shifted(offsets, "row", 1), offsets, shifted(offsets, "row", -1)], axis=0)
    first, near = tied(first, near)
    corner = shifted(first, "col", -1)
    pieces = (object_field, right, first, second, corner)

    kept, sent, own = scan_step(0, False, offsets, probe, measured, table, *pieces)
    total, middle_right, middle_left = place(0, offsets, own, tile, 2)
    around = jnp.concatenate([shifted(near, "col", 1), near, shifted(near, "col", -1)], axis=1)
    dense = density(0, True, around, probe, tile)
    partner = swapped(own, "row", 1)
    came = swapped(sent, "col", 1)
    for bit in range(1, col_bits):
        kept, sent = fold(bit, kept, came)
        came = swapped(sent, "col", 1 << bit)
    came, middle_left, middle_right, around = tied(came, middle_left, middle_right, around)
    sums = kept + came
    right_strips = [shifted(middle_left, "col", -1)]
    left_strips = [shifted(middle_right, "col", 1)]
    for bit in reversed(range(1, row_bits)):
        came = swapped(sums, "row", 1 << bit)
        if bit == row_bits - 1:
            came, dense = tied(came, dense)
        sums = sums + came
    sums, partner, left_strips[0], right_strips[0] = tied(
        sums, partner, left_strips[0], right_strips[0]
    )
    passed = handed_on(partner, "row")
    near_all, near_right, near_left = gather(0, partner_below, near, total, partner, 2)
    right_strips.append(shifted(near_left, "col", -1))
    left_strips.append(shifted(near_right, "col", 1))
    sums = sums + swapped(sums, "row", 1)
    for bit in reversed(range(1, col_bits)):
        sums = join(bit, sums, swapped(sums, "col", 1 << bit))
    probe = illuminate(sums, swapped(sums, "col", 1), probe)
    passed, probe, left_strips[1], right_strips[1] = tied(passed, probe, left_strips[1], right_strips[1])
    far_all, far_right, far_left = gather(0, other_below, near, total, passed, 2)
    right_strips.append(shifted(far_left, "col", -1))
    left_strips.append(shifted(far_right, "col", 1))
    field = widen(pieces, dense, total, near_all, far_all, left_strips, right_strips)

    kept, sent, own = scan_step(1, True, offsets, probe, measured, table, field)
    total, middle_right = place(1, offsets, own, tile, 1)
    dense = density(1, False, around, probe, tile)
    upper = shifted(own, "row", 1)
    came = swapped(sent, "col", 1)
    for bit in range(1, col_bits):
        kept, sent = fold(bit, kept, came)
        came = swapped(sent, "col", 1 << bit)
    came, middle_right, dense = tied(came, middle_right, dense)
    sums = kept + came
    left_rest = shifted(middle_right, "col", 1)
    sums, upper, left_rest = tied(sums, upper, left_rest)
    top, right_top = gather(1, never_below, near, total, upper, 1)
    left_top = shifted(right_top, "col", 1)
    for bit in range(row_bits):
        sums = sums + swapped(sums, "row", 1 << bit)
    sums, left_top = tied(sums, left_top)
    for bit in reversed(range(1, col_bits)):
        sums = join(bit, sums, swapped(sums, "col", 1 << bit))
    other = swapped(sums, "col", 1)
    return renew(field, dense, total, top, left_top, left_rest), illuminate(sums, other, probe)


def solution(mesh):
    placed = (
        P(None, "row", "col"),
        P(),
        P("row", "col", None, None, None, None),
        P("row", "col", None, None, None),
    )

    def whole(object_field, probe, amplitudes, offsets):
        table = jnp.asarray(dft_tables(probe.shape[1]))
        body = jax.shard_map(
            local,
            mesh=mesh,
            in_specs=(P(),) + placed,
            out_specs=(P(None, "row", "col"), P()),
            check_vma=False,
        )
        return body(table, object_field, probe, amplitudes, offsets)

    return whole
```

time: 182 us -> 171 us (0.940)
  starting transfers between devices: 52.3 us -> 33.6 us
  waiting for transfers between devices: 95.5 us -> 108 us
  local copies, waits for them, and re-layouts: 6.45 us -> 2.61 us
    ppermute x14 -> x15, starting transfers between devices: 25.1 us -> 13.1 us  [swapped(): return lax.ppermute(array, axis, [(i, i ^ mask) for i in range(peers)])]
    ppermute x18 -> x17, starting transfers between devices: 27.2 us -> 18.7 us  [shifted(): lax.ppermute(array, axis, [(i, (i + by) % peers) for i in range(peers)])]
    ppermute x18 -> x17, waiting for transfers between devices: 48.2 us -> 54.2 us  [shifted(): lax.ppermute(array, axis, [(i, (i + by) % peers) for i in range(peers)])]
    ppermute x14 -> x15, waiting for transfers between devices: 47.4 us -> 50.8 us  [swapped(): return lax.ppermute(array, axis, [(i, i ^ mask) for i in range(peers)])]
    ppermute x0 -> x1, waiting for transfers between devices: none -> 2.66 us  [handed_on(): lax.ppermute(array, axis, [(i, (i + 2 - 4 * (i % 2)) % peers) for i in ra...]
    pallas_call x6 -> x12, Pallas kernels: 23.8 us -> 24.3 us  [the longest x2 10.3 us: scan_step(): pl.pallas_call(functools.partial(scan_kernel, sweep, last, counts), out_s...]
  transfers between devices with their start and end apart: 32 -> 33, of which waited for: 19 -> 20; matrix products, arithmetic and copies ran while one was open for 2% -> 1% of each run, Pallas kernels for 3% -> 7%
where the time goes in v4:
time: 171 us
  waiting for transfers between devices  108 us (63%)
  starting transfers between devices  33.6 us (20%)
  Pallas kernels  25.7 us (15%)
  local copies, waits for them, and re-layouts  2.61 us (2%)
    ppermute x17, waiting for transfers between devices, shifted(): lax.ppermute(array, axis, [(i, (i + by) % peers) for i in range(peers)])  54.2 us
    ppermute x15, waiting for transfers between devices, swapped(): return lax.ppermute(array, axis, [(i, i ^ mask) for i in range(peers)])  50.8 us
    ppermute x17, starting transfers between devices, shifted(): lax.ppermute(array, axis, [(i, (i + by) % peers) for i in range(peers)])  18.7 us
    ppermute x15, starting transfers between devices, swapped(): return lax.ppermute(array, axis, [(i, i ^ mask) for i in range(peers)])  13.1 us
    pallas_call x2, Pallas kernels, scan_step(): pl.pallas_call(functools.partial(scan_kernel, sweep, last, counts), out_s...  10.3 us
    pallas_call x2, Pallas kernels, density(): pl.pallas_call(functools.partial(density_kernel, sweep, reach), out_shape...  4.23 us
  transfers between devices with their start and end apart: 33, of which 20 were waited for; matrix products, arithmetic and copies ran while one was open for 1% of the time, Pallas kernels for 7%

profile of v4, /device:TPU:0, one launch (start us, length us, event | category | flops | bytes accessed | tf_op | source)
XLA Modules:
  0.0 170.8 jit_solution(4479824913680045227)
XLA Ops:
  1.9 6.1 %collective-permute-start.1 = (f32[2,256,256]{2,1,0:T(8,128)S(1)}, f32[2,256,256]{2,1,0:T(8,128)S(1)}, u32[]{:S(2)}, u32[]{:S(2)}) collective-permute-start(f32[2,256,256]{2,1,0:T(8,128)S(1)} %slice.10), channel_id=1, source_target_pairs={{0,28},{4,0},{8,4},{12,8},{16,12},{20,16},{24,20},{28,24},{1,29},{... | collective-permute-start | bytes 1572872 | tf_op jit(solution)/shard_map/ppermute | solution.py:25
  10.0 4.7 %collective-permute-start.3 = (s32[1,1,2,2,2]{4,3,2,1,0:T(2,128)S(1)}, s32[1,1,2,2,2]{4,3,2,1,0:T(2,128)S(1)}, u32[]{:S(2)}, u32[]{:S(2)}) collective-permute-start(s32[1,1,2,2,2]{4,3,2,1,0:T(2,128)S(1)} %copy-done.2), channel_id=1, source_target_pairs={{0,28},{4,0},{8,4},{12,8},{16,12},{20,16},{24,20},{28,24},{1,29},{... | collective-permute-start | bytes 104 | tf_op jit(solution)/shard_map/ppermute | solution.py:25
  14.8 1.6 collective-permute-done.2
  16.4 4.0 %collective-permute-done.3 = s32[1,1,2,2,2]{4,3,2,1,0:T(2,128)S(1)} collective-permute-done((s32[1,1,2,2,2]{4,3,2,1,0:T(2,128)S(1)}, s32[1,1,2,2,2]{4,3,2,1,0:T(2,128)S(1)}, u32[]{:S(2)}, u32[]{:S(2)}) %collective-permute-start.3) | collective-permute-done | bytes 64 | tf_op jit(solution)/shard_map/ppermute | solution.py:25
  21.0 9.5 %collective-permute-done.4.refs_6_.refs_3_ = f32[2,256,256]{2,1,0:T(8,128)S(1)} collective-permute-done((f32[2,256,256]{2,1,0:T(8,128)S(1)}, f32[2,256,256]{2,1,0:T(8,128)S(1)}, u32[]{:S(2)}, u32[]{:S(2)}) %collective-permute-start.4) | collective-permute-done | bytes 524320 | tf_op jit(solution)/shard_map/ppermute | solution.py:25
  30.5 5.4 %scan.2 = (f32[384,256]{1,0:T(8,128)S(1)}, f32[384,256]{1,0:T(8,128)S(1)}, f32[2,2,256,256]{3,2,1,0:T(8,128)S(1)}) custom-call(s32[1,1,2,2,2]{4,3,2,1,0:T(2,128)S(1)} %copy-done.2, f32[2,256,256]{2,1,0:T(8,128)S(1)} %copy-done.1, bf16[2,2,256,256]{3,2,1,0:T(8,128)(2,1)S(1)} %reorder.1.refs_1_, bf16[8,256,256]{2,1,0:T(8,128)(2,1)S(1)} %copy-done.4, ...), custom_call_target="tpu_custom_call" | custom-call | flops 7000000000 | bytes 12582912 | tf_op jit(solution)/shard_map/scan/pallas_call | solution.py:289
  36.6 1.6 collective-permute-start.9
  42.4 3.3 %collective-permute-done.7 = f32[192,256]{1,0:T(8,128)S(1)} collective-permute-done((f32[192,256]{1,0:T(8,128)S(1)}, f32[192,256]{1,0:T(8,128)S(1)}, u32[]{:S(2)}, u32[]{:S(2)}) %collective-permute-start.7) | collective-permute-done | bytes 196640 | tf_op jit(solution)/shard_map/ppermute | solution.py:30
  45.7 1.7 %collective-permute-start.14 = (f32[2,2,256,128]{3,2,1,0:T(8,128)S(1)}, f32[2,2,256,128]{3,2,1,0:T(8,128)S(1)}, u32[]{:S(2)}, u32[]{:S(2)}) collective-permute-start(f32[2,2,256,128]{3,2,1,0:T(8,128)S(1)} %get-tuple-element.67), channel_id=1, source_target_pairs={{0,3},{1,0},{2,1},{3,2},{4,7},{5,4},{6,5},{7,6},{8,11},{9,8},{10,9... | collective-permute-start | bytes 1572872 | tf_op jit(solution)/shard_map/ppermute | solution.py:25
  47.5 2.7 %collective-permute-start.10 = (f32[192,256]{1,0:T(8,128)S(1)}, f32[192,256]{1,0:T(8,128)S(1)}, u32[]{:S(2)}, u32[]{:S(2)}) collective-permute-start(f32[192,256]{1,0:T(8,128)S(1)} %add.24), channel_id=1, source_target_pairs={{0,16},{4,20},{8,24},{12,28},{16,0},{20,4},{24,8},{28,12},{1,17},{... | collective-permute-start | bytes 589832 | tf_op jit(solution)/shard_map/ppermute | solution.py:30
  50.2 2.5 %density.2.refs_5_ = f32[6,768,128]{2,1,0:T(8,128)S(1)} custom-call(s32[3,3,2,2,2]{4,3,2,1,0:T(2,128)S(1)} %constant_dynamic-update-slice_fusion.offsets_ref, f32[2,256,256]{2,1,0:T(8,128)S(1)} %copy-done.1), custom_call_target="tpu_custom_call" | custom-call | flops 1000000 | bytes 6291456 | tf_op jit(solution)/shard_map/density/pallas_call | solution.py:359
  52.7 6.2 %collective-permute-done.10 = f32[192,256]{1,0:T(8,128)S(1)} collective-permute-done((f32[192,256]{1,0:T(8,128)S(1)}, f32[192,256]{1,0:T(8,128)S(1)}, u32[]{:S(2)}, u32[]{:S(2)}) %collective-permute-start.10) | collective-permute-done | bytes 196640 | tf_op jit(solution)/shard_map/ppermute | solution.py:30
  59.7 5.1 %collective-permute-done.11 = f32[192,256]{1,0:T(8,128)S(1)} collective-permute-done((f32[192,256]{1,0:T(8,128)S(1)}, f32[192,256]{1,0:T(8,128)S(1)}, u32[]{:S(2)}, u32[]{:S(2)}) %collective-permute-start.11) | collective-permute-done | bytes 196640 | tf_op jit(solution)/shard_map/ppermute | solution.py:30
  64.8 1.8 %collective-permute-start.15 = (f32[2,2,256,256]{3,2,1,0:T(8,128)S(1)}, f32[2,2,256,256]{3,2,1,0:T(8,128)S(1)}, u32[]{:S(2)}, u32[]{:S(2)}) collective-permute-start(f32[2,2,256,256]{3,2,1,0:T(8,128)S(1)} %collective-permute-done.12.windows_ref), channel_id=1, source_target_pairs={{0,8},{4,28},{8,16},{12,4},{16,24},{20,12},{24,0},{28,20},{1,9},{5... | collective-permute-start | bytes 3145736 | tf_op jit(solution)/shard_map/ppermute | solution.py:35
  66.6 2.9 %collective-permute-start.16 = (f32[192,256]{1,0:T(8,128)S(1)}, f32[192,256]{1,0:T(8,128)S(1)}, u32[]{:S(2)}, u32[]{:S(2)}) collective-permute-start(f32[192,256]{1,0:T(8,128)S(1)} %add.26), channel_id=1, source_target_pairs={{0,4},{4,0},{8,12},{12,8},{16,20},{20,16},{24,28},{28,24},{1,5},{5... | collective-permute-start | bytes 589832 | tf_op jit(solution)/shard_map/ppermute | solution.py:30
  69.5 4.0 %collective-permute-done.16 = f32[192,256]{1,0:T(8,128)S(1)} collective-permute-done((f32[192,256]{1,0:T(8,128)S(1)}, f32[192,256]{1,0:T(8,128)S(1)}, u32[]{:S(2)}, u32[]{:S(2)}) %collective-permute-start.16) | collective-permute-done | bytes 196640 | tf_op jit(solution)/shard_map/ppermute | solution.py:30
  75.7 1.7 %collective-permute-start.20 = (f32[2,2,256,128]{3,2,1,0:T(8,128)S(1)}, f32[2,2,256,128]{3,2,1,0:T(8,128)S(1)}, u32[]{:S(2)}, u32[]{:S(2)}) collective-permute-start(f32[2,2,256,128]{3,2,1,0:T(8,128)S(1)} %get-tuple-element.72), channel_id=1, source_target_pairs={{0,3},{1,0},{2,1},{3,2},{4,7},{5,4},{6,5},{7,6},{8,11},{9,8},{10,9... | collective-permute-start | bytes 1572872 | tf_op jit(solution)/shard_map/ppermute | solution.py:25
  77.5 2.1 %collective-permute-done.17.other_ref = f32[192,256]{1,0:T(8,128)S(1)} collective-permute-done((f32[192,256]{1,0:T(8,128)S(1)}, f32[192,256]{1,0:T(8,128)S(1)}, u32[]{:S(2)}, u32[]{:S(2)}) %collective-permute-start.17) | collective-permute-done | bytes 196640 | tf_op jit(solution)/shard_map/ppermute | solution.py:30
  79.7 1.7 %collective-permute-done.18.other_ref = f32[384,256]{1,0:T(8,128)S(1)} collective-permute-done((f32[384,256]{1,0:T(8,128)S(1)}, f32[384,256]{1,0:T(8,128)S(1)}, u32[]{:S(2)}, u32[]{:S(2)}) %collective-permute-start.18) | collective-permute-done | bytes 393248 | tf_op jit(solution)/shard_map/ppermute | solution.py:30
  81.6 7.6 %collective-permute-done.19.refs_10_ = f32[2,2,256,128]{3,2,1,0:T(8,128)S(1)} collective-permute-done((f32[2,2,256,128]{3,2,1,0:T(8,128)S(1)}, f32[2,2,256,128]{3,2,1,0:T(8,128)S(1)}, u32[]{:S(2)}, u32[]{:S(2)}) %collective-permute-start.19) | collective-permute-done | bytes 524320 | tf_op jit(solution)/shard_map/ppermute | solution.py:25
  89.3 2.7 %collective-permute-done.15.windows_ref = f32[2,2,256,256]{3,2,1,0:T(8,128)S(1)} collective-permute-done((f32[2,2,256,256]{3,2,1,0:T(8,128)S(1)}, f32[2,2,256,256]{3,2,1,0:T(8,128)S(1)}, u32[]{:S(2)}, u32[]{:S(2)}) %collective-permute-start.15) | collective-permute-done | bytes 1048608 | tf_op jit(solution)/shard_map/ppermute | solution.py:35
  93.1 1.7 %collective-permute-start.22 = (f32[2,2,256,128]{3,2,1,0:T(8,128)S(1)}, f32[2,2,256,128]{3,2,1,0:T(8,128)S(1)}, u32[]{:S(2)}, u32[]{:S(2)}) collective-permute-start(f32[2,2,256,128]{3,2,1,0:T(8,128)S(1)} %get-tuple-element.80), channel_id=1, source_target_pairs={{0,3},{1,0},{2,1},{3,2},{4,7},{5,4},{6,5},{7,6},{8,11},{9,8},{10,9... | collective-permute-start | bytes 1572872 | tf_op jit(solution)/shard_map/ppermute | solution.py:25
  94.9 11.1 %collective-permute-done.21.refs_11_ = f32[2,2,256,128]{3,2,1,0:T(8,128)S(1)} collective-permute-done((f32[2,2,256,128]{3,2,1,0:T(8,128)S(1)}, f32[2,2,256,128]{3,2,1,0:T(8,128)S(1)}, u32[]{:S(2)}, u32[]{:S(2)}) %collective-permute-start.21) | collective-permute-done | bytes 524320 | tf_op jit(solution)/shard_map/ppermute | solution.py:25
  107.4 4.9 %scan.3 = (f32[384,256]{1,0:T(8,128)S(1)}, f32[384,256]{1,0:T(8,128)S(1)}, f32[2,2,256,256]{3,2,1,0:T(8,128)S(1)}) custom-call(s32[1,1,2,2,2]{4,3,2,1,0:T(2,128)S(1)} %copy-done.2, f32[2,256,256]{2,1,0:T(8,128)S(1)} %illuminate.2.refs_0_.probe_ref, bf16[2,2,256,256]{3,2,1,0:T(8,128)(2,1)S(1)} %reorder.1.refs_1_, bf16[8,256,256]{2,1,0:T(8,128)(2,1)S(1)} %copy-done.4, ...), custom_call_target="tpu_custom_call" | custom-call | flops 7000000000 | bytes 12582912 | tf_op jit(solution)/shard_map/scan/pallas_call | solution.py:289
  116.1 1.7 %density.3.density_ref = f32[4,512,128]{2,1,0:T(8,128)S(1)} custom-call(s32[3,3,2,2,2]{4,3,2,1,0:T(2,128)S(1)} %constant_dynamic-update-slice_fusion.offsets_ref, f32[2,256,256]{2,1,0:T(8,128)S(1)} %illuminate.2.refs_0_.probe_ref), custom_call_target="tpu_custom_call" | custom-call | flops 1000000 | bytes 6291456 | tf_op jit(solution)/shard_map/density/pallas_call | solution.py:359
  119.2 3.1 %collective-permute-done.24 = f32[192,256]{1,0:T(8,128)S(1)} collective-permute-done((f32[192,256]{1,0:T(8,128)S(1)}, f32[192,256]{1,0:T(8,128)S(1)}, u32[]{:S(2)}, u32[]{:S(2)}) %collective-permute-start.24) | collective-permute-done | bytes 196640 | tf_op jit(solution)/shard_map/ppermute | solution.py:30
  122.3 19.1 %collective-permute-done.25.windows_ref = f32[2,2,256,256]{3,2,1,0:T(8,128)S(1)} collective-permute-done((f32[2,2,256,256]{3,2,1,0:T(8,128)S(1)}, f32[2,2,256,256]{3,2,1,0:T(8,128)S(1)}, u32[]{:S(2)}, u32[]{:S(2)}) %collective-permute-start.25) | collective-permute-done | bytes 1048608 | tf_op jit(solution)/shard_map/ppermute | solution.py:25
  142.6 4.8 %collective-permute-done.27 = f32[192,256]{1,0:T(8,128)S(1)} collective-permute-done((f32[192,256]{1,0:T(8,128)S(1)}, f32[192,256]{1,0:T(8,128)S(1)}, u32[]{:S(2)}, u32[]{:S(2)}) %collective-permute-start.27) | collective-permute-done | bytes 196640 | tf_op jit(solution)/shard_map/ppermute | solution.py:30
  147.6 5.7 %collective-permute-done.28 = f32[192,256]{1,0:T(8,128)S(1)} collective-permute-done((f32[192,256]{1,0:T(8,128)S(1)}, f32[192,256]{1,0:T(8,128)S(1)}, u32[]{:S(2)}, u32[]{:S(2)}) %collective-permute-start.28) | collective-permute-done | bytes 196640 | tf_op jit(solution)/shard_map/ppermute | solution.py:30
  153.3 8.8 %collective-permute-done.29 = f32[192,256]{1,0:T(8,128)S(1)} collective-permute-done((f32[192,256]{1,0:T(8,128)S(1)}, f32[192,256]{1,0:T(8,128)S(1)}, u32[]{:S(2)}, u32[]{:S(2)}) %collective-permute-start.29) | collective-permute-done | bytes 196640 | tf_op jit(solution)/shard_map/ppermute | solution.py:30
  163.2 4.7 %collective-permute-done.31.other_ref = f32[192,256]{1,0:T(8,128)S(1)} collective-permute-done((f32[192,256]{1,0:T(8,128)S(1)}, f32[192,256]{1,0:T(8,128)S(1)}, u32[]{:S(2)}, u32[]{:S(2)}) %collective-permute-start.31) | collective-permute-done | bytes 196640 | tf_op jit(solution)/shard_map/ppermute | solution.py:30
  168.0 1.8 %renew.1 = f32[2,512,512]{2,1,0:T(8,128)} custom-call(f32[2,6,768,128]{3,2,1,0:T(8,128)S(1)} %widen.1.refs_3_.field_ref, f32[4,512,128]{2,1,0:T(8,128)S(1)} %density.3.density_ref, f32[2,6,768,128]{3,2,1,0:T(8,128)S(1)} %get-tuple-element.89.total_ref, f32[2,6,256,128]{3,2,1,0:T(8,128)S(1)} %get-tuple-element.94.top_ref, ...), custom_call_target="tpu_custom_call" | custom-call | flops 4000000 | bytes 10485760 | tf_op jit(solution)/shard_map/renew/pallas_call | solution.py:496
  (77 shorter events, 23.6 us)
Async XLA Ops:
  1.9 18.4 %collective-permute-start.1 = (f32[2,256,256]{2,1,0:T(8,128)S(1)}, f32[2,256,256]{2,1,0:T(8,128)S(1)}, u32[]{:S(2)}, u32[]{:S(2)}) collective-permute-start(f32[2,256,256]{2,1,0:T(8,128)S(1)} %slice.10), channel_id=1, source_target_pairs={{0,28},{4,0},{8,4},{12,8},{16,12},{20,16},{24,20},{28,24},{1,29},{... | collective-permute-start | bytes 1572872 | tf_op jit(solution)/shard_map/ppermute | solution.py:25
  9.3 21.2 %collective-permute-start = (f32[2,512,256]{2,1,0:T(8,128)S(1)}, f32[2,512,256]{2,1,0:T(8,128)S(1)}, u32[]{:S(2)}, u32[]{:S(2)}) collective-permute-start(f32[2,512,256]{2,1,0:T(8,128)S(1)} %slice.9), channel_id=1, source_target_pairs={{0,3},{1,0},{2,1},{3,2},{4,7},{5,4},{6,5},{7,6},{8,11},{9,8},{10,9... | collective-permute-start | bytes 3145736 | tf_op jit(solution)/shard_map/ppermute | solution.py:25
  10.0 6.4 %collective-permute-start.2 = (s32[1,1,2,2,2]{4,3,2,1,0:T(2,128)S(1)}, s32[1,1,2,2,2]{4,3,2,1,0:T(2,128)S(1)}, u32[]{:S(2)}, u32[]{:S(2)}) collective-permute-start(s32[1,1,2,2,2]{4,3,2,1,0:T(2,128)S(1)} %copy-done.2), channel_id=1, source_target_pairs={{0,4},{4,8},{8,12},{12,16},{16,20},{20,24},{24,28},{28,0},{1,5},{5... | collective-permute-start | bytes 104 | tf_op jit(solution)/shard_map/ppermute | solution.py:25
  10.0 10.4 %collective-permute-start.3 = (s32[1,1,2,2,2]{4,3,2,1,0:T(2,128)S(1)}, s32[1,1,2,2,2]{4,3,2,1,0:T(2,128)S(1)}, u32[]{:S(2)}, u32[]{:S(2)}) collective-permute-start(s32[1,1,2,2,2]{4,3,2,1,0:T(2,128)S(1)} %copy-done.2), channel_id=1, source_target_pairs={{0,28},{4,0},{8,4},{12,8},{16,12},{20,16},{24,20},{28,24},{1,29},{... | collective-permute-start | bytes 104 | tf_op jit(solution)/shard_map/ppermute | solution.py:25
  14.8 15.7 %collective-permute-start.4 = (f32[2,256,256]{2,1,0:T(8,128)S(1)}, f32[2,256,256]{2,1,0:T(8,128)S(1)}, u32[]{:S(2)}, u32[]{:S(2)}) collective-permute-start(f32[2,256,256]{2,1,0:T(8,128)S(1)} %slice.11), channel_id=1, source_target_pairs={{0,28},{4,0},{8,4},{12,8},{16,12},{20,16},{24,20},{28,24},{1,29},{... | collective-permute-start | bytes 1572872 | tf_op jit(solution)/shard_map/ppermute | solution.py:25
  20.4 10.1 %collective-permute-start.5 = (f32[2,256,256]{2,1,0:T(8,128)S(1)}, f32[2,256,256]{2,1,0:T(8,128)S(1)}, u32[]{:S(2)}, u32[]{:S(2)}) collective-permute-start(f32[2,256,256]{2,1,0:T(8,128)S(1)} %collective-permute-done.1.refs_5_.refs_2_), channel_id=1, source_target_pairs={{0,3},{1,0},{2,1},{3,2},{4,7},{5,4},{6,5},{7,6},{8,11},{9,8},{10,9... | collective-permute-start | bytes 1572872 | tf_op jit(solution)/shard_map/ppermute | solution.py:25
  35.8 3.6 %collective-permute-start.6 = (f32[384,256]{1,0:T(8,128)S(1)}, f32[384,256]{1,0:T(8,128)S(1)}, u32[]{:S(2)}, u32[]{:S(2)}) collective-permute-start(f32[384,256]{1,0:T(8,128)S(1)} %get-tuple-element.55), channel_id=1, source_target_pairs={{0,1},{1,0},{2,3},{3,2},{4,5},{5,4},{6,7},{7,6},{8,9},{9,8},{10,11... | collective-permute-start | bytes 1179656 | tf_op jit(solution)/shard_map/ppermute | solution.py:30
  35.9 28.9 %collective-permute-start.12 = (f32[2,2,256,256]{3,2,1,0:T(8,128)S(1)}, f32[2,2,256,256]{3,2,1,0:T(8,128)S(1)}, u32[]{:S(2)}, u32[]{:S(2)}) collective-permute-start(f32[2,2,256,256]{3,2,1,0:T(8,128)S(1)} %get-tuple-element.58.windows_ref), channel_id=1, source_target_pairs={{0,4},{4,0},{8,12},{12,8},{16,20},{20,16},{24,28},{28,24},{1,5},{5... | collective-permute-start | bytes 3145736 | tf_op jit(solution)/shard_map/ppermute | solution.py:30
  36.4 3.1 %collective-permute-start.8 = (s32[3,1,2,2,2]{4,3,2,1,0:T(2,128)S(1)}, s32[3,1,2,2,2]{4,3,2,1,0:T(2,128)S(1)}, u32[]{:S(2)}, u32[]{:S(2)}) collective-permute-start(s32[3,1,2,2,2]{4,3,2,1,0:T(2,128)S(1)} %pad_add_fusion.offsets_ref), channel_id=1, source_target_pairs={{0,1},{1,2},{2,3},{3,0},{4,5},{5,6},{6,7},{7,4},{8,9},{9,10},{10,1... | collective-permute-start | bytes 296 | tf_op jit(solution)/shard_map/ppermute | solution.py:25
  36.6 4.5 %collective-permute-start.9 = (s32[3,1,2,2,2]{4,3,2,1,0:T(2,128)S(1)}, s32[3,1,2,2,2]{4,3,2,1,0:T(2,128)S(1)}, u32[]{:S(2)}, u32[]{:S(2)}) collective-permute-start(s32[3,1,2,2,2]{4,3,2,1,0:T(2,128)S(1)} %pad_add_fusion.offsets_ref), channel_id=1, source_target_pairs={{0,3},{1,0},{2,1},{3,2},{4,7},{5,4},{6,5},{7,6},{8,11},{9,8},{10,9... | collective-permute-start | bytes 296 | tf_op jit(solution)/shard_map/ppermute | solution.py:25
  39.6 6.2 %collective-permute-start.7 = (f32[192,256]{1,0:T(8,128)S(1)}, f32[192,256]{1,0:T(8,128)S(1)}, u32[]{:S(2)}, u32[]{:S(2)}) collective-permute-start(f32[192,256]{1,0:T(8,128)S(1)} %get-tuple-element.57), channel_id=1, source_target_pairs={{0,2},{1,3},{2,0},{3,1},{4,6},{5,7},{6,4},{7,5},{8,10},{9,11},{10,... | collective-permute-start | bytes 589832 | tf_op jit(solution)/shard_map/ppermute | solution.py:30
  45.7 19.1 %collective-permute-start.13 = (f32[2,2,256,128]{3,2,1,0:T(8,128)S(1)}, f32[2,2,256,128]{3,2,1,0:T(8,128)S(1)}, u32[]{:S(2)}, u32[]{:S(2)}) collective-permute-start(f32[2,2,256,128]{3,2,1,0:T(8,128)S(1)} %get-tuple-element.66), channel_id=1, source_target_pairs={{0,1},{1,2},{2,3},{3,0},{4,5},{5,6},{6,7},{7,4},{8,9},{9,10},{10,1... | collective-permute-start | bytes 1572872 | tf_op jit(solution)/shard_map/ppermute | solution.py:25
  45.7 19.1 %collective-permute-start.14 = (f32[2,2,256,128]{3,2,1,0:T(8,128)S(1)}, f32[2,2,256,128]{3,2,1,0:T(8,128)S(1)}, u32[]{:S(2)}, u32[]{:S(2)}) collective-permute-start(f32[2,2,256,128]{3,2,1,0:T(8,128)S(1)} %get-tuple-element.67), channel_id=1, source_target_pairs={{0,3},{1,0},{2,1},{3,2},{4,7},{5,4},{6,5},{7,6},{8,11},{9,8},{10,9... | collective-permute-start | bytes 1572872 | tf_op jit(solution)/shard_map/ppermute | solution.py:25
  47.5 11.4 %collective-permute-start.10 = (f32[192,256]{1,0:T(8,128)S(1)}, f32[192,256]{1,0:T(8,128)S(1)}, u32[]{:S(2)}, u32[]{:S(2)}) collective-permute-start(f32[192,256]{1,0:T(8,128)S(1)} %add.24), channel_id=1, source_target_pairs={{0,16},{4,20},{8,24},{12,28},{16,0},{20,4},{24,8},{28,12},{1,17},{... | collective-permute-start | bytes 589832 | tf_op jit(solution)/shard_map/ppermute | solution.py:30
  58.9 5.8 %collective-permute-start.11 = (f32[192,256]{1,0:T(8,128)S(1)}, f32[192,256]{1,0:T(8,128)S(1)}, u32[]{:S(2)}, u32[]{:S(2)}) collective-permute-start(f32[192,256]{1,0:T(8,128)S(1)} %add.25), channel_id=1, source_target_pairs={{0,8},{4,12},{8,0},{12,4},{16,24},{20,28},{24,16},{28,20},{1,9},{5... | collective-permute-start | bytes 589832 | tf_op jit(solution)/shard_map/ppermute | solution.py:30
  64.8 27.1 %collective-permute-start.15 = (f32[2,2,256,256]{3,2,1,0:T(8,128)S(1)}, f32[2,2,256,256]{3,2,1,0:T(8,128)S(1)}, u32[]{:S(2)}, u32[]{:S(2)}) collective-permute-start(f32[2,2,256,256]{3,2,1,0:T(8,128)S(1)} %collective-permute-done.12.windows_ref), channel_id=1, source_target_pairs={{0,8},{4,28},{8,16},{12,4},{16,24},{20,12},{24,0},{28,20},{1,9},{5... | collective-permute-start | bytes 3145736 | tf_op jit(solution)/shard_map/ppermute | solution.py:35
  66.6 6.8 %collective-permute-start.16 = (f32[192,256]{1,0:T(8,128)S(1)}, f32[192,256]{1,0:T(8,128)S(1)}, u32[]{:S(2)}, u32[]{:S(2)}) collective-permute-start(f32[192,256]{1,0:T(8,128)S(1)} %add.26), channel_id=1, source_target_pairs={{0,4},{4,0},{8,12},{12,8},{16,20},{20,16},{24,28},{28,24},{1,5},{5... | collective-permute-start | bytes 589832 | tf_op jit(solution)/shard_map/ppermute | solution.py:30
  73.5 6.2 %collective-permute-start.17 = (f32[192,256]{1,0:T(8,128)S(1)}, f32[192,256]{1,0:T(8,128)S(1)}, u32[]{:S(2)}, u32[]{:S(2)}) collective-permute-start(f32[192,256]{1,0:T(8,128)S(1)} %add.27.value_ref), channel_id=1, source_target_pairs={{0,2},{1,3},{2,0},{3,1},{4,6},{5,7},{6,4},{7,5},{8,10},{9,11},{10,... | collective-permute-start | bytes 589832 | tf_op jit(solution)/shard_map/ppermute | solution.py:30
  75.7 13.6 %collective-permute-start.19 = (f32[2,2,256,128]{3,2,1,0:T(8,128)S(1)}, f32[2,2,256,128]{3,2,1,0:T(8,128)S(1)}, u32[]{:S(2)}, u32[]{:S(2)}) collective-permute-start(f32[2,2,256,128]{3,2,1,0:T(8,128)S(1)} %get-tuple-element.71), channel_id=1, source_target_pairs={{0,1},{1,2},{2,3},{3,0},{4,5},{5,6},{6,7},{7,4},{8,9},{9,10},{10,1... | collective-permute-start | bytes 1572872 | tf_op jit(solution)/shard_map/ppermute | solution.py:25
  75.7 13.5 %collective-permute-start.20 = (f32[2,2,256,128]{3,2,1,0:T(8,128)S(1)}, f32[2,2,256,128]{3,2,1,0:T(8,128)S(1)}, u32[]{:S(2)}, u32[]{:S(2)}) collective-permute-start(f32[2,2,256,128]{3,2,1,0:T(8,128)S(1)} %get-tuple-element.72), channel_id=1, source_target_pairs={{0,3},{1,0},{2,1},{3,2},{4,7},{5,4},{6,5},{7,6},{8,11},{9,8},{10,9... | collective-permute-start | bytes 1572872 | tf_op jit(solution)/shard_map/ppermute | solution.py:25
  93.1 12.9 %collective-permute-start.21 = (f32[2,2,256,128]{3,2,1,0:T(8,128)S(1)}, f32[2,2,256,128]{3,2,1,0:T(8,128)S(1)}, u32[]{:S(2)}, u32[]{:S(2)}) collective-permute-start(f32[2,2,256,128]{3,2,1,0:T(8,128)S(1)} %get-tuple-element.77), channel_id=1, source_target_pairs={{0,1},{1,2},{2,3},{3,0},{4,5},{5,6},{6,7},{7,4},{8,9},{9,10},{10,1... | collective-permute-start | bytes 1572872 | tf_op jit(solution)/shard_map/ppermute | solution.py:25
  93.1 12.9 %collective-permute-start.22 = (f32[2,2,256,128]{3,2,1,0:T(8,128)S(1)}, f32[2,2,256,128]{3,2,1,0:T(8,128)S(1)}, u32[]{:S(2)}, u32[]{:S(2)}) collective-permute-start(f32[2,2,256,128]{3,2,1,0:T(8,128)S(1)} %get-tuple-element.80), channel_id=1, source_target_pairs={{0,3},{1,0},{2,1},{3,2},{4,7},{5,4},{6,5},{7,6},{8,11},{9,8},{10,9... | collective-permute-start | bytes 1572872 | tf_op jit(solution)/shard_map/ppermute | solution.py:25
  112.4 2.6 %collective-permute-start.23 = (f32[384,256]{1,0:T(8,128)S(1)}, f32[384,256]{1,0:T(8,128)S(1)}, u32[]{:S(2)}, u32[]{:S(2)}) collective-permute-start(f32[384,256]{1,0:T(8,128)S(1)} %get-tuple-element.83), channel_id=1, source_target_pairs={{0,1},{1,0},{2,3},{3,2},{4,5},{5,4},{6,7},{7,6},{8,9},{9,8},{10,11... | collective-permute-start | bytes 1179656 | tf_op jit(solution)/shard_map/ppermute | solution.py:30
  113.6 27.8 %collective-permute-start.25 = (f32[2,2,256,256]{3,2,1,0:T(8,128)S(1)}, f32[2,2,256,256]{3,2,1,0:T(8,128)S(1)}, u32[]{:S(2)}, u32[]{:S(2)}) collective-permute-start(f32[2,2,256,256]{3,2,1,0:T(8,128)S(1)} %get-tuple-element.85.windows_ref), channel_id=1, source_target_pairs={{0,4},{4,8},{8,12},{12,16},{16,20},{20,24},{24,28},{28,0},{1,5},{5... | collective-permute-start | bytes 3145736 | tf_op jit(solution)/shard_map/ppermute | solution.py:25
  115.0 7.2 %collective-permute-start.24 = (f32[192,256]{1,0:T(8,128)S(1)}, f32[192,256]{1,0:T(8,128)S(1)}, u32[]{:S(2)}, u32[]{:S(2)}) collective-permute-start(f32[192,256]{1,0:T(8,128)S(1)} %get-tuple-element.84), channel_id=1, source_target_pairs={{0,2},{1,3},{2,0},{3,1},{4,6},{5,7},{6,4},{7,5},{8,10},{9,11},{10,... | collective-permute-start | bytes 589832 | tf_op jit(solution)/shard_map/ppermute | solution.py:30
  122.3 19.2 %collective-permute-start.26 = (f32[2,2,256,128]{3,2,1,0:T(8,128)S(1)}, f32[2,2,256,128]{3,2,1,0:T(8,128)S(1)}, u32[]{:S(2)}, u32[]{:S(2)}) collective-permute-start(f32[2,2,256,128]{3,2,1,0:T(8,128)S(1)} %get-tuple-element.92), channel_id=1, source_target_pairs={{0,1},{1,2},{2,3},{3,0},{4,5},{5,6},{6,7},{7,4},{8,9},{9,10},{10,1... | collective-permute-start | bytes 1572872 | tf_op jit(solution)/shard_map/ppermute | solution.py:25
  141.4 6.0 %collective-permute-start.27 = (f32[192,256]{1,0:T(8,128)S(1)}, f32[192,256]{1,0:T(8,128)S(1)}, u32[]{:S(2)}, u32[]{:S(2)}) collective-permute-start(f32[192,256]{1,0:T(8,128)S(1)} %add.28), channel_id=1, source_target_pairs={{0,4},{4,0},{8,12},{12,8},{16,20},{20,16},{24,28},{28,24},{1,5},{5... | collective-permute-start | bytes 589832 | tf_op jit(solution)/shard_map/ppermute | solution.py:30
  142.6 19.6 %collective-permute-start.30 = (f32[2,2,256,128]{3,2,1,0:T(8,128)S(1)}, f32[2,2,256,128]{3,2,1,0:T(8,128)S(1)}, u32[]{:S(2)}, u32[]{:S(2)}) collective-permute-start(f32[2,2,256,128]{3,2,1,0:T(8,128)S(1)} %get-tuple-element.96), channel_id=1, source_target_pairs={{0,1},{1,2},{2,3},{3,0},{4,5},{5,6},{6,7},{7,4},{8,9},{9,10},{10,1... | collective-permute-start | bytes 1572872 | tf_op jit(solution)/shard_map/ppermute | solution.py:25
  147.5 5.7 %collective-permute-start.28 = (f32[192,256]{1,0:T(8,128)S(1)}, f32[192,256]{1,0:T(8,128)S(1)}, u32[]{:S(2)}, u32[]{:S(2)}) collective-permute-start(f32[192,256]{1,0:T(8,128)S(1)} %add.29), channel_id=1, source_target_pairs={{0,8},{4,12},{8,0},{12,4},{16,24},{20,28},{24,16},{28,20},{1,9},{5... | collective-permute-start | bytes 589832 | tf_op jit(solution)/shard_map/ppermute | solution.py:30
  153.3 8.9 %collective-permute-start.29 = (f32[192,256]{1,0:T(8,128)S(1)}, f32[192,256]{1,0:T(8,128)S(1)}, u32[]{:S(2)}, u32[]{:S(2)}) collective-permute-start(f32[192,256]{1,0:T(8,128)S(1)} %add.30), channel_id=1, source_target_pairs={{0,16},{4,20},{8,24},{12,28},{16,0},{20,4},{24,8},{28,12},{1,17},{... | collective-permute-start | bytes 589832 | tf_op jit(solution)/shard_map/ppermute | solution.py:30
  162.2 5.7 %collective-permute-start.31 = (f32[192,256]{1,0:T(8,128)S(1)}, f32[192,256]{1,0:T(8,128)S(1)}, u32[]{:S(2)}, u32[]{:S(2)}) collective-permute-start(f32[192,256]{1,0:T(8,128)S(1)} %add.31.value_ref), channel_id=1, source_target_pairs={{0,2},{1,3},{2,0},{3,1},{4,6},{5,7},{6,4},{7,5},{8,10},{9,11},{10,... | collective-permute-start | bytes 589832 | tf_op jit(solution)/shard_map/ppermute | solution.py:30
  168.0 1.9 %collective-permute-start.32 = (f32[384,256]{1,0:T(8,128)S(1)}, f32[384,256]{1,0:T(8,128)S(1)}, u32[]{:S(2)}, u32[]{:S(2)}) collective-permute-start(f32[384,256]{1,0:T(8,128)S(1)} %join.3.value_ref), channel_id=1, source_target_pairs={{0,1},{1,0},{2,3},{3,2},{4,5},{5,4},{6,7},{7,6},{8,9},{9,8},{10,11... | collective-permute-start | bytes 1179656 | tf_op jit(solution)/shard_map/ppermute | solution.py:30
  (6 other events, 102.1 us)

commit v5 on v4

--- a/solution.py
+++ b/solution.py
@@ -597,25 +597,26 @@
     for bit in range(1, col_bits):
         kept, sent = fold(bit, kept, came)
         came = swapped(sent, "col", 1 << bit)
-    came, middle_left, middle_right, around = tied(came, middle_left, middle_right, around)
+    came, around = tied(came, around)
     sums = kept + came
-    right_strips = [shifted(middle_left, "col", -1)]
-    left_strips = [shifted(middle_right, "col", 1)]
     for bit in reversed(range(1, row_bits)):
         came = swapped(sums, "row", 1 << bit)
         if bit == row_bits - 1:
-            came, dense = tied(came, dense)
+            came, dense, middle_left, middle_right = tied(came, dense, middle_left, middle_right)
         sums = sums + came
-    sums, partner, left_strips[0], right_strips[0] = tied(
-        sums, partner, left_strips[0], right_strips[0]
-    )
+    right_strips = [shifted(middle_left, "col", -1)]
+    left_strips = [shifted(middle_right, "col", 1)]
+    sums, partner = tied(sums, partner)
     passed = handed_on(partner, "row")
     near_all, near_right, near_left = gather(0, partner_below, near, total, partner, 2)
     right_strips.append(shifted(near_left, "col", -1))
     left_strips.append(shifted(near_right, "col", 1))
     sums = sums + swapped(sums, "row", 1)
     for bit in reversed(range(1, col_bits)):
-        sums = join(bit, sums, swapped(sums, "col", 1 << bit))
+        other = swapped(sums, "col", 1 << bit)
+        if bit == col_bits - 1:
+            other, left_strips[0], right_strips[0] = tied(other, left_strips[0], right_strips[0])
+        sums = join(bit, sums, other)
     probe = illuminate(sums, swapped(sums, "col", 1), probe)
     passed, probe, left_strips[1], right_strips[1] = tied(passed, probe, left_strips[1], right_strips[1])
     far_all, far_right, far_left = gather(0, other_below, near, total, passed, 2)
@@ -640,10 +641,13 @@
     for bit in range(row_bits):
         sums = sums + swapped(sums, "row", 1 << bit)
     sums, left_top = tied(sums, left_top)
+    field = renew(field, dense, total, top, left_top, left_rest)
     for bit in reversed(range(1, col_bits)):
-        sums = join(bit, sums, swapped(sums, "col", 1 << bit))
-    other = swapped(sums, "col", 1)
-    return renew(field, dense, total, top, left_top, left_rest), illuminate(sums, other, probe)
+        other = swapped(sums, "col", 1 << bit)
+        if bit == 1:
+            other, field = tied(other, field)
+        sums = join(bit, sums, other)
+    return field, illuminate(sums, swapped(sums, "col", 1), probe)
 
 
 def solution(mesh):

time: 171 us -> 168 us (0.982)
  waiting for transfers between devices: 108 us -> 105 us
    ppermute x1, waiting for transfers between devices: 2.66 us -> 0.01 us  [handed_on(): lax.ppermute(array, axis, [(i, (i + 2 - 4 * (i % 2)) % peers) for i in ra...]
  transfers between devices with their start and end apart: 33 -> 33, of which waited for: 20 -> 19; matrix products, arithmetic and copies ran while one was open for 1% -> 1% of each run, Pallas kernels for 7% -> 7%
where the time goes in v5:
time: 168 us
  waiting for transfers between devices  105 us (62%)
  starting transfers between devices  33.3 us (20%)
  Pallas kernels  25.7 us (15%)
  local copies, waits for them, and re-layouts  2.61 us (2%)
    ppermute x17, waiting for transfers between devices, shifted(): lax.ppermute(array, axis, [(i, (i + by) % peers) for i in range(peers)])  53.1 us
    ppermute x15, waiting for transfers between devices, swapped(): return lax.ppermute(array, axis, [(i, i ^ mask) for i in range(peers)])  52.1 us
    ppermute x17, starting transfers between devices, shifted(): lax.ppermute(array, axis, [(i, (i + by) % peers) for i in range(peers)])  19.1 us
    ppermute x15, starting transfers between devices, swapped(): return lax.ppermute(array, axis, [(i, i ^ mask) for i in range(peers)])  13.2 us
    pallas_call x2, Pallas kernels, scan_step(): pl.pallas_call(functools.partial(scan_kernel, sweep, last, counts), out_s...  10.3 us
    pallas_call x2, Pallas kernels, density(): pl.pallas_call(functools.partial(density_kernel, sweep, reach), out_shape...  4.01 us
    pallas_call x3, Pallas kernels, gather(): pl.pallas_call(functools.partial(gather_kernel, sweep, below_of), out_sha...  3.69 us
  transfers between devices with their start and end apart: 33, of which 19 were waited for; matrix products, arithmetic and copies ran while one was open for 1% of the time, Pallas kernels for 7%

profile of v5, /device:TPU:0, one launch (start us, length us, event | category | flops | bytes accessed | tf_op | source)
XLA Modules:
  0.0 168.0 jit_solution(11802598043760215463)
XLA Ops:
  1.9 6.1 %collective-permute-start.1 = (f32[2,256,256]{2,1,0:T(8,128)S(1)}, f32[2,256,256]{2,1,0:T(8,128)S(1)}, u32[]{:S(2)}, u32[]{:S(2)}) collective-permute-start(f32[2,256,256]{2,1,0:T(8,128)S(1)} %slice.10), channel_id=1, source_target_pairs={{0,28},{4,0},{8,4},{12,8},{16,12},{20,16},{24,20},{28,24},{1,29},{... | collective-permute-start | bytes 1572872 | tf_op jit(solution)/shard_map/ppermute | solution.py:25
  12.1 3.4 %collective-permute-start.4 = (f32[2,256,256]{2,1,0:T(8,128)S(1)}, f32[2,256,256]{2,1,0:T(8,128)S(1)}, u32[]{:S(2)}, u32[]{:S(2)}) collective-permute-start(f32[2,256,256]{2,1,0:T(8,128)S(1)} %slice.11), channel_id=1, source_target_pairs={{0,28},{4,0},{8,4},{12,8},{16,12},{20,16},{24,20},{28,24},{1,29},{... | collective-permute-start | bytes 1572872 | tf_op jit(solution)/shard_map/ppermute | solution.py:25
  15.5 4.9 %collective-permute-done.3 = s32[1,1,2,2,2]{4,3,2,1,0:T(2,128)S(1)} collective-permute-done((s32[1,1,2,2,2]{4,3,2,1,0:T(2,128)S(1)}, s32[1,1,2,2,2]{4,3,2,1,0:T(2,128)S(1)}, u32[]{:S(2)}, u32[]{:S(2)}) %collective-permute-start.3) | collective-permute-done | bytes 64 | tf_op jit(solution)/shard_map/ppermute | solution.py:25
  21.0 9.4 %collective-permute-done.4.refs_6_.refs_3_ = f32[2,256,256]{2,1,0:T(8,128)S(1)} collective-permute-done((f32[2,256,256]{2,1,0:T(8,128)S(1)}, f32[2,256,256]{2,1,0:T(8,128)S(1)}, u32[]{:S(2)}, u32[]{:S(2)}) %collective-permute-start.4) | collective-permute-done | bytes 524320 | tf_op jit(solution)/shard_map/ppermute | solution.py:25
  30.5 5.4 %scan.2 = (f32[384,256]{1,0:T(8,128)S(1)}, f32[384,256]{1,0:T(8,128)S(1)}, f32[2,2,256,256]{3,2,1,0:T(8,128)S(1)}) custom-call(s32[1,1,2,2,2]{4,3,2,1,0:T(2,128)S(1)} %copy-done.2, f32[2,256,256]{2,1,0:T(8,128)S(1)} %copy-done.1, bf16[2,2,256,256]{3,2,1,0:T(8,128)(2,1)S(1)} %reorder.1.refs_1_, bf16[8,256,256]{2,1,0:T(8,128)(2,1)S(1)} %copy-done.4, ...), custom_call_target="tpu_custom_call" | custom-call | flops 7000000000 | bytes 12582912 | tf_op jit(solution)/shard_map/scan/pallas_call | solution.py:289
  39.5 1.6 collective-permute-start.7
  41.1 4.6 %collective-permute-done.7 = f32[192,256]{1,0:T(8,128)S(1)} collective-permute-done((f32[192,256]{1,0:T(8,128)S(1)}, f32[192,256]{1,0:T(8,128)S(1)}, u32[]{:S(2)}, u32[]{:S(2)}) %collective-permute-start.7) | collective-permute-done | bytes 196640 | tf_op jit(solution)/shard_map/ppermute | solution.py:30
  45.7 2.7 %collective-permute-start.10 = (f32[192,256]{1,0:T(8,128)S(1)}, f32[192,256]{1,0:T(8,128)S(1)}, u32[]{:S(2)}, u32[]{:S(2)}) collective-permute-start(f32[192,256]{1,0:T(8,128)S(1)} %add.24), channel_id=1, source_target_pairs={{0,16},{4,20},{8,24},{12,28},{16,0},{20,4},{24,8},{28,12},{1,17},{... | collective-permute-start | bytes 589832 | tf_op jit(solution)/shard_map/ppermute | solution.py:30
  48.4 2.3 %density.2.refs_5_ = f32[6,768,128]{2,1,0:T(8,128)S(1)} custom-call(s32[3,3,2,2,2]{4,3,2,1,0:T(2,128)S(1)} %constant_dynamic-update-slice_fusion.offsets_ref, f32[2,256,256]{2,1,0:T(8,128)S(1)} %copy-done.1), custom_call_target="tpu_custom_call" | custom-call | flops 1000000 | bytes 6291456 | tf_op jit(solution)/shard_map/density/pallas_call | solution.py:359
  52.0 4.6 %collective-permute-done.10 = f32[192,256]{1,0:T(8,128)S(1)} collective-permute-done((f32[192,256]{1,0:T(8,128)S(1)}, f32[192,256]{1,0:T(8,128)S(1)}, u32[]{:S(2)}, u32[]{:S(2)}) %collective-permute-start.10) | collective-permute-done | bytes 196640 | tf_op jit(solution)/shard_map/ppermute | solution.py:30
  56.9 5.4 %collective-permute-done.11 = f32[192,256]{1,0:T(8,128)S(1)} collective-permute-done((f32[192,256]{1,0:T(8,128)S(1)}, f32[192,256]{1,0:T(8,128)S(1)}, u32[]{:S(2)}, u32[]{:S(2)}) %collective-permute-start.11) | collective-permute-done | bytes 196640 | tf_op jit(solution)/shard_map/ppermute | solution.py:30
  63.4 3.0 %collective-permute-start.14 = (f32[192,256]{1,0:T(8,128)S(1)}, f32[192,256]{1,0:T(8,128)S(1)}, u32[]{:S(2)}, u32[]{:S(2)}) collective-permute-start(f32[192,256]{1,0:T(8,128)S(1)} %add.26), channel_id=1, source_target_pairs={{0,4},{4,0},{8,12},{12,8},{16,20},{20,16},{24,28},{28,24},{1,5},{5... | collective-permute-start | bytes 589832 | tf_op jit(solution)/shard_map/ppermute | solution.py:30
  66.3 5.6 %collective-permute-done.14 = f32[192,256]{1,0:T(8,128)S(1)} collective-permute-done((f32[192,256]{1,0:T(8,128)S(1)}, f32[192,256]{1,0:T(8,128)S(1)}, u32[]{:S(2)}, u32[]{:S(2)}) %collective-permute-start.14) | collective-permute-done | bytes 196640 | tf_op jit(solution)/shard_map/ppermute | solution.py:30
  72.9 1.4 gather.3
  74.4 1.7 %collective-permute-start.20 = (f32[2,2,256,128]{3,2,1,0:T(8,128)S(1)}, f32[2,2,256,128]{3,2,1,0:T(8,128)S(1)}, u32[]{:S(2)}, u32[]{:S(2)}) collective-permute-start(f32[2,2,256,128]{3,2,1,0:T(8,128)S(1)} %get-tuple-element.74), channel_id=1, source_target_pairs={{0,3},{1,0},{2,1},{3,2},{4,7},{5,4},{6,5},{7,6},{8,11},{9,8},{10,9... | collective-permute-start | bytes 1572872 | tf_op jit(solution)/shard_map/ppermute | solution.py:25
  76.1 3.7 %collective-permute-done.15.other_ref = f32[192,256]{1,0:T(8,128)S(1)} collective-permute-done((f32[192,256]{1,0:T(8,128)S(1)}, f32[192,256]{1,0:T(8,128)S(1)}, u32[]{:S(2)}, u32[]{:S(2)}) %collective-permute-start.15) | collective-permute-done | bytes 196640 | tf_op jit(solution)/shard_map/ppermute | solution.py:30
  79.9 1.7 %collective-permute-done.18.other_ref = f32[384,256]{1,0:T(8,128)S(1)} collective-permute-done((f32[384,256]{1,0:T(8,128)S(1)}, f32[384,256]{1,0:T(8,128)S(1)}, u32[]{:S(2)}, u32[]{:S(2)}) %collective-permute-start.18) | collective-permute-done | bytes 393248 | tf_op jit(solution)/shard_map/ppermute | solution.py:30
  81.8 7.1 %collective-permute-done.19.refs_10_ = f32[2,2,256,128]{3,2,1,0:T(8,128)S(1)} collective-permute-done((f32[2,2,256,128]{3,2,1,0:T(8,128)S(1)}, f32[2,2,256,128]{3,2,1,0:T(8,128)S(1)}, u32[]{:S(2)}, u32[]{:S(2)}) %collective-permute-start.19) | collective-permute-done | bytes 524320 | tf_op jit(solution)/shard_map/ppermute | solution.py:25
  91.9 10.9 %collective-permute-done.21.refs_11_ = f32[2,2,256,128]{3,2,1,0:T(8,128)S(1)} collective-permute-done((f32[2,2,256,128]{3,2,1,0:T(8,128)S(1)}, f32[2,2,256,128]{3,2,1,0:T(8,128)S(1)}, u32[]{:S(2)}, u32[]{:S(2)}) %collective-permute-start.21) | collective-permute-done | bytes 524320 | tf_op jit(solution)/shard_map/ppermute | solution.py:25
  103.0 1.4 widen.1.refs_3_.field_ref
  104.5 4.9 %scan.3 = (f32[384,256]{1,0:T(8,128)S(1)}, f32[384,256]{1,0:T(8,128)S(1)}, f32[2,2,256,256]{3,2,1,0:T(8,128)S(1)}) custom-call(s32[1,1,2,2,2]{4,3,2,1,0:T(2,128)S(1)} %copy-done.2, f32[2,256,256]{2,1,0:T(8,128)S(1)} %illuminate.2.refs_0_.probe_ref, bf16[2,2,256,256]{3,2,1,0:T(8,128)(2,1)S(1)} %reorder.1.refs_1_, bf16[8,256,256]{2,1,0:T(8,128)(2,1)S(1)} %copy-done.4, ...), custom_call_target="tpu_custom_call" | custom-call | flops 7000000000 | bytes 12582912 | tf_op jit(solution)/shard_map/scan/pallas_call | solution.py:289
  110.6 1.5 collective-permute-start.25
  112.2 1.9 %collective-permute-start.24 = (f32[192,256]{1,0:T(8,128)S(1)}, f32[192,256]{1,0:T(8,128)S(1)}, u32[]{:S(2)}, u32[]{:S(2)}) collective-permute-start(f32[192,256]{1,0:T(8,128)S(1)} %get-tuple-element.89), channel_id=1, source_target_pairs={{0,2},{1,3},{2,0},{3,1},{4,6},{5,7},{6,4},{7,5},{8,10},{9,11},{10,... | collective-permute-start | bytes 589832 | tf_op jit(solution)/shard_map/ppermute | solution.py:30
  114.0 1.7 %density.3.density_ref = f32[4,512,128]{2,1,0:T(8,128)S(1)} custom-call(s32[3,3,2,2,2]{4,3,2,1,0:T(2,128)S(1)} %constant_dynamic-update-slice_fusion.offsets_ref, f32[2,256,256]{2,1,0:T(8,128)S(1)} %illuminate.2.refs_0_.probe_ref), custom_call_target="tpu_custom_call" | custom-call | flops 1000000 | bytes 6291456 | tf_op jit(solution)/shard_map/density/pallas_call | solution.py:359
  117.1 2.2 %collective-permute-done.24 = f32[192,256]{1,0:T(8,128)S(1)} collective-permute-done((f32[192,256]{1,0:T(8,128)S(1)}, f32[192,256]{1,0:T(8,128)S(1)}, u32[]{:S(2)}, u32[]{:S(2)}) %collective-permute-start.24) | collective-permute-done | bytes 196640 | tf_op jit(solution)/shard_map/ppermute | solution.py:30
  119.3 19.1 %collective-permute-done.25.windows_ref = f32[2,2,256,256]{3,2,1,0:T(8,128)S(1)} collective-permute-done((f32[2,2,256,256]{3,2,1,0:T(8,128)S(1)}, f32[2,2,256,256]{3,2,1,0:T(8,128)S(1)}, u32[]{:S(2)}, u32[]{:S(2)}) %collective-permute-start.25) | collective-permute-done | bytes 1048608 | tf_op jit(solution)/shard_map/ppermute | solution.py:25
  139.7 4.8 %collective-permute-done.27 = f32[192,256]{1,0:T(8,128)S(1)} collective-permute-done((f32[192,256]{1,0:T(8,128)S(1)}, f32[192,256]{1,0:T(8,128)S(1)}, u32[]{:S(2)}, u32[]{:S(2)}) %collective-permute-start.27) | collective-permute-done | bytes 196640 | tf_op jit(solution)/shard_map/ppermute | solution.py:30
  144.6 5.7 %collective-permute-done.28 = f32[192,256]{1,0:T(8,128)S(1)} collective-permute-done((f32[192,256]{1,0:T(8,128)S(1)}, f32[192,256]{1,0:T(8,128)S(1)}, u32[]{:S(2)}, u32[]{:S(2)}) %collective-permute-start.28) | collective-permute-done | bytes 196640 | tf_op jit(solution)/shard_map/ppermute | solution.py:30
  150.4 9.1 %collective-permute-done.29 = f32[192,256]{1,0:T(8,128)S(1)} collective-permute-done((f32[192,256]{1,0:T(8,128)S(1)}, f32[192,256]{1,0:T(8,128)S(1)}, u32[]{:S(2)}, u32[]{:S(2)}) %collective-permute-start.29) | collective-permute-done | bytes 196640 | tf_op jit(solution)/shard_map/ppermute | solution.py:30
  160.4 1.8 %renew.1 = f32[2,512,512]{2,1,0:T(8,128)} custom-call(f32[2,6,768,128]{3,2,1,0:T(8,128)S(1)} %widen.1.refs_3_.field_ref, f32[4,512,128]{2,1,0:T(8,128)S(1)} %density.3.density_ref, f32[2,6,768,128]{3,2,1,0:T(8,128)S(1)} %get-tuple-element.96.total_ref, f32[2,6,256,128]{3,2,1,0:T(8,128)S(1)} %get-tuple-element.101.top_ref, ...), custom_call_target="tpu_custom_call" | custom-call | flops 4000000 | bytes 10485760 | tf_op jit(solution)/shard_map/renew/pallas_call | solution.py:496
  162.2 3.0 %collective-permute-done.31.other_ref = f32[192,256]{1,0:T(8,128)S(1)} collective-permute-done((f32[192,256]{1,0:T(8,128)S(1)}, f32[192,256]{1,0:T(8,128)S(1)}, u32[]{:S(2)}, u32[]{:S(2)}) %collective-permute-start.31) | collective-permute-done | bytes 196640 | tf_op jit(solution)/shard_map/ppermute | solution.py:30
  165.3 1.7 %collective-permute-done.32.other_ref = f32[384,256]{1,0:T(8,128)S(1)} collective-permute-done((f32[384,256]{1,0:T(8,128)S(1)}, f32[384,256]{1,0:T(8,128)S(1)}, u32[]{:S(2)}, u32[]{:S(2)}) %collective-permute-start.32) | collective-permute-done | bytes 393248 | tf_op jit(solution)/shard_map/ppermute | solution.py:30
  (77 shorter events, 22.8 us)
Async XLA Ops:
  1.9 18.4 %collective-permute-start.1 = (f32[2,256,256]{2,1,0:T(8,128)S(1)}, f32[2,256,256]{2,1,0:T(8,128)S(1)}, u32[]{:S(2)}, u32[]{:S(2)}) collective-permute-start(f32[2,256,256]{2,1,0:T(8,128)S(1)} %slice.10), channel_id=1, source_target_pairs={{0,28},{4,0},{8,4},{12,8},{16,12},{20,16},{24,20},{28,24},{1,29},{... | collective-permute-start | bytes 1572872 | tf_op jit(solution)/shard_map/ppermute | solution.py:25
  9.3 21.2 %collective-permute-start = (f32[2,512,256]{2,1,0:T(8,128)S(1)}, f32[2,512,256]{2,1,0:T(8,128)S(1)}, u32[]{:S(2)}, u32[]{:S(2)}) collective-permute-start(f32[2,512,256]{2,1,0:T(8,128)S(1)} %slice.9), channel_id=1, source_target_pairs={{0,3},{1,0},{2,1},{3,2},{4,7},{5,4},{6,5},{7,6},{8,11},{9,8},{10,9... | collective-permute-start | bytes 3145736 | tf_op jit(solution)/shard_map/ppermute | solution.py:25
  10.0 10.4 %collective-permute-start.3 = (s32[1,1,2,2,2]{4,3,2,1,0:T(2,128)S(1)}, s32[1,1,2,2,2]{4,3,2,1,0:T(2,128)S(1)}, u32[]{:S(2)}, u32[]{:S(2)}) collective-permute-start(s32[1,1,2,2,2]{4,3,2,1,0:T(2,128)S(1)} %copy-done.2), channel_id=1, source_target_pairs={{0,28},{4,0},{8,4},{12,8},{16,12},{20,16},{24,20},{28,24},{1,29},{... | collective-permute-start | bytes 104 | tf_op jit(solution)/shard_map/ppermute | solution.py:25
  10.7 9.7 %collective-permute-start.2 = (s32[1,1,2,2,2]{4,3,2,1,0:T(2,128)S(1)}, s32[1,1,2,2,2]{4,3,2,1,0:T(2,128)S(1)}, u32[]{:S(2)}, u32[]{:S(2)}) collective-permute-start(s32[1,1,2,2,2]{4,3,2,1,0:T(2,128)S(1)} %copy-done.2), channel_id=1, source_target_pairs={{0,4},{4,8},{8,12},{12,16},{16,20},{20,24},{24,28},{28,0},{1,5},{5... | collective-permute-start | bytes 104 | tf_op jit(solution)/shard_map/ppermute | solution.py:25
  12.1 18.4 %collective-permute-start.4 = (f32[2,256,256]{2,1,0:T(8,128)S(1)}, f32[2,256,256]{2,1,0:T(8,128)S(1)}, u32[]{:S(2)}, u32[]{:S(2)}) collective-permute-start(f32[2,256,256]{2,1,0:T(8,128)S(1)} %slice.11), channel_id=1, source_target_pairs={{0,28},{4,0},{8,4},{12,8},{16,12},{20,16},{24,20},{28,24},{1,29},{... | collective-permute-start | bytes 1572872 | tf_op jit(solution)/shard_map/ppermute | solution.py:25
  20.4 10.1 %collective-permute-start.5 = (f32[2,256,256]{2,1,0:T(8,128)S(1)}, f32[2,256,256]{2,1,0:T(8,128)S(1)}, u32[]{:S(2)}, u32[]{:S(2)}) collective-permute-start(f32[2,256,256]{2,1,0:T(8,128)S(1)} %collective-permute-done.1.refs_5_.refs_2_), channel_id=1, source_target_pairs={{0,3},{1,0},{2,1},{3,2},{4,7},{5,4},{6,5},{7,6},{8,11},{9,8},{10,9... | collective-permute-start | bytes 1572872 | tf_op jit(solution)/shard_map/ppermute | solution.py:25
  35.8 26.5 %collective-permute-start.12 = (f32[2,2,256,256]{3,2,1,0:T(8,128)S(1)}, f32[2,2,256,256]{3,2,1,0:T(8,128)S(1)}, u32[]{:S(2)}, u32[]{:S(2)}) collective-permute-start(f32[2,2,256,256]{3,2,1,0:T(8,128)S(1)} %get-tuple-element.63.windows_ref), channel_id=1, source_target_pairs={{0,4},{4,0},{8,12},{12,8},{16,20},{20,16},{24,28},{28,24},{1,5},{5... | collective-permute-start | bytes 3145736 | tf_op jit(solution)/shard_map/ppermute | solution.py:30
  36.3 3.1 %collective-permute-start.6 = (f32[384,256]{1,0:T(8,128)S(1)}, f32[384,256]{1,0:T(8,128)S(1)}, u32[]{:S(2)}, u32[]{:S(2)}) collective-permute-start(f32[384,256]{1,0:T(8,128)S(1)} %get-tuple-element.58), channel_id=1, source_target_pairs={{0,1},{1,0},{2,3},{3,2},{4,5},{5,4},{6,7},{7,6},{8,9},{9,8},{10,11... | collective-permute-start | bytes 1179656 | tf_op jit(solution)/shard_map/ppermute | solution.py:30
  36.3 3.1 %collective-permute-start.8 = (s32[3,1,2,2,2]{4,3,2,1,0:T(2,128)S(1)}, s32[3,1,2,2,2]{4,3,2,1,0:T(2,128)S(1)}, u32[]{:S(2)}, u32[]{:S(2)}) collective-permute-start(s32[3,1,2,2,2]{4,3,2,1,0:T(2,128)S(1)} %pad_add_fusion.offsets_ref), channel_id=1, source_target_pairs={{0,1},{1,2},{2,3},{3,0},{4,5},{5,6},{6,7},{7,4},{8,9},{9,10},{10,1... | collective-permute-start | bytes 296 | tf_op jit(solution)/shard_map/ppermute | solution.py:25
  36.8 4.2 %collective-permute-start.9 = (s32[3,1,2,2,2]{4,3,2,1,0:T(2,128)S(1)}, s32[3,1,2,2,2]{4,3,2,1,0:T(2,128)S(1)}, u32[]{:S(2)}, u32[]{:S(2)}) collective-permute-start(s32[3,1,2,2,2]{4,3,2,1,0:T(2,128)S(1)} %pad_add_fusion.offsets_ref), channel_id=1, source_target_pairs={{0,3},{1,0},{2,1},{3,2},{4,7},{5,4},{6,5},{7,6},{8,11},{9,8},{10,9... | collective-permute-start | bytes 296 | tf_op jit(solution)/shard_map/ppermute | solution.py:25
  39.5 6.2 %collective-permute-start.7 = (f32[192,256]{1,0:T(8,128)S(1)}, f32[192,256]{1,0:T(8,128)S(1)}, u32[]{:S(2)}, u32[]{:S(2)}) collective-permute-start(f32[192,256]{1,0:T(8,128)S(1)} %get-tuple-element.60), channel_id=1, source_target_pairs={{0,2},{1,3},{2,0},{3,1},{4,6},{5,7},{6,4},{7,5},{8,10},{9,11},{10,... | collective-permute-start | bytes 589832 | tf_op jit(solution)/shard_map/ppermute | solution.py:30
  45.7 10.8 %collective-permute-start.10 = (f32[192,256]{1,0:T(8,128)S(1)}, f32[192,256]{1,0:T(8,128)S(1)}, u32[]{:S(2)}, u32[]{:S(2)}) collective-permute-start(f32[192,256]{1,0:T(8,128)S(1)} %add.24), channel_id=1, source_target_pairs={{0,16},{4,20},{8,24},{12,28},{16,0},{20,4},{24,8},{28,12},{1,17},{... | collective-permute-start | bytes 589832 | tf_op jit(solution)/shard_map/ppermute | solution.py:30
  56.6 5.7 %collective-permute-start.11 = (f32[192,256]{1,0:T(8,128)S(1)}, f32[192,256]{1,0:T(8,128)S(1)}, u32[]{:S(2)}, u32[]{:S(2)}) collective-permute-start(f32[192,256]{1,0:T(8,128)S(1)} %add.25), channel_id=1, source_target_pairs={{0,8},{4,12},{8,0},{12,4},{16,24},{20,28},{24,16},{28,20},{1,9},{5... | collective-permute-start | bytes 589832 | tf_op jit(solution)/shard_map/ppermute | solution.py:30
  56.9 17.5 %collective-permute-start.16 = (f32[2,2,256,128]{3,2,1,0:T(8,128)S(1)}, f32[2,2,256,128]{3,2,1,0:T(8,128)S(1)}, u32[]{:S(2)}, u32[]{:S(2)}) collective-permute-start(f32[2,2,256,128]{3,2,1,0:T(8,128)S(1)} %get-tuple-element.69), channel_id=1, source_target_pairs={{0,1},{1,2},{2,3},{3,0},{4,5},{5,6},{6,7},{7,4},{8,9},{9,10},{10,1... | collective-permute-start | bytes 1572872 | tf_op jit(solution)/shard_map/ppermute | solution.py:25
  62.4 26.6 %collective-permute-start.13 = (f32[2,2,256,256]{3,2,1,0:T(8,128)S(1)}, f32[2,2,256,256]{3,2,1,0:T(8,128)S(1)}, u32[]{:S(2)}, u32[]{:S(2)}) collective-permute-start(f32[2,2,256,256]{3,2,1,0:T(8,128)S(1)} %collective-permute-done.12.windows_ref), channel_id=1, source_target_pairs={{0,8},{4,28},{8,16},{12,4},{16,24},{20,12},{24,0},{28,20},{1,9},{5... | collective-permute-start | bytes 3145736 | tf_op jit(solution)/shard_map/ppermute | solution.py:35
  63.4 12.7 %collective-permute-start.17 = (f32[2,2,256,128]{3,2,1,0:T(8,128)S(1)}, f32[2,2,256,128]{3,2,1,0:T(8,128)S(1)}, u32[]{:S(2)}, u32[]{:S(2)}) collective-permute-start(f32[2,2,256,128]{3,2,1,0:T(8,128)S(1)} %get-tuple-element.70), channel_id=1, source_target_pairs={{0,3},{1,0},{2,1},{3,2},{4,7},{5,4},{6,5},{7,6},{8,11},{9,8},{10,9... | collective-permute-start | bytes 1572872 | tf_op jit(solution)/shard_map/ppermute | solution.py:25
  63.4 8.5 %collective-permute-start.14 = (f32[192,256]{1,0:T(8,128)S(1)}, f32[192,256]{1,0:T(8,128)S(1)}, u32[]{:S(2)}, u32[]{:S(2)}) collective-permute-start(f32[192,256]{1,0:T(8,128)S(1)} %add.26), channel_id=1, source_target_pairs={{0,4},{4,0},{8,12},{12,8},{16,20},{20,16},{24,28},{28,24},{1,5},{5... | collective-permute-start | bytes 589832 | tf_op jit(solution)/shard_map/ppermute | solution.py:30
  71.9 7.8 %collective-permute-start.15 = (f32[192,256]{1,0:T(8,128)S(1)}, f32[192,256]{1,0:T(8,128)S(1)}, u32[]{:S(2)}, u32[]{:S(2)}) collective-permute-start(f32[192,256]{1,0:T(8,128)S(1)} %add.27.value_ref), channel_id=1, source_target_pairs={{0,2},{1,3},{2,0},{3,1},{4,6},{5,7},{6,4},{7,5},{8,10},{9,11},{10,... | collective-permute-start | bytes 589832 | tf_op jit(solution)/shard_map/ppermute | solution.py:30
  74.3 14.6 %collective-permute-start.19 = (f32[2,2,256,128]{3,2,1,0:T(8,128)S(1)}, f32[2,2,256,128]{3,2,1,0:T(8,128)S(1)}, u32[]{:S(2)}, u32[]{:S(2)}) collective-permute-start(f32[2,2,256,128]{3,2,1,0:T(8,128)S(1)} %get-tuple-element.73), channel_id=1, source_target_pairs={{0,1},{1,2},{2,3},{3,0},{4,5},{5,6},{6,7},{7,4},{8,9},{9,10},{10,1... | collective-permute-start | bytes 1572872 | tf_op jit(solution)/shard_map/ppermute | solution.py:25
  74.4 14.5 %collective-permute-start.20 = (f32[2,2,256,128]{3,2,1,0:T(8,128)S(1)}, f32[2,2,256,128]{3,2,1,0:T(8,128)S(1)}, u32[]{:S(2)}, u32[]{:S(2)}) collective-permute-start(f32[2,2,256,128]{3,2,1,0:T(8,128)S(1)} %get-tuple-element.74), channel_id=1, source_target_pairs={{0,3},{1,0},{2,1},{3,2},{4,7},{5,4},{6,5},{7,6},{8,11},{9,8},{10,9... | collective-permute-start | bytes 1572872 | tf_op jit(solution)/shard_map/ppermute | solution.py:25
  79.8 1.8 %collective-permute-start.18 = (f32[384,256]{1,0:T(8,128)S(1)}, f32[384,256]{1,0:T(8,128)S(1)}, u32[]{:S(2)}, u32[]{:S(2)}) collective-permute-start(f32[384,256]{1,0:T(8,128)S(1)} %join.2.value_ref), channel_id=1, source_target_pairs={{0,1},{1,0},{2,3},{3,2},{4,5},{5,4},{6,7},{7,6},{8,9},{9,8},{10,11... | collective-permute-start | bytes 1179656 | tf_op jit(solution)/shard_map/ppermute | solution.py:30
  90.1 12.7 %collective-permute-start.21 = (f32[2,2,256,128]{3,2,1,0:T(8,128)S(1)}, f32[2,2,256,128]{3,2,1,0:T(8,128)S(1)}, u32[]{:S(2)}, u32[]{:S(2)}) collective-permute-start(f32[2,2,256,128]{3,2,1,0:T(8,128)S(1)} %get-tuple-element.82), channel_id=1, source_target_pairs={{0,1},{1,2},{2,3},{3,0},{4,5},{5,6},{6,7},{7,4},{8,9},{9,10},{10,1... | collective-permute-start | bytes 1572872 | tf_op jit(solution)/shard_map/ppermute | solution.py:25
  91.0 12.1 %collective-permute-start.22 = (f32[2,2,256,128]{3,2,1,0:T(8,128)S(1)}, f32[2,2,256,128]{3,2,1,0:T(8,128)S(1)}, u32[]{:S(2)}, u32[]{:S(2)}) collective-permute-start(f32[2,2,256,128]{3,2,1,0:T(8,128)S(1)} %get-tuple-element.85), channel_id=1, source_target_pairs={{0,3},{1,0},{2,1},{3,2},{4,7},{5,4},{6,5},{7,6},{8,11},{9,8},{10,9... | collective-permute-start | bytes 1572872 | tf_op jit(solution)/shard_map/ppermute | solution.py:25
  109.4 2.7 %collective-permute-start.23 = (f32[384,256]{1,0:T(8,128)S(1)}, f32[384,256]{1,0:T(8,128)S(1)}, u32[]{:S(2)}, u32[]{:S(2)}) collective-permute-start(f32[384,256]{1,0:T(8,128)S(1)} %get-tuple-element.87), channel_id=1, source_target_pairs={{0,1},{1,0},{2,3},{3,2},{4,5},{5,4},{6,7},{7,6},{8,9},{9,8},{10,11... | collective-permute-start | bytes 1179656 | tf_op jit(solution)/shard_map/ppermute | solution.py:30
  110.6 27.8 %collective-permute-start.25 = (f32[2,2,256,256]{3,2,1,0:T(8,128)S(1)}, f32[2,2,256,256]{3,2,1,0:T(8,128)S(1)}, u32[]{:S(2)}, u32[]{:S(2)}) collective-permute-start(f32[2,2,256,256]{3,2,1,0:T(8,128)S(1)} %get-tuple-element.90.windows_ref), channel_id=1, source_target_pairs={{0,4},{4,8},{8,12},{12,16},{16,20},{20,24},{24,28},{28,0},{1,5},{5... | collective-permute-start | bytes 3145736 | tf_op jit(solution)/shard_map/ppermute | solution.py:25
  112.2 7.1 %collective-permute-start.24 = (f32[192,256]{1,0:T(8,128)S(1)}, f32[192,256]{1,0:T(8,128)S(1)}, u32[]{:S(2)}, u32[]{:S(2)}) collective-permute-start(f32[192,256]{1,0:T(8,128)S(1)} %get-tuple-element.89), channel_id=1, source_target_pairs={{0,2},{1,3},{2,0},{3,1},{4,6},{5,7},{6,4},{7,5},{8,10},{9,11},{10,... | collective-permute-start | bytes 589832 | tf_op jit(solution)/shard_map/ppermute | solution.py:30
  119.3 19.2 %collective-permute-start.26 = (f32[2,2,256,128]{3,2,1,0:T(8,128)S(1)}, f32[2,2,256,128]{3,2,1,0:T(8,128)S(1)}, u32[]{:S(2)}, u32[]{:S(2)}) collective-permute-start(f32[2,2,256,128]{3,2,1,0:T(8,128)S(1)} %get-tuple-element.94), channel_id=1, source_target_pairs={{0,1},{1,2},{2,3},{3,0},{4,5},{5,6},{6,7},{7,4},{8,9},{9,10},{10,1... | collective-permute-start | bytes 1572872 | tf_op jit(solution)/shard_map/ppermute | solution.py:25
  138.5 6.0 %collective-permute-start.27 = (f32[192,256]{1,0:T(8,128)S(1)}, f32[192,256]{1,0:T(8,128)S(1)}, u32[]{:S(2)}, u32[]{:S(2)}) collective-permute-start(f32[192,256]{1,0:T(8,128)S(1)} %add.28), channel_id=1, source_target_pairs={{0,4},{4,0},{8,12},{12,8},{16,20},{20,16},{24,28},{28,24},{1,5},{5... | collective-permute-start | bytes 589832 | tf_op jit(solution)/shard_map/ppermute | solution.py:30
  139.6 19.9 %collective-permute-start.30 = (f32[2,2,256,128]{3,2,1,0:T(8,128)S(1)}, f32[2,2,256,128]{3,2,1,0:T(8,128)S(1)}, u32[]{:S(2)}, u32[]{:S(2)}) collective-permute-start(f32[2,2,256,128]{3,2,1,0:T(8,128)S(1)} %get-tuple-element.98), channel_id=1, source_target_pairs={{0,1},{1,2},{2,3},{3,0},{4,5},{5,6},{6,7},{7,4},{8,9},{9,10},{10,1... | collective-permute-start | bytes 1572872 | tf_op jit(solution)/shard_map/ppermute | solution.py:25
  144.5 5.7 %collective-permute-start.28 = (f32[192,256]{1,0:T(8,128)S(1)}, f32[192,256]{1,0:T(8,128)S(1)}, u32[]{:S(2)}, u32[]{:S(2)}) collective-permute-start(f32[192,256]{1,0:T(8,128)S(1)} %add.29), channel_id=1, source_target_pairs={{0,8},{4,12},{8,0},{12,4},{16,24},{20,28},{24,16},{28,20},{1,9},{5... | collective-permute-start | bytes 589832 | tf_op jit(solution)/shard_map/ppermute | solution.py:30
  150.3 9.2 %collective-permute-start.29 = (f32[192,256]{1,0:T(8,128)S(1)}, f32[192,256]{1,0:T(8,128)S(1)}, u32[]{:S(2)}, u32[]{:S(2)}) collective-permute-start(f32[192,256]{1,0:T(8,128)S(1)} %add.30), channel_id=1, source_target_pairs={{0,16},{4,20},{8,24},{12,28},{16,0},{20,4},{24,8},{28,12},{1,17},{... | collective-permute-start | bytes 589832 | tf_op jit(solution)/shard_map/ppermute | solution.py:30
  159.5 5.7 %collective-permute-start.31 = (f32[192,256]{1,0:T(8,128)S(1)}, f32[192,256]{1,0:T(8,128)S(1)}, u32[]{:S(2)}, u32[]{:S(2)}) collective-permute-start(f32[192,256]{1,0:T(8,128)S(1)} %add.31.value_ref), channel_id=1, source_target_pairs={{0,2},{1,3},{2,0},{3,1},{4,6},{5,7},{6,4},{7,5},{8,10},{9,11},{10,... | collective-permute-start | bytes 589832 | tf_op jit(solution)/shard_map/ppermute | solution.py:30
  (6 other events, 99.4 us)

commit v6 on v5

--- a/solution.py
+++ b/solution.py
@@ -33,6 +33,12 @@
 def handed_on(array, axis):
     peers = lax.axis_size(axis)
     return lax.ppermute(array, axis, [(i, (i + 2 - 4 * (i % 2)) % peers) for i in range(peers)])
+
+
+def swapped_outward(array, axis):
+    peers = lax.axis_size(axis)
+    pairs = [(i, i + 1) for i in range(1, peers - 1, 2)]
+    return lax.ppermute(array, axis, pairs + [(k, i) for i, k in pairs])
 
 
 def dft_tables(length):
@@ -298,6 +304,13 @@
     )(offsets, probe, amplitudes, table, *field)
 
 
+def edge_starts(count, slabs, edge):
+    if count < 2:
+        return [slabs - edge] * count
+    odd = lax.rem(lax.axis_index("col"), 2)
+    return [(1 - odd) * (slabs - edge), odd * (slabs - edge)]
+
+
 def place_kernel(sweep, offsets_ref, windows_ref, total_ref, *edge_refs):
     side = windows_ref.shape[2]
     edge = side // lane
@@ -308,8 +321,8 @@
         first, shift = split_column(column)
         for plane in range(2):
             add_slabs(total_ref, (plane,), row, first, turned(windows_ref[scan, plane], shift))
-    for ref, start in zip(edge_refs, (slabs - edge, 0)):
-        ref[...] = total_ref[:, start : start + edge, side : height - side]
+    for ref, start in zip(edge_refs, edge_starts(len(edge_refs), slabs, edge)):
+        ref[...] = total_ref[:, pl.ds(start, edge), side : height - side]
 
 
 def place(sweep, offsets, windows, tile, sides):
@@ -388,12 +401,9 @@
     base = pl.multiple_of(below * (height - side), 8)
     for plane in range(2):
         for k in range(slabs):
-            value = strip_ref[plane, k, side : 2 * side] + total_ref[plane, k, pl.ds(base, side)]
-            all_ref[plane, k] = value
-            if k >= slabs - edge:
-                edge_refs[0][plane, k - (slabs - edge)] = value
-            elif k < edge and len(edge_refs) > 1:
-                edge_refs[1][plane, k] = value
+            all_ref[plane, k] = strip_ref[plane, k, side : 2 * side] + total_ref[plane, k, pl.ds(base, side)]
+    for ref, start in zip(edge_refs, edge_starts(len(edge_refs), slabs, edge)):
+        ref[...] = all_ref[:, pl.ds(start, edge)]
 
 
 def partner_below():
@@ -425,12 +435,14 @@
 
 def widen_kernel(*refs):
     own_ref, right_ref, first_ref, second_ref, corner_ref, density_ref, total_ref = refs[:7]
-    near_ref, far_ref, left_refs, right_refs, out_ref = refs[7], refs[8], refs[9:12], refs[12:15], refs[15]
+    near_ref, far_ref, inner_refs, outer_refs, out_ref = refs[7], refs[8], refs[9:12], refs[12:15], refs[15]
     side = near_ref.shape[2]
     edge = side // lane
     slabs = out_ref.shape[1] - edge
     rows = out_ref.shape[2] - side
     odd = lax.rem(lax.axis_index("row"), 2) == 1
+    odd_col = lax.rem(lax.axis_index("col"), 2) == 1
+    even_col = jnp.logical_not(odd_col)
     for k in range(slabs + edge):
         for top, bottom in ((0, side), (side, rows), (rows, rows + side)):
             part = 1.0 / (density_ref[k, top:bottom] + object_damping)
@@ -447,24 +459,28 @@
                 else:
                     before = right_ref[plane, top:bottom, columns(k - slabs)]
 
-                def picked(number, refs_of, at):
+                def picked(near, far):
+                    return jnp.where(odd, near, far) if top == 0 else jnp.where(odd, far, near)
+
+                def beside(outward, at):
                     if top == side:
-                        return refs_of[0][plane, at]
-                    near, far = refs_of[1][plane, at], refs_of[2][plane, at]
-                    return jnp.where(odd, near, far) if top == 0 else jnp.where(odd, far, near)
+                        return jnp.where(outward, outer_refs[0][plane, at], inner_refs[0][plane, at])
+                    near = jnp.where(outward, outer_refs[1][plane, at], inner_refs[1][plane, at])
+                    far = jnp.where(outward, outer_refs[2][plane, at], inner_refs[2][plane, at])
+                    return picked(near, far)
 
                 if top == side:
                     terms = total_ref[plane, k, top:bottom]
                 else:
-                    terms = picked(0, (None, near_ref, far_ref), k)
+                    terms = picked(near_ref[plane, k], far_ref[plane, k])
                 if k < edge:
-                    terms += picked(0, left_refs, k)
+                    terms += beside(even_col, k)
                 if k >= slabs:
-                    terms += picked(0, right_refs, k - slabs)
+                    terms += beside(odd_col, k - slabs)
                 out_ref[plane, k, top:bottom] = before + terms * part
 
 
-def widen(pieces, dense, total, near, far, left, right):
+def widen(pieces, dense, total, near, far, inner, outer):
     return pl.pallas_call(
         widen_kernel,
         out_shape=shape_of(*total.shape),
@@ -473,7 +489,7 @@
         compiler_params=pltpu.CompilerParams(vmem_limit_bytes=6 * MIB),
         cost_estimate=cost(4_000_000, 20 * MIB),
         name="widen",
-    )(*pieces, dense, total, near, far, *left, *right)
+    )(*pieces, dense, total, near, far, *inner, *outer)
 
 
 def renew_kernel(field_ref, density_ref, total_ref, top_ref, left_top_ref, left_rest_ref, out_ref):
@@ -589,7 +605,7 @@
     pieces = (object_field, right, first, second, corner)
 
     kept, sent, own = scan_step(0, False, offsets, probe, measured, table, *pieces)
-    total, middle_right, middle_left = place(0, offsets, own, tile, 2)
+    total, middle_inner, middle_outer = place(0, offsets, own, tile, 2)
     around = jnp.concatenate([shifted(near, "col", 1), near, shifted(near, "col", -1)], axis=1)
     dense = density(0, True, around, probe, tile)
     partner = swapped(own, "row", 1)
@@ -602,27 +618,27 @@
     for bit in reversed(range(1, row_bits)):
         came = swapped(sums, "row", 1 << bit)
         if bit == row_bits - 1:
-            came, dense, middle_left, middle_right = tied(came, dense, middle_left, middle_right)
+            came, dense, middle_inner, middle_outer = tied(came, dense, middle_inner, middle_outer)
         sums = sums + came
-    right_strips = [shifted(middle_left, "col", -1)]
-    left_strips = [shifted(middle_right, "col", 1)]
+    inner_strips = [swapped(middle_inner, "col", 1)]
+    outer_strips = [swapped_outward(middle_outer, "col")]
     sums, partner = tied(sums, partner)
     passed = handed_on(partner, "row")
-    near_all, near_right, near_left = gather(0, partner_below, near, total, partner, 2)
-    right_strips.append(shifted(near_left, "col", -1))
-    left_strips.append(shifted(near_right, "col", 1))
+    near_all, near_inner, near_outer = gather(0, partner_below, near, total, partner, 2)
+    inner_strips.append(swapped(near_inner, "col", 1))
+    outer_strips.append(swapped_outward(near_outer, "col"))
     sums = sums + swapped(sums, "row", 1)
     for bit in reversed(range(1, col_bits)):
         other = swapped(sums, "col", 1 << bit)
         if bit == col_bits - 1:
-            other, left_strips[0], right_strips[0] = tied(other, left_strips[0], right_strips[0])
+            other, outer_strips[0], inner_strips[0] = tied(other, outer_strips[0], inner_strips[0])
         sums = join(bit, sums, other)
     probe = illuminate(sums, swapped(sums, "col", 1), probe)
-    passed, probe, left_strips[1], right_strips[1] = tied(passed, probe, left_strips[1], right_strips[1])
-    far_all, far_right, far_left = gather(0, other_below, near, total, passed, 2)
-    right_strips.append(shifted(far_left, "col", -1))
-    left_strips.append(shifted(far_right, "col", 1))
-    field = widen(pieces, dense, total, near_all, far_all, left_strips, right_strips)
+    passed, probe, outer_strips[1], inner_strips[1] = tied(passed, probe, outer_strips[1], inner_strips[1])
+    far_all, far_inner, far_outer = gather(0, other_below, near, total, passed, 2)
+    inner_strips.append(swapped(far_inner, "col", 1))
+    outer_strips.append(swapped_outward(far_outer, "col"))
+    field = widen(pieces, dense, total, near_all, far_all, inner_strips, outer_strips)
 
     kept, sent, own = scan_step(1, True, offsets, probe, measured, table, field)
     total, middle_right = place(1, offsets, own, tile, 1)

time: 168 us -> 165 us (0.982)
  waiting for transfers between devices: 105 us -> 94 us
  starting transfers between devices: 33.3 us -> 40 us
    ppermute x17 -> x11, waiting for transfers between devices: 53.1 us -> 34.8 us  [shifted(): lax.ppermute(array, axis, [(i, (i + by) % peers) for i in range(peers)])]
    ppermute x15 -> x18, starting transfers between devices: 13.2 us -> 22.7 us  [swapped(): return lax.ppermute(array, axis, [(i, i ^ mask) for i in range(peers)])]
    ppermute x1, waiting for transfers between devices: 0.01 us -> 7.45 us  [handed_on(): lax.ppermute(array, axis, [(i, (i + 2 - 4 * (i % 2)) % peers) for i in ra...]
    ppermute x17 -> x11, starting transfers between devices: 19.1 us -> 14.1 us  [shifted(): lax.ppermute(array, axis, [(i, (i + by) % peers) for i in range(peers)])]
    ppermute x0 -> x3, starting transfers between devices: none -> 2.25 us  [swapped_outward(): return lax.ppermute(array, axis, pairs + [(k, i) for i, k in pairs])]
    ppermute x15 -> x18, waiting for transfers between devices: 52.1 us -> 51.8 us  [swapped(): return lax.ppermute(array, axis, [(i, i ^ mask) for i in range(peers)])]
  transfers between devices with their start and end apart: 33 -> 33, of which waited for: 19 -> 19; matrix products, arithmetic and copies ran while one was open for 1% -> 1% of each run, Pallas kernels for 7% -> 8%
where the time goes in v6:
time: 165 us; the launch traced here: 164 us
  waiting for transfers between devices  94 us (57%)
  starting transfers between devices  40 us (24%)
  Pallas kernels  26.7 us (16%)
  local copies, waits for them, and re-layouts  2.61 us (2%)
    ppermute x18, waiting for transfers between devices, swapped(): return lax.ppermute(array, axis, [(i, i ^ mask) for i in range(peers)])  51.8 us
    ppermute x11, waiting for transfers between devices, shifted(): lax.ppermute(array, axis, [(i, (i + by) % peers) for i in range(peers)])  34.8 us
    ppermute x18, starting transfers between devices, swapped(): return lax.ppermute(array, axis, [(i, i ^ mask) for i in range(peers)])  22.7 us
    ppermute x11, starting transfers between devices, shifted(): lax.ppermute(array, axis, [(i, (i + by) % peers) for i in range(peers)])  14.1 us
    pallas_call x2, Pallas kernels, scan_step(): pl.pallas_call(functools.partial(scan_kernel, sweep, last, counts), out_s...  10.3 us
    ppermute x1, waiting for transfers between devices, handed_on(): lax.ppermute(array, axis, [(i, (i + 2 - 4 * (i % 2)) % peers) for i in ra...  7.45 us
    pallas_call x2, Pallas kernels, density(): pl.pallas_call(functools.partial(density_kernel, sweep, reach), out_shape...  4.46 us
    pallas_call x3, Pallas kernels, gather(): pl.pallas_call(functools.partial(gather_kernel, sweep, below_of), out_sha...  3.8 us
  transfers between devices with their start and end apart: 33, of which 19 were waited for; matrix products, arithmetic and copies ran while one was open for 1% of the time, Pallas kernels for 8%

profile of v6, /device:TPU:0, one launch (start us, length us, event | category | flops | bytes accessed | tf_op | source)
XLA Modules:
  0.0 164.5 jit_solution(891444725239016367)
XLA Ops:
  1.9 6.1 %collective-permute-start.1 = (f32[2,256,256]{2,1,0:T(8,128)S(1)}, f32[2,256,256]{2,1,0:T(8,128)S(1)}, u32[]{:S(2)}, u32[]{:S(2)}) collective-permute-start(f32[2,256,256]{2,1,0:T(8,128)S(1)} %slice.10), channel_id=1, source_target_pairs={{0,28},{4,0},{8,4},{12,8},{16,12},{20,16},{24,20},{28,24},{1,29},{... | collective-permute-start | bytes 1572872 | tf_op jit(solution)/shard_map/ppermute | solution.py:25
  10.7 1.4 collective-permute-start.2
  12.1 3.4 %collective-permute-start.4 = (f32[2,256,256]{2,1,0:T(8,128)S(1)}, f32[2,256,256]{2,1,0:T(8,128)S(1)}, u32[]{:S(2)}, u32[]{:S(2)}) collective-permute-start(f32[2,256,256]{2,1,0:T(8,128)S(1)} %slice.11), channel_id=1, source_target_pairs={{0,28},{4,0},{8,4},{12,8},{16,12},{20,16},{24,20},{28,24},{1,29},{... | collective-permute-start | bytes 1572872 | tf_op jit(solution)/shard_map/ppermute | solution.py:25
  15.5 4.9 %collective-permute-done.3 = s32[1,1,2,2,2]{4,3,2,1,0:T(2,128)S(1)} collective-permute-done((s32[1,1,2,2,2]{4,3,2,1,0:T(2,128)S(1)}, s32[1,1,2,2,2]{4,3,2,1,0:T(2,128)S(1)}, u32[]{:S(2)}, u32[]{:S(2)}) %collective-permute-start.3) | collective-permute-done | bytes 64 | tf_op jit(solution)/shard_map/ppermute | solution.py:25
  21.0 9.4 %collective-permute-done.4.refs_6_.refs_3_ = f32[2,256,256]{2,1,0:T(8,128)S(1)} collective-permute-done((f32[2,256,256]{2,1,0:T(8,128)S(1)}, f32[2,256,256]{2,1,0:T(8,128)S(1)}, u32[]{:S(2)}, u32[]{:S(2)}) %collective-permute-start.4) | collective-permute-done | bytes 524320 | tf_op jit(solution)/shard_map/ppermute | solution.py:25
  30.5 5.4 %scan.2 = (f32[384,256]{1,0:T(8,128)S(1)}, f32[384,256]{1,0:T(8,128)S(1)}, f32[2,2,256,256]{3,2,1,0:T(8,128)S(1)}) custom-call(s32[1,1,2,2,2]{4,3,2,1,0:T(2,128)S(1)} %copy-done.2, f32[2,256,256]{2,1,0:T(8,128)S(1)} %copy-done.1, bf16[2,2,256,256]{3,2,1,0:T(8,128)(2,1)S(1)} %reorder.1.refs_1_, bf16[8,256,256]{2,1,0:T(8,128)(2,1)S(1)} %copy-done.4, ...), custom_call_target="tpu_custom_call" | custom-call | flops 7000000000 | bytes 12582912 | tf_op jit(solution)/shard_map/scan/pallas_call | solution.py:295
  39.5 1.6 collective-permute-start.7
  41.0 4.6 %collective-permute-done.7 = f32[192,256]{1,0:T(8,128)S(1)} collective-permute-done((f32[192,256]{1,0:T(8,128)S(1)}, f32[192,256]{1,0:T(8,128)S(1)}, u32[]{:S(2)}, u32[]{:S(2)}) %collective-permute-start.7) | collective-permute-done | bytes 196640 | tf_op jit(solution)/shard_map/ppermute | solution.py:30
  45.7 2.7 %collective-permute-start.10 = (f32[192,256]{1,0:T(8,128)S(1)}, f32[192,256]{1,0:T(8,128)S(1)}, u32[]{:S(2)}, u32[]{:S(2)}) collective-permute-start(f32[192,256]{1,0:T(8,128)S(1)} %add.24), channel_id=1, source_target_pairs={{0,16},{4,20},{8,24},{12,28},{16,0},{20,4},{24,8},{28,12},{1,17},{... | collective-permute-start | bytes 589832 | tf_op jit(solution)/shard_map/ppermute | solution.py:30
  48.4 2.7 %density.2.refs_5_ = f32[6,768,128]{2,1,0:T(8,128)S(1)} custom-call(s32[3,3,2,2,2]{4,3,2,1,0:T(2,128)S(1)} %constant_dynamic-update-slice_fusion.offsets_ref, f32[2,256,256]{2,1,0:T(8,128)S(1)} %copy-done.1), custom_call_target="tpu_custom_call" | custom-call | flops 1000000 | bytes 6291456 | tf_op jit(solution)/shard_map/density/pallas_call | solution.py:372
  52.4 4.1 %collective-permute-done.10 = f32[192,256]{1,0:T(8,128)S(1)} collective-permute-done((f32[192,256]{1,0:T(8,128)S(1)}, f32[192,256]{1,0:T(8,128)S(1)}, u32[]{:S(2)}, u32[]{:S(2)}) %collective-permute-start.10) | collective-permute-done | bytes 196640 | tf_op jit(solution)/shard_map/ppermute | solution.py:30
  57.6 4.7 %collective-permute-done.11 = f32[192,256]{1,0:T(8,128)S(1)} collective-permute-done((f32[192,256]{1,0:T(8,128)S(1)}, f32[192,256]{1,0:T(8,128)S(1)}, u32[]{:S(2)}, u32[]{:S(2)}) %collective-permute-start.11) | collective-permute-done | bytes 196640 | tf_op jit(solution)/shard_map/ppermute | solution.py:30
  63.4 3.0 %collective-permute-start.14 = (f32[192,256]{1,0:T(8,128)S(1)}, f32[192,256]{1,0:T(8,128)S(1)}, u32[]{:S(2)}, u32[]{:S(2)}) collective-permute-start(f32[192,256]{1,0:T(8,128)S(1)} %add.26), channel_id=1, source_target_pairs={{0,4},{4,0},{8,12},{12,8},{16,20},{20,16},{24,28},{28,24},{1,5},{5... | collective-permute-start | bytes 589832 | tf_op jit(solution)/shard_map/ppermute | solution.py:30
  66.4 5.6 %collective-permute-done.14 = f32[192,256]{1,0:T(8,128)S(1)} collective-permute-done((f32[192,256]{1,0:T(8,128)S(1)}, f32[192,256]{1,0:T(8,128)S(1)}, u32[]{:S(2)}, u32[]{:S(2)}) %collective-permute-start.14) | collective-permute-done | bytes 196640 | tf_op jit(solution)/shard_map/ppermute | solution.py:30
  72.8 1.5 gather.3
  75.2 2.3 %collective-permute-start.20 = (f32[2,2,256,128]{3,2,1,0:T(8,128)S(1)}, f32[2,2,256,128]{3,2,1,0:T(8,128)S(1)}, u32[]{:S(2)}, u32[]{:S(2)}) collective-permute-start(f32[2,2,256,128]{3,2,1,0:T(8,128)S(1)} %get-tuple-element.74), channel_id=1, source_target_pairs={{0,1},{1,0},{2,3},{3,2},{4,5},{5,4},{6,7},{7,6},{8,9},{9,8},{10,11... | collective-permute-start | bytes 1572872 | tf_op jit(solution)/shard_map/ppermute | solution.py:30
  78.9 1.7 %collective-permute-done.18.other_ref = f32[384,256]{1,0:T(8,128)S(1)} collective-permute-done((f32[384,256]{1,0:T(8,128)S(1)}, f32[384,256]{1,0:T(8,128)S(1)}, u32[]{:S(2)}, u32[]{:S(2)}) %collective-permute-start.18) | collective-permute-done | bytes 393248 | tf_op jit(solution)/shard_map/ppermute | solution.py:30
  80.8 7.5 %collective-permute-done.13.windows_ref = f32[2,2,256,256]{3,2,1,0:T(8,128)S(1)} collective-permute-done((f32[2,2,256,256]{3,2,1,0:T(8,128)S(1)}, f32[2,2,256,256]{3,2,1,0:T(8,128)S(1)}, u32[]{:S(2)}, u32[]{:S(2)}) %collective-permute-start.13) | collective-permute-done | bytes 1048608 | tf_op jit(solution)/shard_map/ppermute | solution.py:35
  91.4 1.8 %widen.1.refs_3_.field_ref = f32[2,6,768,128]{3,2,1,0:T(8,128)S(1)} custom-call(f32[2,512,512]{2,1,0:T(8,128)S(1)} %copy-done, f32[2,512,256]{2,1,0:T(8,128)S(1)} %collective-permute-done.refs_4_.refs_1_, f32[2,256,256]{2,1,0:T(8,128)S(1)} %collective-permute-done.1.refs_5_.refs_2_, f32[2,256,256]{2,1,0:T(8,128)S(1)} %collective-permute-done.4.refs_6_.refs_3_, ...), custom_call_target="tpu_custom_call" | custom-call | flops 4000000 | bytes 20971520 | tf_op jit(solution)/shard_map/widen/pallas_call | solution.py:484
  93.2 4.9 %scan.3 = (f32[384,256]{1,0:T(8,128)S(1)}, f32[384,256]{1,0:T(8,128)S(1)}, f32[2,2,256,256]{3,2,1,0:T(8,128)S(1)}) custom-call(s32[1,1,2,2,2]{4,3,2,1,0:T(2,128)S(1)} %copy-done.2, f32[2,256,256]{2,1,0:T(8,128)S(1)} %illuminate.2.refs_0_.probe_ref, bf16[2,2,256,256]{3,2,1,0:T(8,128)(2,1)S(1)} %reorder.1.refs_1_, bf16[8,256,256]{2,1,0:T(8,128)(2,1)S(1)} %copy-done.4, ...), custom_call_target="tpu_custom_call" | custom-call | flops 7000000000 | bytes 12582912 | tf_op jit(solution)/shard_map/scan/pallas_call | solution.py:295
  98.1 9.1 %collective-permute-start.23 = (f32[384,256]{1,0:T(8,128)S(1)}, f32[384,256]{1,0:T(8,128)S(1)}, u32[]{:S(2)}, u32[]{:S(2)}) collective-permute-start(f32[384,256]{1,0:T(8,128)S(1)} %get-tuple-element.87), channel_id=1, source_target_pairs={{0,1},{1,0},{2,3},{3,2},{4,5},{5,4},{6,7},{7,6},{8,9},{9,8},{10,11... | collective-permute-start | bytes 1179656 | tf_op jit(solution)/shard_map/ppermute | solution.py:30
  107.3 1.3 collective-permute-done.23.came_ref
  109.0 1.7 %density.3.density_ref = f32[4,512,128]{2,1,0:T(8,128)S(1)} custom-call(s32[3,3,2,2,2]{4,3,2,1,0:T(2,128)S(1)} %constant_dynamic-update-slice_fusion.offsets_ref, f32[2,256,256]{2,1,0:T(8,128)S(1)} %illuminate.2.refs_0_.probe_ref), custom_call_target="tpu_custom_call" | custom-call | flops 1000000 | bytes 6291456 | tf_op jit(solution)/shard_map/density/pallas_call | solution.py:372
  112.1 3.9 %collective-permute-done.24 = f32[192,256]{1,0:T(8,128)S(1)} collective-permute-done((f32[192,256]{1,0:T(8,128)S(1)}, f32[192,256]{1,0:T(8,128)S(1)}, u32[]{:S(2)}, u32[]{:S(2)}) %collective-permute-start.24) | collective-permute-done | bytes 196640 | tf_op jit(solution)/shard_map/ppermute | solution.py:30
  116.0 19.1 %collective-permute-done.25.windows_ref = f32[2,2,256,256]{3,2,1,0:T(8,128)S(1)} collective-permute-done((f32[2,2,256,256]{3,2,1,0:T(8,128)S(1)}, f32[2,2,256,256]{3,2,1,0:T(8,128)S(1)}, u32[]{:S(2)}, u32[]{:S(2)}) %collective-permute-start.25) | collective-permute-done | bytes 1048608 | tf_op jit(solution)/shard_map/ppermute | solution.py:25
  136.3 4.8 %collective-permute-done.27 = f32[192,256]{1,0:T(8,128)S(1)} collective-permute-done((f32[192,256]{1,0:T(8,128)S(1)}, f32[192,256]{1,0:T(8,128)S(1)}, u32[]{:S(2)}, u32[]{:S(2)}) %collective-permute-start.27) | collective-permute-done | bytes 196640 | tf_op jit(solution)/shard_map/ppermute | solution.py:30
  141.2 5.7 %collective-permute-done.28 = f32[192,256]{1,0:T(8,128)S(1)} collective-permute-done((f32[192,256]{1,0:T(8,128)S(1)}, f32[192,256]{1,0:T(8,128)S(1)}, u32[]{:S(2)}, u32[]{:S(2)}) %collective-permute-start.28) | collective-permute-done | bytes 196640 | tf_op jit(solution)/shard_map/ppermute | solution.py:30
  147.0 8.8 %collective-permute-done.29 = f32[192,256]{1,0:T(8,128)S(1)} collective-permute-done((f32[192,256]{1,0:T(8,128)S(1)}, f32[192,256]{1,0:T(8,128)S(1)}, u32[]{:S(2)}, u32[]{:S(2)}) %collective-permute-start.29) | collective-permute-done | bytes 196640 | tf_op jit(solution)/shard_map/ppermute | solution.py:30
  155.8 1.7 %collective-permute-start.31 = (f32[192,256]{1,0:T(8,128)S(1)}, f32[192,256]{1,0:T(8,128)S(1)}, u32[]{:S(2)}, u32[]{:S(2)}) collective-permute-start(f32[192,256]{1,0:T(8,128)S(1)} %add.31.value_ref), channel_id=1, source_target_pairs={{0,2},{1,3},{2,0},{3,1},{4,6},{5,7},{6,4},{7,5},{8,10},{9,11},{10,... | collective-permute-start | bytes 589832 | tf_op jit(solution)/shard_map/ppermute | solution.py:30
  157.5 1.8 %renew.1 = f32[2,512,512]{2,1,0:T(8,128)} custom-call(f32[2,6,768,128]{3,2,1,0:T(8,128)S(1)} %widen.1.refs_3_.field_ref, f32[4,512,128]{2,1,0:T(8,128)S(1)} %density.3.density_ref, f32[2,6,768,128]{3,2,1,0:T(8,128)S(1)} %get-tuple-element.96.total_ref, f32[2,6,256,128]{3,2,1,0:T(8,128)S(1)} %get-tuple-element.101.top_ref, ...), custom_call_target="tpu_custom_call" | custom-call | flops 4000000 | bytes 10485760 | tf_op jit(solution)/shard_map/renew/pallas_call | solution.py:512
  159.3 2.4 %collective-permute-done.31.other_ref = f32[192,256]{1,0:T(8,128)S(1)} collective-permute-done((f32[192,256]{1,0:T(8,128)S(1)}, f32[192,256]{1,0:T(8,128)S(1)}, u32[]{:S(2)}, u32[]{:S(2)}) %collective-permute-start.31) | collective-permute-done | bytes 196640 | tf_op jit(solution)/shard_map/ppermute | solution.py:30
  161.8 1.7 %collective-permute-done.32.other_ref = f32[384,256]{1,0:T(8,128)S(1)} collective-permute-done((f32[384,256]{1,0:T(8,128)S(1)}, f32[384,256]{1,0:T(8,128)S(1)}, u32[]{:S(2)}, u32[]{:S(2)}) %collective-permute-start.32) | collective-permute-done | bytes 393248 | tf_op jit(solution)/shard_map/ppermute | solution.py:30
  (77 shorter events, 22.3 us)
Async XLA Ops:
  1.9 18.4 %collective-permute-start.1 = (f32[2,256,256]{2,1,0:T(8,128)S(1)}, f32[2,256,256]{2,1,0:T(8,128)S(1)}, u32[]{:S(2)}, u32[]{:S(2)}) collective-permute-start(f32[2,256,256]{2,1,0:T(8,128)S(1)} %slice.10), channel_id=1, source_target_pairs={{0,28},{4,0},{8,4},{12,8},{16,12},{20,16},{24,20},{28,24},{1,29},{... | collective-permute-start | bytes 1572872 | tf_op jit(solution)/shard_map/ppermute | solution.py:25
  9.3 21.2 %collective-permute-start = (f32[2,512,256]{2,1,0:T(8,128)S(1)}, f32[2,512,256]{2,1,0:T(8,128)S(1)}, u32[]{:S(2)}, u32[]{:S(2)}) collective-permute-start(f32[2,512,256]{2,1,0:T(8,128)S(1)} %slice.9), channel_id=1, source_target_pairs={{0,3},{1,0},{2,1},{3,2},{4,7},{5,4},{6,5},{7,6},{8,11},{9,8},{10,9... | collective-permute-start | bytes 3145736 | tf_op jit(solution)/shard_map/ppermute | solution.py:25
  10.0 10.4 %collective-permute-start.3 = (s32[1,1,2,2,2]{4,3,2,1,0:T(2,128)S(1)}, s32[1,1,2,2,2]{4,3,2,1,0:T(2,128)S(1)}, u32[]{:S(2)}, u32[]{:S(2)}) collective-permute-start(s32[1,1,2,2,2]{4,3,2,1,0:T(2,128)S(1)} %copy-done.2), channel_id=1, source_target_pairs={{0,28},{4,0},{8,4},{12,8},{16,12},{20,16},{24,20},{28,24},{1,29},{... | collective-permute-start | bytes 104 | tf_op jit(solution)/shard_map/ppermute | solution.py:25
  10.7 9.7 %collective-permute-start.2 = (s32[1,1,2,2,2]{4,3,2,1,0:T(2,128)S(1)}, s32[1,1,2,2,2]{4,3,2,1,0:T(2,128)S(1)}, u32[]{:S(2)}, u32[]{:S(2)}) collective-permute-start(s32[1,1,2,2,2]{4,3,2,1,0:T(2,128)S(1)} %copy-done.2), channel_id=1, source_target_pairs={{0,4},{4,8},{8,12},{12,16},{16,20},{20,24},{24,28},{28,0},{1,5},{5... | collective-permute-start | bytes 104 | tf_op jit(solution)/shard_map/ppermute | solution.py:25
  12.1 18.4 %collective-permute-start.4 = (f32[2,256,256]{2,1,0:T(8,128)S(1)}, f32[2,256,256]{2,1,0:T(8,128)S(1)}, u32[]{:S(2)}, u32[]{:S(2)}) collective-permute-start(f32[2,256,256]{2,1,0:T(8,128)S(1)} %slice.11), channel_id=1, source_target_pairs={{0,28},{4,0},{8,4},{12,8},{16,12},{20,16},{24,20},{28,24},{1,29},{... | collective-permute-start | bytes 1572872 | tf_op jit(solution)/shard_map/ppermute | solution.py:25
  20.4 10.1 %collective-permute-start.5 = (f32[2,256,256]{2,1,0:T(8,128)S(1)}, f32[2,256,256]{2,1,0:T(8,128)S(1)}, u32[]{:S(2)}, u32[]{:S(2)}) collective-permute-start(f32[2,256,256]{2,1,0:T(8,128)S(1)} %collective-permute-done.1.refs_5_.refs_2_), channel_id=1, source_target_pairs={{0,3},{1,0},{2,1},{3,2},{4,7},{5,4},{6,5},{7,6},{8,11},{9,8},{10,9... | collective-permute-start | bytes 1572872 | tf_op jit(solution)/shard_map/ppermute | solution.py:25
  35.8 26.5 %collective-permute-start.12 = (f32[2,2,256,256]{3,2,1,0:T(8,128)S(1)}, f32[2,2,256,256]{3,2,1,0:T(8,128)S(1)}, u32[]{:S(2)}, u32[]{:S(2)}) collective-permute-start(f32[2,2,256,256]{3,2,1,0:T(8,128)S(1)} %get-tuple-element.63.windows_ref), channel_id=1, source_target_pairs={{0,4},{4,0},{8,12},{12,8},{16,20},{20,16},{24,28},{28,24},{1,5},{5... | collective-permute-start | bytes 3145736 | tf_op jit(solution)/shard_map/ppermute | solution.py:30
  36.3 3.1 %collective-permute-start.6 = (f32[384,256]{1,0:T(8,128)S(1)}, f32[384,256]{1,0:T(8,128)S(1)}, u32[]{:S(2)}, u32[]{:S(2)}) collective-permute-start(f32[384,256]{1,0:T(8,128)S(1)} %get-tuple-element.58), channel_id=1, source_target_pairs={{0,1},{1,0},{2,3},{3,2},{4,5},{5,4},{6,7},{7,6},{8,9},{9,8},{10,11... | collective-permute-start | bytes 1179656 | tf_op jit(solution)/shard_map/ppermute | solution.py:30
  36.3 3.1 %collective-permute-start.8 = (s32[3,1,2,2,2]{4,3,2,1,0:T(2,128)S(1)}, s32[3,1,2,2,2]{4,3,2,1,0:T(2,128)S(1)}, u32[]{:S(2)}, u32[]{:S(2)}) collective-permute-start(s32[3,1,2,2,2]{4,3,2,1,0:T(2,128)S(1)} %pad_add_fusion.offsets_ref), channel_id=1, source_target_pairs={{0,1},{1,2},{2,3},{3,0},{4,5},{5,6},{6,7},{7,4},{8,9},{9,10},{10,1... | collective-permute-start | bytes 296 | tf_op jit(solution)/shard_map/ppermute | solution.py:25
  36.8 4.2 %collective-permute-start.9 = (s32[3,1,2,2,2]{4,3,2,1,0:T(2,128)S(1)}, s32[3,1,2,2,2]{4,3,2,1,0:T(2,128)S(1)}, u32[]{:S(2)}, u32[]{:S(2)}) collective-permute-start(s32[3,1,2,2,2]{4,3,2,1,0:T(2,128)S(1)} %pad_add_fusion.offsets_ref), channel_id=1, source_target_pairs={{0,3},{1,0},{2,1},{3,2},{4,7},{5,4},{6,5},{7,6},{8,11},{9,8},{10,9... | collective-permute-start | bytes 296 | tf_op jit(solution)/shard_map/ppermute | solution.py:25
  39.5 6.2 %collective-permute-start.7 = (f32[192,256]{1,0:T(8,128)S(1)}, f32[192,256]{1,0:T(8,128)S(1)}, u32[]{:S(2)}, u32[]{:S(2)}) collective-permute-start(f32[192,256]{1,0:T(8,128)S(1)} %get-tuple-element.60), channel_id=1, source_target_pairs={{0,2},{1,3},{2,0},{3,1},{4,6},{5,7},{6,4},{7,5},{8,10},{9,11},{10,... | collective-permute-start | bytes 589832 | tf_op jit(solution)/shard_map/ppermute | solution.py:30
  45.7 10.8 %collective-permute-start.10 = (f32[192,256]{1,0:T(8,128)S(1)}, f32[192,256]{1,0:T(8,128)S(1)}, u32[]{:S(2)}, u32[]{:S(2)}) collective-permute-start(f32[192,256]{1,0:T(8,128)S(1)} %add.24), channel_id=1, source_target_pairs={{0,16},{4,20},{8,24},{12,28},{16,0},{20,4},{24,8},{28,12},{1,17},{... | collective-permute-start | bytes 589832 | tf_op jit(solution)/shard_map/ppermute | solution.py:30
  56.6 5.7 %collective-permute-start.11 = (f32[192,256]{1,0:T(8,128)S(1)}, f32[192,256]{1,0:T(8,128)S(1)}, u32[]{:S(2)}, u32[]{:S(2)}) collective-permute-start(f32[192,256]{1,0:T(8,128)S(1)} %add.25), channel_id=1, source_target_pairs={{0,8},{4,12},{8,0},{12,4},{16,24},{20,28},{24,16},{28,20},{1,9},{5... | collective-permute-start | bytes 589832 | tf_op jit(solution)/shard_map/ppermute | solution.py:30
  56.9 18.3 %collective-permute-start.16 = (f32[2,2,256,128]{3,2,1,0:T(8,128)S(1)}, f32[2,2,256,128]{3,2,1,0:T(8,128)S(1)}, u32[]{:S(2)}, u32[]{:S(2)}) collective-permute-start(f32[2,2,256,128]{3,2,1,0:T(8,128)S(1)} %get-tuple-element.69), channel_id=1, source_target_pairs={{1,2},{2,1},{5,6},{6,5},{9,10},{10,9},{13,14},{14,13},{17,18},{18,... | collective-permute-start | bytes 1572872 | tf_op jit(solution)/shard_map/ppermute | solution.py:41
  62.3 25.9 %collective-permute-start.13 = (f32[2,2,256,256]{3,2,1,0:T(8,128)S(1)}, f32[2,2,256,256]{3,2,1,0:T(8,128)S(1)}, u32[]{:S(2)}, u32[]{:S(2)}) collective-permute-start(f32[2,2,256,256]{3,2,1,0:T(8,128)S(1)} %collective-permute-done.12.windows_ref), channel_id=1, source_target_pairs={{0,8},{4,28},{8,16},{12,4},{16,24},{20,12},{24,0},{28,20},{1,9},{5... | collective-permute-start | bytes 3145736 | tf_op jit(solution)/shard_map/ppermute | solution.py:35
  63.4 14.1 %collective-permute-start.17 = (f32[2,2,256,128]{3,2,1,0:T(8,128)S(1)}, f32[2,2,256,128]{3,2,1,0:T(8,128)S(1)}, u32[]{:S(2)}, u32[]{:S(2)}) collective-permute-start(f32[2,2,256,128]{3,2,1,0:T(8,128)S(1)} %get-tuple-element.70), channel_id=1, source_target_pairs={{0,1},{1,0},{2,3},{3,2},{4,5},{5,4},{6,7},{7,6},{8,9},{9,8},{10,11... | collective-permute-start | bytes 1572872 | tf_op jit(solution)/shard_map/ppermute | solution.py:30
  63.4 8.5 %collective-permute-start.14 = (f32[192,256]{1,0:T(8,128)S(1)}, f32[192,256]{1,0:T(8,128)S(1)}, u32[]{:S(2)}, u32[]{:S(2)}) collective-permute-start(f32[192,256]{1,0:T(8,128)S(1)} %add.26), channel_id=1, source_target_pairs={{0,4},{4,0},{8,12},{12,8},{16,20},{20,16},{24,28},{28,24},{1,5},{5... | collective-permute-start | bytes 589832 | tf_op jit(solution)/shard_map/ppermute | solution.py:30
  72.0 6.8 %collective-permute-start.15 = (f32[192,256]{1,0:T(8,128)S(1)}, f32[192,256]{1,0:T(8,128)S(1)}, u32[]{:S(2)}, u32[]{:S(2)}) collective-permute-start(f32[192,256]{1,0:T(8,128)S(1)} %add.27.value_ref), channel_id=1, source_target_pairs={{0,2},{1,3},{2,0},{3,1},{4,6},{5,7},{6,4},{7,5},{8,10},{9,11},{10,... | collective-permute-start | bytes 589832 | tf_op jit(solution)/shard_map/ppermute | solution.py:30
  74.3 6.4 %collective-permute-start.19 = (f32[2,2,256,128]{3,2,1,0:T(8,128)S(1)}, f32[2,2,256,128]{3,2,1,0:T(8,128)S(1)}, u32[]{:S(2)}, u32[]{:S(2)}) collective-permute-start(f32[2,2,256,128]{3,2,1,0:T(8,128)S(1)} %get-tuple-element.73), channel_id=1, source_target_pairs={{1,2},{2,1},{5,6},{6,5},{9,10},{10,9},{13,14},{14,13},{17,18},{18,... | collective-permute-start | bytes 1572872 | tf_op jit(solution)/shard_map/ppermute | solution.py:41
  75.2 5.6 %collective-permute-start.20 = (f32[2,2,256,128]{3,2,1,0:T(8,128)S(1)}, f32[2,2,256,128]{3,2,1,0:T(8,128)S(1)}, u32[]{:S(2)}, u32[]{:S(2)}) collective-permute-start(f32[2,2,256,128]{3,2,1,0:T(8,128)S(1)} %get-tuple-element.74), channel_id=1, source_target_pairs={{0,1},{1,0},{2,3},{3,2},{4,5},{5,4},{6,7},{7,6},{8,9},{9,8},{10,11... | collective-permute-start | bytes 1572872 | tf_op jit(solution)/shard_map/ppermute | solution.py:30
  78.8 1.8 %collective-permute-start.18 = (f32[384,256]{1,0:T(8,128)S(1)}, f32[384,256]{1,0:T(8,128)S(1)}, u32[]{:S(2)}, u32[]{:S(2)}) collective-permute-start(f32[384,256]{1,0:T(8,128)S(1)} %join.2.value_ref), channel_id=1, source_target_pairs={{0,1},{1,0},{2,3},{3,2},{4,5},{5,4},{6,7},{7,6},{8,9},{9,8},{10,11... | collective-permute-start | bytes 1179656 | tf_op jit(solution)/shard_map/ppermute | solution.py:30
  89.4 2.0 %collective-permute-start.21 = (f32[2,2,256,128]{3,2,1,0:T(8,128)S(1)}, f32[2,2,256,128]{3,2,1,0:T(8,128)S(1)}, u32[]{:S(2)}, u32[]{:S(2)}) collective-permute-start(f32[2,2,256,128]{3,2,1,0:T(8,128)S(1)} %get-tuple-element.82), channel_id=1, source_target_pairs={{0,1},{1,0},{2,3},{3,2},{4,5},{5,4},{6,7},{7,6},{8,9},{9,8},{10,11... | collective-permute-start | bytes 1572872 | tf_op jit(solution)/shard_map/ppermute | solution.py:30
  89.5 1.9 %collective-permute-start.22 = (f32[2,2,256,128]{3,2,1,0:T(8,128)S(1)}, f32[2,2,256,128]{3,2,1,0:T(8,128)S(1)}, u32[]{:S(2)}, u32[]{:S(2)}) collective-permute-start(f32[2,2,256,128]{3,2,1,0:T(8,128)S(1)} %get-tuple-element.85), channel_id=1, source_target_pairs={{1,2},{2,1},{5,6},{6,5},{9,10},{10,9},{13,14},{14,13},{17,18},{18,... | collective-permute-start | bytes 1572872 | tf_op jit(solution)/shard_map/ppermute | solution.py:41
  98.1 10.5 %collective-permute-start.23 = (f32[384,256]{1,0:T(8,128)S(1)}, f32[384,256]{1,0:T(8,128)S(1)}, u32[]{:S(2)}, u32[]{:S(2)}) collective-permute-start(f32[384,256]{1,0:T(8,128)S(1)} %get-tuple-element.87), channel_id=1, source_target_pairs={{0,1},{1,0},{2,3},{3,2},{4,5},{5,4},{6,7},{7,6},{8,9},{9,8},{10,11... | collective-permute-start | bytes 1179656 | tf_op jit(solution)/shard_map/ppermute | solution.py:30
  107.3 27.8 %collective-permute-start.25 = (f32[2,2,256,256]{3,2,1,0:T(8,128)S(1)}, f32[2,2,256,256]{3,2,1,0:T(8,128)S(1)}, u32[]{:S(2)}, u32[]{:S(2)}) collective-permute-start(f32[2,2,256,256]{3,2,1,0:T(8,128)S(1)} %get-tuple-element.90.windows_ref), channel_id=1, source_target_pairs={{0,4},{4,8},{8,12},{12,16},{16,20},{20,24},{24,28},{28,0},{1,5},{5... | collective-permute-start | bytes 3145736 | tf_op jit(solution)/shard_map/ppermute | solution.py:25
  108.7 7.2 %collective-permute-start.24 = (f32[192,256]{1,0:T(8,128)S(1)}, f32[192,256]{1,0:T(8,128)S(1)}, u32[]{:S(2)}, u32[]{:S(2)}) collective-permute-start(f32[192,256]{1,0:T(8,128)S(1)} %get-tuple-element.89), channel_id=1, source_target_pairs={{0,2},{1,3},{2,0},{3,1},{4,6},{5,7},{6,4},{7,5},{8,10},{9,11},{10,... | collective-permute-start | bytes 589832 | tf_op jit(solution)/shard_map/ppermute | solution.py:30
  115.9 19.2 %collective-permute-start.26 = (f32[2,2,256,128]{3,2,1,0:T(8,128)S(1)}, f32[2,2,256,128]{3,2,1,0:T(8,128)S(1)}, u32[]{:S(2)}, u32[]{:S(2)}) collective-permute-start(f32[2,2,256,128]{3,2,1,0:T(8,128)S(1)} %get-tuple-element.94), channel_id=1, source_target_pairs={{0,1},{1,2},{2,3},{3,0},{4,5},{5,6},{6,7},{7,4},{8,9},{9,10},{10,1... | collective-permute-start | bytes 1572872 | tf_op jit(solution)/shard_map/ppermute | solution.py:25
  135.1 6.0 %collective-permute-start.27 = (f32[192,256]{1,0:T(8,128)S(1)}, f32[192,256]{1,0:T(8,128)S(1)}, u32[]{:S(2)}, u32[]{:S(2)}) collective-permute-start(f32[192,256]{1,0:T(8,128)S(1)} %add.28), channel_id=1, source_target_pairs={{0,4},{4,0},{8,12},{12,8},{16,20},{20,16},{24,28},{28,24},{1,5},{5... | collective-permute-start | bytes 589832 | tf_op jit(solution)/shard_map/ppermute | solution.py:30
  136.2 19.6 %collective-permute-start.30 = (f32[2,2,256,128]{3,2,1,0:T(8,128)S(1)}, f32[2,2,256,128]{3,2,1,0:T(8,128)S(1)}, u32[]{:S(2)}, u32[]{:S(2)}) collective-permute-start(f32[2,2,256,128]{3,2,1,0:T(8,128)S(1)} %get-tuple-element.98), channel_id=1, source_target_pairs={{0,1},{1,2},{2,3},{3,0},{4,5},{5,6},{6,7},{7,4},{8,9},{9,10},{10,1... | collective-permute-start | bytes 1572872 | tf_op jit(solution)/shard_map/ppermute | solution.py:25
  141.2 5.7 %collective-permute-start.28 = (f32[192,256]{1,0:T(8,128)S(1)}, f32[192,256]{1,0:T(8,128)S(1)}, u32[]{:S(2)}, u32[]{:S(2)}) collective-permute-start(f32[192,256]{1,0:T(8,128)S(1)} %add.29), channel_id=1, source_target_pairs={{0,8},{4,12},{8,0},{12,4},{16,24},{20,28},{24,16},{28,20},{1,9},{5... | collective-permute-start | bytes 589832 | tf_op jit(solution)/shard_map/ppermute | solution.py:30
  146.9 8.9 %collective-permute-start.29 = (f32[192,256]{1,0:T(8,128)S(1)}, f32[192,256]{1,0:T(8,128)S(1)}, u32[]{:S(2)}, u32[]{:S(2)}) collective-permute-start(f32[192,256]{1,0:T(8,128)S(1)} %add.30), channel_id=1, source_target_pairs={{0,16},{4,20},{8,24},{12,28},{16,0},{20,4},{24,8},{28,12},{1,17},{... | collective-permute-start | bytes 589832 | tf_op jit(solution)/shard_map/ppermute | solution.py:30
  155.8 5.9 %collective-permute-start.31 = (f32[192,256]{1,0:T(8,128)S(1)}, f32[192,256]{1,0:T(8,128)S(1)}, u32[]{:S(2)}, u32[]{:S(2)}) collective-permute-start(f32[192,256]{1,0:T(8,128)S(1)} %add.31.value_ref), channel_id=1, source_target_pairs={{0,2},{1,3},{2,0},{3,1},{4,6},{5,7},{6,4},{7,5},{8,10},{9,11},{10,... | collective-permute-start | bytes 589832 | tf_op jit(solution)/shard_map/ppermute | solution.py:30
  (6 other events, 99.4 us)

commit v7 on v6

--- a/solution.py
+++ b/solution.py
@@ -260,13 +260,12 @@
             patch_real * patch_real + patch_imag * patch_imag,
         )
         for number, value in enumerate(sums):
-            spot = slice(number * side, (number + 1) * side)
             if scan == 0:
-                sums_ref[spot] = value
+                sums_ref[number] = value
             else:
-                sums_ref[spot] += value
-    kept, sent = halves_of(0, outs_hbm[0].shape[0])
-    outs = [(sums_ref.at[sent], outs_hbm[1]), (sums_ref.at[kept], outs_hbm[0])]
+                sums_ref[number] += value
+    kept, sent = halves_of(0, outs_hbm[0].shape[1])
+    outs = [(sums_ref.at[:, sent], outs_hbm[1]), (sums_ref.at[:, kept], outs_hbm[0])]
     outs = [pltpu.make_async_copy(source, target, out_sem) for source, target in outs]
     for copy in outs:
         copy.start()
@@ -276,12 +275,12 @@
 
 def scan_step(sweep, last, offsets, probe, amplitudes, table, *field):
     side = probe.shape[1]
-    shapes = [shape_of(3 * side // 2, side)] * 2 + [shape_of(2, 2, side, side)]
+    shapes = [shape_of(3, side // 2, side)] * 2 + [shape_of(2, 2, side, side)]
     scratch = [
         VMEM(probe.shape, jnp.float32),
         VMEM(amplitudes.shape[1:], amplitudes.dtype),
         VMEM(table.shape, table.dtype),
-        VMEM((3 * side, side), jnp.float32),
+        VMEM((3, side, side), jnp.float32),
         VMEM((2, 2, side, side), jnp.float32),
         pltpu.SemaphoreType.DMA((3,)),
         pltpu.SemaphoreType.DMA,
@@ -522,16 +521,16 @@
 
 def fold_kernel(bit, value_ref, came_ref, kept_ref, sent_ref, total_ref):
     total_ref[...] = value_ref[...] + came_ref[...]
-    kept, sent = halves_of(bit, kept_ref.shape[0])
-    kept_ref[...] = total_ref[kept]
-    sent_ref[...] = total_ref[sent]
+    kept, sent = halves_of(bit, kept_ref.shape[1])
+    kept_ref[...] = total_ref[:, kept]
+    sent_ref[...] = total_ref[:, sent]
 
 
 def fold(bit, value, came):
-    rows, side = value.shape
+    planes, rows, side = value.shape
     return pl.pallas_call(
         functools.partial(fold_kernel, bit),
-        out_shape=[shape_of(rows // 2, side)] * 2,
+        out_shape=[shape_of(planes, rows // 2, side)] * 2,
         in_specs=whole_spec(2),
         out_specs=whole_spec(2),
         scratch_shapes=[VMEM(value.shape, jnp.float32)],
@@ -542,16 +541,16 @@
 
 
 def join_kernel(bit, value_ref, other_ref, out_ref):
-    kept, sent = halves_of(bit, value_ref.shape[0])
-    out_ref[kept] = value_ref[...]
-    out_ref[sent] = other_ref[...]
+    kept, sent = halves_of(bit, value_ref.shape[1])
+    out_ref[:, kept] = value_ref[...]
+    out_ref[:, sent] = other_ref[...]
 
 
 def join(bit, value, other):
-    rows, side = value.shape
+    planes, rows, side = value.shape
     return pl.pallas_call(
         functools.partial(join_kernel, bit),
-        out_shape=shape_of(2 * rows, side),
+        out_shape=shape_of(planes, 2 * rows, side),
         in_specs=whole_spec(2),
         out_specs=whole_spec(1)[0],
         compiler_params=pltpu.CompilerParams(vmem_limit_bytes=4 * MIB),
@@ -560,28 +559,28 @@
     )(value, other)
 
 
-def illuminate_kernel(value_ref, other_ref, probe_ref, out_ref, total_ref):
-    kept, sent = halves_of(0, value_ref.shape[0])
-    total_ref[kept] = value_ref[...]
-    total_ref[sent] = other_ref[...]
-    side = probe_ref.shape[1]
-    part = 1.0 / (total_ref[2 * side :] + probe_damping)
-    out_ref[0] = probe_ref[0] + total_ref[:side] * part
-    out_ref[1] = probe_ref[1] + total_ref[side : 2 * side] * part
-
-
-def illuminate(value, other, probe):
-    rows, side = value.shape
-    return pl.pallas_call(
-        illuminate_kernel,
-        out_shape=shape_of(*probe.shape),
-        in_specs=whole_spec(3),
+def illuminate_kernel(bits, sums_ref, probe_ref, out_ref):
+    rows = sums_ref.shape[1]
+    start, half = 0, probe_ref.shape[1]
+    for bit in range(bits):
+        half //= 2
+        start += lax.rem(lax.axis_index("col") >> bit, 2) * half
+    spot = pl.ds(pl.multiple_of(start, 8), rows)
+    part = 1.0 / (sums_ref[2] + probe_damping)
+    for plane in range(2):
+        out_ref[plane] = probe_ref[plane, spot] + sums_ref[plane] * part
+
+
+def illuminate(bits, sums, probe):
+    return pl.pallas_call(
+        functools.partial(illuminate_kernel, bits),
+        out_shape=shape_of(2, *sums.shape[1:]),
+        in_specs=whole_spec(2),
         out_specs=whole_spec(1)[0],
-        scratch_shapes=[VMEM((2 * rows, side), jnp.float32)],
-        compiler_params=pltpu.CompilerParams(vmem_limit_bytes=6 * MIB),
-        cost_estimate=cost(1_000_000, 2 * MIB),
+        compiler_params=pltpu.CompilerParams(vmem_limit_bytes=4 * MIB),
+        cost_estimate=cost(100_000, MIB),
         name="illuminate",
-    )(value, other, probe)
+    )(sums, probe)
 
 
 def tied(*values):
@@ -628,12 +627,12 @@
     inner_strips.append(swapped(near_inner, "col", 1))
     outer_strips.append(swapped_outward(near_outer, "col"))
     sums = sums + swapped(sums, "row", 1)
-    for bit in reversed(range(1, col_bits)):
-        other = swapped(sums, "col", 1 << bit)
+    probe = illuminate(col_bits, sums, probe)
+    for bit in reversed(range(col_bits)):
+        other = swapped(probe, "col", 1 << bit)
         if bit == col_bits - 1:
             other, outer_strips[0], inner_strips[0] = tied(other, outer_strips[0], inner_strips[0])
-        sums = join(bit, sums, other)
-    probe = illuminate(sums, swapped(sums, "col", 1), probe)
+        probe = join(bit, probe, other)
     passed, probe, outer_strips[1], inner_strips[1] = tied(passed, probe, outer_strips[1], inner_strips[1])
     far_all, far_inner, far_outer = gather(0, other_below, near, total, passed, 2)
     inner_strips.append(swapped(far_inner, "col", 1))
@@ -658,12 +657,13 @@
         sums = sums + swapped(sums, "row", 1 << bit)
     sums, left_top = tied(sums, left_top)
     field = renew(field, dense, total, top, left_top, left_rest)
-    for bit in reversed(range(1, col_bits)):
-        other = swapped(sums, "col", 1 << bit)
+    probe = illuminate(col_bits, sums, probe)
+    for bit in reversed(range(col_bits)):
+        other = swapped(probe, "col", 1 << bit)
         if bit == 1:
             other, field = tied(other, field)
-        sums = join(bit, sums, other)
-    return field, illuminate(sums, swapped(sums, "col", 1), probe)
+        probe = join(bit, probe, other)
+    return field, probe
 
 
 def solution(mesh):

time: 165 us -> 163 us (0.988)
    ppermute x1, waiting for transfers between devices: 7.45 us -> 2.12 us  [handed_on(): lax.ppermute(array, axis, [(i, (i + 2 - 4 * (i % 2)) % peers) for i in ra...]
    ppermute x18, waiting for transfers between devices: 51.8 us -> 56.3 us  [swapped(): return lax.ppermute(array, axis, [(i, i ^ mask) for i in range(peers)])]
where the time goes in v7:
time: 163 us
  waiting for transfers between devices  93.3 us (57%)
  starting transfers between devices  39.3 us (24%)
  Pallas kernels  26.3 us (16%)
  local copies, waits for them, and re-layouts  2.61 us (2%)
    ppermute x18, waiting for transfers between devices, swapped(): return lax.ppermute(array, axis, [(i, i ^ mask) for i in range(peers)])  56.3 us
    ppermute x11, waiting for transfers between devices, shifted(): lax.ppermute(array, axis, [(i, (i + by) % peers) for i in range(peers)])  34.8 us
    ppermute x18, starting transfers between devices, swapped(): return lax.ppermute(array, axis, [(i, i ^ mask) for i in range(peers)])  22.3 us
    ppermute x11, starting transfers between devices, shifted(): lax.ppermute(array, axis, [(i, (i + by) % peers) for i in range(peers)])  14.1 us
    pallas_call x2, Pallas kernels, scan_step(): pl.pallas_call(functools.partial(scan_kernel, sweep, last, counts), out_s...  9.81 us
    pallas_call x2, Pallas kernels, density(): pl.pallas_call(functools.partial(density_kernel, sweep, reach), out_shape...  4.44 us
    pallas_call x3, Pallas kernels, gather(): pl.pallas_call(functools.partial(gather_kernel, sweep, below_of), out_sha...  4.25 us
  transfers between devices with their start and end apart: 33, of which 19 were waited for; matrix products, arithmetic and copies ran while one was open for 1% of the time, Pallas kernels for 8%

profile of v7, /device:TPU:0, one launch (start us, length us, event | category | flops | bytes accessed | tf_op | source)
XLA Modules:
  0.0 162.7 jit_solution(2378214081513528438)
XLA Ops:
  1.9 6.1 %collective-permute-start.1 = (f32[2,256,256]{2,1,0:T(8,128)S(1)}, f32[2,256,256]{2,1,0:T(8,128)S(1)}, u32[]{:S(2)}, u32[]{:S(2)}) collective-permute-start(f32[2,256,256]{2,1,0:T(8,128)S(1)} %slice.10), channel_id=1, source_target_pairs={{0,28},{4,0},{8,4},{12,8},{16,12},{20,16},{24,20},{28,24},{1,29},{... | collective-permute-start | bytes 1572872 | tf_op jit(solution)/shard_map/ppermute | solution.py:25
  10.7 1.4 collective-permute-start.2
  12.1 3.4 %collective-permute-start.4 = (f32[2,256,256]{2,1,0:T(8,128)S(1)}, f32[2,256,256]{2,1,0:T(8,128)S(1)}, u32[]{:S(2)}, u32[]{:S(2)}) collective-permute-start(f32[2,256,256]{2,1,0:T(8,128)S(1)} %slice.11), channel_id=1, source_target_pairs={{0,28},{4,0},{8,4},{12,8},{16,12},{20,16},{24,20},{28,24},{1,29},{... | collective-permute-start | bytes 1572872 | tf_op jit(solution)/shard_map/ppermute | solution.py:25
  15.5 4.9 %collective-permute-done.3 = s32[1,1,2,2,2]{4,3,2,1,0:T(2,128)S(1)} collective-permute-done((s32[1,1,2,2,2]{4,3,2,1,0:T(2,128)S(1)}, s32[1,1,2,2,2]{4,3,2,1,0:T(2,128)S(1)}, u32[]{:S(2)}, u32[]{:S(2)}) %collective-permute-start.3) | collective-permute-done | bytes 64 | tf_op jit(solution)/shard_map/ppermute | solution.py:25
  21.0 9.4 %collective-permute-done.4.refs_6_.refs_3_ = f32[2,256,256]{2,1,0:T(8,128)S(1)} collective-permute-done((f32[2,256,256]{2,1,0:T(8,128)S(1)}, f32[2,256,256]{2,1,0:T(8,128)S(1)}, u32[]{:S(2)}, u32[]{:S(2)}) %collective-permute-start.4) | collective-permute-done | bytes 524320 | tf_op jit(solution)/shard_map/ppermute | solution.py:25
  30.5 5.1 %scan.2 = (f32[3,128,256]{2,1,0:T(8,128)S(1)}, f32[3,128,256]{2,1,0:T(8,128)S(1)}, f32[2,2,256,256]{3,2,1,0:T(8,128)S(1)}) custom-call(s32[1,1,2,2,2]{4,3,2,1,0:T(2,128)S(1)} %copy-done.2, f32[2,256,256]{2,1,0:T(8,128)S(1)} %copy-done.1, bf16[2,2,256,256]{3,2,1,0:T(8,128)(2,1)S(1)} %reorder.1.refs_1_, bf16[8,256,256]{2,1,0:T(8,128)(2,1)S(1)} %copy-done.4, ...), custom_call_target="tpu_custom_call" | custom-call | flops 7000000000 | bytes 12582912 | tf_op jit(solution)/shard_map/scan/pallas_call | solution.py:294
  39.2 1.5 collective-permute-start.7
  40.8 4.6 %collective-permute-done.7 = f32[3,64,256]{2,1,0:T(8,128)S(1)} collective-permute-done((f32[3,64,256]{2,1,0:T(8,128)S(1)}, f32[3,64,256]{2,1,0:T(8,128)S(1)}, u32[]{:S(2)}, u32[]{:S(2)}) %collective-permute-start.7) | collective-permute-done | bytes 196640 | tf_op jit(solution)/shard_map/ppermute | solution.py:30
  45.4 2.7 %collective-permute-start.10 = (f32[3,64,256]{2,1,0:T(8,128)S(1)}, f32[3,64,256]{2,1,0:T(8,128)S(1)}, u32[]{:S(2)}, u32[]{:S(2)}) collective-permute-start(f32[3,64,256]{2,1,0:T(8,128)S(1)} %add.24), channel_id=1, source_target_pairs={{0,16},{4,20},{8,24},{12,28},{16,0},{20,4},{24,8},{28,12},{1,17},{... | collective-permute-start | bytes 589832 | tf_op jit(solution)/shard_map/ppermute | solution.py:30
  48.1 2.7 %density.2.refs_5_ = f32[6,768,128]{2,1,0:T(8,128)S(1)} custom-call(s32[3,3,2,2,2]{4,3,2,1,0:T(2,128)S(1)} %constant_dynamic-update-slice_fusion.offsets_ref, f32[2,256,256]{2,1,0:T(8,128)S(1)} %copy-done.1), custom_call_target="tpu_custom_call" | custom-call | flops 1000000 | bytes 6291456 | tf_op jit(solution)/shard_map/density/pallas_call | solution.py:371
  52.1 4.1 %collective-permute-done.10 = f32[3,64,256]{2,1,0:T(8,128)S(1)} collective-permute-done((f32[3,64,256]{2,1,0:T(8,128)S(1)}, f32[3,64,256]{2,1,0:T(8,128)S(1)}, u32[]{:S(2)}, u32[]{:S(2)}) %collective-permute-start.10) | collective-permute-done | bytes 196640 | tf_op jit(solution)/shard_map/ppermute | solution.py:30
  56.6 5.5 %collective-permute-done.11 = f32[3,64,256]{2,1,0:T(8,128)S(1)} collective-permute-done((f32[3,64,256]{2,1,0:T(8,128)S(1)}, f32[3,64,256]{2,1,0:T(8,128)S(1)}, u32[]{:S(2)}, u32[]{:S(2)}) %collective-permute-start.11) | collective-permute-done | bytes 196640 | tf_op jit(solution)/shard_map/ppermute | solution.py:30
  63.6 2.6 %collective-permute-start.17 = (f32[2,2,256,128]{3,2,1,0:T(8,128)S(1)}, f32[2,2,256,128]{3,2,1,0:T(8,128)S(1)}, u32[]{:S(2)}, u32[]{:S(2)}) collective-permute-start(f32[2,2,256,128]{3,2,1,0:T(8,128)S(1)} %get-tuple-element.70), channel_id=1, source_target_pairs={{0,1},{1,0},{2,3},{3,2},{4,5},{5,4},{6,7},{7,6},{8,9},{9,8},{10,11... | collective-permute-start | bytes 1572872 | tf_op jit(solution)/shard_map/ppermute | solution.py:30
  66.2 2.8 %collective-permute-start.14 = (f32[3,64,256]{2,1,0:T(8,128)S(1)}, f32[3,64,256]{2,1,0:T(8,128)S(1)}, u32[]{:S(2)}, u32[]{:S(2)}) collective-permute-start(f32[3,64,256]{2,1,0:T(8,128)S(1)} %add.26), channel_id=1, source_target_pairs={{0,4},{4,0},{8,12},{12,8},{16,20},{20,16},{24,28},{28,24},{1,5},{5... | collective-permute-start | bytes 589832 | tf_op jit(solution)/shard_map/ppermute | solution.py:30
  69.0 1.8 %gather.3 = (f32[2,6,256,128]{3,2,1,0:T(8,128)S(1)}, f32[2,2,256,128]{3,2,1,0:T(8,128)S(1)}, f32[2,2,256,128]{3,2,1,0:T(8,128)S(1)}) custom-call(s32[3,1,2,2,2]{4,3,2,1,0:T(2,128)S(1)} %pad_add_fusion.offsets_ref, f32[2,6,768,128]{3,2,1,0:T(8,128)S(1)} %get-tuple-element.72.total_ref.refs_6_, f32[2,2,256,256]{3,2,1,0:T(8,128)S(1)} %collective-permute-done.12.windows_ref), custom_call_target="tpu_custom_call" | custom-call | flops 1000000 | bytes 6291456 | tf_op jit(solution)/shard_map/gather/pallas_call | solution.py:423
  71.5 2.7 %collective-permute-done.14 = f32[3,64,256]{2,1,0:T(8,128)S(1)} collective-permute-done((f32[3,64,256]{2,1,0:T(8,128)S(1)}, f32[3,64,256]{2,1,0:T(8,128)S(1)}, u32[]{:S(2)}, u32[]{:S(2)}) %collective-permute-start.14) | collective-permute-done | bytes 196640 | tf_op jit(solution)/shard_map/ppermute | solution.py:30
  74.7 9.1 %collective-permute-done.15.other_ref = f32[2,64,256]{2,1,0:T(8,128)S(1)} collective-permute-done((f32[2,64,256]{2,1,0:T(8,128)S(1)}, f32[2,64,256]{2,1,0:T(8,128)S(1)}, u32[]{:S(2)}, u32[]{:S(2)}) %collective-permute-start.15) | collective-permute-done | bytes 131104 | tf_op jit(solution)/shard_map/ppermute | solution.py:30
  83.9 1.5 collective-permute-done.18.other_ref
  85.5 2.1 %collective-permute-done.13.windows_ref = f32[2,2,256,256]{3,2,1,0:T(8,128)S(1)} collective-permute-done((f32[2,2,256,256]{3,2,1,0:T(8,128)S(1)}, f32[2,2,256,256]{3,2,1,0:T(8,128)S(1)}, u32[]{:S(2)}, u32[]{:S(2)}) %collective-permute-start.13) | collective-permute-done | bytes 1048608 | tf_op jit(solution)/shard_map/ppermute | solution.py:35
  91.0 1.8 %widen.1.refs_3_.field_ref = f32[2,6,768,128]{3,2,1,0:T(8,128)S(1)} custom-call(f32[2,512,512]{2,1,0:T(8,128)S(1)} %copy-done, f32[2,512,256]{2,1,0:T(8,128)S(1)} %collective-permute-done.refs_4_.refs_1_, f32[2,256,256]{2,1,0:T(8,128)S(1)} %collective-permute-done.1.refs_5_.refs_2_, f32[2,256,256]{2,1,0:T(8,128)S(1)} %collective-permute-done.4.refs_6_.refs_3_, ...), custom_call_target="tpu_custom_call" | custom-call | flops 4000000 | bytes 20971520 | tf_op jit(solution)/shard_map/widen/pallas_call | solution.py:483
  92.7 4.7 %scan.3 = (f32[3,128,256]{2,1,0:T(8,128)S(1)}, f32[3,128,256]{2,1,0:T(8,128)S(1)}, f32[2,2,256,256]{3,2,1,0:T(8,128)S(1)}) custom-call(s32[1,1,2,2,2]{4,3,2,1,0:T(2,128)S(1)} %copy-done.2, f32[2,256,256]{2,1,0:T(8,128)S(1)} %join.5.refs_0_.probe_ref, bf16[2,2,256,256]{3,2,1,0:T(8,128)(2,1)S(1)} %reorder.1.refs_1_, bf16[8,256,256]{2,1,0:T(8,128)(2,1)S(1)} %copy-done.4, ...), custom_call_target="tpu_custom_call" | custom-call | flops 7000000000 | bytes 12582912 | tf_op jit(solution)/shard_map/scan/pallas_call | solution.py:294
  97.4 9.2 %collective-permute-start.23 = (f32[3,128,256]{2,1,0:T(8,128)S(1)}, f32[3,128,256]{2,1,0:T(8,128)S(1)}, u32[]{:S(2)}, u32[]{:S(2)}) collective-permute-start(f32[3,128,256]{2,1,0:T(8,128)S(1)} %get-tuple-element.87), channel_id=1, source_target_pairs={{0,1},{1,0},{2,3},{3,2},{4,5},{5,4},{6,7},{7,6},{8,9},{9,8},{10,11... | collective-permute-start | bytes 1179656 | tf_op jit(solution)/shard_map/ppermute | solution.py:30
  108.3 1.7 %density.3.density_ref = f32[4,512,128]{2,1,0:T(8,128)S(1)} custom-call(s32[3,3,2,2,2]{4,3,2,1,0:T(2,128)S(1)} %constant_dynamic-update-slice_fusion.offsets_ref, f32[2,256,256]{2,1,0:T(8,128)S(1)} %join.5.refs_0_.probe_ref), custom_call_target="tpu_custom_call" | custom-call | flops 1000000 | bytes 6291456 | tf_op jit(solution)/shard_map/density/pallas_call | solution.py:371
  111.4 3.9 %collective-permute-done.24 = f32[3,64,256]{2,1,0:T(8,128)S(1)} collective-permute-done((f32[3,64,256]{2,1,0:T(8,128)S(1)}, f32[3,64,256]{2,1,0:T(8,128)S(1)}, u32[]{:S(2)}, u32[]{:S(2)}) %collective-permute-start.24) | collective-permute-done | bytes 196640 | tf_op jit(solution)/shard_map/ppermute | solution.py:30
  115.3 19.1 %collective-permute-done.25.windows_ref = f32[2,2,256,256]{3,2,1,0:T(8,128)S(1)} collective-permute-done((f32[2,2,256,256]{3,2,1,0:T(8,128)S(1)}, f32[2,2,256,256]{3,2,1,0:T(8,128)S(1)}, u32[]{:S(2)}, u32[]{:S(2)}) %collective-permute-start.25) | collective-permute-done | bytes 1048608 | tf_op jit(solution)/shard_map/ppermute | solution.py:25
  135.6 4.8 %collective-permute-done.27 = f32[3,64,256]{2,1,0:T(8,128)S(1)} collective-permute-done((f32[3,64,256]{2,1,0:T(8,128)S(1)}, f32[3,64,256]{2,1,0:T(8,128)S(1)}, u32[]{:S(2)}, u32[]{:S(2)}) %collective-permute-start.27) | collective-permute-done | bytes 196640 | tf_op jit(solution)/shard_map/ppermute | solution.py:30
  140.6 5.7 %collective-permute-done.28 = f32[3,64,256]{2,1,0:T(8,128)S(1)} collective-permute-done((f32[3,64,256]{2,1,0:T(8,128)S(1)}, f32[3,64,256]{2,1,0:T(8,128)S(1)}, u32[]{:S(2)}, u32[]{:S(2)}) %collective-permute-start.28) | collective-permute-done | bytes 196640 | tf_op jit(solution)/shard_map/ppermute | solution.py:30
  146.3 8.8 %collective-permute-done.29 = f32[3,64,256]{2,1,0:T(8,128)S(1)} collective-permute-done((f32[3,64,256]{2,1,0:T(8,128)S(1)}, f32[3,64,256]{2,1,0:T(8,128)S(1)}, u32[]{:S(2)}, u32[]{:S(2)}) %collective-permute-start.29) | collective-permute-done | bytes 196640 | tf_op jit(solution)/shard_map/ppermute | solution.py:30
  155.2 1.6 %collective-permute-start.31 = (f32[2,64,256]{2,1,0:T(8,128)S(1)}, f32[2,64,256]{2,1,0:T(8,128)S(1)}, u32[]{:S(2)}, u32[]{:S(2)}) collective-permute-start(f32[2,64,256]{2,1,0:T(8,128)S(1)} %illuminate.3.value_ref), channel_id=1, source_target_pairs={{0,2},{1,3},{2,0},{3,1},{4,6},{5,7},{6,4},{7,5},{8,10},{9,11},{10,... | collective-permute-start | bytes 393224 | tf_op jit(solution)/shard_map/ppermute | solution.py:30
  156.8 1.8 %renew.1 = f32[2,512,512]{2,1,0:T(8,128)} custom-call(f32[2,6,768,128]{3,2,1,0:T(8,128)S(1)} %widen.1.refs_3_.field_ref, f32[4,512,128]{2,1,0:T(8,128)S(1)} %density.3.density_ref, f32[2,6,768,128]{3,2,1,0:T(8,128)S(1)} %get-tuple-element.96.total_ref, f32[2,6,256,128]{3,2,1,0:T(8,128)S(1)} %get-tuple-element.101.top_ref, ...), custom_call_target="tpu_custom_call" | custom-call | flops 4000000 | bytes 10485760 | tf_op jit(solution)/shard_map/renew/pallas_call | solution.py:511
  158.6 1.6 collective-permute-done.31.other_ref
  160.3 1.5 collective-permute-done.32.other_ref
  (79 shorter events, 21.5 us)
Async XLA Ops:
  1.9 18.4 %collective-permute-start.1 = (f32[2,256,256]{2,1,0:T(8,128)S(1)}, f32[2,256,256]{2,1,0:T(8,128)S(1)}, u32[]{:S(2)}, u32[]{:S(2)}) collective-permute-start(f32[2,256,256]{2,1,0:T(8,128)S(1)} %slice.10), channel_id=1, source_target_pairs={{0,28},{4,0},{8,4},{12,8},{16,12},{20,16},{24,20},{28,24},{1,29},{... | collective-permute-start | bytes 1572872 | tf_op jit(solution)/shard_map/ppermute | solution.py:25
  9.3 21.2 %collective-permute-start = (f32[2,512,256]{2,1,0:T(8,128)S(1)}, f32[2,512,256]{2,1,0:T(8,128)S(1)}, u32[]{:S(2)}, u32[]{:S(2)}) collective-permute-start(f32[2,512,256]{2,1,0:T(8,128)S(1)} %slice.9), channel_id=1, source_target_pairs={{0,3},{1,0},{2,1},{3,2},{4,7},{5,4},{6,5},{7,6},{8,11},{9,8},{10,9... | collective-permute-start | bytes 3145736 | tf_op jit(solution)/shard_map/ppermute | solution.py:25
  10.0 10.4 %collective-permute-start.3 = (s32[1,1,2,2,2]{4,3,2,1,0:T(2,128)S(1)}, s32[1,1,2,2,2]{4,3,2,1,0:T(2,128)S(1)}, u32[]{:S(2)}, u32[]{:S(2)}) collective-permute-start(s32[1,1,2,2,2]{4,3,2,1,0:T(2,128)S(1)} %copy-done.2), channel_id=1, source_target_pairs={{0,28},{4,0},{8,4},{12,8},{16,12},{20,16},{24,20},{28,24},{1,29},{... | collective-permute-start | bytes 104 | tf_op jit(solution)/shard_map/ppermute | solution.py:25
  10.7 9.7 %collective-permute-start.2 = (s32[1,1,2,2,2]{4,3,2,1,0:T(2,128)S(1)}, s32[1,1,2,2,2]{4,3,2,1,0:T(2,128)S(1)}, u32[]{:S(2)}, u32[]{:S(2)}) collective-permute-start(s32[1,1,2,2,2]{4,3,2,1,0:T(2,128)S(1)} %copy-done.2), channel_id=1, source_target_pairs={{0,4},{4,8},{8,12},{12,16},{16,20},{20,24},{24,28},{28,0},{1,5},{5... | collective-permute-start | bytes 104 | tf_op jit(solution)/shard_map/ppermute | solution.py:25
  12.1 18.4 %collective-permute-start.4 = (f32[2,256,256]{2,1,0:T(8,128)S(1)}, f32[2,256,256]{2,1,0:T(8,128)S(1)}, u32[]{:S(2)}, u32[]{:S(2)}) collective-permute-start(f32[2,256,256]{2,1,0:T(8,128)S(1)} %slice.11), channel_id=1, source_target_pairs={{0,28},{4,0},{8,4},{12,8},{16,12},{20,16},{24,20},{28,24},{1,29},{... | collective-permute-start | bytes 1572872 | tf_op jit(solution)/shard_map/ppermute | solution.py:25
  20.4 10.1 %collective-permute-start.5 = (f32[2,256,256]{2,1,0:T(8,128)S(1)}, f32[2,256,256]{2,1,0:T(8,128)S(1)}, u32[]{:S(2)}, u32[]{:S(2)}) collective-permute-start(f32[2,256,256]{2,1,0:T(8,128)S(1)} %collective-permute-done.1.refs_5_.refs_2_), channel_id=1, source_target_pairs={{0,3},{1,0},{2,1},{3,2},{4,7},{5,4},{6,5},{7,6},{8,11},{9,8},{10,9... | collective-permute-start | bytes 1572872 | tf_op jit(solution)/shard_map/ppermute | solution.py:25
  35.6 26.5 %collective-permute-start.12 = (f32[2,2,256,256]{3,2,1,0:T(8,128)S(1)}, f32[2,2,256,256]{3,2,1,0:T(8,128)S(1)}, u32[]{:S(2)}, u32[]{:S(2)}) collective-permute-start(f32[2,2,256,256]{3,2,1,0:T(8,128)S(1)} %get-tuple-element.63.windows_ref), channel_id=1, source_target_pairs={{0,4},{4,0},{8,12},{12,8},{16,20},{20,16},{24,28},{28,24},{1,5},{5... | collective-permute-start | bytes 3145736 | tf_op jit(solution)/shard_map/ppermute | solution.py:30
  36.1 3.1 %collective-permute-start.6 = (f32[3,128,256]{2,1,0:T(8,128)S(1)}, f32[3,128,256]{2,1,0:T(8,128)S(1)}, u32[]{:S(2)}, u32[]{:S(2)}) collective-permute-start(f32[3,128,256]{2,1,0:T(8,128)S(1)} %get-tuple-element.58), channel_id=1, source_target_pairs={{0,1},{1,0},{2,3},{3,2},{4,5},{5,4},{6,7},{7,6},{8,9},{9,8},{10,11... | collective-permute-start | bytes 1179656 | tf_op jit(solution)/shard_map/ppermute | solution.py:30
  36.1 3.1 %collective-permute-start.8 = (s32[3,1,2,2,2]{4,3,2,1,0:T(2,128)S(1)}, s32[3,1,2,2,2]{4,3,2,1,0:T(2,128)S(1)}, u32[]{:S(2)}, u32[]{:S(2)}) collective-permute-start(s32[3,1,2,2,2]{4,3,2,1,0:T(2,128)S(1)} %pad_add_fusion.offsets_ref), channel_id=1, source_target_pairs={{0,1},{1,2},{2,3},{3,0},{4,5},{5,6},{6,7},{7,4},{8,9},{9,10},{10,1... | collective-permute-start | bytes 296 | tf_op jit(solution)/shard_map/ppermute | solution.py:25
  36.6 4.2 %collective-permute-start.9 = (s32[3,1,2,2,2]{4,3,2,1,0:T(2,128)S(1)}, s32[3,1,2,2,2]{4,3,2,1,0:T(2,128)S(1)}, u32[]{:S(2)}, u32[]{:S(2)}) collective-permute-start(s32[3,1,2,2,2]{4,3,2,1,0:T(2,128)S(1)} %pad_add_fusion.offsets_ref), channel_id=1, source_target_pairs={{0,3},{1,0},{2,1},{3,2},{4,7},{5,4},{6,5},{7,6},{8,11},{9,8},{10,9... | collective-permute-start | bytes 296 | tf_op jit(solution)/shard_map/ppermute | solution.py:25
  39.2 6.2 %collective-permute-start.7 = (f32[3,64,256]{2,1,0:T(8,128)S(1)}, f32[3,64,256]{2,1,0:T(8,128)S(1)}, u32[]{:S(2)}, u32[]{:S(2)}) collective-permute-start(f32[3,64,256]{2,1,0:T(8,128)S(1)} %get-tuple-element.60), channel_id=1, source_target_pairs={{0,2},{1,3},{2,0},{3,1},{4,6},{5,7},{6,4},{7,5},{8,10},{9,11},{10,... | collective-permute-start | bytes 589832 | tf_op jit(solution)/shard_map/ppermute | solution.py:30
  45.4 10.8 %collective-permute-start.10 = (f32[3,64,256]{2,1,0:T(8,128)S(1)}, f32[3,64,256]{2,1,0:T(8,128)S(1)}, u32[]{:S(2)}, u32[]{:S(2)}) collective-permute-start(f32[3,64,256]{2,1,0:T(8,128)S(1)} %add.24), channel_id=1, source_target_pairs={{0,16},{4,20},{8,24},{12,28},{16,0},{20,4},{24,8},{28,12},{1,17},{... | collective-permute-start | bytes 589832 | tf_op jit(solution)/shard_map/ppermute | solution.py:30
  56.3 5.7 %collective-permute-start.11 = (f32[3,64,256]{2,1,0:T(8,128)S(1)}, f32[3,64,256]{2,1,0:T(8,128)S(1)}, u32[]{:S(2)}, u32[]{:S(2)}) collective-permute-start(f32[3,64,256]{2,1,0:T(8,128)S(1)} %add.25), channel_id=1, source_target_pairs={{0,8},{4,12},{8,0},{12,4},{16,24},{20,28},{24,16},{28,20},{1,9},{5... | collective-permute-start | bytes 589832 | tf_op jit(solution)/shard_map/ppermute | solution.py:30
  62.1 25.5 %collective-permute-start.13 = (f32[2,2,256,256]{3,2,1,0:T(8,128)S(1)}, f32[2,2,256,256]{3,2,1,0:T(8,128)S(1)}, u32[]{:S(2)}, u32[]{:S(2)}) collective-permute-start(f32[2,2,256,256]{3,2,1,0:T(8,128)S(1)} %collective-permute-done.12.windows_ref), channel_id=1, source_target_pairs={{0,8},{4,28},{8,16},{12,4},{16,24},{20,12},{24,0},{28,20},{1,9},{5... | collective-permute-start | bytes 3145736 | tf_op jit(solution)/shard_map/ppermute | solution.py:35
  62.9 11.3 %collective-permute-start.16 = (f32[2,2,256,128]{3,2,1,0:T(8,128)S(1)}, f32[2,2,256,128]{3,2,1,0:T(8,128)S(1)}, u32[]{:S(2)}, u32[]{:S(2)}) collective-permute-start(f32[2,2,256,128]{3,2,1,0:T(8,128)S(1)} %get-tuple-element.69), channel_id=1, source_target_pairs={{1,2},{2,1},{5,6},{6,5},{9,10},{10,9},{13,14},{14,13},{17,18},{18,... | collective-permute-start | bytes 1572872 | tf_op jit(solution)/shard_map/ppermute | solution.py:41
  63.6 11.0 %collective-permute-start.17 = (f32[2,2,256,128]{3,2,1,0:T(8,128)S(1)}, f32[2,2,256,128]{3,2,1,0:T(8,128)S(1)}, u32[]{:S(2)}, u32[]{:S(2)}) collective-permute-start(f32[2,2,256,128]{3,2,1,0:T(8,128)S(1)} %get-tuple-element.70), channel_id=1, source_target_pairs={{0,1},{1,0},{2,3},{3,2},{4,5},{5,4},{6,7},{7,6},{8,9},{9,8},{10,11... | collective-permute-start | bytes 1572872 | tf_op jit(solution)/shard_map/ppermute | solution.py:30
  66.2 7.9 %collective-permute-start.14 = (f32[3,64,256]{2,1,0:T(8,128)S(1)}, f32[3,64,256]{2,1,0:T(8,128)S(1)}, u32[]{:S(2)}, u32[]{:S(2)}) collective-permute-start(f32[3,64,256]{2,1,0:T(8,128)S(1)} %add.26), channel_id=1, source_target_pairs={{0,4},{4,0},{8,12},{12,8},{16,20},{20,16},{24,28},{28,24},{1,5},{5... | collective-permute-start | bytes 589832 | tf_op jit(solution)/shard_map/ppermute | solution.py:30
  70.8 14.7 %collective-permute-start.19 = (f32[2,2,256,128]{3,2,1,0:T(8,128)S(1)}, f32[2,2,256,128]{3,2,1,0:T(8,128)S(1)}, u32[]{:S(2)}, u32[]{:S(2)}) collective-permute-start(f32[2,2,256,128]{3,2,1,0:T(8,128)S(1)} %get-tuple-element.73), channel_id=1, source_target_pairs={{1,2},{2,1},{5,6},{6,5},{9,10},{10,9},{13,14},{14,13},{17,18},{18,... | collective-permute-start | bytes 1572872 | tf_op jit(solution)/shard_map/ppermute | solution.py:41
  74.2 11.3 %collective-permute-start.20 = (f32[2,2,256,128]{3,2,1,0:T(8,128)S(1)}, f32[2,2,256,128]{3,2,1,0:T(8,128)S(1)}, u32[]{:S(2)}, u32[]{:S(2)}) collective-permute-start(f32[2,2,256,128]{3,2,1,0:T(8,128)S(1)} %get-tuple-element.74), channel_id=1, source_target_pairs={{0,1},{1,0},{2,3},{3,2},{4,5},{5,4},{6,7},{7,6},{8,9},{9,8},{10,11... | collective-permute-start | bytes 1572872 | tf_op jit(solution)/shard_map/ppermute | solution.py:30
  74.2 9.5 %collective-permute-start.15 = (f32[2,64,256]{2,1,0:T(8,128)S(1)}, f32[2,64,256]{2,1,0:T(8,128)S(1)}, u32[]{:S(2)}, u32[]{:S(2)}) collective-permute-start(f32[2,64,256]{2,1,0:T(8,128)S(1)} %illuminate.2.value_ref), channel_id=1, source_target_pairs={{0,2},{1,3},{2,0},{3,1},{4,6},{5,7},{6,4},{7,5},{8,10},{9,11},{10,... | collective-permute-start | bytes 393224 | tf_op jit(solution)/shard_map/ppermute | solution.py:30
  89.0 2.0 %collective-permute-start.21 = (f32[2,2,256,128]{3,2,1,0:T(8,128)S(1)}, f32[2,2,256,128]{3,2,1,0:T(8,128)S(1)}, u32[]{:S(2)}, u32[]{:S(2)}) collective-permute-start(f32[2,2,256,128]{3,2,1,0:T(8,128)S(1)} %get-tuple-element.82), channel_id=1, source_target_pairs={{0,1},{1,0},{2,3},{3,2},{4,5},{5,4},{6,7},{7,6},{8,9},{9,8},{10,11... | collective-permute-start | bytes 1572872 | tf_op jit(solution)/shard_map/ppermute | solution.py:30
  89.1 1.9 %collective-permute-start.22 = (f32[2,2,256,128]{3,2,1,0:T(8,128)S(1)}, f32[2,2,256,128]{3,2,1,0:T(8,128)S(1)}, u32[]{:S(2)}, u32[]{:S(2)}) collective-permute-start(f32[2,2,256,128]{3,2,1,0:T(8,128)S(1)} %get-tuple-element.85), channel_id=1, source_target_pairs={{1,2},{2,1},{5,6},{6,5},{9,10},{10,9},{13,14},{14,13},{17,18},{18,... | collective-permute-start | bytes 1572872 | tf_op jit(solution)/shard_map/ppermute | solution.py:41
  97.4 10.5 %collective-permute-start.23 = (f32[3,128,256]{2,1,0:T(8,128)S(1)}, f32[3,128,256]{2,1,0:T(8,128)S(1)}, u32[]{:S(2)}, u32[]{:S(2)}) collective-permute-start(f32[3,128,256]{2,1,0:T(8,128)S(1)} %get-tuple-element.87), channel_id=1, source_target_pairs={{0,1},{1,0},{2,3},{3,2},{4,5},{5,4},{6,7},{7,6},{8,9},{9,8},{10,11... | collective-permute-start | bytes 1179656 | tf_op jit(solution)/shard_map/ppermute | solution.py:30
  106.6 27.8 %collective-permute-start.25 = (f32[2,2,256,256]{3,2,1,0:T(8,128)S(1)}, f32[2,2,256,256]{3,2,1,0:T(8,128)S(1)}, u32[]{:S(2)}, u32[]{:S(2)}) collective-permute-start(f32[2,2,256,256]{3,2,1,0:T(8,128)S(1)} %get-tuple-element.90.windows_ref), channel_id=1, source_target_pairs={{0,4},{4,8},{8,12},{12,16},{16,20},{20,24},{24,28},{28,0},{1,5},{5... | collective-permute-start | bytes 3145736 | tf_op jit(solution)/shard_map/ppermute | solution.py:25
  108.0 7.2 %collective-permute-start.24 = (f32[3,64,256]{2,1,0:T(8,128)S(1)}, f32[3,64,256]{2,1,0:T(8,128)S(1)}, u32[]{:S(2)}, u32[]{:S(2)}) collective-permute-start(f32[3,64,256]{2,1,0:T(8,128)S(1)} %get-tuple-element.89), channel_id=1, source_target_pairs={{0,2},{1,3},{2,0},{3,1},{4,6},{5,7},{6,4},{7,5},{8,10},{9,11},{10,... | collective-permute-start | bytes 589832 | tf_op jit(solution)/shard_map/ppermute | solution.py:30
  115.3 19.2 %collective-permute-start.26 = (f32[2,2,256,128]{3,2,1,0:T(8,128)S(1)}, f32[2,2,256,128]{3,2,1,0:T(8,128)S(1)}, u32[]{:S(2)}, u32[]{:S(2)}) collective-permute-start(f32[2,2,256,128]{3,2,1,0:T(8,128)S(1)} %get-tuple-element.94), channel_id=1, source_target_pairs={{0,1},{1,2},{2,3},{3,0},{4,5},{5,6},{6,7},{7,4},{8,9},{9,10},{10,1... | collective-permute-start | bytes 1572872 | tf_op jit(solution)/shard_map/ppermute | solution.py:25
  134.4 6.0 %collective-permute-start.27 = (f32[3,64,256]{2,1,0:T(8,128)S(1)}, f32[3,64,256]{2,1,0:T(8,128)S(1)}, u32[]{:S(2)}, u32[]{:S(2)}) collective-permute-start(f32[3,64,256]{2,1,0:T(8,128)S(1)} %add.28), channel_id=1, source_target_pairs={{0,4},{4,0},{8,12},{12,8},{16,20},{20,16},{24,28},{28,24},{1,5},{5... | collective-permute-start | bytes 589832 | tf_op jit(solution)/shard_map/ppermute | solution.py:30
  135.6 19.6 %collective-permute-start.30 = (f32[2,2,256,128]{3,2,1,0:T(8,128)S(1)}, f32[2,2,256,128]{3,2,1,0:T(8,128)S(1)}, u32[]{:S(2)}, u32[]{:S(2)}) collective-permute-start(f32[2,2,256,128]{3,2,1,0:T(8,128)S(1)} %get-tuple-element.98), channel_id=1, source_target_pairs={{0,1},{1,2},{2,3},{3,0},{4,5},{5,6},{6,7},{7,4},{8,9},{9,10},{10,1... | collective-permute-start | bytes 1572872 | tf_op jit(solution)/shard_map/ppermute | solution.py:25
  140.5 5.7 %collective-permute-start.28 = (f32[3,64,256]{2,1,0:T(8,128)S(1)}, f32[3,64,256]{2,1,0:T(8,128)S(1)}, u32[]{:S(2)}, u32[]{:S(2)}) collective-permute-start(f32[3,64,256]{2,1,0:T(8,128)S(1)} %add.29), channel_id=1, source_target_pairs={{0,8},{4,12},{8,0},{12,4},{16,24},{20,28},{24,16},{28,20},{1,9},{5... | collective-permute-start | bytes 589832 | tf_op jit(solution)/shard_map/ppermute | solution.py:30
  146.2 8.9 %collective-permute-start.29 = (f32[3,64,256]{2,1,0:T(8,128)S(1)}, f32[3,64,256]{2,1,0:T(8,128)S(1)}, u32[]{:S(2)}, u32[]{:S(2)}) collective-permute-start(f32[3,64,256]{2,1,0:T(8,128)S(1)} %add.30), channel_id=1, source_target_pairs={{0,16},{4,20},{8,24},{12,28},{16,0},{20,4},{24,8},{28,12},{1,17},{... | collective-permute-start | bytes 589832 | tf_op jit(solution)/shard_map/ppermute | solution.py:30
  155.2 5.0 %collective-permute-start.31 = (f32[2,64,256]{2,1,0:T(8,128)S(1)}, f32[2,64,256]{2,1,0:T(8,128)S(1)}, u32[]{:S(2)}, u32[]{:S(2)}) collective-permute-start(f32[2,64,256]{2,1,0:T(8,128)S(1)} %illuminate.3.value_ref), channel_id=1, source_target_pairs={{0,2},{1,3},{2,0},{3,1},{4,6},{5,7},{6,4},{7,5},{8,10},{9,11},{10,... | collective-permute-start | bytes 393224 | tf_op jit(solution)/shard_map/ppermute | solution.py:30
  160.2 1.6 collective-permute-start.32
  (6 other events, 99.2 us)

commit v8 on v7

--- a/solution.py
+++ b/solution.py
@@ -32,7 +32,8 @@
 
 def handed_on(array, axis):
     peers = lax.axis_size(axis)
-    return lax.ppermute(array, axis, [(i, (i + 2 - 4 * (i % 2)) % peers) for i in range(peers)])
+    pairs = [(i, i + 2 - 4 * (i % 2)) for i in range(peers)]
+    return lax.ppermute(array, axis, [(i, k) for i, k in pairs if 0 <= k < peers])
 
 
 def swapped_outward(array, axis):

time: 163 us -> 162 us (level)
  waiting for transfers between devices: 93.3 us -> 87 us
  starting transfers between devices: 39.3 us -> 44.4 us
    ppermute x18, waiting for transfers between devices: 56.3 us -> 51.2 us  [swapped(): return lax.ppermute(array, axis, [(i, i ^ mask) for i in range(peers)])]
    ppermute x11, starting transfers between devices: 14.1 us -> 16.2 us  [shifted(): lax.ppermute(array, axis, [(i, (i + by) % peers) for i in range(peers)])]
    ppermute x1, starting transfers between devices: 0.86 us -> 2.77 us  [handed_on(): lax.ppermute(array, axis, [(i, k) for i, k in pairs if 0 <= k < peers])]
  transfers between devices with their start and end apart: 33 -> 33, of which waited for: 19 -> 18; matrix products, arithmetic and copies ran while one was open for 1% -> 1% of each run, Pallas kernels for 8% -> 8%
where the time goes in v8:
time: 162 us; the launch traced here: 161 us
  waiting for transfers between devices  87 us (54%)
  starting transfers between devices  44.4 us (27%)
  Pallas kernels  26.2 us (16%)
  local copies, waits for them, and re-layouts  2.61 us (2%)
    ppermute x18, waiting for transfers between devices, swapped(): return lax.ppermute(array, axis, [(i, i ^ mask) for i in range(peers)])  51.2 us
    ppermute x11, waiting for transfers between devices, shifted(): lax.ppermute(array, axis, [(i, (i + by) % peers) for i in range(peers)])  34.6 us
    ppermute x18, starting transfers between devices, swapped(): return lax.ppermute(array, axis, [(i, i ^ mask) for i in range(peers)])  23.2 us
    ppermute x11, starting transfers between devices, shifted(): lax.ppermute(array, axis, [(i, (i + by) % peers) for i in range(peers)])  16.2 us
    pallas_call x2, Pallas kernels, scan_step(): pl.pallas_call(functools.partial(scan_kernel, sweep, last, counts), out_s...  9.8 us
    pallas_call x2, Pallas kernels, density(): pl.pallas_call(functools.partial(density_kernel, sweep, reach), out_shape...  4.45 us
    pallas_call x3, Pallas kernels, gather(): pl.pallas_call(functools.partial(gather_kernel, sweep, below_of), out_sha...  4.07 us
  transfers between devices with their start and end apart: 33, of which 18 were waited for; matrix products, arithmetic and copies ran while one was open for 1% of the time, Pallas kernels for 8%

profile of v8, /device:TPU:0, one launch (start us, length us, event | category | flops | bytes accessed | tf_op | source)
XLA Modules:
  0.0 161.4 jit_solution(1926082458426978703)
XLA Ops:
  1.9 6.1 %collective-permute-start.1 = (f32[2,256,256]{2,1,0:T(8,128)S(1)}, f32[2,256,256]{2,1,0:T(8,128)S(1)}, u32[]{:S(2)}, u32[]{:S(2)}) collective-permute-start(f32[2,256,256]{2,1,0:T(8,128)S(1)} %slice.10), channel_id=1, source_target_pairs={{0,28},{4,0},{8,4},{12,8},{16,12},{20,16},{24,20},{28,24},{1,29},{... | collective-permute-start | bytes 1572872 | tf_op jit(solution)/shard_map/ppermute | solution.py:25
  12.1 3.4 %collective-permute-start.4 = (f32[2,256,256]{2,1,0:T(8,128)S(1)}, f32[2,256,256]{2,1,0:T(8,128)S(1)}, u32[]{:S(2)}, u32[]{:S(2)}) collective-permute-start(f32[2,256,256]{2,1,0:T(8,128)S(1)} %slice.11), channel_id=1, source_target_pairs={{0,28},{4,0},{8,4},{12,8},{16,12},{20,16},{24,20},{28,24},{1,29},{... | collective-permute-start | bytes 1572872 | tf_op jit(solution)/shard_map/ppermute | solution.py:25
  15.5 4.9 %collective-permute-done.3 = s32[1,1,2,2,2]{4,3,2,1,0:T(2,128)S(1)} collective-permute-done((s32[1,1,2,2,2]{4,3,2,1,0:T(2,128)S(1)}, s32[1,1,2,2,2]{4,3,2,1,0:T(2,128)S(1)}, u32[]{:S(2)}, u32[]{:S(2)}) %collective-permute-start.3) | collective-permute-done | bytes 64 | tf_op jit(solution)/shard_map/ppermute | solution.py:25
  21.0 9.4 %collective-permute-done.4.refs_6_.refs_3_ = f32[2,256,256]{2,1,0:T(8,128)S(1)} collective-permute-done((f32[2,256,256]{2,1,0:T(8,128)S(1)}, f32[2,256,256]{2,1,0:T(8,128)S(1)}, u32[]{:S(2)}, u32[]{:S(2)}) %collective-permute-start.4) | collective-permute-done | bytes 524320 | tf_op jit(solution)/shard_map/ppermute | solution.py:25
  30.5 5.1 %scan.2 = (f32[3,128,256]{2,1,0:T(8,128)S(1)}, f32[3,128,256]{2,1,0:T(8,128)S(1)}, f32[2,2,256,256]{3,2,1,0:T(8,128)S(1)}) custom-call(s32[1,1,2,2,2]{4,3,2,1,0:T(2,128)S(1)} %copy-done.2, f32[2,256,256]{2,1,0:T(8,128)S(1)} %copy-done.1, bf16[2,2,256,256]{3,2,1,0:T(8,128)(2,1)S(1)} %reorder.1.refs_1_, bf16[8,256,256]{2,1,0:T(8,128)(2,1)S(1)} %copy-done.4, ...), custom_call_target="tpu_custom_call" | custom-call | flops 7000000000 | bytes 12582912 | tf_op jit(solution)/shard_map/scan/pallas_call | solution.py:295
  39.2 1.6 collective-permute-start.7
  40.8 4.6 %collective-permute-done.7 = f32[3,64,256]{2,1,0:T(8,128)S(1)} collective-permute-done((f32[3,64,256]{2,1,0:T(8,128)S(1)}, f32[3,64,256]{2,1,0:T(8,128)S(1)}, u32[]{:S(2)}, u32[]{:S(2)}) %collective-permute-start.7) | collective-permute-done | bytes 196640 | tf_op jit(solution)/shard_map/ppermute | solution.py:30
  45.5 2.6 %collective-permute-start.10 = (f32[3,64,256]{2,1,0:T(8,128)S(1)}, f32[3,64,256]{2,1,0:T(8,128)S(1)}, u32[]{:S(2)}, u32[]{:S(2)}) collective-permute-start(f32[3,64,256]{2,1,0:T(8,128)S(1)} %add.24), channel_id=1, source_target_pairs={{0,16},{4,20},{8,24},{12,28},{16,0},{20,4},{24,8},{28,12},{1,17},{... | collective-permute-start | bytes 589832 | tf_op jit(solution)/shard_map/ppermute | solution.py:30
  48.1 2.7 %density.2.refs_5_ = f32[6,768,128]{2,1,0:T(8,128)S(1)} custom-call(s32[3,3,2,2,2]{4,3,2,1,0:T(2,128)S(1)} %constant_dynamic-update-slice_fusion.offsets_ref, f32[2,256,256]{2,1,0:T(8,128)S(1)} %copy-done.1), custom_call_target="tpu_custom_call" | custom-call | flops 1000000 | bytes 6291456 | tf_op jit(solution)/shard_map/density/pallas_call | solution.py:372
  52.1 4.2 %collective-permute-done.10 = f32[3,64,256]{2,1,0:T(8,128)S(1)} collective-permute-done((f32[3,64,256]{2,1,0:T(8,128)S(1)}, f32[3,64,256]{2,1,0:T(8,128)S(1)}, u32[]{:S(2)}, u32[]{:S(2)}) %collective-permute-start.10) | collective-permute-done | bytes 196640 | tf_op jit(solution)/shard_map/ppermute | solution.py:30
  56.6 5.5 %collective-permute-done.11 = f32[3,64,256]{2,1,0:T(8,128)S(1)} collective-permute-done((f32[3,64,256]{2,1,0:T(8,128)S(1)}, f32[3,64,256]{2,1,0:T(8,128)S(1)}, u32[]{:S(2)}, u32[]{:S(2)}) %collective-permute-start.11) | collective-permute-done | bytes 196640 | tf_op jit(solution)/shard_map/ppermute | solution.py:30
  62.1 2.8 %collective-permute-start.13 = (f32[2,2,256,256]{3,2,1,0:T(8,128)S(1)}, f32[2,2,256,256]{3,2,1,0:T(8,128)S(1)}, u32[]{:S(2)}, u32[]{:S(2)}) collective-permute-start(f32[2,2,256,256]{3,2,1,0:T(8,128)S(1)} %collective-permute-done.12.windows_ref), channel_id=1, source_target_pairs={{0,8},{8,16},{12,4},{16,24},{20,12},{28,20},{1,9},{9,17},{13,5},{1... | collective-permute-start | bytes 3145736 | tf_op jit(solution)/shard_map/ppermute | solution.py:36
  65.6 2.0 %collective-permute-start.17 = (f32[2,2,256,128]{3,2,1,0:T(8,128)S(1)}, f32[2,2,256,128]{3,2,1,0:T(8,128)S(1)}, u32[]{:S(2)}, u32[]{:S(2)}) collective-permute-start(f32[2,2,256,128]{3,2,1,0:T(8,128)S(1)} %get-tuple-element.70), channel_id=1, source_target_pairs={{0,1},{1,0},{2,3},{3,2},{4,5},{5,4},{6,7},{7,6},{8,9},{9,8},{10,11... | collective-permute-start | bytes 1572872 | tf_op jit(solution)/shard_map/ppermute | solution.py:30
  67.6 1.8 %gather.3 = (f32[2,6,256,128]{3,2,1,0:T(8,128)S(1)}, f32[2,2,256,128]{3,2,1,0:T(8,128)S(1)}, f32[2,2,256,128]{3,2,1,0:T(8,128)S(1)}) custom-call(s32[3,1,2,2,2]{4,3,2,1,0:T(2,128)S(1)} %pad_add_fusion.offsets_ref, f32[2,6,768,128]{3,2,1,0:T(8,128)S(1)} %get-tuple-element.72.total_ref.refs_6_, f32[2,2,256,256]{3,2,1,0:T(8,128)S(1)} %collective-permute-done.12.windows_ref), custom_call_target="tpu_custom_call" | custom-call | flops 1000000 | bytes 6291456 | tf_op jit(solution)/shard_map/gather/pallas_call | solution.py:424
  70.2 4.2 %collective-permute-done.14 = f32[3,64,256]{2,1,0:T(8,128)S(1)} collective-permute-done((f32[3,64,256]{2,1,0:T(8,128)S(1)}, f32[3,64,256]{2,1,0:T(8,128)S(1)}, u32[]{:S(2)}, u32[]{:S(2)}) %collective-permute-start.14) | collective-permute-done | bytes 196640 | tf_op jit(solution)/shard_map/ppermute | solution.py:30
  74.5 1.4 collective-permute-start.15
  76.0 7.0 %collective-permute-done.15.other_ref = f32[2,64,256]{2,1,0:T(8,128)S(1)} collective-permute-done((f32[2,64,256]{2,1,0:T(8,128)S(1)}, f32[2,64,256]{2,1,0:T(8,128)S(1)}, u32[]{:S(2)}, u32[]{:S(2)}) %collective-permute-start.15) | collective-permute-done | bytes 131104 | tf_op jit(solution)/shard_map/ppermute | solution.py:30
  83.1 1.5 collective-permute-done.18.other_ref
  89.1 1.8 %widen.1.refs_3_.field_ref = f32[2,6,768,128]{3,2,1,0:T(8,128)S(1)} custom-call(f32[2,512,512]{2,1,0:T(8,128)S(1)} %copy-done, f32[2,512,256]{2,1,0:T(8,128)S(1)} %collective-permute-done.refs_4_.refs_1_, f32[2,256,256]{2,1,0:T(8,128)S(1)} %collective-permute-done.1.refs_5_.refs_2_, f32[2,256,256]{2,1,0:T(8,128)S(1)} %collective-permute-done.4.refs_6_.refs_3_, ...), custom_call_target="tpu_custom_call" | custom-call | flops 4000000 | bytes 20971520 | tf_op jit(solution)/shard_map/widen/pallas_call | solution.py:484
  90.9 4.7 %scan.3 = (f32[3,128,256]{2,1,0:T(8,128)S(1)}, f32[3,128,256]{2,1,0:T(8,128)S(1)}, f32[2,2,256,256]{3,2,1,0:T(8,128)S(1)}) custom-call(s32[1,1,2,2,2]{4,3,2,1,0:T(2,128)S(1)} %copy-done.2, f32[2,256,256]{2,1,0:T(8,128)S(1)} %join.5.refs_0_.probe_ref, bf16[2,2,256,256]{3,2,1,0:T(8,128)(2,1)S(1)} %reorder.1.refs_1_, bf16[8,256,256]{2,1,0:T(8,128)(2,1)S(1)} %copy-done.4, ...), custom_call_target="tpu_custom_call" | custom-call | flops 7000000000 | bytes 12582912 | tf_op jit(solution)/shard_map/scan/pallas_call | solution.py:295
  95.6 9.2 %collective-permute-start.23 = (f32[3,128,256]{2,1,0:T(8,128)S(1)}, f32[3,128,256]{2,1,0:T(8,128)S(1)}, u32[]{:S(2)}, u32[]{:S(2)}) collective-permute-start(f32[3,128,256]{2,1,0:T(8,128)S(1)} %get-tuple-element.87), channel_id=1, source_target_pairs={{0,1},{1,0},{2,3},{3,2},{4,5},{5,4},{6,7},{7,6},{8,9},{9,8},{10,11... | collective-permute-start | bytes 1179656 | tf_op jit(solution)/shard_map/ppermute | solution.py:30
  104.7 2.1 %collective-permute-start.25 = (f32[2,2,256,256]{3,2,1,0:T(8,128)S(1)}, f32[2,2,256,256]{3,2,1,0:T(8,128)S(1)}, u32[]{:S(2)}, u32[]{:S(2)}) collective-permute-start(f32[2,2,256,256]{3,2,1,0:T(8,128)S(1)} %get-tuple-element.90.windows_ref), channel_id=1, source_target_pairs={{0,4},{4,8},{8,12},{12,16},{16,20},{20,24},{24,28},{28,0},{1,5},{5... | collective-permute-start | bytes 3145736 | tf_op jit(solution)/shard_map/ppermute | solution.py:25
  107.5 1.7 %density.3.density_ref = f32[4,512,128]{2,1,0:T(8,128)S(1)} custom-call(s32[3,3,2,2,2]{4,3,2,1,0:T(2,128)S(1)} %constant_dynamic-update-slice_fusion.offsets_ref, f32[2,256,256]{2,1,0:T(8,128)S(1)} %join.5.refs_0_.probe_ref), custom_call_target="tpu_custom_call" | custom-call | flops 1000000 | bytes 6291456 | tf_op jit(solution)/shard_map/density/pallas_call | solution.py:372
  110.5 3.1 %collective-permute-done.24 = f32[3,64,256]{2,1,0:T(8,128)S(1)} collective-permute-done((f32[3,64,256]{2,1,0:T(8,128)S(1)}, f32[3,64,256]{2,1,0:T(8,128)S(1)}, u32[]{:S(2)}, u32[]{:S(2)}) %collective-permute-start.24) | collective-permute-done | bytes 196640 | tf_op jit(solution)/shard_map/ppermute | solution.py:30
  113.6 18.9 %collective-permute-done.25.windows_ref = f32[2,2,256,256]{3,2,1,0:T(8,128)S(1)} collective-permute-done((f32[2,2,256,256]{3,2,1,0:T(8,128)S(1)}, f32[2,2,256,256]{3,2,1,0:T(8,128)S(1)}, u32[]{:S(2)}, u32[]{:S(2)}) %collective-permute-start.25) | collective-permute-done | bytes 1048608 | tf_op jit(solution)/shard_map/ppermute | solution.py:25
  133.8 4.8 %collective-permute-done.27 = f32[3,64,256]{2,1,0:T(8,128)S(1)} collective-permute-done((f32[3,64,256]{2,1,0:T(8,128)S(1)}, f32[3,64,256]{2,1,0:T(8,128)S(1)}, u32[]{:S(2)}, u32[]{:S(2)}) %collective-permute-start.27) | collective-permute-done | bytes 196640 | tf_op jit(solution)/shard_map/ppermute | solution.py:30
  139.4 5.0 %collective-permute-done.28 = f32[3,64,256]{2,1,0:T(8,128)S(1)} collective-permute-done((f32[3,64,256]{2,1,0:T(8,128)S(1)}, f32[3,64,256]{2,1,0:T(8,128)S(1)}, u32[]{:S(2)}, u32[]{:S(2)}) %collective-permute-start.28) | collective-permute-done | bytes 196640 | tf_op jit(solution)/shard_map/ppermute | solution.py:30
  144.4 2.8 %collective-permute-start.29 = (f32[3,64,256]{2,1,0:T(8,128)S(1)}, f32[3,64,256]{2,1,0:T(8,128)S(1)}, u32[]{:S(2)}, u32[]{:S(2)}) collective-permute-start(f32[3,64,256]{2,1,0:T(8,128)S(1)} %add.30), channel_id=1, source_target_pairs={{0,16},{4,20},{8,24},{12,28},{16,0},{20,4},{24,8},{28,12},{1,17},{... | collective-permute-start | bytes 589832 | tf_op jit(solution)/shard_map/ppermute | solution.py:30
  147.2 6.6 %collective-permute-done.29 = f32[3,64,256]{2,1,0:T(8,128)S(1)} collective-permute-done((f32[3,64,256]{2,1,0:T(8,128)S(1)}, f32[3,64,256]{2,1,0:T(8,128)S(1)}, u32[]{:S(2)}, u32[]{:S(2)}) %collective-permute-start.29) | collective-permute-done | bytes 196640 | tf_op jit(solution)/shard_map/ppermute | solution.py:30
  155.2 1.8 %renew.1 = f32[2,512,512]{2,1,0:T(8,128)} custom-call(f32[2,6,768,128]{3,2,1,0:T(8,128)S(1)} %widen.1.refs_3_.field_ref, f32[4,512,128]{2,1,0:T(8,128)S(1)} %density.3.density_ref, f32[2,6,768,128]{3,2,1,0:T(8,128)S(1)} %get-tuple-element.96.total_ref, f32[2,6,256,128]{3,2,1,0:T(8,128)S(1)} %get-tuple-element.101.top_ref, ...), custom_call_target="tpu_custom_call" | custom-call | flops 4000000 | bytes 10485760 | tf_op jit(solution)/shard_map/renew/pallas_call | solution.py:512
  157.0 1.9 %collective-permute-done.31.other_ref = f32[2,64,256]{2,1,0:T(8,128)S(1)} collective-permute-done((f32[2,64,256]{2,1,0:T(8,128)S(1)}, f32[2,64,256]{2,1,0:T(8,128)S(1)}, u32[]{:S(2)}, u32[]{:S(2)}) %collective-permute-start.31) | collective-permute-done | bytes 131104 | tf_op jit(solution)/shard_map/ppermute | solution.py:30
  159.0 1.5 collective-permute-done.32.other_ref
  (79 shorter events, 23.6 us)
Async XLA Ops:
  1.9 18.4 %collective-permute-start.1 = (f32[2,256,256]{2,1,0:T(8,128)S(1)}, f32[2,256,256]{2,1,0:T(8,128)S(1)}, u32[]{:S(2)}, u32[]{:S(2)}) collective-permute-start(f32[2,256,256]{2,1,0:T(8,128)S(1)} %slice.10), channel_id=1, source_target_pairs={{0,28},{4,0},{8,4},{12,8},{16,12},{20,16},{24,20},{28,24},{1,29},{... | collective-permute-start | bytes 1572872 | tf_op jit(solution)/shard_map/ppermute | solution.py:25
  9.3 21.2 %collective-permute-start = (f32[2,512,256]{2,1,0:T(8,128)S(1)}, f32[2,512,256]{2,1,0:T(8,128)S(1)}, u32[]{:S(2)}, u32[]{:S(2)}) collective-permute-start(f32[2,512,256]{2,1,0:T(8,128)S(1)} %slice.9), channel_id=1, source_target_pairs={{0,3},{1,0},{2,1},{3,2},{4,7},{5,4},{6,5},{7,6},{8,11},{9,8},{10,9... | collective-permute-start | bytes 3145736 | tf_op jit(solution)/shard_map/ppermute | solution.py:25
  10.0 10.4 %collective-permute-start.3 = (s32[1,1,2,2,2]{4,3,2,1,0:T(2,128)S(1)}, s32[1,1,2,2,2]{4,3,2,1,0:T(2,128)S(1)}, u32[]{:S(2)}, u32[]{:S(2)}) collective-permute-start(s32[1,1,2,2,2]{4,3,2,1,0:T(2,128)S(1)} %copy-done.2), channel_id=1, source_target_pairs={{0,28},{4,0},{8,4},{12,8},{16,12},{20,16},{24,20},{28,24},{1,29},{... | collective-permute-start | bytes 104 | tf_op jit(solution)/shard_map/ppermute | solution.py:25
  10.7 9.7 %collective-permute-start.2 = (s32[1,1,2,2,2]{4,3,2,1,0:T(2,128)S(1)}, s32[1,1,2,2,2]{4,3,2,1,0:T(2,128)S(1)}, u32[]{:S(2)}, u32[]{:S(2)}) collective-permute-start(s32[1,1,2,2,2]{4,3,2,1,0:T(2,128)S(1)} %copy-done.2), channel_id=1, source_target_pairs={{0,4},{4,8},{8,12},{12,16},{16,20},{20,24},{24,28},{28,0},{1,5},{5... | collective-permute-start | bytes 104 | tf_op jit(solution)/shard_map/ppermute | solution.py:25
  12.1 18.4 %collective-permute-start.4 = (f32[2,256,256]{2,1,0:T(8,128)S(1)}, f32[2,256,256]{2,1,0:T(8,128)S(1)}, u32[]{:S(2)}, u32[]{:S(2)}) collective-permute-start(f32[2,256,256]{2,1,0:T(8,128)S(1)} %slice.11), channel_id=1, source_target_pairs={{0,28},{4,0},{8,4},{12,8},{16,12},{20,16},{24,20},{28,24},{1,29},{... | collective-permute-start | bytes 1572872 | tf_op jit(solution)/shard_map/ppermute | solution.py:25
  20.4 10.1 %collective-permute-start.5 = (f32[2,256,256]{2,1,0:T(8,128)S(1)}, f32[2,256,256]{2,1,0:T(8,128)S(1)}, u32[]{:S(2)}, u32[]{:S(2)}) collective-permute-start(f32[2,256,256]{2,1,0:T(8,128)S(1)} %collective-permute-done.1.refs_5_.refs_2_), channel_id=1, source_target_pairs={{0,3},{1,0},{2,1},{3,2},{4,7},{5,4},{6,5},{7,6},{8,11},{9,8},{10,9... | collective-permute-start | bytes 1572872 | tf_op jit(solution)/shard_map/ppermute | solution.py:25
  35.6 26.5 %collective-permute-start.12 = (f32[2,2,256,256]{3,2,1,0:T(8,128)S(1)}, f32[2,2,256,256]{3,2,1,0:T(8,128)S(1)}, u32[]{:S(2)}, u32[]{:S(2)}) collective-permute-start(f32[2,2,256,256]{3,2,1,0:T(8,128)S(1)} %get-tuple-element.63.windows_ref), channel_id=1, source_target_pairs={{0,4},{4,0},{8,12},{12,8},{16,20},{20,16},{24,28},{28,24},{1,5},{5... | collective-permute-start | bytes 3145736 | tf_op jit(solution)/shard_map/ppermute | solution.py:30
  36.1 3.1 %collective-permute-start.6 = (f32[3,128,256]{2,1,0:T(8,128)S(1)}, f32[3,128,256]{2,1,0:T(8,128)S(1)}, u32[]{:S(2)}, u32[]{:S(2)}) collective-permute-start(f32[3,128,256]{2,1,0:T(8,128)S(1)} %get-tuple-element.58), channel_id=1, source_target_pairs={{0,1},{1,0},{2,3},{3,2},{4,5},{5,4},{6,7},{7,6},{8,9},{9,8},{10,11... | collective-permute-start | bytes 1179656 | tf_op jit(solution)/shard_map/ppermute | solution.py:30
  36.1 3.1 %collective-permute-start.8 = (s32[3,1,2,2,2]{4,3,2,1,0:T(2,128)S(1)}, s32[3,1,2,2,2]{4,3,2,1,0:T(2,128)S(1)}, u32[]{:S(2)}, u32[]{:S(2)}) collective-permute-start(s32[3,1,2,2,2]{4,3,2,1,0:T(2,128)S(1)} %pad_add_fusion.offsets_ref), channel_id=1, source_target_pairs={{0,1},{1,2},{2,3},{3,0},{4,5},{5,6},{6,7},{7,4},{8,9},{9,10},{10,1... | collective-permute-start | bytes 296 | tf_op jit(solution)/shard_map/ppermute | solution.py:25
  36.6 4.2 %collective-permute-start.9 = (s32[3,1,2,2,2]{4,3,2,1,0:T(2,128)S(1)}, s32[3,1,2,2,2]{4,3,2,1,0:T(2,128)S(1)}, u32[]{:S(2)}, u32[]{:S(2)}) collective-permute-start(s32[3,1,2,2,2]{4,3,2,1,0:T(2,128)S(1)} %pad_add_fusion.offsets_ref), channel_id=1, source_target_pairs={{0,3},{1,0},{2,1},{3,2},{4,7},{5,4},{6,5},{7,6},{8,11},{9,8},{10,9... | collective-permute-start | bytes 296 | tf_op jit(solution)/shard_map/ppermute | solution.py:25
  39.2 6.2 %collective-permute-start.7 = (f32[3,64,256]{2,1,0:T(8,128)S(1)}, f32[3,64,256]{2,1,0:T(8,128)S(1)}, u32[]{:S(2)}, u32[]{:S(2)}) collective-permute-start(f32[3,64,256]{2,1,0:T(8,128)S(1)} %get-tuple-element.60), channel_id=1, source_target_pairs={{0,2},{1,3},{2,0},{3,1},{4,6},{5,7},{6,4},{7,5},{8,10},{9,11},{10,... | collective-permute-start | bytes 589832 | tf_op jit(solution)/shard_map/ppermute | solution.py:30
  45.5 10.8 %collective-permute-start.10 = (f32[3,64,256]{2,1,0:T(8,128)S(1)}, f32[3,64,256]{2,1,0:T(8,128)S(1)}, u32[]{:S(2)}, u32[]{:S(2)}) collective-permute-start(f32[3,64,256]{2,1,0:T(8,128)S(1)} %add.24), channel_id=1, source_target_pairs={{0,16},{4,20},{8,24},{12,28},{16,0},{20,4},{24,8},{28,12},{1,17},{... | collective-permute-start | bytes 589832 | tf_op jit(solution)/shard_map/ppermute | solution.py:30
  56.3 5.7 %collective-permute-start.11 = (f32[3,64,256]{2,1,0:T(8,128)S(1)}, f32[3,64,256]{2,1,0:T(8,128)S(1)}, u32[]{:S(2)}, u32[]{:S(2)}) collective-permute-start(f32[3,64,256]{2,1,0:T(8,128)S(1)} %add.25), channel_id=1, source_target_pairs={{0,8},{4,12},{8,0},{12,4},{16,24},{20,28},{24,16},{28,20},{1,9},{5... | collective-permute-start | bytes 589832 | tf_op jit(solution)/shard_map/ppermute | solution.py:30
  62.1 23.8 %collective-permute-start.13 = (f32[2,2,256,256]{3,2,1,0:T(8,128)S(1)}, f32[2,2,256,256]{3,2,1,0:T(8,128)S(1)}, u32[]{:S(2)}, u32[]{:S(2)}) collective-permute-start(f32[2,2,256,256]{3,2,1,0:T(8,128)S(1)} %collective-permute-done.12.windows_ref), channel_id=1, source_target_pairs={{0,8},{8,16},{12,4},{16,24},{20,12},{28,20},{1,9},{9,17},{13,5},{1... | collective-permute-start | bytes 3145736 | tf_op jit(solution)/shard_map/ppermute | solution.py:36
  64.9 9.6 %collective-permute-start.16 = (f32[2,2,256,128]{3,2,1,0:T(8,128)S(1)}, f32[2,2,256,128]{3,2,1,0:T(8,128)S(1)}, u32[]{:S(2)}, u32[]{:S(2)}) collective-permute-start(f32[2,2,256,128]{3,2,1,0:T(8,128)S(1)} %get-tuple-element.69), channel_id=1, source_target_pairs={{1,2},{2,1},{5,6},{6,5},{9,10},{10,9},{13,14},{14,13},{17,18},{18,... | collective-permute-start | bytes 1572872 | tf_op jit(solution)/shard_map/ppermute | solution.py:42
  65.6 10.4 %collective-permute-start.17 = (f32[2,2,256,128]{3,2,1,0:T(8,128)S(1)}, f32[2,2,256,128]{3,2,1,0:T(8,128)S(1)}, u32[]{:S(2)}, u32[]{:S(2)}) collective-permute-start(f32[2,2,256,128]{3,2,1,0:T(8,128)S(1)} %get-tuple-element.70), channel_id=1, source_target_pairs={{0,1},{1,0},{2,3},{3,2},{4,5},{5,4},{6,7},{7,6},{8,9},{9,8},{10,11... | collective-permute-start | bytes 1572872 | tf_op jit(solution)/shard_map/ppermute | solution.py:30
  67.6 6.9 %collective-permute-start.14 = (f32[3,64,256]{2,1,0:T(8,128)S(1)}, f32[3,64,256]{2,1,0:T(8,128)S(1)}, u32[]{:S(2)}, u32[]{:S(2)}) collective-permute-start(f32[3,64,256]{2,1,0:T(8,128)S(1)} %add.26), channel_id=1, source_target_pairs={{0,4},{4,0},{8,12},{12,8},{16,20},{20,16},{24,28},{28,24},{1,5},{5... | collective-permute-start | bytes 589832 | tf_op jit(solution)/shard_map/ppermute | solution.py:30
  69.3 15.3 %collective-permute-start.19 = (f32[2,2,256,128]{3,2,1,0:T(8,128)S(1)}, f32[2,2,256,128]{3,2,1,0:T(8,128)S(1)}, u32[]{:S(2)}, u32[]{:S(2)}) collective-permute-start(f32[2,2,256,128]{3,2,1,0:T(8,128)S(1)} %get-tuple-element.73), channel_id=1, source_target_pairs={{1,2},{2,1},{5,6},{6,5},{9,10},{10,9},{13,14},{14,13},{17,18},{18,... | collective-permute-start | bytes 1572872 | tf_op jit(solution)/shard_map/ppermute | solution.py:42
  74.5 10.2 %collective-permute-start.20 = (f32[2,2,256,128]{3,2,1,0:T(8,128)S(1)}, f32[2,2,256,128]{3,2,1,0:T(8,128)S(1)}, u32[]{:S(2)}, u32[]{:S(2)}) collective-permute-start(f32[2,2,256,128]{3,2,1,0:T(8,128)S(1)} %get-tuple-element.74), channel_id=1, source_target_pairs={{0,1},{1,0},{2,3},{3,2},{4,5},{5,4},{6,7},{7,6},{8,9},{9,8},{10,11... | collective-permute-start | bytes 1572872 | tf_op jit(solution)/shard_map/ppermute | solution.py:30
  74.5 8.4 %collective-permute-start.15 = (f32[2,64,256]{2,1,0:T(8,128)S(1)}, f32[2,64,256]{2,1,0:T(8,128)S(1)}, u32[]{:S(2)}, u32[]{:S(2)}) collective-permute-start(f32[2,64,256]{2,1,0:T(8,128)S(1)} %illuminate.2.value_ref), channel_id=1, source_target_pairs={{0,2},{1,3},{2,0},{3,1},{4,6},{5,7},{6,4},{7,5},{8,10},{9,11},{10,... | collective-permute-start | bytes 393224 | tf_op jit(solution)/shard_map/ppermute | solution.py:30
  83.0 1.6 collective-permute-start.18
  87.1 2.0 %collective-permute-start.21 = (f32[2,2,256,128]{3,2,1,0:T(8,128)S(1)}, f32[2,2,256,128]{3,2,1,0:T(8,128)S(1)}, u32[]{:S(2)}, u32[]{:S(2)}) collective-permute-start(f32[2,2,256,128]{3,2,1,0:T(8,128)S(1)} %get-tuple-element.82), channel_id=1, source_target_pairs={{0,1},{1,0},{2,3},{3,2},{4,5},{5,4},{6,7},{7,6},{8,9},{9,8},{10,11... | collective-permute-start | bytes 1572872 | tf_op jit(solution)/shard_map/ppermute | solution.py:30
  87.2 1.9 %collective-permute-start.22 = (f32[2,2,256,128]{3,2,1,0:T(8,128)S(1)}, f32[2,2,256,128]{3,2,1,0:T(8,128)S(1)}, u32[]{:S(2)}, u32[]{:S(2)}) collective-permute-start(f32[2,2,256,128]{3,2,1,0:T(8,128)S(1)} %get-tuple-element.85), channel_id=1, source_target_pairs={{1,2},{2,1},{5,6},{6,5},{9,10},{10,9},{13,14},{14,13},{17,18},{18,... | collective-permute-start | bytes 1572872 | tf_op jit(solution)/shard_map/ppermute | solution.py:42
  95.6 11.3 %collective-permute-start.23 = (f32[3,128,256]{2,1,0:T(8,128)S(1)}, f32[3,128,256]{2,1,0:T(8,128)S(1)}, u32[]{:S(2)}, u32[]{:S(2)}) collective-permute-start(f32[3,128,256]{2,1,0:T(8,128)S(1)} %get-tuple-element.87), channel_id=1, source_target_pairs={{0,1},{1,0},{2,3},{3,2},{4,5},{5,4},{6,7},{7,6},{8,9},{9,8},{10,11... | collective-permute-start | bytes 1179656 | tf_op jit(solution)/shard_map/ppermute | solution.py:30
  104.7 27.8 %collective-permute-start.25 = (f32[2,2,256,256]{3,2,1,0:T(8,128)S(1)}, f32[2,2,256,256]{3,2,1,0:T(8,128)S(1)}, u32[]{:S(2)}, u32[]{:S(2)}) collective-permute-start(f32[2,2,256,256]{3,2,1,0:T(8,128)S(1)} %get-tuple-element.90.windows_ref), channel_id=1, source_target_pairs={{0,4},{4,8},{8,12},{12,16},{16,20},{20,24},{24,28},{28,0},{1,5},{5... | collective-permute-start | bytes 3145736 | tf_op jit(solution)/shard_map/ppermute | solution.py:25
  107.0 6.7 %collective-permute-start.24 = (f32[3,64,256]{2,1,0:T(8,128)S(1)}, f32[3,64,256]{2,1,0:T(8,128)S(1)}, u32[]{:S(2)}, u32[]{:S(2)}) collective-permute-start(f32[3,64,256]{2,1,0:T(8,128)S(1)} %get-tuple-element.89), channel_id=1, source_target_pairs={{0,2},{1,3},{2,0},{3,1},{4,6},{5,7},{6,4},{7,5},{8,10},{9,11},{10,... | collective-permute-start | bytes 589832 | tf_op jit(solution)/shard_map/ppermute | solution.py:30
  113.6 18.9 %collective-permute-start.26 = (f32[2,2,256,128]{3,2,1,0:T(8,128)S(1)}, f32[2,2,256,128]{3,2,1,0:T(8,128)S(1)}, u32[]{:S(2)}, u32[]{:S(2)}) collective-permute-start(f32[2,2,256,128]{3,2,1,0:T(8,128)S(1)} %get-tuple-element.94), channel_id=1, source_target_pairs={{0,1},{1,2},{2,3},{3,0},{4,5},{5,6},{6,7},{7,4},{8,9},{9,10},{10,1... | collective-permute-start | bytes 1572872 | tf_op jit(solution)/shard_map/ppermute | solution.py:25
  132.6 6.0 %collective-permute-start.27 = (f32[3,64,256]{2,1,0:T(8,128)S(1)}, f32[3,64,256]{2,1,0:T(8,128)S(1)}, u32[]{:S(2)}, u32[]{:S(2)}) collective-permute-start(f32[3,64,256]{2,1,0:T(8,128)S(1)} %add.28), channel_id=1, source_target_pairs={{0,4},{4,0},{8,12},{12,8},{16,20},{20,16},{24,28},{28,24},{1,5},{5... | collective-permute-start | bytes 589832 | tf_op jit(solution)/shard_map/ppermute | solution.py:30
  133.7 20.2 %collective-permute-start.30 = (f32[2,2,256,128]{3,2,1,0:T(8,128)S(1)}, f32[2,2,256,128]{3,2,1,0:T(8,128)S(1)}, u32[]{:S(2)}, u32[]{:S(2)}) collective-permute-start(f32[2,2,256,128]{3,2,1,0:T(8,128)S(1)} %get-tuple-element.98), channel_id=1, source_target_pairs={{0,1},{1,2},{2,3},{3,0},{4,5},{5,6},{6,7},{7,4},{8,9},{9,10},{10,1... | collective-permute-start | bytes 1572872 | tf_op jit(solution)/shard_map/ppermute | solution.py:25
  138.6 5.7 %collective-permute-start.28 = (f32[3,64,256]{2,1,0:T(8,128)S(1)}, f32[3,64,256]{2,1,0:T(8,128)S(1)}, u32[]{:S(2)}, u32[]{:S(2)}) collective-permute-start(f32[3,64,256]{2,1,0:T(8,128)S(1)} %add.29), channel_id=1, source_target_pairs={{0,8},{4,12},{8,0},{12,4},{16,24},{20,28},{24,16},{28,20},{1,9},{5... | collective-permute-start | bytes 589832 | tf_op jit(solution)/shard_map/ppermute | solution.py:30
  144.4 9.4 %collective-permute-start.29 = (f32[3,64,256]{2,1,0:T(8,128)S(1)}, f32[3,64,256]{2,1,0:T(8,128)S(1)}, u32[]{:S(2)}, u32[]{:S(2)}) collective-permute-start(f32[3,64,256]{2,1,0:T(8,128)S(1)} %add.30), channel_id=1, source_target_pairs={{0,16},{4,20},{8,24},{12,28},{16,0},{20,4},{24,8},{28,12},{1,17},{... | collective-permute-start | bytes 589832 | tf_op jit(solution)/shard_map/ppermute | solution.py:30
  153.9 5.0 %collective-permute-start.31 = (f32[2,64,256]{2,1,0:T(8,128)S(1)}, f32[2,64,256]{2,1,0:T(8,128)S(1)}, u32[]{:S(2)}, u32[]{:S(2)}) collective-permute-start(f32[2,64,256]{2,1,0:T(8,128)S(1)} %illuminate.3.value_ref), channel_id=1, source_target_pairs={{0,2},{1,3},{2,0},{3,1},{4,6},{5,7},{6,4},{7,5},{8,10},{9,11},{10,... | collective-permute-start | bytes 393224 | tf_op jit(solution)/shard_map/ppermute | solution.py:30
  (6 other events, 99.2 us)

commit v9 on v7

--- a/solution.py
+++ b/solution.py
@@ -23,6 +23,11 @@
 def shifted(array, axis, by):
     peers = lax.axis_size(axis)
     return lax.ppermute(array, axis, [(i, (i + by) % peers) for i in range(peers)])
+
+
+def moved_down(array):
+    peers = lax.axis_size("row")
+    return lax.ppermute(array, "row", [(i, i + 1) for i in range(peers - 1)])
 
 
 def swapped(array, axis, mask):
@@ -642,7 +647,7 @@
     kept, sent, own = scan_step(1, True, offsets, probe, measured, table, field)
     total, middle_right = place(1, offsets, own, tile, 1)
     dense = density(1, False, around, probe, tile)
-    upper = shifted(own, "row", 1)
+    upper = moved_down(own)
     came = swapped(sent, "col", 1)
     for bit in range(1, col_bits):
         kept, sent = fold(bit, kept, came)

time: 163 us -> 162 us (level)
  waiting for transfers between devices: 93.3 us -> 83.2 us
  starting transfers between devices: 39.3 us -> 48.9 us
    ppermute x11 -> x10, waiting for transfers between devices: 34.8 us -> 15.7 us  [shifted(): lax.ppermute(array, axis, [(i, (i + by) % peers) for i in range(peers)])]
    ppermute x0 -> x1, waiting for transfers between devices: none -> 15.5 us  [moved_down(): return lax.ppermute(array, 'row', [(i, i + 1) for i in range(peers - 1)])]
    ppermute x18, starting transfers between devices: 22.3 us -> 30.3 us  [swapped(): return lax.ppermute(array, axis, [(i, i ^ mask) for i in range(peers)])]
    ppermute x18, waiting for transfers between devices: 56.3 us -> 49.8 us  [swapped(): return lax.ppermute(array, axis, [(i, i ^ mask) for i in range(peers)])]
    ppermute x0 -> x1, starting transfers between devices: none -> 1.67 us  [moved_down(): return lax.ppermute(array, 'row', [(i, i + 1) for i in range(peers - 1)])]
    ppermute x11 -> x10, starting transfers between devices: 14.1 us -> 14.1 us  [shifted(): lax.ppermute(array, axis, [(i, (i + by) % peers) for i in range(peers)])]
  transfers between devices with their start and end apart: 33 -> 33, of which waited for: 19 -> 18; matrix products, arithmetic and copies ran while one was open for 1% -> 1% of each run, Pallas kernels for 8% -> 7%
where the time goes in v9:
time: 162 us; the launch traced here: 161 us
  waiting for transfers between devices  83.2 us (51%)
  starting transfers between devices  48.9 us (30%)
  Pallas kernels  25.6 us (16%)
  local copies, waits for them, and re-layouts  2.61 us (2%)
    ppermute x18, waiting for transfers between devices, swapped(): return lax.ppermute(array, axis, [(i, i ^ mask) for i in range(peers)])  49.8 us
    ppermute x18, starting transfers between devices, swapped(): return lax.ppermute(array, axis, [(i, i ^ mask) for i in range(peers)])  30.3 us
    ppermute x10, waiting for transfers between devices, shifted(): lax.ppermute(array, axis, [(i, (i + by) % peers) for i in range(peers)])  15.7 us
    ppermute x1, waiting for transfers between devices, moved_down(): return lax.ppermute(array, 'row', [(i, i + 1) for i in range(peers - 1)])  15.5 us
    ppermute x10, starting transfers between devices, shifted(): lax.ppermute(array, axis, [(i, (i + by) % peers) for i in range(peers)])  14.1 us
    pallas_call x2, Pallas kernels, scan_step(): pl.pallas_call(functools.partial(scan_kernel, sweep, last, counts), out_s...  9.83 us
    pallas_call x2, Pallas kernels, density(): pl.pallas_call(functools.partial(density_kernel, sweep, reach), out_shape...  4.22 us
    pallas_call x3, Pallas kernels, gather(): pl.pallas_call(functools.partial(gather_kernel, sweep, below_of), out_sha...  3.67 us
  transfers between devices with their start and end apart: 33, of which 18 were waited for; matrix products, arithmetic and copies ran while one was open for 1% of the time, Pallas kernels for 7%

profile of v9, /device:TPU:0, one launch (start us, length us, event | category | flops | bytes accessed | tf_op | source)
XLA Modules:
  0.0 161.5 jit_solution(7133453647907135737)
XLA Ops:
  1.9 6.1 %collective-permute-start.1 = (f32[2,256,256]{2,1,0:T(8,128)S(1)}, f32[2,256,256]{2,1,0:T(8,128)S(1)}, u32[]{:S(2)}, u32[]{:S(2)}) collective-permute-start(f32[2,256,256]{2,1,0:T(8,128)S(1)} %slice.10), channel_id=1, source_target_pairs={{0,28},{4,0},{8,4},{12,8},{16,12},{20,16},{24,20},{28,24},{1,29},{... | collective-permute-start | bytes 1572872 | tf_op jit(solution)/shard_map/ppermute | solution.py:25
  12.1 3.4 %collective-permute-start.4 = (f32[2,256,256]{2,1,0:T(8,128)S(1)}, f32[2,256,256]{2,1,0:T(8,128)S(1)}, u32[]{:S(2)}, u32[]{:S(2)}) collective-permute-start(f32[2,256,256]{2,1,0:T(8,128)S(1)} %slice.11), channel_id=1, source_target_pairs={{0,28},{4,0},{8,4},{12,8},{16,12},{20,16},{24,20},{28,24},{1,29},{... | collective-permute-start | bytes 1572872 | tf_op jit(solution)/shard_map/ppermute | solution.py:25
  15.5 4.9 %collective-permute-done.3 = s32[1,1,2,2,2]{4,3,2,1,0:T(2,128)S(1)} collective-permute-done((s32[1,1,2,2,2]{4,3,2,1,0:T(2,128)S(1)}, s32[1,1,2,2,2]{4,3,2,1,0:T(2,128)S(1)}, u32[]{:S(2)}, u32[]{:S(2)}) %collective-permute-start.3) | collective-permute-done | bytes 64 | tf_op jit(solution)/shard_map/ppermute | solution.py:25
  21.0 9.4 %collective-permute-done.4.refs_6_.refs_3_ = f32[2,256,256]{2,1,0:T(8,128)S(1)} collective-permute-done((f32[2,256,256]{2,1,0:T(8,128)S(1)}, f32[2,256,256]{2,1,0:T(8,128)S(1)}, u32[]{:S(2)}, u32[]{:S(2)}) %collective-permute-start.4) | collective-permute-done | bytes 524320 | tf_op jit(solution)/shard_map/ppermute | solution.py:25
  30.5 5.1 %scan.2 = (f32[3,128,256]{2,1,0:T(8,128)S(1)}, f32[3,128,256]{2,1,0:T(8,128)S(1)}, f32[2,2,256,256]{3,2,1,0:T(8,128)S(1)}) custom-call(s32[1,1,2,2,2]{4,3,2,1,0:T(2,128)S(1)} %copy-done.2, f32[2,256,256]{2,1,0:T(8,128)S(1)} %copy-done.1, bf16[2,2,256,256]{3,2,1,0:T(8,128)(2,1)S(1)} %reorder.1.refs_1_, bf16[8,256,256]{2,1,0:T(8,128)(2,1)S(1)} %copy-done.4, ...), custom_call_target="tpu_custom_call" | custom-call | flops 7000000000 | bytes 12582912 | tf_op jit(solution)/shard_map/scan/pallas_call | solution.py:299
  39.2 1.5 collective-permute-start.7
  40.8 4.6 %collective-permute-done.7 = f32[3,64,256]{2,1,0:T(8,128)S(1)} collective-permute-done((f32[3,64,256]{2,1,0:T(8,128)S(1)}, f32[3,64,256]{2,1,0:T(8,128)S(1)}, u32[]{:S(2)}, u32[]{:S(2)}) %collective-permute-start.7) | collective-permute-done | bytes 196640 | tf_op jit(solution)/shard_map/ppermute | solution.py:35
  45.4 2.7 %collective-permute-start.10 = (f32[3,64,256]{2,1,0:T(8,128)S(1)}, f32[3,64,256]{2,1,0:T(8,128)S(1)}, u32[]{:S(2)}, u32[]{:S(2)}) collective-permute-start(f32[3,64,256]{2,1,0:T(8,128)S(1)} %add.24), channel_id=1, source_target_pairs={{0,16},{4,20},{8,24},{12,28},{16,0},{20,4},{24,8},{28,12},{1,17},{... | collective-permute-start | bytes 589832 | tf_op jit(solution)/shard_map/ppermute | solution.py:35
  48.1 2.5 %density.2.refs_5_ = f32[6,768,128]{2,1,0:T(8,128)S(1)} custom-call(s32[3,3,2,2,2]{4,3,2,1,0:T(2,128)S(1)} %constant_dynamic-update-slice_fusion.offsets_ref, f32[2,256,256]{2,1,0:T(8,128)S(1)} %copy-done.1), custom_call_target="tpu_custom_call" | custom-call | flops 1000000 | bytes 6291456 | tf_op jit(solution)/shard_map/density/pallas_call | solution.py:376
  51.9 4.4 %collective-permute-done.10 = f32[3,64,256]{2,1,0:T(8,128)S(1)} collective-permute-done((f32[3,64,256]{2,1,0:T(8,128)S(1)}, f32[3,64,256]{2,1,0:T(8,128)S(1)}, u32[]{:S(2)}, u32[]{:S(2)}) %collective-permute-start.10) | collective-permute-done | bytes 196640 | tf_op jit(solution)/shard_map/ppermute | solution.py:35
  56.7 5.3 %collective-permute-done.11 = f32[3,64,256]{2,1,0:T(8,128)S(1)} collective-permute-done((f32[3,64,256]{2,1,0:T(8,128)S(1)}, f32[3,64,256]{2,1,0:T(8,128)S(1)}, u32[]{:S(2)}, u32[]{:S(2)}) %collective-permute-start.11) | collective-permute-done | bytes 196640 | tf_op jit(solution)/shard_map/ppermute | solution.py:35
  65.2 3.9 %collective-permute-start.14 = (f32[3,64,256]{2,1,0:T(8,128)S(1)}, f32[3,64,256]{2,1,0:T(8,128)S(1)}, u32[]{:S(2)}, u32[]{:S(2)}) collective-permute-start(f32[3,64,256]{2,1,0:T(8,128)S(1)} %add.26), channel_id=1, source_target_pairs={{0,4},{4,0},{8,12},{12,8},{16,20},{20,16},{24,28},{28,24},{1,5},{5... | collective-permute-start | bytes 589832 | tf_op jit(solution)/shard_map/ppermute | solution.py:35
  70.9 3.3 %collective-permute-done.14 = f32[3,64,256]{2,1,0:T(8,128)S(1)} collective-permute-done((f32[3,64,256]{2,1,0:T(8,128)S(1)}, f32[3,64,256]{2,1,0:T(8,128)S(1)}, u32[]{:S(2)}, u32[]{:S(2)}) %collective-permute-start.14) | collective-permute-done | bytes 196640 | tf_op jit(solution)/shard_map/ppermute | solution.py:35
  74.7 9.1 %collective-permute-done.15.other_ref = f32[2,64,256]{2,1,0:T(8,128)S(1)} collective-permute-done((f32[2,64,256]{2,1,0:T(8,128)S(1)}, f32[2,64,256]{2,1,0:T(8,128)S(1)}, u32[]{:S(2)}, u32[]{:S(2)}) %collective-permute-start.15) | collective-permute-done | bytes 131104 | tf_op jit(solution)/shard_map/ppermute | solution.py:35
  83.9 1.5 collective-permute-done.18.other_ref
  85.5 2.1 %collective-permute-done.13.windows_ref = f32[2,2,256,256]{3,2,1,0:T(8,128)S(1)} collective-permute-done((f32[2,2,256,256]{3,2,1,0:T(8,128)S(1)}, f32[2,2,256,256]{3,2,1,0:T(8,128)S(1)}, u32[]{:S(2)}, u32[]{:S(2)}) %collective-permute-start.13) | collective-permute-done | bytes 1048608 | tf_op jit(solution)/shard_map/ppermute | solution.py:40
  91.0 1.8 %widen.1.refs_3_.field_ref = f32[2,6,768,128]{3,2,1,0:T(8,128)S(1)} custom-call(f32[2,512,512]{2,1,0:T(8,128)S(1)} %copy-done, f32[2,512,256]{2,1,0:T(8,128)S(1)} %collective-permute-done.refs_4_.refs_1_, f32[2,256,256]{2,1,0:T(8,128)S(1)} %collective-permute-done.1.refs_5_.refs_2_, f32[2,256,256]{2,1,0:T(8,128)S(1)} %collective-permute-done.4.refs_6_.refs_3_, ...), custom_call_target="tpu_custom_call" | custom-call | flops 4000000 | bytes 20971520 | tf_op jit(solution)/shard_map/widen/pallas_call | solution.py:488
  92.8 4.7 %scan.3 = (f32[3,128,256]{2,1,0:T(8,128)S(1)}, f32[3,128,256]{2,1,0:T(8,128)S(1)}, f32[2,2,256,256]{3,2,1,0:T(8,128)S(1)}) custom-call(s32[1,1,2,2,2]{4,3,2,1,0:T(2,128)S(1)} %copy-done.2, f32[2,256,256]{2,1,0:T(8,128)S(1)} %join.5.refs_0_.probe_ref, bf16[2,2,256,256]{3,2,1,0:T(8,128)(2,1)S(1)} %reorder.1.refs_1_, bf16[8,256,256]{2,1,0:T(8,128)(2,1)S(1)} %copy-done.4, ...), custom_call_target="tpu_custom_call" | custom-call | flops 7000000000 | bytes 12582912 | tf_op jit(solution)/shard_map/scan/pallas_call | solution.py:299
  97.5 9.1 %collective-permute-start.23 = (f32[3,128,256]{2,1,0:T(8,128)S(1)}, f32[3,128,256]{2,1,0:T(8,128)S(1)}, u32[]{:S(2)}, u32[]{:S(2)}) collective-permute-start(f32[3,128,256]{2,1,0:T(8,128)S(1)} %get-tuple-element.87), channel_id=1, source_target_pairs={{0,1},{1,0},{2,3},{3,2},{4,5},{5,4},{6,7},{7,6},{8,9},{9,8},{10,11... | collective-permute-start | bytes 1179656 | tf_op jit(solution)/shard_map/ppermute | solution.py:35
  106.6 1.7 %collective-permute-start.25 = (f32[2,2,256,256]{3,2,1,0:T(8,128)S(1)}, f32[2,2,256,256]{3,2,1,0:T(8,128)S(1)}, u32[]{:S(2)}, u32[]{:S(2)}) collective-permute-start(f32[2,2,256,256]{3,2,1,0:T(8,128)S(1)} %get-tuple-element.90.windows_ref), channel_id=1, source_target_pairs={{0,4},{4,8},{8,12},{12,16},{16,20},{20,24},{24,28},{1,5},{5,9},{9,... | collective-permute-start | bytes 3145736 | tf_op jit(solution)/shard_map/ppermute | solution.py:30
  108.5 1.7 %density.3.density_ref = f32[4,512,128]{2,1,0:T(8,128)S(1)} custom-call(s32[3,3,2,2,2]{4,3,2,1,0:T(2,128)S(1)} %constant_dynamic-update-slice_fusion.offsets_ref, f32[2,256,256]{2,1,0:T(8,128)S(1)} %join.5.refs_0_.probe_ref), custom_call_target="tpu_custom_call" | custom-call | flops 1000000 | bytes 6291456 | tf_op jit(solution)/shard_map/density/pallas_call | solution.py:376
  111.5 3.8 %collective-permute-done.24 = f32[3,64,256]{2,1,0:T(8,128)S(1)} collective-permute-done((f32[3,64,256]{2,1,0:T(8,128)S(1)}, f32[3,64,256]{2,1,0:T(8,128)S(1)}, u32[]{:S(2)}, u32[]{:S(2)}) %collective-permute-start.24) | collective-permute-done | bytes 196640 | tf_op jit(solution)/shard_map/ppermute | solution.py:35
  115.3 15.5 %collective-permute-done.25.windows_ref = f32[2,2,256,256]{3,2,1,0:T(8,128)S(1)} collective-permute-done((f32[2,2,256,256]{3,2,1,0:T(8,128)S(1)}, f32[2,2,256,256]{3,2,1,0:T(8,128)S(1)}, u32[]{:S(2)}, u32[]{:S(2)}) %collective-permute-start.25) | collective-permute-done | bytes 1048608 | tf_op jit(solution)/shard_map/ppermute | solution.py:30
  130.8 2.5 %collective-permute-start.27 = (f32[3,64,256]{2,1,0:T(8,128)S(1)}, f32[3,64,256]{2,1,0:T(8,128)S(1)}, u32[]{:S(2)}, u32[]{:S(2)}) collective-permute-start(f32[3,64,256]{2,1,0:T(8,128)S(1)} %add.28), channel_id=1, source_target_pairs={{0,4},{4,0},{8,12},{12,8},{16,20},{20,16},{24,28},{28,24},{1,5},{5... | collective-permute-start | bytes 589832 | tf_op jit(solution)/shard_map/ppermute | solution.py:35
  134.5 3.0 %collective-permute-done.27 = f32[3,64,256]{2,1,0:T(8,128)S(1)} collective-permute-done((f32[3,64,256]{2,1,0:T(8,128)S(1)}, f32[3,64,256]{2,1,0:T(8,128)S(1)}, u32[]{:S(2)}, u32[]{:S(2)}) %collective-permute-start.27) | collective-permute-done | bytes 196640 | tf_op jit(solution)/shard_map/ppermute | solution.py:35
  137.6 2.5 %collective-permute-start.28 = (f32[3,64,256]{2,1,0:T(8,128)S(1)}, f32[3,64,256]{2,1,0:T(8,128)S(1)}, u32[]{:S(2)}, u32[]{:S(2)}) collective-permute-start(f32[3,64,256]{2,1,0:T(8,128)S(1)} %add.29), channel_id=1, source_target_pairs={{0,8},{4,12},{8,0},{12,4},{16,24},{20,28},{24,16},{28,20},{1,9},{5... | collective-permute-start | bytes 589832 | tf_op jit(solution)/shard_map/ppermute | solution.py:35
  140.1 3.6 %collective-permute-done.28 = f32[3,64,256]{2,1,0:T(8,128)S(1)} collective-permute-done((f32[3,64,256]{2,1,0:T(8,128)S(1)}, f32[3,64,256]{2,1,0:T(8,128)S(1)}, u32[]{:S(2)}, u32[]{:S(2)}) %collective-permute-start.28) | collective-permute-done | bytes 196640 | tf_op jit(solution)/shard_map/ppermute | solution.py:35
  143.8 3.4 %collective-permute-start.29 = (f32[3,64,256]{2,1,0:T(8,128)S(1)}, f32[3,64,256]{2,1,0:T(8,128)S(1)}, u32[]{:S(2)}, u32[]{:S(2)}) collective-permute-start(f32[3,64,256]{2,1,0:T(8,128)S(1)} %add.30), channel_id=1, source_target_pairs={{0,16},{4,20},{8,24},{12,28},{16,0},{20,4},{24,8},{28,12},{1,17},{... | collective-permute-start | bytes 589832 | tf_op jit(solution)/shard_map/ppermute | solution.py:35
  147.2 6.7 %collective-permute-done.29 = f32[3,64,256]{2,1,0:T(8,128)S(1)} collective-permute-done((f32[3,64,256]{2,1,0:T(8,128)S(1)}, f32[3,64,256]{2,1,0:T(8,128)S(1)}, u32[]{:S(2)}, u32[]{:S(2)}) %collective-permute-start.29) | collective-permute-done | bytes 196640 | tf_op jit(solution)/shard_map/ppermute | solution.py:35
  155.5 1.8 %renew.1 = f32[2,512,512]{2,1,0:T(8,128)} custom-call(f32[2,6,768,128]{3,2,1,0:T(8,128)S(1)} %widen.1.refs_3_.field_ref, f32[4,512,128]{2,1,0:T(8,128)S(1)} %density.3.density_ref, f32[2,6,768,128]{3,2,1,0:T(8,128)S(1)} %get-tuple-element.96.total_ref, f32[2,6,256,128]{3,2,1,0:T(8,128)S(1)} %get-tuple-element.101.top_ref, ...), custom_call_target="tpu_custom_call" | custom-call | flops 4000000 | bytes 10485760 | tf_op jit(solution)/shard_map/renew/pallas_call | solution.py:516
  157.3 1.7 %collective-permute-done.31.other_ref = f32[2,64,256]{2,1,0:T(8,128)S(1)} collective-permute-done((f32[2,64,256]{2,1,0:T(8,128)S(1)}, f32[2,64,256]{2,1,0:T(8,128)S(1)}, u32[]{:S(2)}, u32[]{:S(2)}) %collective-permute-start.31) | collective-permute-done | bytes 131104 | tf_op jit(solution)/shard_map/ppermute | solution.py:35
  159.1 1.5 collective-permute-done.32.other_ref
  (79 shorter events, 25.5 us)
Async XLA Ops:
  1.9 18.4 %collective-permute-start.1 = (f32[2,256,256]{2,1,0:T(8,128)S(1)}, f32[2,256,256]{2,1,0:T(8,128)S(1)}, u32[]{:S(2)}, u32[]{:S(2)}) collective-permute-start(f32[2,256,256]{2,1,0:T(8,128)S(1)} %slice.10), channel_id=1, source_target_pairs={{0,28},{4,0},{8,4},{12,8},{16,12},{20,16},{24,20},{28,24},{1,29},{... | collective-permute-start | bytes 1572872 | tf_op jit(solution)/shard_map/ppermute | solution.py:25
  9.3 21.2 %collective-permute-start = (f32[2,512,256]{2,1,0:T(8,128)S(1)}, f32[2,512,256]{2,1,0:T(8,128)S(1)}, u32[]{:S(2)}, u32[]{:S(2)}) collective-permute-start(f32[2,512,256]{2,1,0:T(8,128)S(1)} %slice.9), channel_id=1, source_target_pairs={{0,3},{1,0},{2,1},{3,2},{4,7},{5,4},{6,5},{7,6},{8,11},{9,8},{10,9... | collective-permute-start | bytes 3145736 | tf_op jit(solution)/shard_map/ppermute | solution.py:25
  10.0 10.4 %collective-permute-start.3 = (s32[1,1,2,2,2]{4,3,2,1,0:T(2,128)S(1)}, s32[1,1,2,2,2]{4,3,2,1,0:T(2,128)S(1)}, u32[]{:S(2)}, u32[]{:S(2)}) collective-permute-start(s32[1,1,2,2,2]{4,3,2,1,0:T(2,128)S(1)} %copy-done.2), channel_id=1, source_target_pairs={{0,28},{4,0},{8,4},{12,8},{16,12},{20,16},{24,20},{28,24},{1,29},{... | collective-permute-start | bytes 104 | tf_op jit(solution)/shard_map/ppermute | solution.py:25
  10.7 9.7 %collective-permute-start.2 = (s32[1,1,2,2,2]{4,3,2,1,0:T(2,128)S(1)}, s32[1,1,2,2,2]{4,3,2,1,0:T(2,128)S(1)}, u32[]{:S(2)}, u32[]{:S(2)}) collective-permute-start(s32[1,1,2,2,2]{4,3,2,1,0:T(2,128)S(1)} %copy-done.2), channel_id=1, source_target_pairs={{0,4},{4,8},{8,12},{12,16},{16,20},{20,24},{24,28},{28,0},{1,5},{5... | collective-permute-start | bytes 104 | tf_op jit(solution)/shard_map/ppermute | solution.py:25
  12.1 18.4 %collective-permute-start.4 = (f32[2,256,256]{2,1,0:T(8,128)S(1)}, f32[2,256,256]{2,1,0:T(8,128)S(1)}, u32[]{:S(2)}, u32[]{:S(2)}) collective-permute-start(f32[2,256,256]{2,1,0:T(8,128)S(1)} %slice.11), channel_id=1, source_target_pairs={{0,28},{4,0},{8,4},{12,8},{16,12},{20,16},{24,20},{28,24},{1,29},{... | collective-permute-start | bytes 1572872 | tf_op jit(solution)/shard_map/ppermute | solution.py:25
  20.4 10.1 %collective-permute-start.5 = (f32[2,256,256]{2,1,0:T(8,128)S(1)}, f32[2,256,256]{2,1,0:T(8,128)S(1)}, u32[]{:S(2)}, u32[]{:S(2)}) collective-permute-start(f32[2,256,256]{2,1,0:T(8,128)S(1)} %collective-permute-done.1.refs_5_.refs_2_), channel_id=1, source_target_pairs={{0,3},{1,0},{2,1},{3,2},{4,7},{5,4},{6,5},{7,6},{8,11},{9,8},{10,9... | collective-permute-start | bytes 1572872 | tf_op jit(solution)/shard_map/ppermute | solution.py:25
  35.6 26.5 %collective-permute-start.12 = (f32[2,2,256,256]{3,2,1,0:T(8,128)S(1)}, f32[2,2,256,256]{3,2,1,0:T(8,128)S(1)}, u32[]{:S(2)}, u32[]{:S(2)}) collective-permute-start(f32[2,2,256,256]{3,2,1,0:T(8,128)S(1)} %get-tuple-element.63.windows_ref), channel_id=1, source_target_pairs={{0,4},{4,0},{8,12},{12,8},{16,20},{20,16},{24,28},{28,24},{1,5},{5... | collective-permute-start | bytes 3145736 | tf_op jit(solution)/shard_map/ppermute | solution.py:35
  36.1 3.1 %collective-permute-start.6 = (f32[3,128,256]{2,1,0:T(8,128)S(1)}, f32[3,128,256]{2,1,0:T(8,128)S(1)}, u32[]{:S(2)}, u32[]{:S(2)}) collective-permute-start(f32[3,128,256]{2,1,0:T(8,128)S(1)} %get-tuple-element.58), channel_id=1, source_target_pairs={{0,1},{1,0},{2,3},{3,2},{4,5},{5,4},{6,7},{7,6},{8,9},{9,8},{10,11... | collective-permute-start | bytes 1179656 | tf_op jit(solution)/shard_map/ppermute | solution.py:35
  36.1 3.1 %collective-permute-start.8 = (s32[3,1,2,2,2]{4,3,2,1,0:T(2,128)S(1)}, s32[3,1,2,2,2]{4,3,2,1,0:T(2,128)S(1)}, u32[]{:S(2)}, u32[]{:S(2)}) collective-permute-start(s32[3,1,2,2,2]{4,3,2,1,0:T(2,128)S(1)} %pad_add_fusion.offsets_ref), channel_id=1, source_target_pairs={{0,1},{1,2},{2,3},{3,0},{4,5},{5,6},{6,7},{7,4},{8,9},{9,10},{10,1... | collective-permute-start | bytes 296 | tf_op jit(solution)/shard_map/ppermute | solution.py:25
  36.6 4.2 %collective-permute-start.9 = (s32[3,1,2,2,2]{4,3,2,1,0:T(2,128)S(1)}, s32[3,1,2,2,2]{4,3,2,1,0:T(2,128)S(1)}, u32[]{:S(2)}, u32[]{:S(2)}) collective-permute-start(s32[3,1,2,2,2]{4,3,2,1,0:T(2,128)S(1)} %pad_add_fusion.offsets_ref), channel_id=1, source_target_pairs={{0,3},{1,0},{2,1},{3,2},{4,7},{5,4},{6,5},{7,6},{8,11},{9,8},{10,9... | collective-permute-start | bytes 296 | tf_op jit(solution)/shard_map/ppermute | solution.py:25
  39.2 6.2 %collective-permute-start.7 = (f32[3,64,256]{2,1,0:T(8,128)S(1)}, f32[3,64,256]{2,1,0:T(8,128)S(1)}, u32[]{:S(2)}, u32[]{:S(2)}) collective-permute-start(f32[3,64,256]{2,1,0:T(8,128)S(1)} %get-tuple-element.60), channel_id=1, source_target_pairs={{0,2},{1,3},{2,0},{3,1},{4,6},{5,7},{6,4},{7,5},{8,10},{9,11},{10,... | collective-permute-start | bytes 589832 | tf_op jit(solution)/shard_map/ppermute | solution.py:35
  45.4 10.8 %collective-permute-start.10 = (f32[3,64,256]{2,1,0:T(8,128)S(1)}, f32[3,64,256]{2,1,0:T(8,128)S(1)}, u32[]{:S(2)}, u32[]{:S(2)}) collective-permute-start(f32[3,64,256]{2,1,0:T(8,128)S(1)} %add.24), channel_id=1, source_target_pairs={{0,16},{4,20},{8,24},{12,28},{16,0},{20,4},{24,8},{28,12},{1,17},{... | collective-permute-start | bytes 589832 | tf_op jit(solution)/shard_map/ppermute | solution.py:35
  56.3 5.7 %collective-permute-start.11 = (f32[3,64,256]{2,1,0:T(8,128)S(1)}, f32[3,64,256]{2,1,0:T(8,128)S(1)}, u32[]{:S(2)}, u32[]{:S(2)}) collective-permute-start(f32[3,64,256]{2,1,0:T(8,128)S(1)} %add.25), channel_id=1, source_target_pairs={{0,8},{4,12},{8,0},{12,4},{16,24},{20,28},{24,16},{28,20},{1,9},{5... | collective-permute-start | bytes 589832 | tf_op jit(solution)/shard_map/ppermute | solution.py:35
  62.1 25.6 %collective-permute-start.13 = (f32[2,2,256,256]{3,2,1,0:T(8,128)S(1)}, f32[2,2,256,256]{3,2,1,0:T(8,128)S(1)}, u32[]{:S(2)}, u32[]{:S(2)}) collective-permute-start(f32[2,2,256,256]{3,2,1,0:T(8,128)S(1)} %collective-permute-done.12.windows_ref), channel_id=1, source_target_pairs={{0,8},{4,28},{8,16},{12,4},{16,24},{20,12},{24,0},{28,20},{1,9},{5... | collective-permute-start | bytes 3145736 | tf_op jit(solution)/shard_map/ppermute | solution.py:40
  63.0 11.3 %collective-permute-start.16 = (f32[2,2,256,128]{3,2,1,0:T(8,128)S(1)}, f32[2,2,256,128]{3,2,1,0:T(8,128)S(1)}, u32[]{:S(2)}, u32[]{:S(2)}) collective-permute-start(f32[2,2,256,128]{3,2,1,0:T(8,128)S(1)} %get-tuple-element.69), channel_id=1, source_target_pairs={{1,2},{2,1},{5,6},{6,5},{9,10},{10,9},{13,14},{14,13},{17,18},{18,... | collective-permute-start | bytes 1572872 | tf_op jit(solution)/shard_map/ppermute | solution.py:46
  63.7 11.0 %collective-permute-start.17 = (f32[2,2,256,128]{3,2,1,0:T(8,128)S(1)}, f32[2,2,256,128]{3,2,1,0:T(8,128)S(1)}, u32[]{:S(2)}, u32[]{:S(2)}) collective-permute-start(f32[2,2,256,128]{3,2,1,0:T(8,128)S(1)} %get-tuple-element.70), channel_id=1, source_target_pairs={{0,1},{1,0},{2,3},{3,2},{4,5},{5,4},{6,7},{7,6},{8,9},{9,8},{10,11... | collective-permute-start | bytes 1572872 | tf_op jit(solution)/shard_map/ppermute | solution.py:35
  65.2 9.0 %collective-permute-start.14 = (f32[3,64,256]{2,1,0:T(8,128)S(1)}, f32[3,64,256]{2,1,0:T(8,128)S(1)}, u32[]{:S(2)}, u32[]{:S(2)}) collective-permute-start(f32[3,64,256]{2,1,0:T(8,128)S(1)} %add.26), channel_id=1, source_target_pairs={{0,4},{4,0},{8,12},{12,8},{16,20},{20,16},{24,28},{28,24},{1,5},{5... | collective-permute-start | bytes 589832 | tf_op jit(solution)/shard_map/ppermute | solution.py:35
  70.2 15.3 %collective-permute-start.19 = (f32[2,2,256,128]{3,2,1,0:T(8,128)S(1)}, f32[2,2,256,128]{3,2,1,0:T(8,128)S(1)}, u32[]{:S(2)}, u32[]{:S(2)}) collective-permute-start(f32[2,2,256,128]{3,2,1,0:T(8,128)S(1)} %get-tuple-element.73), channel_id=1, source_target_pairs={{1,2},{2,1},{5,6},{6,5},{9,10},{10,9},{13,14},{14,13},{17,18},{18,... | collective-permute-start | bytes 1572872 | tf_op jit(solution)/shard_map/ppermute | solution.py:46
  74.2 11.3 %collective-permute-start.20 = (f32[2,2,256,128]{3,2,1,0:T(8,128)S(1)}, f32[2,2,256,128]{3,2,1,0:T(8,128)S(1)}, u32[]{:S(2)}, u32[]{:S(2)}) collective-permute-start(f32[2,2,256,128]{3,2,1,0:T(8,128)S(1)} %get-tuple-element.74), channel_id=1, source_target_pairs={{0,1},{1,0},{2,3},{3,2},{4,5},{5,4},{6,7},{7,6},{8,9},{9,8},{10,11... | collective-permute-start | bytes 1572872 | tf_op jit(solution)/shard_map/ppermute | solution.py:35
  74.3 9.5 %collective-permute-start.15 = (f32[2,64,256]{2,1,0:T(8,128)S(1)}, f32[2,64,256]{2,1,0:T(8,128)S(1)}, u32[]{:S(2)}, u32[]{:S(2)}) collective-permute-start(f32[2,64,256]{2,1,0:T(8,128)S(1)} %illuminate.2.value_ref), channel_id=1, source_target_pairs={{0,2},{1,3},{2,0},{3,1},{4,6},{5,7},{6,4},{7,5},{8,10},{9,11},{10,... | collective-permute-start | bytes 393224 | tf_op jit(solution)/shard_map/ppermute | solution.py:35
  83.8 1.6 collective-permute-start.18
  89.0 2.0 %collective-permute-start.21 = (f32[2,2,256,128]{3,2,1,0:T(8,128)S(1)}, f32[2,2,256,128]{3,2,1,0:T(8,128)S(1)}, u32[]{:S(2)}, u32[]{:S(2)}) collective-permute-start(f32[2,2,256,128]{3,2,1,0:T(8,128)S(1)} %get-tuple-element.82), channel_id=1, source_target_pairs={{0,1},{1,0},{2,3},{3,2},{4,5},{5,4},{6,7},{7,6},{8,9},{9,8},{10,11... | collective-permute-start | bytes 1572872 | tf_op jit(solution)/shard_map/ppermute | solution.py:35
  89.1 1.9 %collective-permute-start.22 = (f32[2,2,256,128]{3,2,1,0:T(8,128)S(1)}, f32[2,2,256,128]{3,2,1,0:T(8,128)S(1)}, u32[]{:S(2)}, u32[]{:S(2)}) collective-permute-start(f32[2,2,256,128]{3,2,1,0:T(8,128)S(1)} %get-tuple-element.85), channel_id=1, source_target_pairs={{1,2},{2,1},{5,6},{6,5},{9,10},{10,9},{13,14},{14,13},{17,18},{18,... | collective-permute-start | bytes 1572872 | tf_op jit(solution)/shard_map/ppermute | solution.py:46
  97.5 10.8 %collective-permute-start.23 = (f32[3,128,256]{2,1,0:T(8,128)S(1)}, f32[3,128,256]{2,1,0:T(8,128)S(1)}, u32[]{:S(2)}, u32[]{:S(2)}) collective-permute-start(f32[3,128,256]{2,1,0:T(8,128)S(1)} %get-tuple-element.87), channel_id=1, source_target_pairs={{0,1},{1,0},{2,3},{3,2},{4,5},{5,4},{6,7},{7,6},{8,9},{9,8},{10,11... | collective-permute-start | bytes 1179656 | tf_op jit(solution)/shard_map/ppermute | solution.py:35
  106.6 24.2 %collective-permute-start.25 = (f32[2,2,256,256]{3,2,1,0:T(8,128)S(1)}, f32[2,2,256,256]{3,2,1,0:T(8,128)S(1)}, u32[]{:S(2)}, u32[]{:S(2)}) collective-permute-start(f32[2,2,256,256]{3,2,1,0:T(8,128)S(1)} %get-tuple-element.90.windows_ref), channel_id=1, source_target_pairs={{0,4},{4,8},{8,12},{12,16},{16,20},{20,24},{24,28},{1,5},{5,9},{9,... | collective-permute-start | bytes 3145736 | tf_op jit(solution)/shard_map/ppermute | solution.py:30
  108.4 6.9 %collective-permute-start.24 = (f32[3,64,256]{2,1,0:T(8,128)S(1)}, f32[3,64,256]{2,1,0:T(8,128)S(1)}, u32[]{:S(2)}, u32[]{:S(2)}) collective-permute-start(f32[3,64,256]{2,1,0:T(8,128)S(1)} %get-tuple-element.89), channel_id=1, source_target_pairs={{0,2},{1,3},{2,0},{3,1},{4,6},{5,7},{6,4},{7,5},{8,10},{9,11},{10,... | collective-permute-start | bytes 589832 | tf_op jit(solution)/shard_map/ppermute | solution.py:35
  115.3 15.5 %collective-permute-start.26 = (f32[2,2,256,128]{3,2,1,0:T(8,128)S(1)}, f32[2,2,256,128]{3,2,1,0:T(8,128)S(1)}, u32[]{:S(2)}, u32[]{:S(2)}) collective-permute-start(f32[2,2,256,128]{3,2,1,0:T(8,128)S(1)} %get-tuple-element.94), channel_id=1, source_target_pairs={{0,1},{1,2},{2,3},{3,0},{4,5},{5,6},{6,7},{7,4},{8,9},{9,10},{10,1... | collective-permute-start | bytes 1572872 | tf_op jit(solution)/shard_map/ppermute | solution.py:25
  130.8 6.7 %collective-permute-start.27 = (f32[3,64,256]{2,1,0:T(8,128)S(1)}, f32[3,64,256]{2,1,0:T(8,128)S(1)}, u32[]{:S(2)}, u32[]{:S(2)}) collective-permute-start(f32[3,64,256]{2,1,0:T(8,128)S(1)} %add.28), channel_id=1, source_target_pairs={{0,4},{4,0},{8,12},{12,8},{16,20},{20,16},{24,28},{28,24},{1,5},{5... | collective-permute-start | bytes 589832 | tf_op jit(solution)/shard_map/ppermute | solution.py:35
  134.4 19.5 %collective-permute-start.30 = (f32[2,2,256,128]{3,2,1,0:T(8,128)S(1)}, f32[2,2,256,128]{3,2,1,0:T(8,128)S(1)}, u32[]{:S(2)}, u32[]{:S(2)}) collective-permute-start(f32[2,2,256,128]{3,2,1,0:T(8,128)S(1)} %get-tuple-element.98), channel_id=1, source_target_pairs={{0,1},{1,2},{2,3},{3,0},{4,5},{5,6},{6,7},{7,4},{8,9},{9,10},{10,1... | collective-permute-start | bytes 1572872 | tf_op jit(solution)/shard_map/ppermute | solution.py:25
  137.6 6.2 %collective-permute-start.28 = (f32[3,64,256]{2,1,0:T(8,128)S(1)}, f32[3,64,256]{2,1,0:T(8,128)S(1)}, u32[]{:S(2)}, u32[]{:S(2)}) collective-permute-start(f32[3,64,256]{2,1,0:T(8,128)S(1)} %add.29), channel_id=1, source_target_pairs={{0,8},{4,12},{8,0},{12,4},{16,24},{20,28},{24,16},{28,20},{1,9},{5... | collective-permute-start | bytes 589832 | tf_op jit(solution)/shard_map/ppermute | solution.py:35
  143.8 10.1 %collective-permute-start.29 = (f32[3,64,256]{2,1,0:T(8,128)S(1)}, f32[3,64,256]{2,1,0:T(8,128)S(1)}, u32[]{:S(2)}, u32[]{:S(2)}) collective-permute-start(f32[3,64,256]{2,1,0:T(8,128)S(1)} %add.30), channel_id=1, source_target_pairs={{0,16},{4,20},{8,24},{12,28},{16,0},{20,4},{24,8},{28,12},{1,17},{... | collective-permute-start | bytes 589832 | tf_op jit(solution)/shard_map/ppermute | solution.py:35
  154.0 5.0 %collective-permute-start.31 = (f32[2,64,256]{2,1,0:T(8,128)S(1)}, f32[2,64,256]{2,1,0:T(8,128)S(1)}, u32[]{:S(2)}, u32[]{:S(2)}) collective-permute-start(f32[2,64,256]{2,1,0:T(8,128)S(1)} %illuminate.3.value_ref), channel_id=1, source_target_pairs={{0,2},{1,3},{2,0},{3,1},{4,6},{5,7},{6,4},{7,5},{8,10},{9,11},{10,... | collective-permute-start | bytes 393224 | tf_op jit(solution)/shard_map/ppermute | solution.py:35
  (6 other events, 99.2 us)

commit v10 on v7

--- a/solution.py
+++ b/solution.py
@@ -23,6 +23,11 @@
 def shifted(array, axis, by):
     peers = lax.axis_size(axis)
     return lax.ppermute(array, axis, [(i, (i + by) % peers) for i in range(peers)])
+
+
+def moved_on(array, axis):
+    peers = lax.axis_size(axis)
+    return lax.ppermute(array, axis, [(i, i + 1) for i in range(peers - 1)])
 
 
 def swapped(array, axis, mask):
@@ -642,17 +647,17 @@
     kept, sent, own = scan_step(1, True, offsets, probe, measured, table, field)
     total, middle_right = place(1, offsets, own, tile, 1)
     dense = density(1, False, around, probe, tile)
-    upper = shifted(own, "row", 1)
+    upper = moved_on(own, "row")
     came = swapped(sent, "col", 1)
     for bit in range(1, col_bits):
         kept, sent = fold(bit, kept, came)
         came = swapped(sent, "col", 1 << bit)
     came, middle_right, dense = tied(came, middle_right, dense)
     sums = kept + came
-    left_rest = shifted(middle_right, "col", 1)
+    left_rest = moved_on(middle_right, "col")
     sums, upper, left_rest = tied(sums, upper, left_rest)
     top, right_top = gather(1, never_below, near, total, upper, 1)
-    left_top = shifted(right_top, "col", 1)
+    left_top = moved_on(right_top, "col")
     for bit in range(row_bits):
         sums = sums + swapped(sums, "row", 1 << bit)
     sums, left_top = tied(sums, left_top)

time: 163 us -> 163 us (level)
  starting transfers between devices: 39.3 us -> 50.7 us
  waiting for transfers between devices: 93.3 us -> 82.1 us
    ppermute x11 -> x8, waiting for transfers between devices: 34.8 us -> 15.7 us  [shifted(): lax.ppermute(array, axis, [(i, (i + by) % peers) for i in range(peers)])]
    ppermute x0 -> x3, waiting for transfers between devices: none -> 14.2 us  [moved_on(): return lax.ppermute(array, axis, [(i, i + 1) for i in range(peers - 1)])]
    ppermute x18, starting transfers between devices: 22.3 us -> 29.5 us  [swapped(): return lax.ppermute(array, axis, [(i, i ^ mask) for i in range(peers)])]
    ppermute x18, waiting for transfers between devices: 56.3 us -> 49.8 us  [swapped(): return lax.ppermute(array, axis, [(i, i ^ mask) for i in range(peers)])]
    ppermute x0 -> x3, starting transfers between devices: none -> 4.29 us  [moved_on(): return lax.ppermute(array, axis, [(i, i + 1) for i in range(peers - 1)])]
    ppermute x11 -> x8, starting transfers between devices: 14.1 us -> 14 us  [shifted(): lax.ppermute(array, axis, [(i, (i + by) % peers) for i in range(peers)])]
  transfers between devices with their start and end apart: 33 -> 33, of which waited for: 19 -> 18; matrix products, arithmetic and copies ran while one was open for 1% -> 1% of each run, Pallas kernels for 8% -> 7%
where the time goes in v10:
time: 163 us; the launch traced here: 162 us
  waiting for transfers between devices  82.1 us (50%)
  starting transfers between devices  50.7 us (31%)
  Pallas kernels  25.8 us (16%)
  local copies, waits for them, and re-layouts  2.61 us (2%)
    ppermute x18, waiting for transfers between devices, swapped(): return lax.ppermute(array, axis, [(i, i ^ mask) for i in range(peers)])  49.8 us
    ppermute x18, starting transfers between devices, swapped(): return lax.ppermute(array, axis, [(i, i ^ mask) for i in range(peers)])  29.5 us
    ppermute x8, waiting for transfers between devices, shifted(): lax.ppermute(array, axis, [(i, (i + by) % peers) for i in range(peers)])  15.7 us
    ppermute x3, waiting for transfers between devices, moved_on(): return lax.ppermute(array, axis, [(i, i + 1) for i in range(peers - 1)])  14.2 us
    ppermute x8, starting transfers between devices, shifted(): lax.ppermute(array, axis, [(i, (i + by) % peers) for i in range(peers)])  14 us
    pallas_call x2, Pallas kernels, scan_step(): pl.pallas_call(functools.partial(scan_kernel, sweep, last, counts), out_s...  9.8 us
    ppermute x3, starting transfers between devices, moved_on(): return lax.ppermute(array, axis, [(i, i + 1) for i in range(peers - 1)])  4.29 us
    pallas_call x2, Pallas kernels, density(): pl.pallas_call(functools.partial(density_kernel, sweep, reach), out_shape...  4.22 us
  transfers between devices with their start and end apart: 33, of which 18 were waited for; matrix products, arithmetic and copies ran while one was open for 1% of the time, Pallas kernels for 7%

profile of v10, /device:TPU:0, one launch (start us, length us, event | category | flops | bytes accessed | tf_op | source)
XLA Modules:
  0.0 162.5 jit_solution(8316063840389526190)
XLA Ops:
  1.9 6.1 %collective-permute-start.1 = (f32[2,256,256]{2,1,0:T(8,128)S(1)}, f32[2,256,256]{2,1,0:T(8,128)S(1)}, u32[]{:S(2)}, u32[]{:S(2)}) collective-permute-start(f32[2,256,256]{2,1,0:T(8,128)S(1)} %slice.10), channel_id=1, source_target_pairs={{0,28},{4,0},{8,4},{12,8},{16,12},{20,16},{24,20},{28,24},{1,29},{... | collective-permute-start | bytes 1572872 | tf_op jit(solution)/shard_map/ppermute | solution.py:25
  12.1 3.4 %collective-permute-start.4 = (f32[2,256,256]{2,1,0:T(8,128)S(1)}, f32[2,256,256]{2,1,0:T(8,128)S(1)}, u32[]{:S(2)}, u32[]{:S(2)}) collective-permute-start(f32[2,256,256]{2,1,0:T(8,128)S(1)} %slice.11), channel_id=1, source_target_pairs={{0,28},{4,0},{8,4},{12,8},{16,12},{20,16},{24,20},{28,24},{1,29},{... | collective-permute-start | bytes 1572872 | tf_op jit(solution)/shard_map/ppermute | solution.py:25
  15.5 4.9 %collective-permute-done.3 = s32[1,1,2,2,2]{4,3,2,1,0:T(2,128)S(1)} collective-permute-done((s32[1,1,2,2,2]{4,3,2,1,0:T(2,128)S(1)}, s32[1,1,2,2,2]{4,3,2,1,0:T(2,128)S(1)}, u32[]{:S(2)}, u32[]{:S(2)}) %collective-permute-start.3) | collective-permute-done | bytes 64 | tf_op jit(solution)/shard_map/ppermute | solution.py:25
  21.0 9.4 %collective-permute-done.4.refs_6_.refs_3_ = f32[2,256,256]{2,1,0:T(8,128)S(1)} collective-permute-done((f32[2,256,256]{2,1,0:T(8,128)S(1)}, f32[2,256,256]{2,1,0:T(8,128)S(1)}, u32[]{:S(2)}, u32[]{:S(2)}) %collective-permute-start.4) | collective-permute-done | bytes 524320 | tf_op jit(solution)/shard_map/ppermute | solution.py:25
  30.5 5.1 %scan.2 = (f32[3,128,256]{2,1,0:T(8,128)S(1)}, f32[3,128,256]{2,1,0:T(8,128)S(1)}, f32[2,2,256,256]{3,2,1,0:T(8,128)S(1)}) custom-call(s32[1,1,2,2,2]{4,3,2,1,0:T(2,128)S(1)} %copy-done.2, f32[2,256,256]{2,1,0:T(8,128)S(1)} %copy-done.1, bf16[2,2,256,256]{3,2,1,0:T(8,128)(2,1)S(1)} %reorder.1.refs_1_, bf16[8,256,256]{2,1,0:T(8,128)(2,1)S(1)} %copy-done.4, ...), custom_call_target="tpu_custom_call" | custom-call | flops 7000000000 | bytes 12582912 | tf_op jit(solution)/shard_map/scan/pallas_call | solution.py:299
  39.2 1.5 collective-permute-start.7
  40.8 4.6 %collective-permute-done.7 = f32[3,64,256]{2,1,0:T(8,128)S(1)} collective-permute-done((f32[3,64,256]{2,1,0:T(8,128)S(1)}, f32[3,64,256]{2,1,0:T(8,128)S(1)}, u32[]{:S(2)}, u32[]{:S(2)}) %collective-permute-start.7) | collective-permute-done | bytes 196640 | tf_op jit(solution)/shard_map/ppermute | solution.py:35
  45.4 2.7 %collective-permute-start.10 = (f32[3,64,256]{2,1,0:T(8,128)S(1)}, f32[3,64,256]{2,1,0:T(8,128)S(1)}, u32[]{:S(2)}, u32[]{:S(2)}) collective-permute-start(f32[3,64,256]{2,1,0:T(8,128)S(1)} %add.24), channel_id=1, source_target_pairs={{0,16},{4,20},{8,24},{12,28},{16,0},{20,4},{24,8},{28,12},{1,17},{... | collective-permute-start | bytes 589832 | tf_op jit(solution)/shard_map/ppermute | solution.py:35
  48.1 2.5 %density.2.refs_5_ = f32[6,768,128]{2,1,0:T(8,128)S(1)} custom-call(s32[3,3,2,2,2]{4,3,2,1,0:T(2,128)S(1)} %constant_dynamic-update-slice_fusion.offsets_ref, f32[2,256,256]{2,1,0:T(8,128)S(1)} %copy-done.1), custom_call_target="tpu_custom_call" | custom-call | flops 1000000 | bytes 6291456 | tf_op jit(solution)/shard_map/density/pallas_call | solution.py:376
  51.9 4.4 %collective-permute-done.10 = f32[3,64,256]{2,1,0:T(8,128)S(1)} collective-permute-done((f32[3,64,256]{2,1,0:T(8,128)S(1)}, f32[3,64,256]{2,1,0:T(8,128)S(1)}, u32[]{:S(2)}, u32[]{:S(2)}) %collective-permute-start.10) | collective-permute-done | bytes 196640 | tf_op jit(solution)/shard_map/ppermute | solution.py:35
  56.6 5.5 %collective-permute-done.11 = f32[3,64,256]{2,1,0:T(8,128)S(1)} collective-permute-done((f32[3,64,256]{2,1,0:T(8,128)S(1)}, f32[3,64,256]{2,1,0:T(8,128)S(1)}, u32[]{:S(2)}, u32[]{:S(2)}) %collective-permute-start.11) | collective-permute-done | bytes 196640 | tf_op jit(solution)/shard_map/ppermute | solution.py:35
  63.7 1.5 collective-permute-start.17
  65.2 3.8 %collective-permute-start.14 = (f32[3,64,256]{2,1,0:T(8,128)S(1)}, f32[3,64,256]{2,1,0:T(8,128)S(1)}, u32[]{:S(2)}, u32[]{:S(2)}) collective-permute-start(f32[3,64,256]{2,1,0:T(8,128)S(1)} %add.26), channel_id=1, source_target_pairs={{0,4},{4,0},{8,12},{12,8},{16,20},{20,16},{24,28},{28,24},{1,5},{5... | collective-permute-start | bytes 589832 | tf_op jit(solution)/shard_map/ppermute | solution.py:35
  71.2 3.0 %collective-permute-done.14 = f32[3,64,256]{2,1,0:T(8,128)S(1)} collective-permute-done((f32[3,64,256]{2,1,0:T(8,128)S(1)}, f32[3,64,256]{2,1,0:T(8,128)S(1)}, u32[]{:S(2)}, u32[]{:S(2)}) %collective-permute-start.14) | collective-permute-done | bytes 196640 | tf_op jit(solution)/shard_map/ppermute | solution.py:35
  74.6 8.9 %collective-permute-done.15.other_ref = f32[2,64,256]{2,1,0:T(8,128)S(1)} collective-permute-done((f32[2,64,256]{2,1,0:T(8,128)S(1)}, f32[2,64,256]{2,1,0:T(8,128)S(1)}, u32[]{:S(2)}, u32[]{:S(2)}) %collective-permute-start.15) | collective-permute-done | bytes 131104 | tf_op jit(solution)/shard_map/ppermute | solution.py:35
  83.6 1.5 collective-permute-done.18.other_ref
  85.2 2.5 %collective-permute-done.13.windows_ref = f32[2,2,256,256]{3,2,1,0:T(8,128)S(1)} collective-permute-done((f32[2,2,256,256]{3,2,1,0:T(8,128)S(1)}, f32[2,2,256,256]{3,2,1,0:T(8,128)S(1)}, u32[]{:S(2)}, u32[]{:S(2)}) %collective-permute-start.13) | collective-permute-done | bytes 1048608 | tf_op jit(solution)/shard_map/ppermute | solution.py:40
  91.0 1.8 %widen.1.refs_3_.field_ref = f32[2,6,768,128]{3,2,1,0:T(8,128)S(1)} custom-call(f32[2,512,512]{2,1,0:T(8,128)S(1)} %copy-done, f32[2,512,256]{2,1,0:T(8,128)S(1)} %collective-permute-done.refs_4_.refs_1_, f32[2,256,256]{2,1,0:T(8,128)S(1)} %collective-permute-done.1.refs_5_.refs_2_, f32[2,256,256]{2,1,0:T(8,128)S(1)} %collective-permute-done.4.refs_6_.refs_3_, ...), custom_call_target="tpu_custom_call" | custom-call | flops 4000000 | bytes 20971520 | tf_op jit(solution)/shard_map/widen/pallas_call | solution.py:488
  92.8 4.7 %scan.3 = (f32[3,128,256]{2,1,0:T(8,128)S(1)}, f32[3,128,256]{2,1,0:T(8,128)S(1)}, f32[2,2,256,256]{3,2,1,0:T(8,128)S(1)}) custom-call(s32[1,1,2,2,2]{4,3,2,1,0:T(2,128)S(1)} %copy-done.2, f32[2,256,256]{2,1,0:T(8,128)S(1)} %join.5.refs_0_.probe_ref, bf16[2,2,256,256]{3,2,1,0:T(8,128)(2,1)S(1)} %reorder.1.refs_1_, bf16[8,256,256]{2,1,0:T(8,128)(2,1)S(1)} %copy-done.4, ...), custom_call_target="tpu_custom_call" | custom-call | flops 7000000000 | bytes 12582912 | tf_op jit(solution)/shard_map/scan/pallas_call | solution.py:299
  97.4 9.2 %collective-permute-start.23 = (f32[3,128,256]{2,1,0:T(8,128)S(1)}, f32[3,128,256]{2,1,0:T(8,128)S(1)}, u32[]{:S(2)}, u32[]{:S(2)}) collective-permute-start(f32[3,128,256]{2,1,0:T(8,128)S(1)} %get-tuple-element.87), channel_id=1, source_target_pairs={{0,1},{1,0},{2,3},{3,2},{4,5},{5,4},{6,7},{7,6},{8,9},{9,8},{10,11... | collective-permute-start | bytes 1179656 | tf_op jit(solution)/shard_map/ppermute | solution.py:35
  106.6 1.7 %collective-permute-start.25 = (f32[2,2,256,256]{3,2,1,0:T(8,128)S(1)}, f32[2,2,256,256]{3,2,1,0:T(8,128)S(1)}, u32[]{:S(2)}, u32[]{:S(2)}) collective-permute-start(f32[2,2,256,256]{3,2,1,0:T(8,128)S(1)} %get-tuple-element.90.windows_ref), channel_id=1, source_target_pairs={{0,4},{4,8},{8,12},{12,16},{16,20},{20,24},{24,28},{1,5},{5,9},{9,... | collective-permute-start | bytes 3145736 | tf_op jit(solution)/shard_map/ppermute | solution.py:30
  108.7 1.7 %density.3.density_ref = f32[4,512,128]{2,1,0:T(8,128)S(1)} custom-call(s32[3,3,2,2,2]{4,3,2,1,0:T(2,128)S(1)} %constant_dynamic-update-slice_fusion.offsets_ref, f32[2,256,256]{2,1,0:T(8,128)S(1)} %join.5.refs_0_.probe_ref), custom_call_target="tpu_custom_call" | custom-call | flops 1000000 | bytes 6291456 | tf_op jit(solution)/shard_map/density/pallas_call | solution.py:376
  111.8 3.5 %collective-permute-done.24 = f32[3,64,256]{2,1,0:T(8,128)S(1)} collective-permute-done((f32[3,64,256]{2,1,0:T(8,128)S(1)}, f32[3,64,256]{2,1,0:T(8,128)S(1)}, u32[]{:S(2)}, u32[]{:S(2)}) %collective-permute-start.24) | collective-permute-done | bytes 196640 | tf_op jit(solution)/shard_map/ppermute | solution.py:35
  116.6 14.2 %collective-permute-done.25.windows_ref = f32[2,2,256,256]{3,2,1,0:T(8,128)S(1)} collective-permute-done((f32[2,2,256,256]{3,2,1,0:T(8,128)S(1)}, f32[2,2,256,256]{3,2,1,0:T(8,128)S(1)}, u32[]{:S(2)}, u32[]{:S(2)}) %collective-permute-start.25) | collective-permute-done | bytes 1048608 | tf_op jit(solution)/shard_map/ppermute | solution.py:30
  130.8 2.5 %collective-permute-start.27 = (f32[3,64,256]{2,1,0:T(8,128)S(1)}, f32[3,64,256]{2,1,0:T(8,128)S(1)}, u32[]{:S(2)}, u32[]{:S(2)}) collective-permute-start(f32[3,64,256]{2,1,0:T(8,128)S(1)} %add.28), channel_id=1, source_target_pairs={{0,4},{4,0},{8,12},{12,8},{16,20},{20,16},{24,28},{28,24},{1,5},{5... | collective-permute-start | bytes 589832 | tf_op jit(solution)/shard_map/ppermute | solution.py:35
  135.8 1.8 %collective-permute-done.27 = f32[3,64,256]{2,1,0:T(8,128)S(1)} collective-permute-done((f32[3,64,256]{2,1,0:T(8,128)S(1)}, f32[3,64,256]{2,1,0:T(8,128)S(1)}, u32[]{:S(2)}, u32[]{:S(2)}) %collective-permute-start.27) | collective-permute-done | bytes 196640 | tf_op jit(solution)/shard_map/ppermute | solution.py:35
  137.6 2.3 %collective-permute-start.28 = (f32[3,64,256]{2,1,0:T(8,128)S(1)}, f32[3,64,256]{2,1,0:T(8,128)S(1)}, u32[]{:S(2)}, u32[]{:S(2)}) collective-permute-start(f32[3,64,256]{2,1,0:T(8,128)S(1)} %add.29), channel_id=1, source_target_pairs={{0,8},{4,12},{8,0},{12,4},{16,24},{20,28},{24,16},{28,20},{1,9},{5... | collective-permute-start | bytes 589832 | tf_op jit(solution)/shard_map/ppermute | solution.py:35
  139.8 4.3 %collective-permute-done.28 = f32[3,64,256]{2,1,0:T(8,128)S(1)} collective-permute-done((f32[3,64,256]{2,1,0:T(8,128)S(1)}, f32[3,64,256]{2,1,0:T(8,128)S(1)}, u32[]{:S(2)}, u32[]{:S(2)}) %collective-permute-start.28) | collective-permute-done | bytes 196640 | tf_op jit(solution)/shard_map/ppermute | solution.py:35
  144.1 3.4 %collective-permute-start.29 = (f32[3,64,256]{2,1,0:T(8,128)S(1)}, f32[3,64,256]{2,1,0:T(8,128)S(1)}, u32[]{:S(2)}, u32[]{:S(2)}) collective-permute-start(f32[3,64,256]{2,1,0:T(8,128)S(1)} %add.30), channel_id=1, source_target_pairs={{0,16},{4,20},{8,24},{12,28},{16,0},{20,4},{24,8},{28,12},{1,17},{... | collective-permute-start | bytes 589832 | tf_op jit(solution)/shard_map/ppermute | solution.py:35
  147.6 7.3 %collective-permute-done.29 = f32[3,64,256]{2,1,0:T(8,128)S(1)} collective-permute-done((f32[3,64,256]{2,1,0:T(8,128)S(1)}, f32[3,64,256]{2,1,0:T(8,128)S(1)}, u32[]{:S(2)}, u32[]{:S(2)}) %collective-permute-start.29) | collective-permute-done | bytes 196640 | tf_op jit(solution)/shard_map/ppermute | solution.py:35
  155.8 1.8 %renew.1 = f32[2,512,512]{2,1,0:T(8,128)} custom-call(f32[2,6,768,128]{3,2,1,0:T(8,128)S(1)} %widen.1.refs_3_.field_ref, f32[4,512,128]{2,1,0:T(8,128)S(1)} %density.3.density_ref, f32[2,6,768,128]{3,2,1,0:T(8,128)S(1)} %get-tuple-element.96.total_ref, f32[2,6,256,128]{3,2,1,0:T(8,128)S(1)} %get-tuple-element.101.top_ref, ...), custom_call_target="tpu_custom_call" | custom-call | flops 4000000 | bytes 10485760 | tf_op jit(solution)/shard_map/renew/pallas_call | solution.py:516
  157.6 2.4 %collective-permute-done.31.other_ref = f32[2,64,256]{2,1,0:T(8,128)S(1)} collective-permute-done((f32[2,64,256]{2,1,0:T(8,128)S(1)}, f32[2,64,256]{2,1,0:T(8,128)S(1)}, u32[]{:S(2)}, u32[]{:S(2)}) %collective-permute-start.31) | collective-permute-done | bytes 131104 | tf_op jit(solution)/shard_map/ppermute | solution.py:35
  (79 shorter events, 27.8 us)
Async XLA Ops:
  1.9 18.4 %collective-permute-start.1 = (f32[2,256,256]{2,1,0:T(8,128)S(1)}, f32[2,256,256]{2,1,0:T(8,128)S(1)}, u32[]{:S(2)}, u32[]{:S(2)}) collective-permute-start(f32[2,256,256]{2,1,0:T(8,128)S(1)} %slice.10), channel_id=1, source_target_pairs={{0,28},{4,0},{8,4},{12,8},{16,12},{20,16},{24,20},{28,24},{1,29},{... | collective-permute-start | bytes 1572872 | tf_op jit(solution)/shard_map/ppermute | solution.py:25
  9.3 21.2 %collective-permute-start = (f32[2,512,256]{2,1,0:T(8,128)S(1)}, f32[2,512,256]{2,1,0:T(8,128)S(1)}, u32[]{:S(2)}, u32[]{:S(2)}) collective-permute-start(f32[2,512,256]{2,1,0:T(8,128)S(1)} %slice.9), channel_id=1, source_target_pairs={{0,3},{1,0},{2,1},{3,2},{4,7},{5,4},{6,5},{7,6},{8,11},{9,8},{10,9... | collective-permute-start | bytes 3145736 | tf_op jit(solution)/shard_map/ppermute | solution.py:25
  10.0 10.4 %collective-permute-start.3 = (s32[1,1,2,2,2]{4,3,2,1,0:T(2,128)S(1)}, s32[1,1,2,2,2]{4,3,2,1,0:T(2,128)S(1)}, u32[]{:S(2)}, u32[]{:S(2)}) collective-permute-start(s32[1,1,2,2,2]{4,3,2,1,0:T(2,128)S(1)} %copy-done.2), channel_id=1, source_target_pairs={{0,28},{4,0},{8,4},{12,8},{16,12},{20,16},{24,20},{28,24},{1,29},{... | collective-permute-start | bytes 104 | tf_op jit(solution)/shard_map/ppermute | solution.py:25
  10.7 9.7 %collective-permute-start.2 = (s32[1,1,2,2,2]{4,3,2,1,0:T(2,128)S(1)}, s32[1,1,2,2,2]{4,3,2,1,0:T(2,128)S(1)}, u32[]{:S(2)}, u32[]{:S(2)}) collective-permute-start(s32[1,1,2,2,2]{4,3,2,1,0:T(2,128)S(1)} %copy-done.2), channel_id=1, source_target_pairs={{0,4},{4,8},{8,12},{12,16},{16,20},{20,24},{24,28},{28,0},{1,5},{5... | collective-permute-start | bytes 104 | tf_op jit(solution)/shard_map/ppermute | solution.py:25
  12.1 18.4 %collective-permute-start.4 = (f32[2,256,256]{2,1,0:T(8,128)S(1)}, f32[2,256,256]{2,1,0:T(8,128)S(1)}, u32[]{:S(2)}, u32[]{:S(2)}) collective-permute-start(f32[2,256,256]{2,1,0:T(8,128)S(1)} %slice.11), channel_id=1, source_target_pairs={{0,28},{4,0},{8,4},{12,8},{16,12},{20,16},{24,20},{28,24},{1,29},{... | collective-permute-start | bytes 1572872 | tf_op jit(solution)/shard_map/ppermute | solution.py:25
  20.4 10.1 %collective-permute-start.5 = (f32[2,256,256]{2,1,0:T(8,128)S(1)}, f32[2,256,256]{2,1,0:T(8,128)S(1)}, u32[]{:S(2)}, u32[]{:S(2)}) collective-permute-start(f32[2,256,256]{2,1,0:T(8,128)S(1)} %collective-permute-done.1.refs_5_.refs_2_), channel_id=1, source_target_pairs={{0,3},{1,0},{2,1},{3,2},{4,7},{5,4},{6,5},{7,6},{8,11},{9,8},{10,9... | collective-permute-start | bytes 1572872 | tf_op jit(solution)/shard_map/ppermute | solution.py:25
  35.6 26.5 %collective-permute-start.12 = (f32[2,2,256,256]{3,2,1,0:T(8,128)S(1)}, f32[2,2,256,256]{3,2,1,0:T(8,128)S(1)}, u32[]{:S(2)}, u32[]{:S(2)}) collective-permute-start(f32[2,2,256,256]{3,2,1,0:T(8,128)S(1)} %get-tuple-element.63.windows_ref), channel_id=1, source_target_pairs={{0,4},{4,0},{8,12},{12,8},{16,20},{20,16},{24,28},{28,24},{1,5},{5... | collective-permute-start | bytes 3145736 | tf_op jit(solution)/shard_map/ppermute | solution.py:35
  36.1 3.1 %collective-permute-start.6 = (f32[3,128,256]{2,1,0:T(8,128)S(1)}, f32[3,128,256]{2,1,0:T(8,128)S(1)}, u32[]{:S(2)}, u32[]{:S(2)}) collective-permute-start(f32[3,128,256]{2,1,0:T(8,128)S(1)} %get-tuple-element.58), channel_id=1, source_target_pairs={{0,1},{1,0},{2,3},{3,2},{4,5},{5,4},{6,7},{7,6},{8,9},{9,8},{10,11... | collective-permute-start | bytes 1179656 | tf_op jit(solution)/shard_map/ppermute | solution.py:35
  36.1 3.1 %collective-permute-start.8 = (s32[3,1,2,2,2]{4,3,2,1,0:T(2,128)S(1)}, s32[3,1,2,2,2]{4,3,2,1,0:T(2,128)S(1)}, u32[]{:S(2)}, u32[]{:S(2)}) collective-permute-start(s32[3,1,2,2,2]{4,3,2,1,0:T(2,128)S(1)} %pad_add_fusion.offsets_ref), channel_id=1, source_target_pairs={{0,1},{1,2},{2,3},{3,0},{4,5},{5,6},{6,7},{7,4},{8,9},{9,10},{10,1... | collective-permute-start | bytes 296 | tf_op jit(solution)/shard_map/ppermute | solution.py:25
  36.6 4.2 %collective-permute-start.9 = (s32[3,1,2,2,2]{4,3,2,1,0:T(2,128)S(1)}, s32[3,1,2,2,2]{4,3,2,1,0:T(2,128)S(1)}, u32[]{:S(2)}, u32[]{:S(2)}) collective-permute-start(s32[3,1,2,2,2]{4,3,2,1,0:T(2,128)S(1)} %pad_add_fusion.offsets_ref), channel_id=1, source_target_pairs={{0,3},{1,0},{2,1},{3,2},{4,7},{5,4},{6,5},{7,6},{8,11},{9,8},{10,9... | collective-permute-start | bytes 296 | tf_op jit(solution)/shard_map/ppermute | solution.py:25
  39.2 6.2 %collective-permute-start.7 = (f32[3,64,256]{2,1,0:T(8,128)S(1)}, f32[3,64,256]{2,1,0:T(8,128)S(1)}, u32[]{:S(2)}, u32[]{:S(2)}) collective-permute-start(f32[3,64,256]{2,1,0:T(8,128)S(1)} %get-tuple-element.60), channel_id=1, source_target_pairs={{0,2},{1,3},{2,0},{3,1},{4,6},{5,7},{6,4},{7,5},{8,10},{9,11},{10,... | collective-permute-start | bytes 589832 | tf_op jit(solution)/shard_map/ppermute | solution.py:35
  45.4 10.8 %collective-permute-start.10 = (f32[3,64,256]{2,1,0:T(8,128)S(1)}, f32[3,64,256]{2,1,0:T(8,128)S(1)}, u32[]{:S(2)}, u32[]{:S(2)}) collective-permute-start(f32[3,64,256]{2,1,0:T(8,128)S(1)} %add.24), channel_id=1, source_target_pairs={{0,16},{4,20},{8,24},{12,28},{16,0},{20,4},{24,8},{28,12},{1,17},{... | collective-permute-start | bytes 589832 | tf_op jit(solution)/shard_map/ppermute | solution.py:35
  56.3 5.7 %collective-permute-start.11 = (f32[3,64,256]{2,1,0:T(8,128)S(1)}, f32[3,64,256]{2,1,0:T(8,128)S(1)}, u32[]{:S(2)}, u32[]{:S(2)}) collective-permute-start(f32[3,64,256]{2,1,0:T(8,128)S(1)} %add.25), channel_id=1, source_target_pairs={{0,8},{4,12},{8,0},{12,4},{16,24},{20,28},{24,16},{28,20},{1,9},{5... | collective-permute-start | bytes 589832 | tf_op jit(solution)/shard_map/ppermute | solution.py:35
  62.1 25.6 %collective-permute-start.13 = (f32[2,2,256,256]{3,2,1,0:T(8,128)S(1)}, f32[2,2,256,256]{3,2,1,0:T(8,128)S(1)}, u32[]{:S(2)}, u32[]{:S(2)}) collective-permute-start(f32[2,2,256,256]{3,2,1,0:T(8,128)S(1)} %collective-permute-done.12.windows_ref), channel_id=1, source_target_pairs={{0,8},{4,28},{8,16},{12,4},{16,24},{20,12},{24,0},{28,20},{1,9},{5... | collective-permute-start | bytes 3145736 | tf_op jit(solution)/shard_map/ppermute | solution.py:40
  63.0 11.3 %collective-permute-start.16 = (f32[2,2,256,128]{3,2,1,0:T(8,128)S(1)}, f32[2,2,256,128]{3,2,1,0:T(8,128)S(1)}, u32[]{:S(2)}, u32[]{:S(2)}) collective-permute-start(f32[2,2,256,128]{3,2,1,0:T(8,128)S(1)} %get-tuple-element.69), channel_id=1, source_target_pairs={{1,2},{2,1},{5,6},{6,5},{9,10},{10,9},{13,14},{14,13},{17,18},{18,... | collective-permute-start | bytes 1572872 | tf_op jit(solution)/shard_map/ppermute | solution.py:46
  63.7 11.0 %collective-permute-start.17 = (f32[2,2,256,128]{3,2,1,0:T(8,128)S(1)}, f32[2,2,256,128]{3,2,1,0:T(8,128)S(1)}, u32[]{:S(2)}, u32[]{:S(2)}) collective-permute-start(f32[2,2,256,128]{3,2,1,0:T(8,128)S(1)} %get-tuple-element.70), channel_id=1, source_target_pairs={{0,1},{1,0},{2,3},{3,2},{4,5},{5,4},{6,7},{7,6},{8,9},{9,8},{10,11... | collective-permute-start | bytes 1572872 | tf_op jit(solution)/shard_map/ppermute | solution.py:35
  65.2 9.0 %collective-permute-start.14 = (f32[3,64,256]{2,1,0:T(8,128)S(1)}, f32[3,64,256]{2,1,0:T(8,128)S(1)}, u32[]{:S(2)}, u32[]{:S(2)}) collective-permute-start(f32[3,64,256]{2,1,0:T(8,128)S(1)} %add.26), channel_id=1, source_target_pairs={{0,4},{4,0},{8,12},{12,8},{16,20},{20,16},{24,28},{28,24},{1,5},{5... | collective-permute-start | bytes 589832 | tf_op jit(solution)/shard_map/ppermute | solution.py:35
  70.5 14.7 %collective-permute-start.19 = (f32[2,2,256,128]{3,2,1,0:T(8,128)S(1)}, f32[2,2,256,128]{3,2,1,0:T(8,128)S(1)}, u32[]{:S(2)}, u32[]{:S(2)}) collective-permute-start(f32[2,2,256,128]{3,2,1,0:T(8,128)S(1)} %get-tuple-element.73), channel_id=1, source_target_pairs={{1,2},{2,1},{5,6},{6,5},{9,10},{10,9},{13,14},{14,13},{17,18},{18,... | collective-permute-start | bytes 1572872 | tf_op jit(solution)/shard_map/ppermute | solution.py:46
  74.2 11.0 %collective-permute-start.20 = (f32[2,2,256,128]{3,2,1,0:T(8,128)S(1)}, f32[2,2,256,128]{3,2,1,0:T(8,128)S(1)}, u32[]{:S(2)}, u32[]{:S(2)}) collective-permute-start(f32[2,2,256,128]{3,2,1,0:T(8,128)S(1)} %get-tuple-element.74), channel_id=1, source_target_pairs={{0,1},{1,0},{2,3},{3,2},{4,5},{5,4},{6,7},{7,6},{8,9},{9,8},{10,11... | collective-permute-start | bytes 1572872 | tf_op jit(solution)/shard_map/ppermute | solution.py:35
  74.2 9.3 %collective-permute-start.15 = (f32[2,64,256]{2,1,0:T(8,128)S(1)}, f32[2,64,256]{2,1,0:T(8,128)S(1)}, u32[]{:S(2)}, u32[]{:S(2)}) collective-permute-start(f32[2,64,256]{2,1,0:T(8,128)S(1)} %illuminate.2.value_ref), channel_id=1, source_target_pairs={{0,2},{1,3},{2,0},{3,1},{4,6},{5,7},{6,4},{7,5},{8,10},{9,11},{10,... | collective-permute-start | bytes 393224 | tf_op jit(solution)/shard_map/ppermute | solution.py:35
  89.0 2.0 %collective-permute-start.21 = (f32[2,2,256,128]{3,2,1,0:T(8,128)S(1)}, f32[2,2,256,128]{3,2,1,0:T(8,128)S(1)}, u32[]{:S(2)}, u32[]{:S(2)}) collective-permute-start(f32[2,2,256,128]{3,2,1,0:T(8,128)S(1)} %get-tuple-element.82), channel_id=1, source_target_pairs={{0,1},{1,0},{2,3},{3,2},{4,5},{5,4},{6,7},{7,6},{8,9},{9,8},{10,11... | collective-permute-start | bytes 1572872 | tf_op jit(solution)/shard_map/ppermute | solution.py:35
  89.1 1.9 %collective-permute-start.22 = (f32[2,2,256,128]{3,2,1,0:T(8,128)S(1)}, f32[2,2,256,128]{3,2,1,0:T(8,128)S(1)}, u32[]{:S(2)}, u32[]{:S(2)}) collective-permute-start(f32[2,2,256,128]{3,2,1,0:T(8,128)S(1)} %get-tuple-element.85), channel_id=1, source_target_pairs={{1,2},{2,1},{5,6},{6,5},{9,10},{10,9},{13,14},{14,13},{17,18},{18,... | collective-permute-start | bytes 1572872 | tf_op jit(solution)/shard_map/ppermute | solution.py:46
  97.4 10.8 %collective-permute-start.23 = (f32[3,128,256]{2,1,0:T(8,128)S(1)}, f32[3,128,256]{2,1,0:T(8,128)S(1)}, u32[]{:S(2)}, u32[]{:S(2)}) collective-permute-start(f32[3,128,256]{2,1,0:T(8,128)S(1)} %get-tuple-element.87), channel_id=1, source_target_pairs={{0,1},{1,0},{2,3},{3,2},{4,5},{5,4},{6,7},{7,6},{8,9},{9,8},{10,11... | collective-permute-start | bytes 1179656 | tf_op jit(solution)/shard_map/ppermute | solution.py:35
  106.6 24.2 %collective-permute-start.25 = (f32[2,2,256,256]{3,2,1,0:T(8,128)S(1)}, f32[2,2,256,256]{3,2,1,0:T(8,128)S(1)}, u32[]{:S(2)}, u32[]{:S(2)}) collective-permute-start(f32[2,2,256,256]{3,2,1,0:T(8,128)S(1)} %get-tuple-element.90.windows_ref), channel_id=1, source_target_pairs={{0,4},{4,8},{8,12},{12,16},{16,20},{20,24},{24,28},{1,5},{5,9},{9,... | collective-permute-start | bytes 3145736 | tf_op jit(solution)/shard_map/ppermute | solution.py:30
  108.4 6.9 %collective-permute-start.24 = (f32[3,64,256]{2,1,0:T(8,128)S(1)}, f32[3,64,256]{2,1,0:T(8,128)S(1)}, u32[]{:S(2)}, u32[]{:S(2)}) collective-permute-start(f32[3,64,256]{2,1,0:T(8,128)S(1)} %get-tuple-element.89), channel_id=1, source_target_pairs={{0,2},{1,3},{2,0},{3,1},{4,6},{5,7},{6,4},{7,5},{8,10},{9,11},{10,... | collective-permute-start | bytes 589832 | tf_op jit(solution)/shard_map/ppermute | solution.py:35
  115.3 15.5 %collective-permute-start.26 = (f32[2,2,256,128]{3,2,1,0:T(8,128)S(1)}, f32[2,2,256,128]{3,2,1,0:T(8,128)S(1)}, u32[]{:S(2)}, u32[]{:S(2)}) collective-permute-start(f32[2,2,256,128]{3,2,1,0:T(8,128)S(1)} %get-tuple-element.94), channel_id=1, source_target_pairs={{0,1},{1,2},{2,3},{4,5},{5,6},{6,7},{8,9},{9,10},{10,11},{12,13},{... | collective-permute-start | bytes 1572872 | tf_op jit(solution)/shard_map/ppermute | solution.py:30
  130.8 6.7 %collective-permute-start.27 = (f32[3,64,256]{2,1,0:T(8,128)S(1)}, f32[3,64,256]{2,1,0:T(8,128)S(1)}, u32[]{:S(2)}, u32[]{:S(2)}) collective-permute-start(f32[3,64,256]{2,1,0:T(8,128)S(1)} %add.28), channel_id=1, source_target_pairs={{0,4},{4,0},{8,12},{12,8},{16,20},{20,16},{24,28},{28,24},{1,5},{5... | collective-permute-start | bytes 589832 | tf_op jit(solution)/shard_map/ppermute | solution.py:35
  134.4 20.5 %collective-permute-start.30 = (f32[2,2,256,128]{3,2,1,0:T(8,128)S(1)}, f32[2,2,256,128]{3,2,1,0:T(8,128)S(1)}, u32[]{:S(2)}, u32[]{:S(2)}) collective-permute-start(f32[2,2,256,128]{3,2,1,0:T(8,128)S(1)} %get-tuple-element.98), channel_id=1, source_target_pairs={{0,1},{1,2},{2,3},{4,5},{5,6},{6,7},{8,9},{9,10},{10,11},{12,13},{... | collective-permute-start | bytes 1572872 | tf_op jit(solution)/shard_map/ppermute | solution.py:30
  137.6 6.6 %collective-permute-start.28 = (f32[3,64,256]{2,1,0:T(8,128)S(1)}, f32[3,64,256]{2,1,0:T(8,128)S(1)}, u32[]{:S(2)}, u32[]{:S(2)}) collective-permute-start(f32[3,64,256]{2,1,0:T(8,128)S(1)} %add.29), channel_id=1, source_target_pairs={{0,8},{4,12},{8,0},{12,4},{16,24},{20,28},{24,16},{28,20},{1,9},{5... | collective-permute-start | bytes 589832 | tf_op jit(solution)/shard_map/ppermute | solution.py:35
  144.1 10.8 %collective-permute-start.29 = (f32[3,64,256]{2,1,0:T(8,128)S(1)}, f32[3,64,256]{2,1,0:T(8,128)S(1)}, u32[]{:S(2)}, u32[]{:S(2)}) collective-permute-start(f32[3,64,256]{2,1,0:T(8,128)S(1)} %add.30), channel_id=1, source_target_pairs={{0,16},{4,20},{8,24},{12,28},{16,0},{20,4},{24,8},{28,12},{1,17},{... | collective-permute-start | bytes 589832 | tf_op jit(solution)/shard_map/ppermute | solution.py:35
  155.0 5.0 %collective-permute-start.31 = (f32[2,64,256]{2,1,0:T(8,128)S(1)}, f32[2,64,256]{2,1,0:T(8,128)S(1)}, u32[]{:S(2)}, u32[]{:S(2)}) collective-permute-start(f32[2,64,256]{2,1,0:T(8,128)S(1)} %illuminate.3.value_ref), channel_id=1, source_target_pairs={{0,2},{1,3},{2,0},{3,1},{4,6},{5,7},{6,4},{7,5},{8,10},{9,11},{10,... | collective-permute-start | bytes 393224 | tf_op jit(solution)/shard_map/ppermute | solution.py:35
  160.0 1.6 collective-permute-start.32
  (6 other events, 99.2 us)
